TPU v7x, 32 devices: a whole 2x2x4 slice. The times are simulated.
32 devices in a mesh: grp: 2 (over x), dof: 16 (over z, y, core).
Axes of the slice: x: 2, y: 2, z: 4, core: 2. Of those that a mesh axis runs over, the one named last changes fastest.
Arguments:
- forces: bfloat16 [2, 4096, 12288], P('grp', None, 'dof'), parts along dimension 0, may hold values from -6 to 6
- mode_shapes: bfloat16 [12288, 448], P('dof'), may hold values from -0.1875 to 0.1875
- frf: bfloat16 [512, 2, 448, 448], P('dof'), may hold values from -5 to 5
Outputs:
- displaced: bfloat16 [2, 4096, 12288], P('grp', None, 'dof'), parts along dimension 0
There are 2 independent parts, one for each index of `grp`. A program takes and returns all parts, laid end to end along the dimension named above; an argument that names none is the same for every part. Nothing has to cross between parts.
All inputs are finite; a program needn't handle non-finite values.
Results may differ from a plain program's by a relative error of at most 0.015.
Values may be sent and summed in bfloat16 or wider, within the bound.
No kernel may reach another device: no remote copies, remote signals or barrier semaphores. Data moves between devices by JAX's collectives and lax.ppermute only.
A program may use at most 192 MiB of HBM per device.

v0:
```python
import math

import jax
import jax.numpy as jnp
from jax import lax
from jax.sharding import PartitionSpec as P

FREQS = 512


def forward_table(steps, freqs):
    step_ids = jnp.arange(steps, dtype=jnp.int32)
    freq_ids = jnp.arange(freqs, dtype=jnp.int32)
    phase = step_ids[:, None] * freq_ids[None, :] % steps
    angle = phase.astype(jnp.float32) * (2.0 * math.pi / steps)
    table = jnp.stack([jnp.cos(angle), -jnp.sin(angle)], axis=1) * (1.0 / math.sqrt(steps))
    return table.astype(jnp.bfloat16)


def inverse_table(steps, freqs):
    step_ids = jnp.arange(steps, dtype=jnp.int32)
    freq_ids = jnp.arange(freqs, dtype=jnp.int32)
    phase = freq_ids[:, None] * step_ids[None, :] % steps
    angle = phase.astype(jnp.float32) * (2.0 * math.pi / steps)
    weights = jnp.where(freq_ids == 0, 0.5, 1.0).astype(jnp.float32)
    table = jnp.stack([jnp.cos(angle), -jnp.sin(angle)], axis=0) * weights[None, :, None]
    return (table * (2.0 / math.sqrt(steps))).astype(jnp.bfloat16)


def split_parts(values):
    upper = values.astype(jnp.bfloat16)
    lower = (values - upper.astype(jnp.float32)).astype(jnp.bfloat16)
    return (upper, lower)


def on_device(forces, mode_shapes, frf):
    steps = forces.shape[1]
    fwd = forward_table(steps, FREQS)
    columns = mode_shapes
    modal_force = lax.psum_scatter(
        jnp.einsum("rtd,dm->mrt", forces, columns, preferred_element_type=jnp.float32),
        "dof",
        scatter_dimension=0,
        tiled=True,
    )
    upper, lower = split_parts(modal_force)
    local_spec = jnp.einsum("mrt,tcf->frcm", upper, fwd, preferred_element_type=jnp.float32)
    local_spec = local_spec + jnp.einsum(
        "mrt,tcf->frcm", lower, fwd, preferred_element_type=jnp.float32
    )
    modal_spec = lax.all_to_all(
        local_spec.astype(jnp.bfloat16), "dof", split_axis=0, concat_axis=3, tiled=True
    )
    products = jnp.einsum("fanm,frbm->frabn", frf, modal_spec, preferred_element_type=jnp.float32)
    real_part = products[:, :, 0, 0] - products[:, :, 1, 1]
    imag_part = products[:, :, 0, 1] + products[:, :, 1, 0]
    response_spec = jnp.stack([real_part, imag_part], axis=2).astype(jnp.bfloat16)
    by_mode = lax.all_to_all(response_spec, "dof", split_axis=3, concat_axis=0, tiled=True)
    inv = inverse_table(steps, FREQS)
    modal_resp = jnp.einsum(
        "frcm,cft->mrt", by_mode, inv, preferred_element_type=jnp.float32
    ).astype(jnp.bfloat16)
    columns = mode_shapes
    displaced = jnp.einsum(
        "mrt,dm->rtd",
        lax.all_gather(modal_resp, "dof", axis=0, tiled=True),
        columns,
        preferred_element_type=jnp.float32,
    )
    return displaced.astype(jnp.bfloat16)


def solution(mesh):
    return jax.shard_map(
        on_device,
        mesh=mesh,
        in_specs=(P("grp", None, "dof"), P("dof", None), P("dof", None, None, None)),
        out_specs=P("grp", None, "dof"),
        check_vma=False,
    )
```

profile of v0, /device:TPU:0, one launch (start us, length us, event | category | flops | bytes accessed | tf_op | source)
XLA Modules:
  0.0 358.1 jit_solution(12627534911797543133)
XLA Ops:
  6.5 0.0 copy-start
  6.5 0.0 all-reduce.3.cloned.1.call-start
  6.5 1.1 copy-done
  7.6 5.2 %fusion.19 = f32[448,1,4096]{2,0,1:T(8,128)S(1)} fusion(bf16[768,448]{0,1:T(8,128)(2,1)S(1)} %copy-done, bf16[1,4096,768]{2,1,0:T(8,128)(2,1)} %param.3), kind=kOutput, calls=%fused_computation.29 | convolution fusion | flops 2818572288 | bytes 14319616 | tf_op jit(solution)/shard_map/rtd,dm->mrt/dot_general | solution.py:41
  12.8 0.0 copy-start.2
  12.8 9.0 %copy.28 = f32[448,1,4096]{2,1,0:T(1,128)} copy(f32[448,1,4096]{2,0,1:T(8,128)S(1)} %fusion.19) | data formatting | bytes 14680064 | tf_op jit(solution)/shard_map/rtd,dm->mrt/dot_general | solution.py:41
  21.8 0.0 all-reduce.3.cloned.1.call-update
  21.8 0.0 copy-done.2
  21.8 0.6 dynamic-slice
  23.0 34.6 %sine_negate_fusion = (f32[4096,1,512]{2,0,1:T(8,128)}, f32[4096,1,512]{2,0,1:T(8,128)}) fusion(), kind=kLoop, calls=%fused_computation.17 | loop fusion | flops 31457280 | bytes 16777216 | tf_op jit(solution)/shard_map/neg | solution.py:16
  57.7 121.7 %all-reduce.3.cloned.1.call-done = f32[448,1,4096]{2,1,0:T(1,128)} async-done(((f32[448,1,4096]{2,1,0:T(1,128)}), f32[448,1,4096]{2,1,0:T(1,128)}) %all-reduce.3.cloned.1.call-update) | async-done | bytes 7340048
  179.4 0.0 slice-start
  179.4 1.2 constant_dynamic-slice_fusion
  180.6 0.0 slice-start.1
  180.6 0.0 copy-start.1
  180.6 6.9 %fusion.41 = f32[2,512,28]{1,2,0:T(8,128)S(1)} fusion(f32[4096,1,512]{2,0,1:T(8,128)} %get-tuple-element.7, f32[4096,1,512]{2,0,1:T(8,128)} %get-tuple-element.8, f32[28,1,4096]{2,1,0:T(1,128)S(1)} %constant_dynamic-slice_fusion), kind=kOutput, calls=%fused_computation.46 | convolution fusion | flops 247463936 | bytes 17350656 | tf_op jit(solution)/shard_map/mrt,tcf->frcm/dot_general | solution.py:47
  187.5 0.0 slice-done
  187.5 0.6 slice-done.1
  188.1 2.4 copy-done.1
  190.4 1.5 fusion.37
  192.0 0.2 copy.31
  192.2 1.1 reshape.287
  193.3 4.7 %all-to-all-start = ((bf16[16,2,896]{2,1,0:T(2,128)(2,1)}), bf16[16,2,896]{2,1,0:T(2,128)(2,1)S(1)}, u32[]{:S(2)}, u32[]{:S(2)}) async-start(bf16[16,2,896]{2,1,0:T(2,128)(2,1)} %reshape.287), calls=%async_computation | async-start | bytes 114688 | tf_op jit(solution)/shard_map/all_to_all | solution.py:51
  197.9 34.5 %sine_negate_fusion.1 = (f32[1,512,4096]{2,1,0:T(8,128)}, f32[1,512,4096]{2,1,0:T(8,128)}) fusion(), kind=kLoop, calls=%fused_computation.20 | loop fusion | flops 31457280 | bytes 16777216 | tf_op jit(solution)/shard_map/neg | solution.py:26
  232.5 0.0 all-to-all-done
  232.5 0.6 reshape.288
  233.1 0.5 copy.41
  233.6 0.6 copy.42
  234.2 0.3 reshape.281
  234.5 13.3 %convolution_bitcast_fusion = f32[32,1,2,2,448]{4,3,2,0,1:T(2,128)S(1)} fusion(bf16[32,2,448,448]{3,2,1,0:T(8,128)(2,1)} %param.5, bf16[32,2,448,1]{2,1,0,3:T(2,128)(2,1)S(1)} %reshape.281), kind=kOutput, calls=%fused_computation.38 | convolution fusion | flops 51380224 | bytes 25976832 | tf_op jit(solution)/shard_map/fanm,frbm->frabn/dot_general | solution.py:54
  247.8 0.1 fusion.46
  248.0 0.2 copy.35
  248.2 0.9 reshape.289
  249.1 6.0 %all-to-all-start.1 = ((bf16[16,2,896]{2,1,0:T(2,128)(2,1)}), bf16[16,2,896]{2,1,0:T(2,128)(2,1)S(1)}, u32[]{:S(2)}, u32[]{:S(2)}) async-start(bf16[16,2,896]{2,1,0:T(2,128)(2,1)} %reshape.289), calls=%async_computation.1 | async-start | bytes 114688 | tf_op jit(solution)/shard_map/all_to_all | solution.py:58
  255.1 0.2 all-gather.2.cloned.1.call-start
  255.3 6.6 %all-to-all-done.1 = bf16[16,2,896]{2,1,0:T(2,128)(2,1)S(1)} async-done(((bf16[16,2,896]{2,1,0:T(2,128)(2,1)}), bf16[16,2,896]{2,1,0:T(2,128)(2,1)S(1)}, u32[]{:S(2)}, u32[]{:S(2)}) %all-to-all-start.1) | async-done | bytes 57376 | tf_op jit(solution)/shard_map/all_to_all | solution.py:58
  261.9 0.2 reshape.290
  262.1 0.2 reshape.285
  262.3 6.9 %fusion.29 = bf16[28,1,4096]{2,0,1:T(8,128)(2,1)S(1)} fusion(bf16[512,2,28]{0,2,1:T(8,128)(2,1)S(1)} %reshape.285, f32[1,512,4096]{2,1,0:T(8,128)} %get-tuple-element.9, f32[1,512,4096]{2,1,0:T(8,128)} %get-tuple-element.10, f32[512]{0:T(512)S(1)} %fusion.48), kind=kOutput, calls=%fused_computation.33 | convolution fusion | flops 251772928 | bytes 17065984 | tf_op jit(solution)/shard_map/frcm,cft->mrt/dot_general | solution.py:60
  269.3 1.3 copy.39
  270.5 0.0 all-gather.2.cloned.1.call-update
  270.6 65.7 %all-gather.2.cloned.1.call-done = bf16[448,1,4096]{2,1,0:T(2,128)(2,1)} async-done(((bf16[28,1,4096]{2,1,0:T(2,128)(2,1)}), bf16[448,1,4096]{2,1,0:T(2,128)(2,1)}) %all-gather.2.cloned.1.call-update) | async-done | bytes 3670032 | tf_op jit(solution)/shard_map/all_gather | solution.py:66
  336.3 15.0 %fusion.22 = bf16[1,4096,768]{2,1,0:T(8,128)(2,1)} fusion(bf16[768,448]{0,1:T(8,128)(2,1)S(1)} %copy-done, bf16[448,1,4096]{2,1,0:T(2,128)(2,1)} %all-gather.2.cloned.1.call-done), kind=kOutput, calls=%fused_computation.30 | convolution fusion | flops 2821718016 | bytes 10649600 | tf_op jit(solution)/shard_map/mrt,dm->rtd/dot_general | solution.py:64
  (6 shorter events, 0.1 us)
Async XLA Ops:
  6.5 1.1 copy-start
  6.5 172.8 %all-reduce.3.cloned.1.call-start = ((), (), s32[]{:S(2)}) async-start(), calls=%async_computation.3 | async-start | bytes 14680064
  12.8 9.0 %copy-start.2 = (u32[32]{0:T(128)S(1)}, u32[32]{0:T(128)}, u32[]{:S(2)}) copy-start(u32[32]{0:T(128)} %constant.38) | copy-start | bytes 388
  179.4 8.1 %slice-start = ((s8[8388608]{0:T(1024)(128)(4,1)}), s8[4194304]{0:T(1024)(128)(4,1)S(1)}, s32[]{:S(2)}) async-start(s8[8388608]{0:T(1024)(128)(4,1)} %bitcast.69), calls=%async_computation.4 | async-start | bytes 8388608
  180.6 7.5 %slice-start.1 = ((s8[8388608]{0:T(1024)(128)(4,1)}), s8[4194304]{0:T(1024)(128)(4,1)S(1)}, s32[]{:S(2)}) async-start(s8[8388608]{0:T(1024)(128)(4,1)} %bitcast.69), calls=%async_computation.5 | async-start | bytes 8388608
  180.6 9.8 %copy-start.1 = (f32[4096,1,512]{2,0,1:T(8,128)S(1)}, f32[4096,1,512]{2,0,1:T(8,128)}, u32[]{:S(2)}) copy-start(f32[4096,1,512]{2,0,1:T(8,128)} %get-tuple-element.8) | copy-start | bytes 25165828
  193.3 39.2 %all-to-all-start = ((bf16[16,2,896]{2,1,0:T(2,128)(2,1)}), bf16[16,2,896]{2,1,0:T(2,128)(2,1)S(1)}, u32[]{:S(2)}, u32[]{:S(2)}) async-start(bf16[16,2,896]{2,1,0:T(2,128)(2,1)} %reshape.287), calls=%async_computation | async-start | bytes 114688 | tf_op jit(solution)/shard_map/all_to_all | solution.py:51
  249.1 12.8 %all-to-all-start.1 = ((bf16[16,2,896]{2,1,0:T(2,128)(2,1)}), bf16[16,2,896]{2,1,0:T(2,128)(2,1)S(1)}, u32[]{:S(2)}, u32[]{:S(2)}) async-start(bf16[16,2,896]{2,1,0:T(2,128)(2,1)} %reshape.289), calls=%async_computation.1 | async-start | bytes 114688 | tf_op jit(solution)/shard_map/all_to_all | solution.py:58
  255.1 81.2 %all-gather.2.cloned.1.call-start = ((), (), s32[]{:S(2)}) async-start(), calls=%async_computation.2 | async-start | bytes 7798784 | tf_op jit(solution)/shard_map/all_gather | solution.py:66
Sparse Core Ops, SparseCore 0:
  21.9 157.4 all-reduce.2
  270.7 65.5 all-gather.1
where the time goes:
time: 358 us
  waiting for transfers between devices  194 us (54%)
  other arithmetic  69.3 us (19%)
  matrix products  48.8 us (14%)
  local copies, waits for them, and re-layouts  20.9 us (6%)
  between operations  14.2 us (4%)
  starting transfers between devices  10.9 us (3%)
    unnamed x3, waiting for transfers between devices  122 us
    all_gather x1, waiting for transfers between devices, on_device(): lax.all_gather(modal_resp, 'dof', axis=0, tiled=True)  65.7 us
    neg x1, other arithmetic, forward_table(): -jnp.sin(angle)  34.6 us
    neg x1, other arithmetic, inverse_table(): -jnp.sin(angle)  34.5 us
    dot_general x1, matrix products, on_device(): jnp.einsum('mrt,dm->rtd', lax.all_gather(modal_resp, 'dof', axis=0, tiled...  15 us
    dot_general x1, matrix products, on_device(): jnp.einsum('fanm,frbm->frabn', frf, modal_spec, preferred_element_type=jn...  13.3 us
    dot_general x1, local copies, waits for them, and re-layouts, on_device(): jnp.einsum('rtd,dm->mrt', forces, columns, preferred_element_type=jnp.flo...  8.96 us
    unnamed x18, local copies, waits for them, and re-layouts  8.69 us
  transfers between devices with their start and end apart: 4, of which 3 were waited for; matrix products, arithmetic and copies ran while one was open for 19% of the time, Pallas kernels for 0%

commit v1 on v0

v1 whole, which is shorter than its diff:
```python
import math

import jax
import jax.numpy as jnp
import numpy as np
from jax import lax
from jax.sharding import PartitionSpec as P

FREQS = 512


def half_tables(steps, devices):
    half = steps // 2
    freqs = np.arange(FREQS).reshape(devices, FREQS // devices // 2, 2)
    tables = []
    for parity in range(2):
        ids = freqs[:, :, parity].reshape(-1)
        phase = ids[:, None].astype(np.int64) * np.arange(half)[None, :] % steps
        angle = phase * (2.0 * math.pi / steps)
        table = np.stack([np.cos(angle), -np.sin(angle)], axis=1) / math.sqrt(steps)
        tables.append(table.reshape(FREQS, half))
    return np.stack(tables)


def inverse_scale(devices):
    scale = np.full((devices, 2, FREQS // devices // 2, 2, 1), 2.0, np.float32)
    scale[0, 0, 0] = 1.0
    return scale


def on_device(devices, forces, mode_shapes, frf):
    _, steps, dofs = forces.shape
    modes = mode_shapes.shape[1]
    half = steps // 2
    mine = FREQS // devices // 2
    table = jnp.asarray(half_tables(steps, devices).astype(jnp.bfloat16))
    low = forces[0, :half].astype(jnp.float32)
    high = forces[0, half:].astype(jnp.float32)
    folded = jnp.stack([low + high, low - high]).astype(jnp.bfloat16)
    spec = jnp.einsum("pft,ptd->pfd", table, folded, preferred_element_type=jnp.float32)
    partial = jnp.einsum(
        "pfd,dm->pfm", spec.astype(jnp.bfloat16), mode_shapes, preferred_element_type=jnp.float32
    )
    partial = partial.reshape(2, devices, 2 * mine, modes).transpose(1, 0, 2, 3)
    partial = partial.reshape(devices * 4 * mine, modes).astype(jnp.bfloat16)
    modal_spec = lax.psum_scatter(partial, "dof", scatter_dimension=0, tiled=True)
    modal_spec = modal_spec.reshape(2, mine, 2, modes).transpose(1, 0, 2, 3)
    modal_spec = modal_spec.reshape(2 * mine, 2, modes)
    products = jnp.einsum("fanm,fbm->fabn", frf, modal_spec, preferred_element_type=jnp.float32)
    real_part = products[:, 0, 0] - products[:, 1, 1]
    imag_part = products[:, 0, 1] + products[:, 1, 0]
    response = jnp.stack([real_part, imag_part], axis=1).astype(jnp.bfloat16)
    response = response.reshape(mine, 2, 2, modes).transpose(1, 0, 2, 3)
    response = response.reshape(4 * mine, modes)
    gathered = lax.all_gather(response, "dof", axis=0, tiled=True)
    gathered = gathered.reshape(devices, 2, mine, 2, modes).astype(jnp.float32)
    gathered = (gathered * inverse_scale(devices)).astype(jnp.bfloat16)
    gathered = gathered.transpose(1, 0, 2, 3, 4).reshape(2, FREQS, modes)
    moved = jnp.einsum("pfm,dm->pfd", gathered, mode_shapes, preferred_element_type=jnp.float32)
    waves = jnp.einsum(
        "pft,pfd->ptd", table, moved.astype(jnp.bfloat16), preferred_element_type=jnp.float32
    )
    out = jnp.concatenate([waves[0] + waves[1], waves[0] - waves[1]], axis=0)
    return out.astype(jnp.bfloat16)[None]


def solution(mesh):
    devices = mesh.shape["dof"]

    def run(forces, mode_shapes, frf):
        return on_device(devices, forces, mode_shapes, frf)

    return jax.shard_map(
        run,
        mesh=mesh,
        in_specs=(P("grp", None, "dof"), P("dof", None), P("dof", None, None, None)),
        out_specs=P("grp", None, "dof"),
        check_vma=False,
    )
```

time: 358 us -> 169 us (0.47)
  waiting for transfers between devices: 194 us -> 60.2 us
  other arithmetic: 69.3 us -> 17.7 us
  blocking collectives: 0 us -> 24.2 us
  matrix products: 48.8 us -> 30.5 us
  starting transfers between devices: 10.9 us -> 0.01 us
    unnamed x3 -> x1, waiting for transfers between devices: 122 us -> 0.02 us
    neg x2 -> x0, other arithmetic: 69.1 us -> none  [the longest x1 34.6 us: forward_table(): -jnp.sin(angle)]
    all_gather x1 -> x0, waiting for transfers between devices: 65.7 us -> none  [on_device(): lax.all_gather(modal_resp, 'dof', axis=0, tiled=True)]
    reduce_scatter x0 -> x1, waiting for transfers between devices: none -> 60.2 us  [on_device(): lax.psum_scatter(partial, 'dof', scatter_dimension=0, tiled=True)]
    all_gather x0 -> x1, blocking collectives: none -> 24.2 us  [on_device(): gathered = lax.all_gather(response, 'dof', axis=0, tiled=True)]
    dot_general x6 -> x3, matrix products: 48.8 us -> 30.5 us  [the longest x1 13.3 us: on_device(): jnp.einsum('fanm,fbm->fabn', frf, modal_spec, preferred_element_type=jnp....]
    another operation x2 -> x3, other arithmetic: 0.16 us -> 13.5 us
    all_to_all x2 -> x0, starting transfers between devices: 10.7 us -> none  [the longest x1 6.01 us: on_device(): lax.all_to_all(response_spec, 'dof', split_axis=3, concat_axis=0, tiled=T...]
  transfers between devices with their start and end apart: 4 -> 1, of which waited for: 3 -> 1; matrix products, arithmetic and copies ran while one was open for 19% -> 0% of each run, Pallas kernels for 0% -> 0%
where the time goes in v1:
time: 169 us; the launch traced here: 168 us
  waiting for transfers between devices  60.2 us (36%)
  matrix products  30.5 us (18%)
  blocking collectives  24.2 us (14%)
  local copies, waits for them, and re-layouts  22.1 us (13%)
  other arithmetic  17.7 us (10%)
  between operations  13.5 us (8%)
    reduce_scatter x1, waiting for transfers between devices, on_device(): lax.psum_scatter(partial, 'dof', scatter_dimension=0, tiled=True)  60.2 us
    all_gather x1, blocking collectives, on_device(): gathered = lax.all_gather(response, 'dof', axis=0, tiled=True)  24.2 us
    another operation x3, other arithmetic  13.5 us
    dot_general x1, matrix products, on_device(): jnp.einsum('fanm,fbm->fabn', frf, modal_spec, preferred_element_type=jnp....  13.3 us
    unnamed x6, local copies, waits for them, and re-layouts  9.36 us
    dot_general x1, matrix products, on_device(): jnp.einsum('pft,pfd->ptd', table, moved.astype(jnp.bfloat16), preferred_e...  9.05 us
    dot_general x1, matrix products, on_device(): jnp.einsum('pfd,dm->pfm', spec.astype(jnp.bfloat16), mode_shapes, preferr...  8.2 us
    slice x1, local copies, waits for them, and re-layouts, on_device(): low = forces[0, :half].astype(jnp.float32)  6 us
  transfers between devices with their start and end apart: 1, of which 1 were waited for; matrix products, arithmetic and copies ran while one was open for 0% of the time, Pallas kernels for 0%

profile of v1, /device:TPU:0, one launch (start us, length us, event | category | flops | bytes accessed | tf_op | source)
XLA Modules:
  0.0 168.3 jit_solution(2991950416914396696)
XLA Ops:
  6.5 0.0 copy-start
  6.5 0.0 reduce-scatter.2.cloned.1.call-start
  6.5 6.0 %fusion.32 = (bf16[1,2048,768]{2,1,0:T(8,128)(2,1)}, bf16[1,2048,768]{2,1,0:T(8,128)(2,1)}) fusion(bf16[1,4096,768]{2,1,0:T(8,128)(2,1)} %param.5), kind=kLoop, calls=%fused_computation.31 | loop fusion | bytes 12582912 | tf_op jit(solution)/shard_map/slice | solution.py:37
  12.5 4.7 %copy.25 = bf16[1,2048,768]{1,2,0:T(8,128)(2,1)} copy(bf16[1,2048,768]{2,1,0:T(8,128)(2,1)} %get-tuple-element.11) | data formatting | bytes 6291456
  17.3 4.6 %copy.26 = bf16[1,2048,768]{1,2,0:T(8,128)(2,1)} copy(bf16[1,2048,768]{2,1,0:T(8,128)(2,1)} %get-tuple-element.12) | data formatting | bytes 6291456
  21.9 7.8 %fusion = (bf16[1,2048,768]{1,2,0:T(8,128)(2,1)}, bf16[1,2048,768]{1,2,0:T(8,128)(2,1)}) fusion(bf16[1,2048,768]{1,2,0:T(8,128)(2,1)} %copy.26, bf16[1,2048,768]{1,2,0:T(8,128)(2,1)} %copy.25), kind=kLoop, calls=%fused_computation.2 | loop fusion | flops 9437184 | bytes 12582912 | tf_op jit(solution)/shard_map/convert.7
  29.7 0.0 copy-done
  29.7 8.2 %fusion.11 = bf16[2,512,448]{1,2,0:T(8,128)(2,1)S(1)} fusion(bf16[768,448]{0,1:T(8,128)(2,1)S(1)} %copy-done, bf16[2,512,2048]{2,1,0:T(8,128)(2,1)} %constant.4.clone, bf16[1,2048,768]{1,2,0:T(8,128)(2,1)} %get-tuple-element.10, bf16[1,2048,768]{1,2,0:T(8,128)(2,1)} %get-tuple-element.9), kind=kOutput, calls=%fused_computation.16 | convolution fusion | flops 3930259456 | bytes 12091392 | tf_op jit(solution)/shard_map/pfd,dm->pfm/dot_general | solution.py:41
  37.9 0.5 copy.13
  38.5 1.0 copy.14
  39.5 0.0 reduce-scatter.2.cloned.1.call-update
  39.5 60.2 %reduce-scatter.2.cloned.1.call-done = bf16[64,448]{1,0:T(8,128)(2,1)} async-done(((bf16[1024,448]{1,0:T(8,128)(2,1)}), bf16[64,448]{1,0:T(8,128)(2,1)}) %reduce-scatter.2.cloned.1.call-update) | async-done | bytes 57360 | tf_op jit(solution)/shard_map/reduce_scatter | solution.py:46
  99.8 0.9 reshape.87
  100.7 13.3 %convolution_bitcast_fusion = f32[32,2,2,448]{3,2,1,0:T(2,128)S(1)} fusion(bf16[32,2,448,1]{2,1,3,0:T(2,128)(2,1)S(1)} %bitcast.35, bf16[32,2,448,448]{3,2,1,0:T(8,128)(2,1)} %param.7), kind=kOutput, calls=%fused_computation.17 | convolution fusion | flops 51380224 | bytes 25976832 | tf_op jit(solution)/shard_map/fanm,fbm->fabn/dot_general | solution.py:49
  114.0 0.0 copy-start.1
  114.0 0.4 fusion.28
  114.5 0.1 maximum_bitcast_fusion
  114.6 0.1 copy.16
  114.7 0.1 reshape.89
  114.7 24.2 %all_gather.3 = bf16[1024,448]{1,0:T(8,128)(2,1)} all-gather(bf16[64,448]{1,0:T(8,128)(2,1)S(1)} %reshape.89), channel_id=1, replica_groups=mesh['grp'=2,'dof'=16] {'dof'}, dimensions={0}, use_global_device_ids=true | all-gather | bytes 974848 | tf_op jit(solution)/shard_map/all_gather | solution.py:55
  138.9 2.4 %reshape.91 = f32[16,2,16,2,448]{4,3,2,1,0:T(2,128)S(1)} reshape(bf16[1024,448]{1,0:T(8,128)(2,1)} %all_gather.3) | data formatting | bytes 2752512 | tf_op jit(solution)/shard_map/convert_element_type | solution.py:56
  141.3 0.0 copy-done.1
  141.3 1.0 fusion.14
  142.3 1.6 copy.17
  143.9 9.0 %fusion.17 = f32[2,2048,768]{2,1,0:T(8,128)} fusion(bf16[2,512,2048]{2,1,0:T(8,128)(2,1)} %constant.4.clone, bf16[2,512,448]{2,0,1:T(2,128)(2,1)S(1)} %bitcast.34, bf16[768,448]{0,1:T(8,128)(2,1)S(1)} %copy-done), kind=kOutput, calls=%fused_computation.20 | convolution fusion | flops 3926654976 | bytes 18382848 | tf_op jit(solution)/shard_map/pft,pfd->ptd/dot_general | solution.py:60
  153.0 5.3 %add_convert_fusion = (bf16[1,2048,768]{2,1,0:T(8,128)(2,1)S(1)}, bf16[1,2048,768]{2,1,0:T(8,128)(2,1)S(1)}) fusion(f32[2,2048,768]{2,1,0:T(8,128)} %fusion.17), kind=kLoop, calls=%fused_computation.10 | loop fusion | flops 6291456 | bytes 18874368 | tf_op jit(solution)/shard_map/convert.1
  158.3 3.1 %pad_maximum_fusion = bf16[1,4096,768]{2,1,0:T(8,128)(2,1)} fusion(bf16[1,2048,768]{2,1,0:T(8,128)(2,1)S(1)} %get-tuple-element.8, bf16[1,2048,768]{2,1,0:T(8,128)(2,1)S(1)} %get-tuple-element.7), kind=kLoop, calls=%fused_computation.8 | loop fusion | flops 12582912 | bytes 12582912 | tf_op jit(solution)/shard_map/concatenate | solution.py:63
  (3 shorter events, 0.1 us)
Async XLA Ops:
  6.5 23.2 %copy-start = (bf16[768,448]{0,1:T(8,128)(2,1)S(1)}, bf16[768,448]{0,1:T(8,128)(2,1)}, u32[]{:S(2)}) copy-start(bf16[768,448]{0,1:T(8,128)(2,1)} %param.6) | copy-start | bytes 2064388
  6.5 93.2 %reduce-scatter.2.cloned.1.call-start = ((), (), s32[]{:S(2)}) async-start(), calls=%async_computation.1 | async-start | bytes 1114112 | tf_op jit(solution)/shard_map/reduce_scatter | solution.py:46
  114.0 27.3 %copy-start.1 = (f32[16,2,16,2]{3,2,1,0:T(8,128)S(1)}, f32[16,2,16,2]{3,2,1,0:T(8,128)}, u32[]{:S(2)}) copy-start(f32[16,2,16,2]{3,2,1,0:T(8,128)} %constant.7) | copy-start | bytes 12292
Sparse Core Ops, SparseCore 0:
  39.7 60.0 reduce-scatter.1

commit v2 on v1

v2 whole, which is shorter than its diff:
```python
import functools
import math

import jax
import jax.numpy as jnp
import numpy as np
from jax import lax
from jax.experimental import pallas as pl
from jax.experimental.pallas import tpu as pltpu
from jax.sharding import PartitionSpec as P

FREQS = 512
CORES = 2
MIB = 1 << 20


def frequency_order(chips, parity):
    mine = FREQS // (chips * CORES)
    owned = np.arange(FREQS).reshape(chips, CORES, mine // 2, 2)
    return owned[:, :, :, parity].transpose(1, 0, 2).reshape(-1)


def forward_tables(steps, chips):
    times = np.arange(steps // 2, dtype=np.int64)
    tables = []
    for parity in range(2):
        ids = frequency_order(chips, parity)
        angle = (ids[:, None] * times[None, :] % steps) * (2.0 * math.pi / steps)
        table = np.stack([np.cos(angle), -np.sin(angle)], axis=1) / math.sqrt(steps)
        tables.append(table.reshape(FREQS, steps // 2))
    return np.stack(tables)


def inverse_tables(steps, chips):
    tables = forward_tables(steps, chips) * 2.0
    for parity in range(2):
        weights = np.where(frequency_order(chips, parity) == 0, 0.5, 1.0)
        tables[parity] *= np.repeat(weights, 2)[:, None]
    return tables.transpose(0, 2, 1)


def forward_kernel(core_ref, table_ref, forces_ref, shapes_ref, keep_ref, send_ref, acc_ref):
    step = pl.program_id(0)
    chips, _, rows, modes = keep_ref.shape
    low, high = forces_ref[0], forces_ref[1]

    @pl.when(step == 0)
    def _():
        acc_ref[...] = jnp.zeros_like(acc_ref)

    for parity, folded in enumerate((low + high, low - high)):
        acc_ref[parity] += jnp.dot(table_ref[parity], folded, preferred_element_type=jnp.float32)

    @pl.when(step == pl.num_programs(0) - 1)
    def _():
        first = core_ref[0] == 0
        for parity in range(2):
            spec = lax.dot_general(
                acc_ref[parity].astype(jnp.bfloat16),
                shapes_ref[...],
                (((1,), (1,)), ((), ())),
                preferred_element_type=jnp.float32,
            ).reshape(CORES, chips, rows, modes)
            keep_ref[:, parity] = jnp.where(first, spec[0], spec[1]).astype(jnp.bfloat16)
            send_ref[:, parity] = jnp.where(first, spec[1], spec[0]).astype(jnp.bfloat16)


def forward(core, table, forces, shapes_t, chips):
    _, half, dofs = forces.shape
    modes = shapes_t.shape[0]
    block = 512
    rows = FREQS // (chips * CORES)
    out = jax.ShapeDtypeStruct((chips, 2, rows, modes), jnp.bfloat16)
    whole = pl.BlockSpec((chips, 2, rows, modes), lambda i: (0, 0, 0, 0))
    return pl.pallas_call(
        forward_kernel,
        grid=(half // block,),
        in_specs=[
            pl.BlockSpec(memory_space=pltpu.SMEM),
            pl.BlockSpec((2, FREQS, block), lambda i: (0, 0, i)),
            pl.BlockSpec((2, block, dofs), lambda i: (0, i, 0)),
            pl.BlockSpec((modes, dofs), lambda i: (0, 0)),
        ],
        out_specs=[whole, whole],
        out_shape=[out, out],
        scratch_shapes=[pltpu.VMEM((2, FREQS, dofs), jnp.float32)],
        compiler_params=pltpu.CompilerParams(vmem_limit_bytes=32 * MIB),
        cost_estimate=pl.CostEstimate(
            flops=4 * FREQS * dofs * (half + modes), bytes_accessed=12 * MIB, transcendentals=0
        ),
        name="forward",
    )(core, table, forces, shapes_t)


def respond_kernel(pieces_ref, frf_ref, out_ref, direct_ref, turned_ref, acc_ref):
    step = pl.program_id(0)
    _, rows, modes = out_ref.shape
    each = frf_ref.shape[0]

    @pl.when(step == 0)
    def _():
        total = jnp.sum(pieces_ref[...].astype(jnp.float32), axis=0).reshape(2 * rows, modes)
        total = total.astype(jnp.bfloat16).astype(jnp.float32)
        row = lax.broadcasted_iota(jnp.int32, total.shape, 0)
        turned = jnp.where(
            row % 2 == 0, -jnp.roll(total, -1, axis=0), jnp.roll(total, 1, axis=0)
        )
        direct_ref[...] = total.T.astype(jnp.bfloat16)
        turned_ref[...] = turned.T.astype(jnp.bfloat16)
        acc_ref[...] = jnp.zeros_like(acc_ref)

    real = frf_ref[:, 0].reshape(each * modes, modes)
    imag = frf_ref[:, 1].reshape(each * modes, modes)
    products = jnp.dot(real, direct_ref[...], preferred_element_type=jnp.float32)
    products += jnp.dot(imag, turned_ref[...], preferred_element_type=jnp.float32)
    products = products.reshape(each, modes, 2 * rows)
    pair = lax.broadcasted_iota(jnp.int32, (modes, 2 * rows), 1) // 2
    acc = acc_ref[...]
    for i in range(each):
        f = step * each + i
        acc = jnp.where(pair == (f % 2) * (rows // 2) + f // 2, products[i], acc)
    acc_ref[...] = acc

    @pl.when(step == pl.num_programs(0) - 1)
    def _():
        out_ref[...] = acc_ref[...].T.reshape(2, rows, modes).astype(jnp.bfloat16)


def respond(pieces, frf):
    mine, _, modes, _ = frf.shape
    rows = mine
    each = 4
    return pl.pallas_call(
        respond_kernel,
        grid=(mine // each,),
        in_specs=[
            pl.BlockSpec(pieces.shape, lambda i: (0, 0, 0, 0)),
            pl.BlockSpec((each, 2, modes, modes), lambda i: (i, 0, 0, 0)),
        ],
        out_specs=pl.BlockSpec((2, rows, modes), lambda i: (0, 0, 0)),
        out_shape=jax.ShapeDtypeStruct((2, rows, modes), jnp.bfloat16),
        scratch_shapes=[
            pltpu.VMEM((modes, 2 * rows), jnp.bfloat16),
            pltpu.VMEM((modes, 2 * rows), jnp.bfloat16),
            pltpu.VMEM((modes, 2 * rows), jnp.float32),
        ],
        compiler_params=pltpu.CompilerParams(vmem_limit_bytes=24 * MIB),
        cost_estimate=pl.CostEstimate(
            flops=8 * mine * modes * modes, bytes_accessed=frf.size * 2, transcendentals=0
        ),
        name="respond",
    )(pieces, frf)


def inverse_kernel(chips, place_ref, table_ref, shapes_ref, *refs):
    shards, (out_ref, order_ref, moved_ref) = refs[: CORES * chips], refs[CORES * chips :]
    _, rows, modes = shards[0].shape

    @pl.when(pl.program_id(0) == 0)
    def _():
        core, chip = place_ref[0], place_ref[1]
        for far in range(CORES):
            for k in range(chips):
                values = shards[far * chips + k][...]
                for parity in range(2):
                    order_ref[parity, core ^ far, chip ^ k] = values[parity].astype(jnp.float32)
        for parity in range(2):
            moved_ref[parity] = jnp.dot(
                order_ref[parity].reshape(FREQS, modes).astype(jnp.bfloat16),
                shapes_ref[...],
                preferred_element_type=jnp.float32,
            ).astype(jnp.bfloat16)

    even = jnp.dot(table_ref[0], moved_ref[0], preferred_element_type=jnp.float32)
    odd = jnp.dot(table_ref[1], moved_ref[1], preferred_element_type=jnp.float32)
    out_ref[0] = (even + odd).astype(jnp.bfloat16)
    out_ref[1] = (even - odd).astype(jnp.bfloat16)


def inverse(place, table, shapes_t, shards, chips):
    _, half, _ = table.shape
    modes, dofs = shapes_t.shape
    block = 256
    rows = shards[0].shape[1]
    return pl.pallas_call(
        functools.partial(inverse_kernel, chips),
        grid=(half // block,),
        in_specs=[
            pl.BlockSpec(memory_space=pltpu.SMEM),
            pl.BlockSpec((2, block, FREQS), lambda i: (0, i, 0)),
            pl.BlockSpec((modes, dofs), lambda i: (0, 0)),
        ]
        + [pl.BlockSpec((2, rows, modes), lambda i: (0, 0, 0))] * len(shards),
        out_specs=pl.BlockSpec((2, block, dofs), lambda i: (0, i, 0)),
        out_shape=jax.ShapeDtypeStruct((2, half, dofs), jnp.bfloat16),
        scratch_shapes=[
            pltpu.VMEM((2, CORES, chips, rows, modes), jnp.float32),
            pltpu.VMEM((2, FREQS, dofs), jnp.bfloat16),
        ],
        compiler_params=pltpu.CompilerParams(vmem_limit_bytes=32 * MIB),
        cost_estimate=pl.CostEstimate(
            flops=4 * FREQS * dofs * (half + modes), bytes_accessed=12 * MIB, transcendentals=0
        ),
        name="inverse",
    )(place, table, shapes_t, *shards)


def on_device(devices, forces, mode_shapes, frf):
    _, steps, dofs = forces.shape
    half = steps // 2
    chips = devices // CORES
    to_core = [(i, i ^ 1) for i in range(devices)]
    to_chip = [[(i, i ^ (CORES * k)) for i in range(devices)] for k in range(chips)]
    same_core = [[chip * CORES + core for chip in range(chips)] for core in range(CORES)]
    index = lax.axis_index("dof")
    place = jnp.stack([index % CORES, index // CORES]).astype(jnp.int32)
    shapes_t = mode_shapes.T
    fwd = jnp.asarray(forward_tables(steps, chips).astype(jnp.bfloat16))
    inv = jnp.asarray(inverse_tables(steps, chips).astype(jnp.bfloat16))

    keep, send = forward(place, fwd, forces.reshape(2, half, dofs), shapes_t, chips)
    came = lax.ppermute(send, "dof", to_core)
    pair = (keep.astype(jnp.float32) + came.astype(jnp.float32)).astype(jnp.bfloat16)
    pieces = lax.all_to_all(
        pair, "dof", split_axis=0, concat_axis=0, axis_index_groups=same_core, tiled=True
    )
    response = respond(pieces, frf)
    near = [response] + [lax.ppermute(response, "dof", to_chip[k]) for k in range(1, chips)]
    far = [lax.ppermute(shard, "dof", to_core) for shard in near]
    out = inverse(place, inv, shapes_t, near + far, chips)
    return out.reshape(1, steps, dofs)


def solution(mesh):
    devices = mesh.shape["dof"]
    return jax.shard_map(
        functools.partial(on_device, devices),
        mesh=mesh,
        in_specs=(P("grp", None, "dof"), P("dof", None), P("dof", None, None, None)),
        out_specs=P("grp", None, "dof"),
        check_vma=False,
    )
```

time: 169 us -> 82.4 us (0.49)
  waiting for transfers between devices: 60.2 us -> 6.16 us
  matrix products: 30.5 us -> 0 us
  Pallas kernels: 0 us -> 24.3 us
  other arithmetic: 17.7 us -> 0.24 us
  starting transfers between devices: 0.01 us -> 14.1 us
  between operations: 13.5 us -> 0.05 us
  local copies, waits for them, and re-layouts: 22.1 us -> 15.4 us
  blocking collectives: 24.2 us -> 21.8 us
    reduce_scatter x1 -> x0, waiting for transfers between devices: 60.2 us -> none  [on_device(): lax.psum_scatter(partial, 'dof', scatter_dimension=0, tiled=True)]
    dot_general x3 -> x0, matrix products: 30.5 us -> none  [the longest x1 13.3 us: on_device(): jnp.einsum('fanm,fbm->fabn', frf, modal_spec, preferred_element_type=jnp....]
    pallas_call x0 -> x3, Pallas kernels: none -> 24.3 us  [the longest x1 9.3 us: respond(): pl.pallas_call(respond_kernel, grid=(mine // each,), in_specs=[pl.BlockSp...]
    all_gather x1 -> x0, blocking collectives: 24.2 us -> none  [on_device(): gathered = lax.all_gather(response, 'dof', axis=0, tiled=True)]
    all_to_all x0 -> x1, blocking collectives: none -> 21.8 us  [on_device(): lax.all_to_all(pair, 'dof', split_axis=0, concat_axis=0, axis_index_group...]
    ppermute x0 -> x16, starting transfers between devices: none -> 14.1 us  [the longest x7 12 us: on_device(): lax.ppermute(response, 'dof', to_chip[k])]
    another operation x3 -> x1, other arithmetic: 13.5 us -> 0.07 us  [on_device(): place = jnp.stack([index % CORES, index // CORES]).astype(jnp.int32)]
    ppermute x0 -> x16, waiting for transfers between devices: none -> 6.16 us  [the longest x7 3.71 us: on_device(): lax.ppermute(response, 'dof', to_chip[k])]
  transfers between devices with their start and end apart: 1 -> 16, of which waited for: 1 -> 8; matrix products, arithmetic and copies ran while one was open for 0% -> 0% of each run, Pallas kernels for 0% -> 0%
where the time goes in v2:
time: 82.4 us; the launch traced here: 82.1 us
  Pallas kernels  24.3 us (29%)
  blocking collectives  21.8 us (26%)
  local copies, waits for them, and re-layouts  15.4 us (19%)
  starting transfers between devices  14.1 us (17%)
  waiting for transfers between devices  6.16 us (7%)
    all_to_all x1, blocking collectives, on_device(): lax.all_to_all(pair, 'dof', split_axis=0, concat_axis=0, axis_index_group...  21.8 us
    unnamed x12, local copies, waits for them, and re-layouts  15.4 us
    ppermute x7, starting transfers between devices, on_device(): lax.ppermute(response, 'dof', to_chip[k])  12 us
    pallas_call x1, Pallas kernels, respond(): pl.pallas_call(respond_kernel, grid=(mine // each,), in_specs=[pl.BlockSp...  9.3 us
    pallas_call x1, Pallas kernels, inverse(): pl.pallas_call(functools.partial(inverse_kernel, chips), grid=(half // bl...  8.3 us
    pallas_call x1, Pallas kernels, forward(): pl.pallas_call(forward_kernel, grid=(half // block,), in_specs=[pl.BlockS...  6.75 us
    ppermute x7, waiting for transfers between devices, on_device(): lax.ppermute(response, 'dof', to_chip[k])  3.71 us
  transfers between devices with their start and end apart: 16, of which 8 were waited for; matrix products, arithmetic and copies ran while one was open for 0% of the time, Pallas kernels for 0%

profile of v2, /device:TPU:0, one launch (start us, length us, event | category | flops | bytes accessed | tf_op | source)
XLA Modules:
  0.0 82.1 jit_solution(16342075365987817361)
XLA Ops:
  0.0 0.1 pad_add_fusion.core_ref.place_ref
  0.1 0.0 copy-start.1
  0.1 2.8 %copy-done.1 = bf16[1,4096,768]{2,1,0:T(8,128)(2,1)S(1)} copy-done((bf16[1,4096,768]{2,1,0:T(8,128)(2,1)S(1)}, bf16[1,4096,768]{2,1,0:T(8,128)(2,1)}, u32[]{:S(2)}) %copy-start.1) | copy-done | bytes 6291480
  2.9 0.0 copy-start.2
  2.9 1.1 %copy-done.2 = bf16[768,448]{0,1:T(8,128)(2,1)S(1)} copy-done((bf16[768,448]{0,1:T(8,128)(2,1)S(1)}, bf16[768,448]{0,1:T(8,128)(2,1)}, u32[]{:S(2)}) %copy-start.2) | copy-done | bytes 688152
  4.0 0.0 copy-start.5
  4.0 2.2 %copy-done.5 = bf16[2,512,2048]{2,1,0:T(8,128)(2,1)S(1)} copy-done((bf16[2,512,2048]{2,1,0:T(8,128)(2,1)S(1)}, bf16[2,512,2048]{2,1,0:T(8,128)(2,1)}, u32[]{:S(2)}) %copy-start.5) | copy-done | bytes 4194328
  6.1 6.7 %forward.1 = (bf16[8,2,32,448]{3,2,1,0:T(8,128)(2,1)S(1)}, bf16[8,2,32,448]{3,2,1,0:T(8,128)(2,1)S(1)}) custom-call(s32[2]{0:T(128)S(1)} %pad_add_fusion.core_ref.place_ref, bf16[2,512,2048]{2,1,0:T(8,128)(2,1)S(1)} %copy-done.5, bf16[2,2048,768]{2,1,0:T(8,128)(2,1)S(1)} %bitcast.5, bf16[448,768]{1,0:T(8,128)(2,1)S(1)} %bitcast.6), custom_call_target="tpu_custom_call" | custom-call | flops 3925868544 | bytes 12582912 | tf_op jit(solution)/shard_map/forward/pallas_call | solution.py:75
  12.9 0.5 collective-permute-start
  13.4 1.5 %collective-permute-done = bf16[8,2,32,448]{3,2,1,0:T(8,128)(2,1)S(1)} collective-permute-done((bf16[8,2,32,448]{3,2,1,0:T(8,128)(2,1)S(1)}, bf16[8,2,32,448]{3,2,1,0:T(8,128)(2,1)S(1)}, u32[]{:S(2)}, u32[]{:S(2)}) %collective-permute-start) | collective-permute-done | bytes 458784 | tf_op jit(solution)/shard_map/ppermute | solution.py:222
  15.0 0.2 add_convert_fusion
  15.1 21.8 %all_to_all.5.pieces_ref = bf16[8,2,32,448]{3,2,1,0:T(8,128)(2,1)S(1)} all-to-all(bf16[8,2,32,448]{3,2,1,0:T(8,128)(2,1)S(1)} %add_convert_fusion), channel_id=1, replica_groups={{0,2,4,6,8,10,12,14},{1,3,5,7,9,11,13,15},{16,18,20,22,24,26,28,30},{17..., dimensions={0} | all-to-all | bytes 917504 | tf_op jit(solution)/shard_map/all_to_all | solution.py:224
  36.9 0.0 copy-start
  36.9 9.3 %copy-done = bf16[32,2,448,448]{3,2,1,0:T(8,128)(2,1)S(1)} copy-done((bf16[32,2,448,448]{3,2,1,0:T(8,128)(2,1)S(1)}, bf16[32,2,448,448]{3,2,1,0:T(8,128)(2,1)}, u32[]{:S(2)}) %copy-start) | copy-done | bytes 25690136
  46.3 9.3 %respond.1.refs_0_ = bf16[2,32,448]{2,1,0:T(8,128)(2,1)S(1)} custom-call(bf16[8,2,32,448]{3,2,1,0:T(8,128)(2,1)S(1)} %all_to_all.5.pieces_ref, bf16[32,2,448,448]{3,2,1,0:T(8,128)(2,1)S(1)} %copy-done), custom_call_target="tpu_custom_call" | custom-call | flops 51380224 | bytes 25690112 | tf_op jit(solution)/shard_map/respond/pallas_call | solution.py:133
  55.6 0.1 collective-permute-start.8
  55.7 2.4 %collective-permute-start.7 = (bf16[2,32,448]{2,1,0:T(8,128)(2,1)S(1)}, bf16[2,32,448]{2,1,0:T(8,128)(2,1)S(1)}, u32[]{:S(2)}, u32[]{:S(2)}) collective-permute-start(bf16[2,32,448]{2,1,0:T(8,128)(2,1)S(1)} %respond.1.refs_0_), channel_id=1, source_target_pairs={{0,14},{1,15},{2,12},{3,13},{4,10},{5,11},{6,8},{7,9},{8,6},{9,7},... | collective-permute-start | bytes 172040 | tf_op jit(solution)/shard_map/ppermute | solution.py:228
  58.1 2.4 %collective-permute-start.6 = (bf16[2,32,448]{2,1,0:T(8,128)(2,1)S(1)}, bf16[2,32,448]{2,1,0:T(8,128)(2,1)S(1)}, u32[]{:S(2)}, u32[]{:S(2)}) collective-permute-start(bf16[2,32,448]{2,1,0:T(8,128)(2,1)S(1)} %respond.1.refs_0_), channel_id=1, source_target_pairs={{0,12},{1,13},{2,14},{3,15},{4,8},{5,9},{6,10},{7,11},{8,4},{9,5},... | collective-permute-start | bytes 172040 | tf_op jit(solution)/shard_map/ppermute | solution.py:228
  60.5 0.0 collective-permute-start.5
  60.5 2.9 %collective-permute-start.4 = (bf16[2,32,448]{2,1,0:T(8,128)(2,1)S(1)}, bf16[2,32,448]{2,1,0:T(8,128)(2,1)S(1)}, u32[]{:S(2)}, u32[]{:S(2)}) collective-permute-start(bf16[2,32,448]{2,1,0:T(8,128)(2,1)S(1)} %respond.1.refs_0_), channel_id=1, source_target_pairs={{0,8},{1,9},{2,10},{3,11},{4,12},{5,13},{6,14},{7,15},{8,0},{9,1},... | collective-permute-start | bytes 172040 | tf_op jit(solution)/shard_map/ppermute | solution.py:228
  63.4 0.0 collective-permute-done.8.refs_8_
  63.4 0.0 collective-permute-start.3
  63.4 0.0 collective-permute-done.7.refs_7_
  63.4 4.3 %collective-permute-start.2 = (bf16[2,32,448]{2,1,0:T(8,128)(2,1)S(1)}, bf16[2,32,448]{2,1,0:T(8,128)(2,1)S(1)}, u32[]{:S(2)}, u32[]{:S(2)}) collective-permute-start(bf16[2,32,448]{2,1,0:T(8,128)(2,1)S(1)} %respond.1.refs_0_), channel_id=1, source_target_pairs={{0,4},{1,5},{2,6},{3,7},{4,0},{5,1},{6,2},{7,3},{8,12},{9,13},{10,... | collective-permute-start | bytes 172040 | tf_op jit(solution)/shard_map/ppermute | solution.py:228
  67.7 0.0 collective-permute-done.6.refs_6_
  67.7 0.0 collective-permute-start.1
  67.7 2.8 %collective-permute-done.5.refs_5_ = bf16[2,32,448]{2,1,0:T(8,128)(2,1)S(1)} collective-permute-done((bf16[2,32,448]{2,1,0:T(8,128)(2,1)S(1)}, bf16[2,32,448]{2,1,0:T(8,128)(2,1)S(1)}, u32[]{:S(2)}, u32[]{:S(2)}) %collective-permute-start.5) | collective-permute-done | bytes 57376 | tf_op jit(solution)/shard_map/ppermute | solution.py:228
  70.5 0.0 collective-permute-start.15
  70.5 0.0 collective-permute-done.4.refs_4_
  70.5 0.5 collective-permute-start.14
  71.1 0.0 collective-permute-done.3.refs_3_
  71.1 0.1 collective-permute-start.13
  71.1 0.7 collective-permute-done.2.refs_2_
  71.8 0.0 collective-permute-start.12
  71.8 0.1 collective-permute-done.1.refs_1_
  72.0 0.4 collective-permute-start.11
  72.4 0.0 collective-permute-done.15.refs_15_
  72.4 0.1 collective-permute-start.10
  72.5 0.0 collective-permute-done.14.refs_14_
  72.5 0.4 collective-permute-start.9
  72.9 0.0 collective-permute-done.13.refs_13_
  72.9 0.2 collective-permute-done.12.refs_12_
  73.1 0.2 collective-permute-done.11.refs_11_
  73.3 0.4 collective-permute-done.10.refs_10_
  73.6 0.2 collective-permute-done.9.refs_9_
  73.8 0.0 copy-done.3
  73.8 0.0 copy-done.4
  73.8 8.3 %inverse.1 = bf16[2,2048,768]{2,1,0:T(8,128)(2,1)} custom-call(s32[2]{0:T(128)S(1)} %pad_add_fusion.core_ref.place_ref, bf16[2,2048,512]{2,1,0:T(8,128)(2,1)S(1)} %copy-done.4, bf16[448,768]{1,0:T(8,128)(2,1)S(1)} %bitcast.7, bf16[2,32,448]{2,1,0:T(8,128)(2,1)S(1)} %respond.1.refs_0_, bf16[2,32,448]{2,1,0:T(8,128)(2,1)S(1)} %collective-permute-done.1.refs_1_, ...), custom_call_target="tpu_custom_call" | custom-call | flops 3925868544 | bytes 12582912 | tf_op jit(solution)/shard_map/inverse/pallas_call | solution.py:185
  (2 shorter events, 0.0 us)
Async XLA Ops:
  0.1 2.8 %copy-start.1 = (bf16[1,4096,768]{2,1,0:T(8,128)(2,1)S(1)}, bf16[1,4096,768]{2,1,0:T(8,128)(2,1)}, u32[]{:S(2)}) copy-start(bf16[1,4096,768]{2,1,0:T(8,128)(2,1)} %param.5) | copy-start | bytes 18874372
  2.9 1.1 %copy-start.2 = (bf16[768,448]{0,1:T(8,128)(2,1)S(1)}, bf16[768,448]{0,1:T(8,128)(2,1)}, u32[]{:S(2)}) copy-start(bf16[768,448]{0,1:T(8,128)(2,1)} %param.6) | copy-start | bytes 2064388
  4.0 2.2 %copy-start.5 = (bf16[2,512,2048]{2,1,0:T(8,128)(2,1)S(1)}, bf16[2,512,2048]{2,1,0:T(8,128)(2,1)}, u32[]{:S(2)}) copy-start(bf16[2,512,2048]{2,1,0:T(8,128)(2,1)} %constant.32.clone.table_ref) | copy-start | bytes 12582916
  12.9 2.1 %collective-permute-start = (bf16[8,2,32,448]{3,2,1,0:T(8,128)(2,1)S(1)}, bf16[8,2,32,448]{3,2,1,0:T(8,128)(2,1)S(1)}, u32[]{:S(2)}, u32[]{:S(2)}) collective-permute-start(bf16[8,2,32,448]{3,2,1,0:T(8,128)(2,1)S(1)} %get-tuple-element.8), channel_id=1, source_target_pairs={{0,1},{1,0},{2,3},{3,2},{4,5},{5,4},{6,7},{7,6},{8,9},{9,8},{10,11... | collective-permute-start | bytes 1376264 | tf_op jit(solution)/shard_map/ppermute | solution.py:222
  36.9 9.4 %copy-start = (bf16[32,2,448,448]{3,2,1,0:T(8,128)(2,1)S(1)}, bf16[32,2,448,448]{3,2,1,0:T(8,128)(2,1)}, u32[]{:S(2)}) copy-start(bf16[32,2,448,448]{3,2,1,0:T(8,128)(2,1)} %frf_ref.1) | copy-start | bytes 77070336
  46.3 27.5 %copy-start.3 = (bf16[768,448]{0,1:T(8,128)(2,1)S(1)}, bf16[768,448]{0,1:T(8,128)(2,1)}, u32[]{:S(2)}) copy-start(bf16[768,448]{0,1:T(8,128)(2,1)} %param.6) | copy-start | bytes 2064388
  46.3 27.5 %copy-start.4 = (bf16[2,2048,512]{2,1,0:T(8,128)(2,1)S(1)}, bf16[2,2048,512]{2,1,0:T(8,128)(2,1)}, u32[]{:S(2)}) copy-start(bf16[2,2048,512]{2,1,0:T(8,128)(2,1)} %constant.33.clone.table_ref) | copy-start | bytes 12582916
  55.6 7.8 %collective-permute-start.8 = (bf16[2,32,448]{2,1,0:T(8,128)(2,1)S(1)}, bf16[2,32,448]{2,1,0:T(8,128)(2,1)S(1)}, u32[]{:S(2)}, u32[]{:S(2)}) collective-permute-start(bf16[2,32,448]{2,1,0:T(8,128)(2,1)S(1)} %respond.1.refs_0_), channel_id=1, source_target_pairs={{0,1},{1,0},{2,3},{3,2},{4,5},{5,4},{6,7},{7,6},{8,9},{9,8},{10,11... | collective-permute-start | bytes 172040 | tf_op jit(solution)/shard_map/ppermute | solution.py:229
  55.7 7.8 %collective-permute-start.7 = (bf16[2,32,448]{2,1,0:T(8,128)(2,1)S(1)}, bf16[2,32,448]{2,1,0:T(8,128)(2,1)S(1)}, u32[]{:S(2)}, u32[]{:S(2)}) collective-permute-start(bf16[2,32,448]{2,1,0:T(8,128)(2,1)S(1)} %respond.1.refs_0_), channel_id=1, source_target_pairs={{0,14},{1,15},{2,12},{3,13},{4,10},{5,11},{6,8},{7,9},{8,6},{9,7},... | collective-permute-start | bytes 172040 | tf_op jit(solution)/shard_map/ppermute | solution.py:228
  58.1 9.6 %collective-permute-start.6 = (bf16[2,32,448]{2,1,0:T(8,128)(2,1)S(1)}, bf16[2,32,448]{2,1,0:T(8,128)(2,1)S(1)}, u32[]{:S(2)}, u32[]{:S(2)}) collective-permute-start(bf16[2,32,448]{2,1,0:T(8,128)(2,1)S(1)} %respond.1.refs_0_), channel_id=1, source_target_pairs={{0,12},{1,13},{2,14},{3,15},{4,8},{5,9},{6,10},{7,11},{8,4},{9,5},... | collective-permute-start | bytes 172040 | tf_op jit(solution)/shard_map/ppermute | solution.py:228
  60.5 10.1 %collective-permute-start.5 = (bf16[2,32,448]{2,1,0:T(8,128)(2,1)S(1)}, bf16[2,32,448]{2,1,0:T(8,128)(2,1)S(1)}, u32[]{:S(2)}, u32[]{:S(2)}) collective-permute-start(bf16[2,32,448]{2,1,0:T(8,128)(2,1)S(1)} %respond.1.refs_0_), channel_id=1, source_target_pairs={{0,10},{1,11},{2,8},{3,9},{4,14},{5,15},{6,12},{7,13},{8,2},{9,3},... | collective-permute-start | bytes 172040 | tf_op jit(solution)/shard_map/ppermute | solution.py:228
  60.5 10.1 %collective-permute-start.4 = (bf16[2,32,448]{2,1,0:T(8,128)(2,1)S(1)}, bf16[2,32,448]{2,1,0:T(8,128)(2,1)S(1)}, u32[]{:S(2)}, u32[]{:S(2)}) collective-permute-start(bf16[2,32,448]{2,1,0:T(8,128)(2,1)S(1)} %respond.1.refs_0_), channel_id=1, source_target_pairs={{0,8},{1,9},{2,10},{3,11},{4,12},{5,13},{6,14},{7,15},{8,0},{9,1},... | collective-permute-start | bytes 172040 | tf_op jit(solution)/shard_map/ppermute | solution.py:228
  63.4 7.7 %collective-permute-start.3 = (bf16[2,32,448]{2,1,0:T(8,128)(2,1)S(1)}, bf16[2,32,448]{2,1,0:T(8,128)(2,1)S(1)}, u32[]{:S(2)}, u32[]{:S(2)}) collective-permute-start(bf16[2,32,448]{2,1,0:T(8,128)(2,1)S(1)} %respond.1.refs_0_), channel_id=1, source_target_pairs={{0,6},{1,7},{2,4},{3,5},{4,2},{5,3},{6,0},{7,1},{8,14},{9,15},{10,... | collective-permute-start | bytes 172040 | tf_op jit(solution)/shard_map/ppermute | solution.py:228
  63.4 8.4 %collective-permute-start.2 = (bf16[2,32,448]{2,1,0:T(8,128)(2,1)S(1)}, bf16[2,32,448]{2,1,0:T(8,128)(2,1)S(1)}, u32[]{:S(2)}, u32[]{:S(2)}) collective-permute-start(bf16[2,32,448]{2,1,0:T(8,128)(2,1)S(1)} %respond.1.refs_0_), channel_id=1, source_target_pairs={{0,4},{1,5},{2,6},{3,7},{4,0},{5,1},{6,2},{7,3},{8,12},{9,13},{10,... | collective-permute-start | bytes 172040 | tf_op jit(solution)/shard_map/ppermute | solution.py:228
  67.7 4.3 %collective-permute-start.1 = (bf16[2,32,448]{2,1,0:T(8,128)(2,1)S(1)}, bf16[2,32,448]{2,1,0:T(8,128)(2,1)S(1)}, u32[]{:S(2)}, u32[]{:S(2)}) collective-permute-start(bf16[2,32,448]{2,1,0:T(8,128)(2,1)S(1)} %respond.1.refs_0_), channel_id=1, source_target_pairs={{0,2},{1,3},{2,0},{3,1},{4,6},{5,7},{6,4},{7,5},{8,10},{9,11},{10,... | collective-permute-start | bytes 172040 | tf_op jit(solution)/shard_map/ppermute | solution.py:228
  70.5 1.8 %collective-permute-start.15 = (bf16[2,32,448]{2,1,0:T(8,128)(2,1)S(1)}, bf16[2,32,448]{2,1,0:T(8,128)(2,1)S(1)}, u32[]{:S(2)}, u32[]{:S(2)}) collective-permute-start(bf16[2,32,448]{2,1,0:T(8,128)(2,1)S(1)} %collective-permute-done.7.refs_7_), channel_id=1, source_target_pairs={{0,1},{1,0},{2,3},{3,2},{4,5},{5,4},{6,7},{7,6},{8,9},{9,8},{10,11... | collective-permute-start | bytes 172040 | tf_op jit(solution)/shard_map/ppermute | solution.py:229
  70.5 2.0 %collective-permute-start.14 = (bf16[2,32,448]{2,1,0:T(8,128)(2,1)S(1)}, bf16[2,32,448]{2,1,0:T(8,128)(2,1)S(1)}, u32[]{:S(2)}, u32[]{:S(2)}) collective-permute-start(bf16[2,32,448]{2,1,0:T(8,128)(2,1)S(1)} %collective-permute-done.6.refs_6_), channel_id=1, source_target_pairs={{0,1},{1,0},{2,3},{3,2},{4,5},{5,4},{6,7},{7,6},{8,9},{9,8},{10,11... | collective-permute-start | bytes 172040 | tf_op jit(solution)/shard_map/ppermute | solution.py:229
  71.1 1.8 %collective-permute-start.13 = (bf16[2,32,448]{2,1,0:T(8,128)(2,1)S(1)}, bf16[2,32,448]{2,1,0:T(8,128)(2,1)S(1)}, u32[]{:S(2)}, u32[]{:S(2)}) collective-permute-start(bf16[2,32,448]{2,1,0:T(8,128)(2,1)S(1)} %collective-permute-done.5.refs_5_), channel_id=1, source_target_pairs={{0,1},{1,0},{2,3},{3,2},{4,5},{5,4},{6,7},{7,6},{8,9},{9,8},{10,11... | collective-permute-start | bytes 172040 | tf_op jit(solution)/shard_map/ppermute | solution.py:229
  71.8 1.3 %collective-permute-start.12 = (bf16[2,32,448]{2,1,0:T(8,128)(2,1)S(1)}, bf16[2,32,448]{2,1,0:T(8,128)(2,1)S(1)}, u32[]{:S(2)}, u32[]{:S(2)}) collective-permute-start(bf16[2,32,448]{2,1,0:T(8,128)(2,1)S(1)} %collective-permute-done.4.refs_4_), channel_id=1, source_target_pairs={{0,1},{1,0},{2,3},{3,2},{4,5},{5,4},{6,7},{7,6},{8,9},{9,8},{10,11... | collective-permute-start | bytes 172040 | tf_op jit(solution)/shard_map/ppermute | solution.py:229
  72.0 1.3 %collective-permute-start.11 = (bf16[2,32,448]{2,1,0:T(8,128)(2,1)S(1)}, bf16[2,32,448]{2,1,0:T(8,128)(2,1)S(1)}, u32[]{:S(2)}, u32[]{:S(2)}) collective-permute-start(bf16[2,32,448]{2,1,0:T(8,128)(2,1)S(1)} %collective-permute-done.3.refs_3_), channel_id=1, source_target_pairs={{0,1},{1,0},{2,3},{3,2},{4,5},{5,4},{6,7},{7,6},{8,9},{9,8},{10,11... | collective-permute-start | bytes 172040 | tf_op jit(solution)/shard_map/ppermute | solution.py:229
  72.4 1.3 %collective-permute-start.10 = (bf16[2,32,448]{2,1,0:T(8,128)(2,1)S(1)}, bf16[2,32,448]{2,1,0:T(8,128)(2,1)S(1)}, u32[]{:S(2)}, u32[]{:S(2)}) collective-permute-start(bf16[2,32,448]{2,1,0:T(8,128)(2,1)S(1)} %collective-permute-done.2.refs_2_), channel_id=1, source_target_pairs={{0,1},{1,0},{2,3},{3,2},{4,5},{5,4},{6,7},{7,6},{8,9},{9,8},{10,11... | collective-permute-start | bytes 172040 | tf_op jit(solution)/shard_map/ppermute | solution.py:229
  72.5 1.3 %collective-permute-start.9 = (bf16[2,32,448]{2,1,0:T(8,128)(2,1)S(1)}, bf16[2,32,448]{2,1,0:T(8,128)(2,1)S(1)}, u32[]{:S(2)}, u32[]{:S(2)}) collective-permute-start(bf16[2,32,448]{2,1,0:T(8,128)(2,1)S(1)} %collective-permute-done.1.refs_1_), channel_id=1, source_target_pairs={{0,1},{1,0},{2,3},{3,2},{4,5},{5,4},{6,7},{7,6},{8,9},{9,8},{10,11... | collective-permute-start | bytes 172040 | tf_op jit(solution)/shard_map/ppermute | solution.py:229

commit v3 on v1

v3 whole, which is shorter than its diff:
```python
import functools
import math

import jax
import jax.numpy as jnp
import numpy as np
from jax import lax
from jax.experimental import pallas as pl
from jax.experimental.pallas import tpu as pltpu
from jax.sharding import PartitionSpec as P

FREQS = 512
CORES = 2
MIB = 1 << 20


def frequency_order(chips, parity):
    mine = FREQS // (chips * CORES)
    owned = np.arange(FREQS).reshape(chips, CORES, mine // 2, 2)
    return owned[:, :, :, parity].transpose(1, 0, 2).reshape(-1)


def forward_tables(steps, chips):
    times = np.arange(steps // 2, dtype=np.int64)
    tables = []
    for parity in range(2):
        ids = frequency_order(chips, parity)
        angle = (ids[:, None] * times[None, :] % steps) * (2.0 * math.pi / steps)
        table = np.stack([np.cos(angle), -np.sin(angle)], axis=1) / math.sqrt(steps)
        tables.append(table.reshape(FREQS, steps // 2))
    return np.stack(tables)


def inverse_tables(steps, chips):
    tables = forward_tables(steps, chips) * 2.0
    for parity in range(2):
        weights = np.where(frequency_order(chips, parity) == 0, 0.5, 1.0)
        tables[parity] *= np.repeat(weights, 2)[:, None]
    return tables.transpose(0, 2, 1)


def chunk_list(half):
    unit = half // 8
    sizes = (unit, unit, 2 * unit, 4 * unit)
    starts = (0, unit, 2 * unit, 4 * unit)
    return tuple(zip(starts, sizes))


def forward_kernel(
    place_ref, table_ref, forces_ref, shapes_ref, frf_ref, keep_ref, send_ref, held_ref,
    table_buf, forces_buf, shapes_buf, acc_ref, table_sem, forces_sem, shapes_sem, held_sem,
):
    _, zs, _, rows, modes = keep_ref.shape
    chips = 2 * zs
    chunks = chunk_list(forces_ref.shape[1])
    copies = []
    for n, (start, size) in enumerate(chunks):
        part = pl.ds(start, size)
        pair = (
            pltpu.make_async_copy(
                forces_ref.at[:, part], forces_buf.at[:, part], forces_sem.at[n]
            ),
            pltpu.make_async_copy(
                table_ref.at[:, :, part], table_buf.at[:, :, part], table_sem.at[n]
            ),
        )
        for copy in pair:
            copy.start()
        copies.append(pair)
    shapes_copy = pltpu.make_async_copy(shapes_ref, shapes_buf, shapes_sem)
    shapes_copy.start()
    held_copy = pltpu.make_async_copy(
        frf_ref.at[pl.ds(0, held_ref.shape[0])], held_ref, held_sem
    )
    held_copy.start()

    for n, (start, size) in enumerate(chunks):
        for copy in copies[n]:
            copy.wait()
        low = forces_buf[0, start : start + size]
        high = forces_buf[1, start : start + size]
        for parity, folded in enumerate((low + high, low - high)):
            part = jnp.dot(
                table_buf[parity, :, start : start + size],
                folded,
                preferred_element_type=jnp.float32,
            )
            if n == 0:
                acc_ref[parity] = part
            else:
                acc_ref[parity] += part

    shapes_copy.wait()
    first, chip = place_ref[0] == 0, place_ref[1]
    for parity in range(2):
        spec = lax.dot_general(
            acc_ref[parity].astype(jnp.bfloat16),
            shapes_buf[...],
            (((1,), (1,)), ((), ())),
            preferred_element_type=jnp.float32,
        ).reshape(CORES, chips, rows, modes)
        keep = jnp.where(first, spec[0], spec[1]).astype(jnp.bfloat16)
        send = jnp.where(first, spec[1], spec[0]).astype(jnp.bfloat16)
        for j in range(chips):
            slot = chip ^ j
            keep_ref[slot % 2, slot // 2, parity] = keep[j]
            send_ref[slot % 2, slot // 2, parity] = send[j]
    held_copy.wait()


def in_hbm(array):
    return pltpu.with_memory_space_constraint(array, pltpu.HBM)


def forward(place, table, forces, shapes_t, frf, held, chips):
    _, half, dofs = forces.shape
    modes = shapes_t.shape[0]
    rows = FREQS // (chips * CORES)
    out = jax.ShapeDtypeStruct((2, chips // 2, 2, rows, modes), jnp.bfloat16)
    vmem, hbm = pl.BlockSpec(memory_space=pltpu.VMEM), pl.BlockSpec(memory_space=pltpu.HBM)
    count = len(chunk_list(half))
    return pl.pallas_call(
        forward_kernel,
        in_specs=[pl.BlockSpec(memory_space=pltpu.SMEM), hbm, hbm, hbm, hbm],
        out_specs=[vmem, vmem, vmem],
        out_shape=[out, out, pltpu.VMEM((held,) + frf.shape[1:], jnp.bfloat16)],
        scratch_shapes=[
            pltpu.VMEM(table.shape, jnp.bfloat16),
            pltpu.VMEM(forces.shape, jnp.bfloat16),
            pltpu.VMEM(shapes_t.shape, jnp.bfloat16),
            pltpu.VMEM((2, FREQS, dofs), jnp.float32),
            pltpu.SemaphoreType.DMA((count,)),
            pltpu.SemaphoreType.DMA((count,)),
            pltpu.SemaphoreType.DMA,
            pltpu.SemaphoreType.DMA,
        ],
        compiler_params=pltpu.CompilerParams(vmem_limit_bytes=24 * MIB),
        cost_estimate=pl.CostEstimate(
            flops=4 * FREQS * dofs * (half + modes), bytes_accessed=20 * MIB, transcendentals=0
        ),
        name="forward",
    )(place, in_hbm(table), in_hbm(forces), in_hbm(shapes_t), in_hbm(frf))


def load_kernel(start, frf_ref, after_ref, held_ref, sem):
    copy = pltpu.make_async_copy(
        frf_ref.at[pl.ds(start, held_ref.shape[0])], held_ref, sem
    )
    copy.start()
    copy.wait()


def load(frf, start, size, after):
    hbm, anywhere = pl.BlockSpec(memory_space=pltpu.HBM), pl.BlockSpec(memory_space=pl.ANY)
    return pl.pallas_call(
        functools.partial(load_kernel, start),
        in_specs=[hbm, anywhere],
        out_specs=pl.BlockSpec(memory_space=pltpu.VMEM),
        out_shape=pltpu.VMEM((size,) + frf.shape[1:], jnp.bfloat16),
        scratch_shapes=[pltpu.SemaphoreType.DMA],
        compiler_params=pltpu.CompilerParams(vmem_limit_bytes=2 * MIB),
        cost_estimate=pl.CostEstimate(
            flops=0, bytes_accessed=4 * size * math.prod(frf.shape[1:]), transcendentals=0
        ),
        name="load",
    )(in_hbm(frf), after)


def respond_kernel(count, *refs):
    pieces, parts = refs[:count], refs[count:-4]
    out_ref, direct_ref, turned_ref, acc_ref = refs[-4:]
    _, rows, modes = out_ref.shape
    total = sum(piece[...].astype(jnp.float32) for piece in pieces).reshape(2 * rows, modes)
    total = total.astype(jnp.bfloat16).astype(jnp.float32)
    row = lax.broadcasted_iota(jnp.int32, total.shape, 0)
    turned = jnp.where(row % 2 == 0, -jnp.roll(total, -1, axis=0), jnp.roll(total, 1, axis=0))
    direct_ref[...] = total.T.astype(jnp.bfloat16)
    turned_ref[...] = turned.T.astype(jnp.bfloat16)
    acc_ref[...] = jnp.zeros_like(acc_ref)
    each = math.gcd(4, *(part.shape[0] for part in parts))
    pair = lax.broadcasted_iota(jnp.int32, (modes, 2 * rows), 1) // 2
    base = 0
    for part in parts:

        @pl.loop(0, part.shape[0] // each)
        def _(step, part=part, base=base):
            block = part.at[pl.ds(step * each, each)]
            real = block[:, 0].reshape(each * modes, modes)
            imag = block[:, 1].reshape(each * modes, modes)
            products = jnp.dot(real, direct_ref[...], preferred_element_type=jnp.float32)
            products += jnp.dot(imag, turned_ref[...], preferred_element_type=jnp.float32)
            products = products.reshape(each, modes, 2 * rows)
            acc = acc_ref[...]
            for i in range(each):
                f = base + step * each + i
                acc = jnp.where(pair == (f % 2) * (rows // 2) + f // 2, products[i], acc)
            acc_ref[...] = acc

        base += part.shape[0]

    out_ref[...] = acc_ref[...].T.reshape(2, rows, modes).astype(jnp.bfloat16)


def respond(pieces, parts):
    rows, modes = pieces[0].shape[1:]
    vmem = pl.BlockSpec(memory_space=pltpu.VMEM)
    size = sum(part.size for part in parts)
    return pl.pallas_call(
        functools.partial(respond_kernel, len(pieces)),
        in_specs=[vmem] * (len(pieces) + len(parts)),
        out_specs=vmem,
        out_shape=jax.ShapeDtypeStruct((2, rows, modes), jnp.bfloat16),
        scratch_shapes=[
            pltpu.VMEM((modes, 2 * rows), jnp.bfloat16),
            pltpu.VMEM((modes, 2 * rows), jnp.bfloat16),
            pltpu.VMEM((modes, 2 * rows), jnp.float32),
        ],
        compiler_params=pltpu.CompilerParams(vmem_limit_bytes=12 * MIB),
        cost_estimate=pl.CostEstimate(flops=4 * size, bytes_accessed=2 * size, transcendentals=0),
        name="respond",
    )(*pieces, *parts)


def inverse_kernel(
    place_ref, table_ref, shapes_ref, own_ref, across_ref, twin_ref, twin_across_ref,
    out_ref, order_ref, moved_ref, out_buf, out_sem,
):
    zs, _, rows, modes = own_ref.shape
    half, block = out_ref.shape[1], out_buf.shape[2]
    core, chip = place_ref[0], place_ref[1]
    for far, near_y in enumerate(((own_ref, across_ref), (twin_ref, twin_across_ref))):
        for rel_y, shard_ref in enumerate(near_y):
            for k in range(zs):
                for parity in range(2):
                    order_ref[parity, core ^ far, chip ^ (2 * k + rel_y)] = shard_ref[
                        k, parity
                    ].astype(jnp.float32)
    for parity in range(2):
        moved_ref[parity] = jnp.dot(
            order_ref[parity].reshape(FREQS, modes).astype(jnp.bfloat16),
            shapes_ref[...],
            preferred_element_type=jnp.float32,
        ).astype(jnp.bfloat16)

    def copy_out(step, slot):
        return pltpu.make_async_copy(
            out_buf.at[slot], out_ref.at[:, pl.ds(step * block, block)], out_sem.at[slot]
        )

    for step in range(half // block):
        slot = step % 2
        part = slice(step * block, (step + 1) * block)
        even = jnp.dot(table_ref[0, part], moved_ref[0], preferred_element_type=jnp.float32)
        odd = jnp.dot(table_ref[1, part], moved_ref[1], preferred_element_type=jnp.float32)
        if step >= 2:
            copy_out(step - 2, slot).wait()
        out_buf[slot, 0] = (even + odd).astype(jnp.bfloat16)
        out_buf[slot, 1] = (even - odd).astype(jnp.bfloat16)
        copy_out(step, slot).start()
    for step in range(half // block - 2, half // block):
        copy_out(step, step % 2).wait()


def inverse(place, table, shapes_t, shards, chips):
    _, half, _ = table.shape
    modes, dofs = shapes_t.shape
    block = 512
    rows = shards[0].shape[2]
    vmem = pl.BlockSpec(memory_space=pltpu.VMEM)
    return pl.pallas_call(
        inverse_kernel,
        in_specs=[pl.BlockSpec(memory_space=pltpu.SMEM)] + [vmem] * 6,
        out_specs=pl.BlockSpec(memory_space=pltpu.HBM),
        out_shape=jax.ShapeDtypeStruct((2, half, dofs), jnp.bfloat16),
        scratch_shapes=[
            pltpu.VMEM((2, CORES, chips, rows, modes), jnp.float32),
            pltpu.VMEM((2, FREQS, dofs), jnp.bfloat16),
            pltpu.VMEM((2, 2, block, dofs), jnp.bfloat16),
            pltpu.SemaphoreType.DMA((2,)),
        ],
        compiler_params=pltpu.CompilerParams(vmem_limit_bytes=24 * MIB),
        cost_estimate=pl.CostEstimate(
            flops=4 * FREQS * dofs * (half + modes), bytes_accessed=12 * MIB, transcendentals=0
        ),
        name="inverse",
    )(place, table, shapes_t, *shards)


def add_kernel(ours_ref, came_ref, after_ref, *out_refs):
    for n, out_ref in enumerate(out_refs):
        total = ours_ref[n].astype(jnp.float32) + came_ref[n].astype(jnp.float32)
        out_ref[...] = total.astype(jnp.bfloat16)


def add(ours, came, after):
    vmem, anywhere = pl.BlockSpec(memory_space=pltpu.VMEM), pl.BlockSpec(memory_space=pl.ANY)
    return pl.pallas_call(
        add_kernel,
        in_specs=[vmem, vmem, anywhere],
        out_specs=[vmem] * ours.shape[0],
        out_shape=[jax.ShapeDtypeStruct(ours.shape[1:], jnp.bfloat16)] * ours.shape[0],
        compiler_params=pltpu.CompilerParams(vmem_limit_bytes=8 * MIB),
        cost_estimate=pl.CostEstimate(
            flops=ours.size, bytes_accessed=6 * ours.size, transcendentals=0
        ),
        name="add",
    )(ours, came, after)


def on_device(devices, forces, mode_shapes, frf):
    _, steps, dofs = forces.shape
    half = steps // 2
    chips = devices // CORES
    zs = chips // 2

    def swap(values, distance):
        pairs = [(i, i ^ distance) for i in range(devices)]
        return lax.ppermute(values, "dof", pairs)

    index = lax.axis_index("dof")
    place = jnp.stack([index % CORES, index // CORES]).astype(jnp.int32)
    shapes_t = mode_shapes.T
    fwd = jnp.asarray(forward_tables(steps, chips).astype(jnp.bfloat16))
    inv = jnp.asarray(inverse_tables(steps, chips).astype(jnp.bfloat16))

    mine = frf.shape[0]
    first, second = mine // 4, 3 * mine // 8
    keep, send, part0 = forward(
        place, fwd, forces.reshape(2, half, dofs), shapes_t, frf, first, chips
    )
    here, there = add(keep, swap(send, 1), send)
    part1 = load(frf, first, second, there)
    pieces = add(here, swap(there, 2), part1)
    part2 = load(frf, first + second, mine - first - second, pieces[0])
    pieces = [pieces[0]] + [swap(pieces[k], 4 * k) for k in range(1, zs)]
    response = respond(pieces, (part0, part1, part2))
    own = jnp.stack([response] + [swap(response, 4 * k) for k in range(1, zs)])
    across = swap(own, 2)
    twin = swap(own, 1)
    twin_across = swap(across, 1)
    out = inverse(place, inv, shapes_t, (own, across, twin, twin_across), chips)
    return out.reshape(1, steps, dofs)


def solution(mesh):
    devices = mesh.shape["dof"]
    return jax.shard_map(
        functools.partial(on_device, devices),
        mesh=mesh,
        in_specs=(P("grp", None, "dof"), P("dof", None), P("dof", None, None, None)),
        out_specs=P("grp", None, "dof"),
        check_vma=False,
    )
```

time: 169 us -> 62.1 us (0.37)
  waiting for transfers between devices: 60.2 us -> 15.5 us
  Pallas kernels: 0 us -> 32.3 us
  matrix products: 30.5 us -> 0 us
  blocking collectives: 24.2 us -> 0 us
  local copies, waits for them, and re-layouts: 22.1 us -> 0.01 us
  other arithmetic: 17.7 us -> 0.12 us
  starting transfers between devices: 0.01 us -> 14 us
  between operations: 13.5 us -> 0.07 us
    reduce_scatter x1 -> x0, waiting for transfers between devices: 60.2 us -> none  [on_device(): lax.psum_scatter(partial, 'dof', scatter_dimension=0, tiled=True)]
    pallas_call x0 -> x7, Pallas kernels: none -> 32.3 us  [the longest x1 9.21 us: respond(): pl.pallas_call(functools.partial(respond_kernel, len(pieces)), in_specs=[...]
    dot_general x3 -> x0, matrix products: 30.5 us -> none  [the longest x1 13.3 us: on_device(): jnp.einsum('fanm,fbm->fabn', frf, modal_spec, preferred_element_type=jnp....]
    all_gather x1 -> x0, blocking collectives: 24.2 us -> none  [on_device(): gathered = lax.all_gather(response, 'dof', axis=0, tiled=True)]
    ppermute x0 -> x11, waiting for transfers between devices: none -> 15.5 us  [swap(): return lax.ppermute(values, 'dof', pairs)]
    ppermute x0 -> x11, starting transfers between devices: none -> 14 us  [swap(): return lax.ppermute(values, 'dof', pairs)]
    another operation x3 -> x2, other arithmetic: 13.5 us -> 0.12 us  [the longest x1 0.07 us: on_device(): place = jnp.stack([index % CORES, index // CORES]).astype(jnp.int32)]
    unnamed x6 -> x4, local copies, waits for them, and re-layouts: 9.36 us -> 0.01 us
  transfers between devices with their start and end apart: 1 -> 11, of which waited for: 1 -> 7; matrix products, arithmetic and copies ran while one was open for 0% -> 0% of each run, Pallas kernels for 0% -> 13%
where the time goes in v3:
time: 62.1 us; the launch traced here: 62 us
  Pallas kernels  32.3 us (52%)
  waiting for transfers between devices  15.5 us (25%)
  starting transfers between devices  14 us (23%)
    ppermute x11, waiting for transfers between devices, swap(): return lax.ppermute(values, 'dof', pairs)  15.5 us
    ppermute x11, starting transfers between devices, swap(): return lax.ppermute(values, 'dof', pairs)  14 us
    pallas_call x1, Pallas kernels, respond(): pl.pallas_call(functools.partial(respond_kernel, len(pieces)), in_specs=[...  9.21 us
    pallas_call x2, Pallas kernels, load(): pl.pallas_call(functools.partial(load_kernel, start), in_specs=[hbm, anyw...  8.27 us
    pallas_call x1, Pallas kernels, forward(): pl.pallas_call(forward_kernel, in_specs=[pl.BlockSpec(memory_space=pltpu....  7.55 us
    pallas_call x1, Pallas kernels, inverse(): pl.pallas_call(inverse_kernel, in_specs=[pl.BlockSpec(memory_space=pltpu....  7.05 us
  transfers between devices with their start and end apart: 11, of which 7 were waited for; matrix products, arithmetic and copies ran while one was open for 0% of the time, Pallas kernels for 13%

profile of v3, /device:TPU:0, one launch (start us, length us, event | category | flops | bytes accessed | tf_op | source)
XLA Modules:
  0.0 62.0 jit_solution(5070802362360618443)
XLA Ops:
  0.0 0.1 pad_add_fusion.place_ref
  0.1 7.6 %forward.1 = (bf16[2,4,2,32,448]{4,3,2,1,0:T(8,128)(2,1)S(1)}, bf16[2,4,2,32,448]{4,3,2,1,0:T(8,128)(2,1)S(1)}, bf16[8,2,448,448]{3,2,1,0:T(8,128)(2,1)S(1)}) custom-call(s32[2]{0:T(128)S(1)} %pad_add_fusion.place_ref, bf16[2,512,2048]{2,1,0:T(8,128)(2,1)} %constant.32.clone.table_ref, bf16[2,2048,768]{2,1,0:T(8,128)(2,1)} %bitcast.12, ...), custom_call_target="tpu_custom_call" | custom-call | flops 3925868544 | bytes 20971520 | tf_op jit(solution)/shard_map/forward/pallas_call | solution.py:122
  7.6 0.5 collective-permute-start
  8.2 1.5 %collective-permute-done.came_ref = bf16[2,4,2,32,448]{4,3,2,1,0:T(8,128)(2,1)S(1)} collective-permute-done((bf16[2,4,2,32,448]{4,3,2,1,0:T(8,128)(2,1)S(1)}, bf16[2,4,2,32,448]{4,3,2,1,0:T(8,128)(2,1)S(1)}, u32[]{:S(2)}, u32[]{:S(2)}) %collective-permute-start) | collective-permute-done | bytes 458784 | tf_op jit(solution)/shard_map/ppermute | solution.py:318
  9.7 0.1 add.10
  9.8 3.0 %collective-permute-start.1 = (bf16[4,2,32,448]{3,2,1,0:T(8,128)(2,1)S(1)}, bf16[4,2,32,448]{3,2,1,0:T(8,128)(2,1)S(1)}, u32[]{:S(2)}, u32[]{:S(2)}) collective-permute-start(bf16[4,2,32,448]{3,2,1,0:T(8,128)(2,1)S(1)} %get-tuple-element.17.after_ref), channel_id=1, source_target_pairs={{0,2},{1,3},{2,0},{3,1},{4,6},{5,7},{6,4},{7,5},{8,10},{9,11},{10,... | collective-permute-start | bytes 688136 | tf_op jit(solution)/shard_map/ppermute | solution.py:318
  12.8 4.1 %load.2.after_ref.refs_5_ = bf16[12,2,448,448]{3,2,1,0:T(8,128)(2,1)S(1)} custom-call(bf16[32,2,448,448]{3,2,1,0:T(8,128)(2,1)} %frf_ref.5, bf16[4,2,32,448]{3,2,1,0:T(8,128)(2,1)S(1)} %get-tuple-element.17.after_ref), custom_call_target="tpu_custom_call" | custom-call | bytes 19267584 | tf_op jit(solution)/shard_map/load/pallas_call | solution.py:155
  16.9 2.5 %collective-permute-done.1.came_ref = bf16[4,2,32,448]{3,2,1,0:T(8,128)(2,1)S(1)} collective-permute-done((bf16[4,2,32,448]{3,2,1,0:T(8,128)(2,1)S(1)}, bf16[4,2,32,448]{3,2,1,0:T(8,128)(2,1)S(1)}, u32[]{:S(2)}, u32[]{:S(2)}) %collective-permute-start.1) | collective-permute-done | bytes 229408 | tf_op jit(solution)/shard_map/ppermute | solution.py:318
  19.4 0.1 add.11
  19.4 1.9 %collective-permute-start.2 = (bf16[2,32,448]{2,1,0:T(8,128)(2,1)S(1)}, bf16[2,32,448]{2,1,0:T(8,128)(2,1)S(1)}, u32[]{:S(2)}, u32[]{:S(2)}) collective-permute-start(bf16[2,32,448]{2,1,0:T(8,128)(2,1)S(1)} %get-tuple-element.19), channel_id=1, source_target_pairs={{0,4},{1,5},{2,6},{3,7},{4,0},{5,1},{6,2},{7,3},{8,12},{9,13},{10,... | collective-permute-start | bytes 172040 | tf_op jit(solution)/shard_map/ppermute | solution.py:318
  21.3 2.6 %collective-permute-start.3 = (bf16[2,32,448]{2,1,0:T(8,128)(2,1)S(1)}, bf16[2,32,448]{2,1,0:T(8,128)(2,1)S(1)}, u32[]{:S(2)}, u32[]{:S(2)}) collective-permute-start(bf16[2,32,448]{2,1,0:T(8,128)(2,1)S(1)} %get-tuple-element.20), channel_id=1, source_target_pairs={{0,8},{1,9},{2,10},{3,11},{4,12},{5,13},{6,14},{7,15},{8,0},{9,1},... | collective-permute-start | bytes 172040 | tf_op jit(solution)/shard_map/ppermute | solution.py:318
  23.9 0.0 collective-permute-start.4
  23.9 4.1 %load.3.refs_6_ = bf16[12,2,448,448]{3,2,1,0:T(8,128)(2,1)S(1)} custom-call(bf16[32,2,448,448]{3,2,1,0:T(8,128)(2,1)} %frf_ref.5, bf16[2,32,448]{2,1,0:T(8,128)(2,1)S(1)} %get-tuple-element.18.after_ref.refs_0_), custom_call_target="tpu_custom_call" | custom-call | bytes 19267584 | tf_op jit(solution)/shard_map/load/pallas_call | solution.py:155
  28.0 0.0 collective-permute-done.2.refs_1_
  28.1 0.0 collective-permute-done.3.refs_2_
  28.1 1.9 %collective-permute-done.4.refs_3_ = bf16[2,32,448]{2,1,0:T(8,128)(2,1)S(1)} collective-permute-done((bf16[2,32,448]{2,1,0:T(8,128)(2,1)S(1)}, bf16[2,32,448]{2,1,0:T(8,128)(2,1)S(1)}, u32[]{:S(2)}, u32[]{:S(2)}) %collective-permute-start.4) | collective-permute-done | bytes 57376 | tf_op jit(solution)/shard_map/ppermute | solution.py:318
  30.0 0.0 copy-start
  30.0 0.0 copy-start.1
  30.0 9.2 %respond.1 = bf16[2,32,448]{2,1,0:T(8,128)(2,1)S(1)} custom-call(bf16[2,32,448]{2,1,0:T(8,128)(2,1)S(1)} %get-tuple-element.18.after_ref.refs_0_, bf16[2,32,448]{2,1,0:T(8,128)(2,1)S(1)} %collective-permute-done.2.refs_1_, bf16[2,32,448]{2,1,0:T(8,128)(2,1)S(1)} %collective-permute-done.3.refs_2_, bf16[2,32,448]{2,1,0:T(8,128)(2,1)S(1)} %collective-permute-done.4.refs_3_, ...), custom_call_target="tpu_custom_call" | custom-call | flops 51380224 | bytes 25690112 | tf_op jit(solution)/shard_map/respond/pallas_call | solution.py:208
  39.2 2.0 %collective-permute-start.7 = (bf16[2,32,448]{2,1,0:T(8,128)(2,1)S(1)}, bf16[2,32,448]{2,1,0:T(8,128)(2,1)S(1)}, u32[]{:S(2)}, u32[]{:S(2)}) collective-permute-start(bf16[2,32,448]{2,1,0:T(8,128)(2,1)S(1)} %respond.1), channel_id=1, source_target_pairs={{0,12},{1,13},{2,14},{3,15},{4,8},{5,9},{6,10},{7,11},{8,4},{9,5},... | collective-permute-start | bytes 172040 | tf_op jit(solution)/shard_map/ppermute | solution.py:318
  41.2 0.0 collective-permute-start.6
  41.2 2.4 %collective-permute-start.5 = (bf16[2,32,448]{2,1,0:T(8,128)(2,1)S(1)}, bf16[2,32,448]{2,1,0:T(8,128)(2,1)S(1)}, u32[]{:S(2)}, u32[]{:S(2)}) collective-permute-start(bf16[2,32,448]{2,1,0:T(8,128)(2,1)S(1)} %respond.1), channel_id=1, source_target_pairs={{0,4},{1,5},{2,6},{3,7},{4,0},{5,1},{6,2},{7,3},{8,12},{9,13},{10,... | collective-permute-start | bytes 172040 | tf_op jit(solution)/shard_map/ppermute | solution.py:318
  43.6 1.9 %collective-permute-done.7 = bf16[2,32,448]{2,1,0:T(8,128)(2,1)S(1)} collective-permute-done((bf16[2,32,448]{2,1,0:T(8,128)(2,1)S(1)}, bf16[2,32,448]{2,1,0:T(8,128)(2,1)S(1)}, u32[]{:S(2)}, u32[]{:S(2)}) %collective-permute-start.7) | collective-permute-done | bytes 57376 | tf_op jit(solution)/shard_map/ppermute | solution.py:318
  45.5 1.4 %collective-permute-done.6 = bf16[2,32,448]{2,1,0:T(8,128)(2,1)S(1)} collective-permute-done((bf16[2,32,448]{2,1,0:T(8,128)(2,1)S(1)}, bf16[2,32,448]{2,1,0:T(8,128)(2,1)S(1)}, u32[]{:S(2)}, u32[]{:S(2)}) %collective-permute-start.6) | collective-permute-done | bytes 57376 | tf_op jit(solution)/shard_map/ppermute | solution.py:318
  46.9 0.0 collective-permute-done.5
  46.9 1.6 %collective-permute-start.8 = (bf16[4,2,32,448]{3,2,1,0:T(8,128)(2,1)S(1)}, bf16[4,2,32,448]{3,2,1,0:T(8,128)(2,1)S(1)}, u32[]{:S(2)}, u32[]{:S(2)}) collective-permute-start(bf16[4,2,32,448]{3,2,1,0:T(8,128)(2,1)S(1)} %pad_maximum_fusion.own_ref), channel_id=1, source_target_pairs={{0,2},{1,3},{2,0},{3,1},{4,6},{5,7},{6,4},{7,5},{8,10},{9,11},{10,... | collective-permute-start | bytes 688136 | tf_op jit(solution)/shard_map/ppermute | solution.py:318
  48.5 0.0 collective-permute-start.9
  48.5 4.9 %collective-permute-done.8.across_ref = bf16[4,2,32,448]{3,2,1,0:T(8,128)(2,1)S(1)} collective-permute-done((bf16[4,2,32,448]{3,2,1,0:T(8,128)(2,1)S(1)}, bf16[4,2,32,448]{3,2,1,0:T(8,128)(2,1)S(1)}, u32[]{:S(2)}, u32[]{:S(2)}) %collective-permute-start.8) | collective-permute-done | bytes 229408 | tf_op jit(solution)/shard_map/ppermute | solution.py:318
  53.4 0.0 collective-permute-start.10
  53.4 0.0 collective-permute-done.9.twin_ref
  53.4 1.5 %collective-permute-done.10.twin_across_ref = bf16[4,2,32,448]{3,2,1,0:T(8,128)(2,1)S(1)} collective-permute-done((bf16[4,2,32,448]{3,2,1,0:T(8,128)(2,1)S(1)}, bf16[4,2,32,448]{3,2,1,0:T(8,128)(2,1)S(1)}, u32[]{:S(2)}, u32[]{:S(2)}) %collective-permute-start.10) | collective-permute-done | bytes 229408 | tf_op jit(solution)/shard_map/ppermute | solution.py:318
  54.9 0.0 copy-done
  54.9 0.0 copy-done.1
  54.9 7.1 %inverse.1 = bf16[2,2048,768]{2,1,0:T(8,128)(2,1)} custom-call(s32[2]{0:T(128)S(1)} %pad_add_fusion.place_ref, bf16[2,2048,512]{2,1,0:T(8,128)(2,1)S(1)} %copy-done.1, bf16[448,768]{1,0:T(8,128)(2,1)S(1)} %bitcast.10, bf16[4,2,32,448]{3,2,1,0:T(8,128)(2,1)S(1)} %pad_maximum_fusion.own_ref, bf16[4,2,32,448]{3,2,1,0:T(8,128)(2,1)S(1)} %collective-permute-done.8.across_ref, ...), custom_call_target="tpu_custom_call" | custom-call | flops 3925868544 | bytes 12582912 | tf_op jit(solution)/shard_map/inverse/pallas_call | solution.py:270
  (1 shorter events, 0.0 us)
Async XLA Ops:
  7.6 2.1 %collective-permute-start = (bf16[2,4,2,32,448]{4,3,2,1,0:T(8,128)(2,1)S(1)}, bf16[2,4,2,32,448]{4,3,2,1,0:T(8,128)(2,1)S(1)}, u32[]{:S(2)}, u32[]{:S(2)}) collective-permute-start(bf16[2,4,2,32,448]{4,3,2,1,0:T(8,128)(2,1)S(1)} %get-tuple-element.15.after_ref), channel_id=1, source_target_pairs={{0,1},{1,0},{2,3},{3,2},{4,5},{5,4},{6,7},{7,6},{8,9},{9,8},{10,11... | collective-permute-start | bytes 1376264 | tf_op jit(solution)/shard_map/ppermute | solution.py:318
  9.8 9.6 %collective-permute-start.1 = (bf16[4,2,32,448]{3,2,1,0:T(8,128)(2,1)S(1)}, bf16[4,2,32,448]{3,2,1,0:T(8,128)(2,1)S(1)}, u32[]{:S(2)}, u32[]{:S(2)}) collective-permute-start(bf16[4,2,32,448]{3,2,1,0:T(8,128)(2,1)S(1)} %get-tuple-element.17.after_ref), channel_id=1, source_target_pairs={{0,2},{1,3},{2,0},{3,1},{4,6},{5,7},{6,4},{7,5},{8,10},{9,11},{10,... | collective-permute-start | bytes 688136 | tf_op jit(solution)/shard_map/ppermute | solution.py:318
  19.4 8.6 %collective-permute-start.2 = (bf16[2,32,448]{2,1,0:T(8,128)(2,1)S(1)}, bf16[2,32,448]{2,1,0:T(8,128)(2,1)S(1)}, u32[]{:S(2)}, u32[]{:S(2)}) collective-permute-start(bf16[2,32,448]{2,1,0:T(8,128)(2,1)S(1)} %get-tuple-element.19), channel_id=1, source_target_pairs={{0,4},{1,5},{2,6},{3,7},{4,0},{5,1},{6,2},{7,3},{8,12},{9,13},{10,... | collective-permute-start | bytes 172040 | tf_op jit(solution)/shard_map/ppermute | solution.py:318
  21.3 6.7 %collective-permute-start.3 = (bf16[2,32,448]{2,1,0:T(8,128)(2,1)S(1)}, bf16[2,32,448]{2,1,0:T(8,128)(2,1)S(1)}, u32[]{:S(2)}, u32[]{:S(2)}) collective-permute-start(bf16[2,32,448]{2,1,0:T(8,128)(2,1)S(1)} %get-tuple-element.20), channel_id=1, source_target_pairs={{0,8},{1,9},{2,10},{3,11},{4,12},{5,13},{6,14},{7,15},{8,0},{9,1},... | collective-permute-start | bytes 172040 | tf_op jit(solution)/shard_map/ppermute | solution.py:318
  23.9 6.1 %collective-permute-start.4 = (bf16[2,32,448]{2,1,0:T(8,128)(2,1)S(1)}, bf16[2,32,448]{2,1,0:T(8,128)(2,1)S(1)}, u32[]{:S(2)}, u32[]{:S(2)}) collective-permute-start(bf16[2,32,448]{2,1,0:T(8,128)(2,1)S(1)} %get-tuple-element.21), channel_id=1, source_target_pairs={{0,12},{1,13},{2,14},{3,15},{4,8},{5,9},{6,10},{7,11},{8,4},{9,5},... | collective-permute-start | bytes 172040 | tf_op jit(solution)/shard_map/ppermute | solution.py:318
  30.0 24.9 %copy-start = (bf16[768,448]{0,1:T(8,128)(2,1)S(1)}, bf16[768,448]{0,1:T(8,128)(2,1)}, u32[]{:S(2)}) copy-start(bf16[768,448]{0,1:T(8,128)(2,1)} %param.6) | copy-start | bytes 2064388
  30.0 24.9 %copy-start.1 = (bf16[2,2048,512]{2,1,0:T(8,128)(2,1)S(1)}, bf16[2,2048,512]{2,1,0:T(8,128)(2,1)}, u32[]{:S(2)}) copy-start(bf16[2,2048,512]{2,1,0:T(8,128)(2,1)} %constant.33.clone.table_ref) | copy-start | bytes 12582916
  39.2 6.3 %collective-permute-start.7 = (bf16[2,32,448]{2,1,0:T(8,128)(2,1)S(1)}, bf16[2,32,448]{2,1,0:T(8,128)(2,1)S(1)}, u32[]{:S(2)}, u32[]{:S(2)}) collective-permute-start(bf16[2,32,448]{2,1,0:T(8,128)(2,1)S(1)} %respond.1), channel_id=1, source_target_pairs={{0,12},{1,13},{2,14},{3,15},{4,8},{5,9},{6,10},{7,11},{8,4},{9,5},... | collective-permute-start | bytes 172040 | tf_op jit(solution)/shard_map/ppermute | solution.py:318
  41.2 5.7 %collective-permute-start.6 = (bf16[2,32,448]{2,1,0:T(8,128)(2,1)S(1)}, bf16[2,32,448]{2,1,0:T(8,128)(2,1)S(1)}, u32[]{:S(2)}, u32[]{:S(2)}) collective-permute-start(bf16[2,32,448]{2,1,0:T(8,128)(2,1)S(1)} %respond.1), channel_id=1, source_target_pairs={{0,8},{1,9},{2,10},{3,11},{4,12},{5,13},{6,14},{7,15},{8,0},{9,1},... | collective-permute-start | bytes 172040 | tf_op jit(solution)/shard_map/ppermute | solution.py:318
  41.2 5.7 %collective-permute-start.5 = (bf16[2,32,448]{2,1,0:T(8,128)(2,1)S(1)}, bf16[2,32,448]{2,1,0:T(8,128)(2,1)S(1)}, u32[]{:S(2)}, u32[]{:S(2)}) collective-permute-start(bf16[2,32,448]{2,1,0:T(8,128)(2,1)S(1)} %respond.1), channel_id=1, source_target_pairs={{0,4},{1,5},{2,6},{3,7},{4,0},{5,1},{6,2},{7,3},{8,12},{9,13},{10,... | collective-permute-start | bytes 172040 | tf_op jit(solution)/shard_map/ppermute | solution.py:318
  46.9 6.4 %collective-permute-start.8 = (bf16[4,2,32,448]{3,2,1,0:T(8,128)(2,1)S(1)}, bf16[4,2,32,448]{3,2,1,0:T(8,128)(2,1)S(1)}, u32[]{:S(2)}, u32[]{:S(2)}) collective-permute-start(bf16[4,2,32,448]{3,2,1,0:T(8,128)(2,1)S(1)} %pad_maximum_fusion.own_ref), channel_id=1, source_target_pairs={{0,2},{1,3},{2,0},{3,1},{4,6},{5,7},{6,4},{7,5},{8,10},{9,11},{10,... | collective-permute-start | bytes 688136 | tf_op jit(solution)/shard_map/ppermute | solution.py:318
  48.5 4.9 %collective-permute-start.9 = (bf16[4,2,32,448]{3,2,1,0:T(8,128)(2,1)S(1)}, bf16[4,2,32,448]{3,2,1,0:T(8,128)(2,1)S(1)}, u32[]{:S(2)}, u32[]{:S(2)}) collective-permute-start(bf16[4,2,32,448]{3,2,1,0:T(8,128)(2,1)S(1)} %pad_maximum_fusion.own_ref), channel_id=1, source_target_pairs={{0,1},{1,0},{2,3},{3,2},{4,5},{5,4},{6,7},{7,6},{8,9},{9,8},{10,11... | collective-permute-start | bytes 688136 | tf_op jit(solution)/shard_map/ppermute | solution.py:318
  53.4 1.5 %collective-permute-start.10 = (bf16[4,2,32,448]{3,2,1,0:T(8,128)(2,1)S(1)}, bf16[4,2,32,448]{3,2,1,0:T(8,128)(2,1)S(1)}, u32[]{:S(2)}, u32[]{:S(2)}) collective-permute-start(bf16[4,2,32,448]{3,2,1,0:T(8,128)(2,1)S(1)} %collective-permute-done.8.across_ref), channel_id=1, source_target_pairs={{0,1},{1,0},{2,3},{3,2},{4,5},{5,4},{6,7},{7,6},{8,9},{9,8},{10,11... | collective-permute-start | bytes 688136 | tf_op jit(solution)/shard_map/ppermute | solution.py:318

commit v4 on v3

v4 whole, which is shorter than its diff:
```python
import functools
import math

import jax
import jax.numpy as jnp
import numpy as np
from jax import lax
from jax.experimental import pallas as pl
from jax.experimental.pallas import tpu as pltpu
from jax.sharding import PartitionSpec as P

FREQS = 512
CORES = 2
MIB = 1 << 20


def frequency_order(chips, parity):
    mine = FREQS // (chips * CORES)
    owned = np.arange(FREQS).reshape(chips // 2, 2, CORES, mine // 2, 2)
    return owned[..., parity].transpose(1, 2, 0, 3).reshape(-1)


def forward_tables(steps, chips):
    times = np.arange(steps // 2, dtype=np.int64)
    tables = []
    for parity in range(2):
        ids = frequency_order(chips, parity)
        angle = (ids[:, None] * times[None, :] % steps) * (2.0 * math.pi / steps)
        table = np.stack([np.cos(angle), -np.sin(angle)], axis=1) / math.sqrt(steps)
        tables.append(table.reshape(FREQS, steps // 2))
    return np.stack(tables)


def inverse_tables(steps, chips):
    tables = forward_tables(steps, chips) * 2.0
    for parity in range(2):
        weights = np.where(frequency_order(chips, parity) == 0, 0.5, 1.0)
        tables[parity] *= np.repeat(weights, 2)[:, None]
    return tables.reshape(2, 2, FREQS // 2, steps // 2).transpose(0, 1, 3, 2)


def chunk_list(half):
    unit = half // 8
    sizes = (unit, unit, 2 * unit, 4 * unit)
    starts = (0, unit, 2 * unit, 4 * unit)
    return tuple(zip(starts, sizes))


def forward_kernel(
    place_ref, table_ref, forces_ref, shapes_ref, frf_ref, keep_ref, send_ref, held_ref,
    table_buf, forces_buf, shapes_buf, acc_ref, table_sem, forces_sem, shapes_sem, held_sem,
):
    _, zs, _, rows, modes = keep_ref.shape
    chunks = chunk_list(forces_ref.shape[1])
    copies = []
    for n, (start, size) in enumerate(chunks):
        part = pl.ds(start, size)
        pair = (
            pltpu.make_async_copy(
                forces_ref.at[:, part], forces_buf.at[:, part], forces_sem.at[n]
            ),
            pltpu.make_async_copy(
                table_ref.at[:, :, part], table_buf.at[:, :, part], table_sem.at[n]
            ),
        )
        for copy in pair:
            copy.start()
        copies.append(pair)
    shapes_copy = pltpu.make_async_copy(shapes_ref, shapes_buf, shapes_sem)
    shapes_copy.start()
    held_copy = pltpu.make_async_copy(
        frf_ref.at[pl.ds(0, held_ref.shape[0])], held_ref, held_sem
    )
    held_copy.start()

    for n, (start, size) in enumerate(chunks):
        for copy in copies[n]:
            copy.wait()
        low = forces_buf[0, start : start + size]
        high = forces_buf[1, start : start + size]
        for parity, folded in enumerate((low + high, low - high)):
            part = jnp.dot(
                table_buf[parity, :, start : start + size],
                folded,
                preferred_element_type=jnp.float32,
            )
            if n == 0:
                acc_ref[parity] = part
            else:
                acc_ref[parity] += part

    shapes_copy.wait()
    first, chip = place_ref[0] == 0, place_ref[1]
    for parity in range(2):
        spec = lax.dot_general(
            acc_ref[parity].astype(jnp.bfloat16),
            shapes_buf[...],
            (((1,), (1,)), ((), ())),
            preferred_element_type=jnp.float32,
        ).reshape(2, CORES, zs, rows, modes)
        for y in range(2):
            keep = jnp.where(first, spec[y, 0], spec[y, 1]).astype(jnp.bfloat16)
            send = jnp.where(first, spec[y, 1], spec[y, 0]).astype(jnp.bfloat16)
            for z in range(zs):
                slot = chip ^ (2 * z + y)
                keep_ref[slot % 2, slot // 2, parity] = keep[z]
                send_ref[slot % 2, slot // 2, parity] = send[z]
    held_copy.wait()


def in_hbm(array):
    return pltpu.with_memory_space_constraint(array, pltpu.HBM)


def forward(place, table, forces, shapes_t, frf, held, chips):
    _, half, dofs = forces.shape
    modes = shapes_t.shape[0]
    rows = FREQS // (chips * CORES)
    out = jax.ShapeDtypeStruct((2, chips // 2, 2, rows, modes), jnp.bfloat16)
    vmem, hbm = pl.BlockSpec(memory_space=pltpu.VMEM), pl.BlockSpec(memory_space=pltpu.HBM)
    count = len(chunk_list(half))
    return pl.pallas_call(
        forward_kernel,
        in_specs=[pl.BlockSpec(memory_space=pltpu.SMEM), hbm, hbm, hbm, hbm],
        out_specs=[vmem, vmem, vmem],
        out_shape=[out, out, pltpu.VMEM((held,) + frf.shape[1:], jnp.bfloat16)],
        scratch_shapes=[
            pltpu.VMEM(table.shape, jnp.bfloat16),
            pltpu.VMEM(forces.shape, jnp.bfloat16),
            pltpu.VMEM(shapes_t.shape, jnp.bfloat16),
            pltpu.VMEM((2, FREQS, dofs), jnp.float32),
            pltpu.SemaphoreType.DMA((count,)),
            pltpu.SemaphoreType.DMA((count,)),
            pltpu.SemaphoreType.DMA,
            pltpu.SemaphoreType.DMA,
        ],
        compiler_params=pltpu.CompilerParams(vmem_limit_bytes=24 * MIB),
        cost_estimate=pl.CostEstimate(
            flops=4 * FREQS * dofs * (half + modes), bytes_accessed=20 * MIB, transcendentals=0
        ),
        name="forward",
    )(place, in_hbm(table), in_hbm(forces), in_hbm(shapes_t), in_hbm(frf))


def load_copies(start, frf_ref, held_ref, sem):
    count = sem.shape[0]
    size = held_ref.shape[0] // count
    return [
        pltpu.make_async_copy(
            frf_ref.at[pl.ds(start + n * size, size)],
            held_ref.at[pl.ds(n * size, size)],
            sem.at[n],
        )
        for n in range(count)
    ]


def load_kernel(start, frf_ref, after_ref, held_ref, sem):
    copies = load_copies(start, frf_ref, held_ref, sem)
    for copy in copies:
        copy.start()
    for copy in copies:
        copy.wait()


def load(frf, start, size, after):
    hbm, anywhere = pl.BlockSpec(memory_space=pltpu.HBM), pl.BlockSpec(memory_space=pl.ANY)
    return pl.pallas_call(
        functools.partial(load_kernel, start),
        in_specs=[hbm, anywhere],
        out_specs=pl.BlockSpec(memory_space=pltpu.VMEM),
        out_shape=pltpu.VMEM((size,) + frf.shape[1:], jnp.bfloat16),
        scratch_shapes=[pltpu.SemaphoreType.DMA((math.gcd(size, 4),))],
        compiler_params=pltpu.CompilerParams(vmem_limit_bytes=2 * MIB),
        cost_estimate=pl.CostEstimate(
            flops=0, bytes_accessed=4 * size * math.prod(frf.shape[1:]), transcendentals=0
        ),
        name="load",
    )(in_hbm(frf), after)


def respond_kernel(count, *refs):
    pieces, parts = refs[:count], refs[count:-4]
    out_ref, direct_ref, turned_ref, result_ref = refs[-4:]
    _, rows, modes = out_ref.shape
    total = sum(piece[0].astype(jnp.float32) for piece in pieces).reshape(2 * rows, modes)
    total = total.astype(jnp.bfloat16).astype(jnp.float32)
    row = lax.broadcasted_iota(jnp.int32, total.shape, 0)
    turned = jnp.where(row % 2 == 0, -jnp.roll(total, -1, axis=0), jnp.roll(total, 1, axis=0))

    def place(f):
        return (f % 2) * rows + f // 2 * 2

    direct_ref[...] = jnp.zeros_like(direct_ref)
    turned_ref[...] = jnp.zeros_like(turned_ref)
    for f in range(rows):
        at = place(f)
        direct_ref[f, 0:2] = total[at : at + 2]
        turned_ref[f, 0:2] = turned[at : at + 2]
    base = 0
    for part in parts:

        @pl.loop(0, part.shape[0], unroll=math.gcd(4, part.shape[0]))
        def _(step, part=part, base=base):
            f = base + step
            products = [
                lax.dot_general(
                    ref[f].astype(jnp.bfloat16),
                    part[step, which],
                    (((1,), (1,)), ((), ())),
                    preferred_element_type=jnp.float32,
                )
                for which, ref in enumerate((direct_ref, turned_ref))
            ]
            result_ref[f] = products[0] + products[1]

        base += part.shape[0]

    for f in range(rows):
        at = place(f)
        direct_ref[at // 8, at % 8 : at % 8 + 2] = result_ref[f, 0:2]
    out_ref[...] = (
        direct_ref[: 2 * rows // 8].reshape(2, rows, modes).astype(jnp.bfloat16)
    )


def respond(pieces, parts):
    rows, modes = pieces[0].shape[2:]
    vmem = pl.BlockSpec(memory_space=pltpu.VMEM)
    size = sum(part.size for part in parts)
    return pl.pallas_call(
        functools.partial(respond_kernel, len(pieces)),
        in_specs=[vmem] * (len(pieces) + len(parts)),
        out_specs=vmem,
        out_shape=jax.ShapeDtypeStruct((2, rows, modes), jnp.bfloat16),
        scratch_shapes=[pltpu.VMEM((rows, 8, modes), jnp.float32)] * 3,
        compiler_params=pltpu.CompilerParams(vmem_limit_bytes=12 * MIB),
        cost_estimate=pl.CostEstimate(flops=4 * size, bytes_accessed=2 * size, transcendentals=0),
        name="respond",
    )(*pieces, *parts)


def project(place_ref, shards, shapes_ref, order_ref, moved_ref):
    _, _, zs, rows, modes = order_ref.shape
    core, z = place_ref[0], place_ref[1] // 2
    start = 0
    for own_ref, twin_ref in zip(shards[::2], shards[1::2]):
        for far, shard_ref in enumerate((own_ref, twin_ref)):
            for k in range(shard_ref.shape[0]):
                for parity in range(2):
                    order_ref[parity, core ^ far, z ^ (start + k)] = shard_ref[
                        k, parity
                    ].astype(jnp.float32)
        start += own_ref.shape[0]
    for parity in range(2):
        moved_ref[parity] = jnp.dot(
            order_ref[parity].reshape(FREQS // 2, modes).astype(jnp.bfloat16),
            shapes_ref[...],
            preferred_element_type=jnp.float32,
        ).astype(jnp.bfloat16)


def early_kernel(place_ref, table_ref, shapes_ref, *refs):
    shards, (waves_ref, order_ref, moved_ref) = refs[:-3], refs[-3:]
    project(place_ref, shards, shapes_ref, order_ref, moved_ref)
    y = place_ref[1] % 2
    block = waves_ref.shape[1] // 4
    for step in range(4):
        part = slice(step * block, (step + 1) * block)
        for parity in range(2):
            waves_ref[parity, part] = jnp.dot(
                table_ref[parity, y, part], moved_ref[parity], preferred_element_type=jnp.float32
            )


def late_kernel(place_ref, table_ref, shapes_ref, *refs):
    shards, (waves_ref, out_ref, order_ref, moved_ref, out_buf, out_sem) = refs[:-6], refs[-6:]
    project(place_ref, shards, shapes_ref, order_ref, moved_ref)
    y = (place_ref[1] % 2) ^ 1
    count = out_sem.shape[0]
    block = out_ref.shape[1] // count

    def copy_out(step):
        part = pl.ds(step * block, block)
        return pltpu.make_async_copy(
            out_buf.at[:, part], out_ref.at[:, part], out_sem.at[step]
        )

    for step in range(count):
        part = slice(step * block, (step + 1) * block)
        even, odd = (
            waves_ref[parity, part]
            + jnp.dot(
                table_ref[parity, y, part], moved_ref[parity], preferred_element_type=jnp.float32
            )
            for parity in range(2)
        )
        out_buf[0, part] = (even + odd).astype(jnp.bfloat16)
        out_buf[1, part] = (even - odd).astype(jnp.bfloat16)
        copy_out(step).start()
    for step in range(count):
        copy_out(step).wait()


def inverse(place, table, shapes_t, shards, waves=None):
    half = table.shape[2]
    modes, dofs = shapes_t.shape
    rows = shards[0].shape[2]
    zs = sum(shard.shape[0] for shard in shards) // 2
    vmem = pl.BlockSpec(memory_space=pltpu.VMEM)
    scratch = [
        pltpu.VMEM((2, CORES, zs, rows, modes), jnp.float32),
        pltpu.VMEM((2, FREQS // 2, dofs), jnp.bfloat16),
    ]
    given = (place, table, shapes_t) + shards
    in_specs = [pl.BlockSpec(memory_space=pltpu.SMEM)] + [vmem] * (len(given) - 1)
    params = pltpu.CompilerParams(vmem_limit_bytes=20 * MIB)
    cost = pl.CostEstimate(
        flops=2 * FREQS * dofs * (half + modes), bytes_accessed=8 * MIB, transcendentals=0
    )
    if waves is None:
        return pl.pallas_call(
            early_kernel,
            in_specs=in_specs,
            out_specs=vmem,
            out_shape=pltpu.VMEM((2, half, dofs), jnp.float32),
            scratch_shapes=scratch,
            compiler_params=params,
            cost_estimate=cost,
            name="early",
        )(*given)
    return pl.pallas_call(
        late_kernel,
        in_specs=in_specs + [vmem],
        out_specs=pl.BlockSpec(memory_space=pltpu.HBM),
        out_shape=jax.ShapeDtypeStruct((2, half, dofs), jnp.bfloat16),
        scratch_shapes=scratch
        + [pltpu.VMEM((2, half, dofs), jnp.bfloat16), pltpu.SemaphoreType.DMA((8,))],
        compiler_params=params,
        cost_estimate=cost,
        name="late",
    )(*given, waves)


def add_kernel(start, splits, ours_ref, came_ref, after_ref, *out_refs):
    at = 0
    for size, out_ref in zip(splits, out_refs):
        for n in range(size):
            total = ours_ref[start + at + n].astype(jnp.float32) + came_ref[at + n].astype(
                jnp.float32
            )
            out_ref[n] = total.astype(jnp.bfloat16)
        at += size


def add(ours, came, start, splits, after):
    vmem, anywhere = pl.BlockSpec(memory_space=pltpu.VMEM), pl.BlockSpec(memory_space=pl.ANY)
    return pl.pallas_call(
        functools.partial(add_kernel, start, splits),
        in_specs=[vmem, vmem, anywhere],
        out_specs=[vmem] * len(splits),
        out_shape=[
            jax.ShapeDtypeStruct((size,) + ours.shape[1:], jnp.bfloat16) for size in splits
        ],
        compiler_params=pltpu.CompilerParams(vmem_limit_bytes=8 * MIB),
        cost_estimate=pl.CostEstimate(
            flops=came.size, bytes_accessed=6 * came.size, transcendentals=0
        ),
        name="add",
    )(ours, came, after)


def on_device(devices, forces, mode_shapes, frf):
    _, steps, dofs = forces.shape
    half = steps // 2
    chips = devices // CORES
    zs = chips // 2

    def swap(values, distance):
        pairs = [(i, i ^ distance) for i in range(devices)]
        return lax.ppermute(values, "dof", pairs)

    index = lax.axis_index("dof")
    place = jnp.stack([index % CORES, index // CORES]).astype(jnp.int32)
    shapes_t = mode_shapes.T
    fwd = jnp.asarray(forward_tables(steps, chips).astype(jnp.bfloat16))
    inv = jnp.asarray(inverse_tables(steps, chips).astype(jnp.bfloat16))

    unit = frf.shape[0] // 8
    keep, send, part0 = forward(
        place, fwd, forces.reshape(2, half, dofs), shapes_t, frf, 2 * unit, chips
    )
    part1 = load(frf, 2 * unit, unit, send)
    slots = (2 * zs,) + keep.shape[2:]
    here, there_near, there_far = add(
        keep.reshape(slots), swap(send, 1).reshape(slots), 0, (zs, 1, zs - 1), part1
    )
    came_far, came_near = swap(there_far, 2), swap(there_near, 2)
    part2 = load(frf, 3 * unit, 3 * unit, there_far)
    pieces = add(here, came_far, 1, (1,) * (zs - 1), part2)
    part3 = load(frf, 6 * unit, 2 * unit, pieces[0])
    came = [swap(piece, 4 * k) for k, piece in enumerate(pieces, 1)]
    response = respond([here[:1], came_near, *came], (part0, part1, part2, part3))

    across = swap(response[None], 2)
    shards = [swap(response, 4 * k) for k in range(1, zs)]
    far, across = lax.optimization_barrier((jnp.stack(shards), across))
    across_far = swap(far, 2)
    own = jnp.concatenate([response[None], far])
    twin, twin_across = swap(own, 1), swap(across, 1)
    waves = inverse(place, inv, shapes_t, (own, twin))
    across_far, waves = lax.optimization_barrier((across_far, waves))
    groups = (across, twin_across, across_far, swap(across_far, 1))
    out = inverse(place, inv, shapes_t, groups, waves)
    return out.reshape(1, steps, dofs)


def solution(mesh):
    devices = mesh.shape["dof"]
    return jax.shard_map(
        functools.partial(on_device, devices),
        mesh=mesh,
        in_specs=(P("grp", None, "dof"), P("dof", None), P("dof", None, None, None)),
        out_specs=P("grp", None, "dof"),
        check_vma=False,
    )
```

time: 62.1 us -> 58.8 us (0.947)
  waiting for transfers between devices: 15.5 us -> 9.4 us
  starting transfers between devices: 14 us -> 15.8 us
  Pallas kernels: 32.3 us -> 33.2 us
    ppermute x11 -> x14, waiting for transfers between devices: 15.5 us -> 9.4 us  [swap(): return lax.ppermute(values, 'dof', pairs)]
    ppermute x11 -> x14, starting transfers between devices: 14 us -> 15.8 us  [swap(): return lax.ppermute(values, 'dof', pairs)]
    pallas_call x2 -> x3, Pallas kernels: 8.27 us -> 9.47 us  [load(): pl.pallas_call(functools.partial(load_kernel, start), in_specs=[hbm, anyw...]
    pallas_call x3 -> x4, Pallas kernels: 7.24 us -> 7.48 us  [the longest x1 4.5 us: inverse(): pl.pallas_call(late_kernel, in_specs=in_specs + [vmem], out_specs=pl.Bloc...]
  transfers between devices with their start and end apart: 11 -> 14, of which waited for: 7 -> 8; matrix products, arithmetic and copies ran while one was open for 0% -> 0% of each run, Pallas kernels for 13% -> 21%
where the time goes in v4:
time: 58.8 us; the launch traced here: 58.7 us
  Pallas kernels  33.2 us (56%)
  starting transfers between devices  15.8 us (27%)
  waiting for transfers between devices  9.4 us (16%)
    ppermute x14, starting transfers between devices, swap(): return lax.ppermute(values, 'dof', pairs)  15.8 us
    pallas_call x3, Pallas kernels, load(): pl.pallas_call(functools.partial(load_kernel, start), in_specs=[hbm, anyw...  9.47 us
    ppermute x14, waiting for transfers between devices, swap(): return lax.ppermute(values, 'dof', pairs)  9.4 us
    pallas_call x1, Pallas kernels, respond(): pl.pallas_call(functools.partial(respond_kernel, len(pieces)), in_specs=[...  8.71 us
    pallas_call x1, Pallas kernels, forward(): pl.pallas_call(forward_kernel, in_specs=[pl.BlockSpec(memory_space=pltpu....  7.55 us
    pallas_call x1, Pallas kernels, inverse(): pl.pallas_call(late_kernel, in_specs=in_specs + [vmem], out_specs=pl.Bloc...  4.5 us
    pallas_call x1, Pallas kernels, inverse(): pl.pallas_call(early_kernel, in_specs=in_specs, out_specs=vmem, out_shape...  2.8 us
  transfers between devices with their start and end apart: 14, of which 8 were waited for; matrix products, arithmetic and copies ran while one was open for 0% of the time, Pallas kernels for 21%

profile of v4, /device:TPU:0, one launch (start us, length us, event | category | flops | bytes accessed | tf_op | source)
XLA Modules:
  0.0 58.7 jit_solution(5807154274827966621)
XLA Ops:
  0.0 0.1 pad_add_fusion.place_ref
  0.1 7.6 %forward.1 = (bf16[2,4,2,32,448]{4,3,2,1,0:T(8,128)(2,1)S(1)}, bf16[2,4,2,32,448]{4,3,2,1,0:T(8,128)(2,1)S(1)}, bf16[8,2,448,448]{3,2,1,0:T(8,128)(2,1)S(1)}) custom-call(s32[2]{0:T(128)S(1)} %pad_add_fusion.place_ref, bf16[2,512,2048]{2,1,0:T(8,128)(2,1)} %constant.32.clone.table_ref, bf16[2,2048,768]{2,1,0:T(8,128)(2,1)} %bitcast.18, ...), custom_call_target="tpu_custom_call" | custom-call | flops 3925868544 | bytes 20971520 | tf_op jit(solution)/shard_map/forward/pallas_call | solution.py:122
  7.6 0.5 collective-permute-start
  8.2 2.0 %load.3.after_ref.refs_6_ = bf16[4,2,448,448]{3,2,1,0:T(8,128)(2,1)S(1)} custom-call(bf16[32,2,448,448]{3,2,1,0:T(8,128)(2,1)} %frf_ref.7, bf16[2,4,2,32,448]{4,3,2,1,0:T(8,128)(2,1)S(1)} %get-tuple-element.19.after_ref), custom_call_target="tpu_custom_call" | custom-call | bytes 6422528 | tf_op jit(solution)/shard_map/load/pallas_call | solution.py:168
  10.2 0.0 collective-permute-done
  10.2 0.1 add.10
  10.3 2.6 %collective-permute-start.2 = (bf16[3,2,32,448]{3,2,1,0:T(8,128)(2,1)S(1)}, bf16[3,2,32,448]{3,2,1,0:T(8,128)(2,1)S(1)}, u32[]{:S(2)}, u32[]{:S(2)}) collective-permute-start(bf16[3,2,32,448]{3,2,1,0:T(8,128)(2,1)S(1)} %get-tuple-element.22.after_ref), channel_id=1, source_target_pairs={{0,2},{1,3},{2,0},{3,1},{4,6},{5,7},{6,4},{7,5},{8,10},{9,11},{10,... | collective-permute-start | bytes 516104 | tf_op jit(solution)/shard_map/ppermute | solution.py:381
  12.9 4.2 %load.4.after_ref.refs_7_ = bf16[12,2,448,448]{3,2,1,0:T(8,128)(2,1)S(1)} custom-call(bf16[32,2,448,448]{3,2,1,0:T(8,128)(2,1)} %frf_ref.7, bf16[3,2,32,448]{3,2,1,0:T(8,128)(2,1)S(1)} %get-tuple-element.22.after_ref), custom_call_target="tpu_custom_call" | custom-call | bytes 19267584 | tf_op jit(solution)/shard_map/load/pallas_call | solution.py:168
  17.2 0.1 collective-permute-start.1
  17.3 1.2 %collective-permute-done.2.came_ref = bf16[3,2,32,448]{3,2,1,0:T(8,128)(2,1)S(1)} collective-permute-done((bf16[3,2,32,448]{3,2,1,0:T(8,128)(2,1)S(1)}, bf16[3,2,32,448]{3,2,1,0:T(8,128)(2,1)S(1)}, u32[]{:S(2)}, u32[]{:S(2)}) %collective-permute-start.2) | collective-permute-done | bytes 172064 | tf_op jit(solution)/shard_map/ppermute | solution.py:381
  18.6 2.9 %collective-permute-start.4 = (bf16[1,2,32,448]{3,2,1,0:T(8,128)(2,1)S(1)}, bf16[1,2,32,448]{3,2,1,0:T(8,128)(2,1)S(1)}, u32[]{:S(2)}, u32[]{:S(2)}) collective-permute-start(bf16[1,2,32,448]{3,2,1,0:T(8,128)(2,1)S(1)} %get-tuple-element.24), channel_id=1, source_target_pairs={{0,8},{1,9},{2,10},{3,11},{4,12},{5,13},{6,14},{7,15},{8,0},{9,1},... | collective-permute-start | bytes 172040 | tf_op jit(solution)/shard_map/ppermute | solution.py:381
  21.4 1.4 %collective-permute-start.5 = (bf16[1,2,32,448]{3,2,1,0:T(8,128)(2,1)S(1)}, bf16[1,2,32,448]{3,2,1,0:T(8,128)(2,1)S(1)}, u32[]{:S(2)}, u32[]{:S(2)}) collective-permute-start(bf16[1,2,32,448]{3,2,1,0:T(8,128)(2,1)S(1)} %get-tuple-element.25), channel_id=1, source_target_pairs={{0,12},{1,13},{2,14},{3,15},{4,8},{5,9},{6,10},{7,11},{8,4},{9,5},... | collective-permute-start | bytes 172040 | tf_op jit(solution)/shard_map/ppermute | solution.py:381
  22.8 0.2 collective-permute-start.3
  23.0 3.2 %load.5.refs_8_ = bf16[8,2,448,448]{3,2,1,0:T(8,128)(2,1)S(1)} custom-call(bf16[32,2,448,448]{3,2,1,0:T(8,128)(2,1)} %frf_ref.7, bf16[1,2,32,448]{3,2,1,0:T(8,128)(2,1)S(1)} %get-tuple-element.23.after_ref), custom_call_target="tpu_custom_call" | custom-call | bytes 12845056 | tf_op jit(solution)/shard_map/load/pallas_call | solution.py:168
  26.2 0.0 collective-permute-done.1.refs_1_
  26.2 0.0 collective-permute-done.4.refs_3_
  26.2 1.4 %collective-permute-done.5.refs_4_ = bf16[1,2,32,448]{3,2,1,0:T(8,128)(2,1)S(1)} collective-permute-done((bf16[1,2,32,448]{3,2,1,0:T(8,128)(2,1)S(1)}, bf16[1,2,32,448]{3,2,1,0:T(8,128)(2,1)S(1)}, u32[]{:S(2)}, u32[]{:S(2)}) %collective-permute-start.5) | collective-permute-done | bytes 57376 | tf_op jit(solution)/shard_map/ppermute | solution.py:381
  27.6 0.1 collective-permute-done.3.refs_2_
  27.7 0.0 copy-start
  27.7 0.0 copy-start.1
  27.8 8.7 %respond.1 = bf16[2,32,448]{2,1,0:T(8,128)(2,1)S(1)} custom-call(bf16[1,2,32,448]{3,2,1,0:T(8,128)(2,1)S(1)} %slice.3.refs_0_, bf16[1,2,32,448]{3,2,1,0:T(8,128)(2,1)S(1)} %collective-permute-done.1.refs_1_, bf16[1,2,32,448]{3,2,1,0:T(8,128)(2,1)S(1)} %collective-permute-done.3.refs_2_, bf16[1,2,32,448]{3,2,1,0:T(8,128)(2,1)S(1)} %collective-permute-done.4.refs_3_, ...), custom_call_target="tpu_custom_call" | custom-call | flops 51380224 | bytes 25690112 | tf_op jit(solution)/shard_map/respond/pallas_call | solution.py:231
  36.5 2.9 %collective-permute-start.8 = (bf16[2,32,448]{2,1,0:T(8,128)(2,1)S(1)}, bf16[2,32,448]{2,1,0:T(8,128)(2,1)S(1)}, u32[]{:S(2)}, u32[]{:S(2)}) collective-permute-start(bf16[2,32,448]{2,1,0:T(8,128)(2,1)S(1)} %respond.1), channel_id=1, source_target_pairs={{0,12},{1,13},{2,14},{3,15},{4,8},{5,9},{6,10},{7,11},{8,4},{9,5},... | collective-permute-start | bytes 172040 | tf_op jit(solution)/shard_map/ppermute | solution.py:381
  39.3 0.0 collective-permute-start.7
  39.3 1.6 %collective-permute-start.6 = (bf16[2,32,448]{2,1,0:T(8,128)(2,1)S(1)}, bf16[2,32,448]{2,1,0:T(8,128)(2,1)S(1)}, u32[]{:S(2)}, u32[]{:S(2)}) collective-permute-start(bf16[2,32,448]{2,1,0:T(8,128)(2,1)S(1)} %respond.1), channel_id=1, source_target_pairs={{0,4},{1,5},{2,6},{3,7},{4,0},{5,1},{6,2},{7,3},{8,12},{9,13},{10,... | collective-permute-start | bytes 172040 | tf_op jit(solution)/shard_map/ppermute | solution.py:381
  40.9 1.5 %collective-permute-start.9 = (bf16[1,2,32,448]{3,2,1,0:T(8,128)(2,1)S(1)}, bf16[1,2,32,448]{3,2,1,0:T(8,128)(2,1)S(1)}, u32[]{:S(2)}, u32[]{:S(2)}) collective-permute-start(bf16[1,2,32,448]{3,2,1,0:T(8,128)(2,1)S(1)} %bitcast.16), channel_id=1, source_target_pairs={{0,2},{1,3},{2,0},{3,1},{4,6},{5,7},{6,4},{7,5},{8,10},{9,11},{10,... | collective-permute-start | bytes 172040 | tf_op jit(solution)/shard_map/ppermute | solution.py:381
  42.4 0.9 %collective-permute-done.8 = bf16[2,32,448]{2,1,0:T(8,128)(2,1)S(1)} collective-permute-done((bf16[2,32,448]{2,1,0:T(8,128)(2,1)S(1)}, bf16[2,32,448]{2,1,0:T(8,128)(2,1)S(1)}, u32[]{:S(2)}, u32[]{:S(2)}) %collective-permute-start.8) | collective-permute-done | bytes 57376 | tf_op jit(solution)/shard_map/ppermute | solution.py:381
  43.4 1.7 %collective-permute-done.7 = bf16[2,32,448]{2,1,0:T(8,128)(2,1)S(1)} collective-permute-done((bf16[2,32,448]{2,1,0:T(8,128)(2,1)S(1)}, bf16[2,32,448]{2,1,0:T(8,128)(2,1)S(1)}, u32[]{:S(2)}, u32[]{:S(2)}) %collective-permute-start.7) | collective-permute-done | bytes 57376 | tf_op jit(solution)/shard_map/ppermute | solution.py:381
  45.1 0.0 collective-permute-done.6
  45.1 0.1 collective-permute-done.9.refs_0_
  45.2 0.1 collective-permute-start.12
  45.3 1.6 %collective-permute-start.11 = (bf16[3,2,32,448]{3,2,1,0:T(8,128)(2,1)S(1)}, bf16[3,2,32,448]{3,2,1,0:T(8,128)(2,1)S(1)}, u32[]{:S(2)}, u32[]{:S(2)}) collective-permute-start(bf16[3,2,32,448]{3,2,1,0:T(8,128)(2,1)S(1)} %pad_maximum_fusion.1), channel_id=1, source_target_pairs={{0,2},{1,3},{2,0},{3,1},{4,6},{5,7},{6,4},{7,5},{8,10},{9,11},{10,... | collective-permute-start | bytes 516104 | tf_op jit(solution)/shard_map/ppermute | solution.py:381
  46.9 0.0 collective-permute-done.12.refs_1_
  46.9 0.0 copy-done
  46.9 0.0 copy-done.1
  46.9 2.8 %early.1.refs_4_ = f32[2,2048,768]{2,1,0:T(8,128)S(1)} custom-call(s32[2]{0:T(128)S(1)} %pad_add_fusion.place_ref, bf16[2,2,2048,256]{3,2,1,0:T(8,128)(2,1)S(1)} %copy-done, bf16[448,768]{1,0:T(8,128)(2,1)S(1)} %bitcast.12, bf16[4,2,32,448]{3,2,1,0:T(8,128)(2,1)S(1)} %pad_maximum_fusion.refs_0_, bf16[4,2,32,448]{3,2,1,0:T(8,128)(2,1)S(1)} %collective-permute-done.12.refs_1_), custom_call_target="tpu_custom_call" | custom-call | flops 1962934272 | bytes 8388608 | tf_op jit(solution)/shard_map/early/pallas_call | solution.py:322
  49.7 2.9 %collective-permute-done.11.refs_2_ = bf16[3,2,32,448]{3,2,1,0:T(8,128)(2,1)S(1)} collective-permute-done((bf16[3,2,32,448]{3,2,1,0:T(8,128)(2,1)S(1)}, bf16[3,2,32,448]{3,2,1,0:T(8,128)(2,1)S(1)}, u32[]{:S(2)}, u32[]{:S(2)}) %collective-permute-start.11) | collective-permute-done | bytes 172064 | tf_op jit(solution)/shard_map/ppermute | solution.py:381
  52.6 0.0 collective-permute-start.13
  52.6 0.5 collective-permute-start.10
  53.1 1.0 %collective-permute-done.10.refs_1_ = bf16[1,2,32,448]{3,2,1,0:T(8,128)(2,1)S(1)} collective-permute-done((bf16[1,2,32,448]{3,2,1,0:T(8,128)(2,1)S(1)}, bf16[1,2,32,448]{3,2,1,0:T(8,128)(2,1)S(1)}, u32[]{:S(2)}, u32[]{:S(2)}) %collective-permute-start.10) | collective-permute-done | bytes 57376 | tf_op jit(solution)/shard_map/ppermute | solution.py:381
  54.2 0.0 collective-permute-done.13.refs_3_
  54.2 4.5 %late.1 = bf16[2,2048,768]{2,1,0:T(8,128)(2,1)} custom-call(s32[2]{0:T(128)S(1)} %pad_add_fusion.place_ref, bf16[2,2,2048,256]{3,2,1,0:T(8,128)(2,1)S(1)} %copy-done, bf16[448,768]{1,0:T(8,128)(2,1)S(1)} %bitcast.13, bf16[1,2,32,448]{3,2,1,0:T(8,128)(2,1)S(1)} %collective-permute-done.9.refs_0_, bf16[1,2,32,448]{3,2,1,0:T(8,128)(2,1)S(1)} %collective-permute-done.10.refs_1_, ...), custom_call_target="tpu_custom_call" | custom-call | flops 1962934272 | bytes 8388608 | tf_op jit(solution)/shard_map/late/pallas_call | solution.py:332
  (4 shorter events, 0.1 us)
Async XLA Ops:
  7.6 2.6 %collective-permute-start = (bf16[2,4,2,32,448]{4,3,2,1,0:T(8,128)(2,1)S(1)}, bf16[2,4,2,32,448]{4,3,2,1,0:T(8,128)(2,1)S(1)}, u32[]{:S(2)}, u32[]{:S(2)}) collective-permute-start(bf16[2,4,2,32,448]{4,3,2,1,0:T(8,128)(2,1)S(1)} %get-tuple-element.19.after_ref), channel_id=1, source_target_pairs={{0,1},{1,0},{2,3},{3,2},{4,5},{5,4},{6,7},{7,6},{8,9},{9,8},{10,11... | collective-permute-start | bytes 1376264 | tf_op jit(solution)/shard_map/ppermute | solution.py:381
  10.3 8.2 %collective-permute-start.2 = (bf16[3,2,32,448]{3,2,1,0:T(8,128)(2,1)S(1)}, bf16[3,2,32,448]{3,2,1,0:T(8,128)(2,1)S(1)}, u32[]{:S(2)}, u32[]{:S(2)}) collective-permute-start(bf16[3,2,32,448]{3,2,1,0:T(8,128)(2,1)S(1)} %get-tuple-element.22.after_ref), channel_id=1, source_target_pairs={{0,2},{1,3},{2,0},{3,1},{4,6},{5,7},{6,4},{7,5},{8,10},{9,11},{10,... | collective-permute-start | bytes 516104 | tf_op jit(solution)/shard_map/ppermute | solution.py:381
  17.2 9.0 %collective-permute-start.1 = (bf16[1,2,32,448]{3,2,1,0:T(8,128)(2,1)S(1)}, bf16[1,2,32,448]{3,2,1,0:T(8,128)(2,1)S(1)}, u32[]{:S(2)}, u32[]{:S(2)}) collective-permute-start(bf16[1,2,32,448]{3,2,1,0:T(8,128)(2,1)S(1)} %get-tuple-element.21), channel_id=1, source_target_pairs={{0,2},{1,3},{2,0},{3,1},{4,6},{5,7},{6,4},{7,5},{8,10},{9,11},{10,... | collective-permute-start | bytes 172040 | tf_op jit(solution)/shard_map/ppermute | solution.py:381
  18.6 7.7 %collective-permute-start.4 = (bf16[1,2,32,448]{3,2,1,0:T(8,128)(2,1)S(1)}, bf16[1,2,32,448]{3,2,1,0:T(8,128)(2,1)S(1)}, u32[]{:S(2)}, u32[]{:S(2)}) collective-permute-start(bf16[1,2,32,448]{3,2,1,0:T(8,128)(2,1)S(1)} %get-tuple-element.24), channel_id=1, source_target_pairs={{0,8},{1,9},{2,10},{3,11},{4,12},{5,13},{6,14},{7,15},{8,0},{9,1},... | collective-permute-start | bytes 172040 | tf_op jit(solution)/shard_map/ppermute | solution.py:381
  21.4 6.2 %collective-permute-start.5 = (bf16[1,2,32,448]{3,2,1,0:T(8,128)(2,1)S(1)}, bf16[1,2,32,448]{3,2,1,0:T(8,128)(2,1)S(1)}, u32[]{:S(2)}, u32[]{:S(2)}) collective-permute-start(bf16[1,2,32,448]{3,2,1,0:T(8,128)(2,1)S(1)} %get-tuple-element.25), channel_id=1, source_target_pairs={{0,12},{1,13},{2,14},{3,15},{4,8},{5,9},{6,10},{7,11},{8,4},{9,5},... | collective-permute-start | bytes 172040 | tf_op jit(solution)/shard_map/ppermute | solution.py:381
  22.8 5.0 %collective-permute-start.3 = (bf16[1,2,32,448]{3,2,1,0:T(8,128)(2,1)S(1)}, bf16[1,2,32,448]{3,2,1,0:T(8,128)(2,1)S(1)}, u32[]{:S(2)}, u32[]{:S(2)}) collective-permute-start(bf16[1,2,32,448]{3,2,1,0:T(8,128)(2,1)S(1)} %get-tuple-element.23.after_ref), channel_id=1, source_target_pairs={{0,4},{1,5},{2,6},{3,7},{4,0},{5,1},{6,2},{7,3},{8,12},{9,13},{10,... | collective-permute-start | bytes 172040 | tf_op jit(solution)/shard_map/ppermute | solution.py:381
  27.7 19.1 %copy-start = (bf16[2,2,2048,256]{3,2,1,0:T(8,128)(2,1)S(1)}, bf16[2,2,2048,256]{3,2,1,0:T(8,128)(2,1)}, u32[]{:S(2)}) copy-start(bf16[2,2,2048,256]{3,2,1,0:T(8,128)(2,1)} %constant.33.clone.table_ref) | copy-start | bytes 12582916
  27.7 19.1 %copy-start.1 = (bf16[768,448]{0,1:T(8,128)(2,1)S(1)}, bf16[768,448]{0,1:T(8,128)(2,1)}, u32[]{:S(2)}) copy-start(bf16[768,448]{0,1:T(8,128)(2,1)} %param.6) | copy-start | bytes 2064388
  36.5 6.9 %collective-permute-start.8 = (bf16[2,32,448]{2,1,0:T(8,128)(2,1)S(1)}, bf16[2,32,448]{2,1,0:T(8,128)(2,1)S(1)}, u32[]{:S(2)}, u32[]{:S(2)}) collective-permute-start(bf16[2,32,448]{2,1,0:T(8,128)(2,1)S(1)} %respond.1), channel_id=1, source_target_pairs={{0,12},{1,13},{2,14},{3,15},{4,8},{5,9},{6,10},{7,11},{8,4},{9,5},... | collective-permute-start | bytes 172040 | tf_op jit(solution)/shard_map/ppermute | solution.py:381
  39.3 5.8 %collective-permute-start.7 = (bf16[2,32,448]{2,1,0:T(8,128)(2,1)S(1)}, bf16[2,32,448]{2,1,0:T(8,128)(2,1)S(1)}, u32[]{:S(2)}, u32[]{:S(2)}) collective-permute-start(bf16[2,32,448]{2,1,0:T(8,128)(2,1)S(1)} %respond.1), channel_id=1, source_target_pairs={{0,8},{1,9},{2,10},{3,11},{4,12},{5,13},{6,14},{7,15},{8,0},{9,1},... | collective-permute-start | bytes 172040 | tf_op jit(solution)/shard_map/ppermute | solution.py:381
  39.3 5.8 %collective-permute-start.6 = (bf16[2,32,448]{2,1,0:T(8,128)(2,1)S(1)}, bf16[2,32,448]{2,1,0:T(8,128)(2,1)S(1)}, u32[]{:S(2)}, u32[]{:S(2)}) collective-permute-start(bf16[2,32,448]{2,1,0:T(8,128)(2,1)S(1)} %respond.1), channel_id=1, source_target_pairs={{0,4},{1,5},{2,6},{3,7},{4,0},{5,1},{6,2},{7,3},{8,12},{9,13},{10,... | collective-permute-start | bytes 172040 | tf_op jit(solution)/shard_map/ppermute | solution.py:381
  40.9 4.3 %collective-permute-start.9 = (bf16[1,2,32,448]{3,2,1,0:T(8,128)(2,1)S(1)}, bf16[1,2,32,448]{3,2,1,0:T(8,128)(2,1)S(1)}, u32[]{:S(2)}, u32[]{:S(2)}) collective-permute-start(bf16[1,2,32,448]{3,2,1,0:T(8,128)(2,1)S(1)} %bitcast.16), channel_id=1, source_target_pairs={{0,2},{1,3},{2,0},{3,1},{4,6},{5,7},{6,4},{7,5},{8,10},{9,11},{10,... | collective-permute-start | bytes 172040 | tf_op jit(solution)/shard_map/ppermute | solution.py:381
  45.2 1.7 %collective-permute-start.12 = (bf16[4,2,32,448]{3,2,1,0:T(8,128)(2,1)S(1)}, bf16[4,2,32,448]{3,2,1,0:T(8,128)(2,1)S(1)}, u32[]{:S(2)}, u32[]{:S(2)}) collective-permute-start(bf16[4,2,32,448]{3,2,1,0:T(8,128)(2,1)S(1)} %pad_maximum_fusion.refs_0_), channel_id=1, source_target_pairs={{0,1},{1,0},{2,3},{3,2},{4,5},{5,4},{6,7},{7,6},{8,9},{9,8},{10,11... | collective-permute-start | bytes 688136 | tf_op jit(solution)/shard_map/ppermute | solution.py:381
  45.3 7.3 %collective-permute-start.11 = (bf16[3,2,32,448]{3,2,1,0:T(8,128)(2,1)S(1)}, bf16[3,2,32,448]{3,2,1,0:T(8,128)(2,1)S(1)}, u32[]{:S(2)}, u32[]{:S(2)}) collective-permute-start(bf16[3,2,32,448]{3,2,1,0:T(8,128)(2,1)S(1)} %pad_maximum_fusion.1), channel_id=1, source_target_pairs={{0,2},{1,3},{2,0},{3,1},{4,6},{5,7},{6,4},{7,5},{8,10},{9,11},{10,... | collective-permute-start | bytes 516104 | tf_op jit(solution)/shard_map/ppermute | solution.py:381
  52.6 1.5 %collective-permute-start.13 = (bf16[3,2,32,448]{3,2,1,0:T(8,128)(2,1)S(1)}, bf16[3,2,32,448]{3,2,1,0:T(8,128)(2,1)S(1)}, u32[]{:S(2)}, u32[]{:S(2)}) collective-permute-start(bf16[3,2,32,448]{3,2,1,0:T(8,128)(2,1)S(1)} %collective-permute-done.11.refs_2_), channel_id=1, source_target_pairs={{0,1},{1,0},{2,3},{3,2},{4,5},{5,4},{6,7},{7,6},{8,9},{9,8},{10,11... | collective-permute-start | bytes 516104 | tf_op jit(solution)/shard_map/ppermute | solution.py:381
  52.6 1.5 %collective-permute-start.10 = (bf16[1,2,32,448]{3,2,1,0:T(8,128)(2,1)S(1)}, bf16[1,2,32,448]{3,2,1,0:T(8,128)(2,1)S(1)}, u32[]{:S(2)}, u32[]{:S(2)}) collective-permute-start(bf16[1,2,32,448]{3,2,1,0:T(8,128)(2,1)S(1)} %collective-permute-done.9.refs_0_), channel_id=1, source_target_pairs={{0,1},{1,0},{2,3},{3,2},{4,5},{5,4},{6,7},{7,6},{8,9},{9,8},{10,11... | collective-permute-start | bytes 172040 | tf_op jit(solution)/shard_map/ppermute | solution.py:381

commit v5 on v4

--- a/solution.py
+++ b/solution.py
@@ -28,15 +28,15 @@
         angle = (ids[:, None] * times[None, :] % steps) * (2.0 * math.pi / steps)
         table = np.stack([np.cos(angle), -np.sin(angle)], axis=1) / math.sqrt(steps)
         tables.append(table.reshape(FREQS, steps // 2))
-    return np.stack(tables)
+    return np.stack(tables).reshape(2, 2, FREQS // 2, steps // 2)
 
 
 def inverse_tables(steps, chips):
     tables = forward_tables(steps, chips) * 2.0
     for parity in range(2):
         weights = np.where(frequency_order(chips, parity) == 0, 0.5, 1.0)
-        tables[parity] *= np.repeat(weights, 2)[:, None]
-    return tables.reshape(2, 2, FREQS // 2, steps // 2).transpose(0, 1, 3, 2)
+        tables[parity] *= np.repeat(weights, 2).reshape(2, FREQS // 2, 1)
+    return tables.transpose(0, 1, 3, 2)
 
 
 def chunk_list(half):
@@ -46,11 +46,28 @@
     return tuple(zip(starts, sizes))
 
 
-def forward_kernel(
-    place_ref, table_ref, forces_ref, shapes_ref, frf_ref, keep_ref, send_ref, held_ref,
-    table_buf, forces_buf, shapes_buf, acc_ref, table_sem, forces_sem, shapes_sem, held_sem,
+def split_cores(place_ref, spec, shapes_ref, parity, keep_ref, send_ref):
+    zs, _, rows, modes = keep_ref.shape
+    first, z = place_ref[0] == 0, place_ref[1] // 2
+    spec = lax.dot_general(
+        spec.astype(jnp.bfloat16),
+        shapes_ref[...],
+        (((1,), (1,)), ((), ())),
+        preferred_element_type=jnp.float32,
+    ).reshape(CORES, zs, rows, modes)
+    keep = jnp.where(first, spec[0], spec[1]).astype(jnp.bfloat16)
+    send = jnp.where(first, spec[1], spec[0]).astype(jnp.bfloat16)
+    for k in range(zs):
+        keep_ref[z ^ k, parity] = keep[k]
+        send_ref[z ^ k, parity] = send[k]
+
+
+def across_kernel(
+    place_ref, table_ref, forces_ref, shapes_ref,
+    keep_ref, send_ref, folded_ref, rest_ref, shapes_buf,
+    table_buf, forces_buf, acc_ref, table_sem, forces_sem, rest_sem, shapes_sem,
 ):
-    _, zs, _, rows, modes = keep_ref.shape
+    y = place_ref[1] % 2
     chunks = chunk_list(forces_ref.shape[1])
     copies = []
     for n, (start, size) in enumerate(chunks):
@@ -60,18 +77,18 @@
                 forces_ref.at[:, part], forces_buf.at[:, part], forces_sem.at[n]
             ),
             pltpu.make_async_copy(
-                table_ref.at[:, :, part], table_buf.at[:, :, part], table_sem.at[n]
+                table_ref.at[:, y ^ 1, :, part], table_buf.at[:, :, part], table_sem.at[n]
             ),
         )
         for copy in pair:
             copy.start()
         copies.append(pair)
-    shapes_copy = pltpu.make_async_copy(shapes_ref, shapes_buf, shapes_sem)
-    shapes_copy.start()
-    held_copy = pltpu.make_async_copy(
-        frf_ref.at[pl.ds(0, held_ref.shape[0])], held_ref, held_sem
+    later = (
+        pltpu.make_async_copy(shapes_ref, shapes_buf, shapes_sem),
+        pltpu.make_async_copy(table_ref.at[:, y], rest_ref, rest_sem),
     )
-    held_copy.start()
+    for copy in later:
+        copy.start()
 
     for n, (start, size) in enumerate(chunks):
         for copy in copies[n]:
@@ -79,6 +96,7 @@
         low = forces_buf[0, start : start + size]
         high = forces_buf[1, start : start + size]
         for parity, folded in enumerate((low + high, low - high)):
+            folded_ref[parity, start : start + size] = folded
             part = jnp.dot(
                 table_buf[parity, :, start : start + size],
                 folded,
@@ -89,57 +107,83 @@
             else:
                 acc_ref[parity] += part
 
-    shapes_copy.wait()
-    first, chip = place_ref[0] == 0, place_ref[1]
+    later[0].wait()
     for parity in range(2):
-        spec = lax.dot_general(
-            acc_ref[parity].astype(jnp.bfloat16),
-            shapes_buf[...],
-            (((1,), (1,)), ((), ())),
-            preferred_element_type=jnp.float32,
-        ).reshape(2, CORES, zs, rows, modes)
-        for y in range(2):
-            keep = jnp.where(first, spec[y, 0], spec[y, 1]).astype(jnp.bfloat16)
-            send = jnp.where(first, spec[y, 1], spec[y, 0]).astype(jnp.bfloat16)
-            for z in range(zs):
-                slot = chip ^ (2 * z + y)
-                keep_ref[slot % 2, slot // 2, parity] = keep[z]
-                send_ref[slot % 2, slot // 2, parity] = send[z]
-    held_copy.wait()
-
-
-def in_hbm(array):
-    return pltpu.with_memory_space_constraint(array, pltpu.HBM)
-
-
-def forward(place, table, forces, shapes_t, frf, held, chips):
+        split_cores(place_ref, acc_ref[parity], shapes_buf, parity, keep_ref, send_ref)
+    later[1].wait()
+
+
+def across(place, table, forces, shapes_t, zs):
     _, half, dofs = forces.shape
     modes = shapes_t.shape[0]
-    rows = FREQS // (chips * CORES)
-    out = jax.ShapeDtypeStruct((2, chips // 2, 2, rows, modes), jnp.bfloat16)
+    rows = FREQS // (2 * CORES * zs)
+    out = jax.ShapeDtypeStruct((zs, 2, rows, modes), jnp.bfloat16)
     vmem, hbm = pl.BlockSpec(memory_space=pltpu.VMEM), pl.BlockSpec(memory_space=pltpu.HBM)
     count = len(chunk_list(half))
     return pl.pallas_call(
-        forward_kernel,
-        in_specs=[pl.BlockSpec(memory_space=pltpu.SMEM), hbm, hbm, hbm, hbm],
-        out_specs=[vmem, vmem, vmem],
-        out_shape=[out, out, pltpu.VMEM((held,) + frf.shape[1:], jnp.bfloat16)],
+        across_kernel,
+        in_specs=[pl.BlockSpec(memory_space=pltpu.SMEM), hbm, hbm, hbm],
+        out_specs=[vmem] * 5,
+        out_shape=[
+            out,
+            out,
+            pltpu.VMEM(forces.shape, jnp.bfloat16),
+            pltpu.VMEM((2, FREQS // 2, half), jnp.bfloat16),
+            pltpu.VMEM(shapes_t.shape, jnp.bfloat16),
+        ],
         scratch_shapes=[
-            pltpu.VMEM(table.shape, jnp.bfloat16),
+            pltpu.VMEM((2, FREQS // 2, half), jnp.bfloat16),
             pltpu.VMEM(forces.shape, jnp.bfloat16),
-            pltpu.VMEM(shapes_t.shape, jnp.bfloat16),
-            pltpu.VMEM((2, FREQS, dofs), jnp.float32),
+            pltpu.VMEM((2, FREQS // 2, dofs), jnp.float32),
             pltpu.SemaphoreType.DMA((count,)),
             pltpu.SemaphoreType.DMA((count,)),
             pltpu.SemaphoreType.DMA,
             pltpu.SemaphoreType.DMA,
         ],
-        compiler_params=pltpu.CompilerParams(vmem_limit_bytes=24 * MIB),
+        compiler_params=pltpu.CompilerParams(vmem_limit_bytes=20 * MIB),
         cost_estimate=pl.CostEstimate(
-            flops=4 * FREQS * dofs * (half + modes), bytes_accessed=20 * MIB, transcendentals=0
+            flops=2 * FREQS * dofs * (half + modes), bytes_accessed=12 * MIB, transcendentals=0
         ),
-        name="forward",
-    )(place, in_hbm(table), in_hbm(forces), in_hbm(shapes_t), in_hbm(frf))
+        name="across",
+    )(place, in_hbm(table), in_hbm(forces), in_hbm(shapes_t))
+
+
+def within_kernel(
+    parity, start, place_ref, table_ref, folded_ref, shapes_ref, frf_ref, after_ref,
+    keep_ref, send_ref, held_ref, sem,
+):
+    copies = load_copies(start, frf_ref, held_ref, sem)
+    for copy in copies:
+        copy.start()
+    spec = jnp.dot(table_ref[parity], folded_ref[parity], preferred_element_type=jnp.float32)
+    split_cores(place_ref, spec, shapes_ref, 0, keep_ref, send_ref)
+    for copy in copies:
+        copy.wait()
+
+
+def within(parity, place, table, folded, shapes_t, frf, start, held, after, zs):
+    _, half, dofs = folded.shape
+    modes = shapes_t.shape[0]
+    rows = FREQS // (2 * CORES * zs)
+    out = jax.ShapeDtypeStruct((zs, 1, rows, modes), jnp.bfloat16)
+    vmem, hbm = pl.BlockSpec(memory_space=pltpu.VMEM), pl.BlockSpec(memory_space=pltpu.HBM)
+    return pl.pallas_call(
+        functools.partial(within_kernel, parity, start),
+        in_specs=[pl.BlockSpec(memory_space=pltpu.SMEM), vmem, vmem, vmem, hbm]
+        + [pl.BlockSpec(memory_space=pl.ANY)],
+        out_specs=[vmem] * 3,
+        out_shape=[out, out, pltpu.VMEM((held,) + frf.shape[1:], jnp.bfloat16)],
+        scratch_shapes=[pltpu.SemaphoreType.DMA((math.gcd(held, 4),))],
+        compiler_params=pltpu.CompilerParams(vmem_limit_bytes=8 * MIB),
+        cost_estimate=pl.CostEstimate(
+            flops=FREQS * dofs * (half + modes), bytes_accessed=8 * MIB, transcendentals=0
+        ),
+        name="within",
+    )(place, table, folded, shapes_t, in_hbm(frf), after)
+
+
+def in_hbm(array):
+    return pltpu.with_memory_space_constraint(array, pltpu.HBM)
 
 
 def load_copies(start, frf_ref, held_ref, sem):
@@ -326,7 +370,7 @@
             out_shape=pltpu.VMEM((2, half, dofs), jnp.float32),
             scratch_shapes=scratch,
             compiler_params=params,
-            cost_estimate=cost,
+            cost_estimate=pl.CostEstimate(flops=1000, bytes_accessed=1000, transcendentals=0),
             name="early",
         )(*given)
     return pl.pallas_call(
@@ -342,32 +386,50 @@
     )(*given, waves)
 
 
-def add_kernel(start, splits, ours_ref, came_ref, after_ref, *out_refs):
-    at = 0
-    for size, out_ref in zip(splits, out_refs):
-        for n in range(size):
-            total = ours_ref[start + at + n].astype(jnp.float32) + came_ref[at + n].astype(
-                jnp.float32
-            )
-            out_ref[n] = total.astype(jnp.bfloat16)
-        at += size
-
-
-def add(ours, came, start, splits, after):
-    vmem, anywhere = pl.BlockSpec(memory_space=pltpu.VMEM), pl.BlockSpec(memory_space=pl.ANY)
-    return pl.pallas_call(
-        functools.partial(add_kernel, start, splits),
-        in_specs=[vmem, vmem, anywhere],
-        out_specs=[vmem] * len(splits),
-        out_shape=[
-            jax.ShapeDtypeStruct((size,) + ours.shape[1:], jnp.bfloat16) for size in splits
-        ],
+def add_kernel(ours_ref, came_ref, out_ref):
+    total = ours_ref[...].astype(jnp.float32) + came_ref[...].astype(jnp.float32)
+    out_ref[...] = total.astype(jnp.bfloat16)
+
+
+def add(ours, came):
+    vmem = pl.BlockSpec(memory_space=pltpu.VMEM)
+    return pl.pallas_call(
+        add_kernel,
+        in_specs=[vmem] * 2,
+        out_specs=vmem,
+        out_shape=jax.ShapeDtypeStruct(ours.shape, jnp.bfloat16),
         compiler_params=pltpu.CompilerParams(vmem_limit_bytes=8 * MIB),
         cost_estimate=pl.CostEstimate(
             flops=came.size, bytes_accessed=6 * came.size, transcendentals=0
         ),
         name="add",
-    )(ours, came, after)
+    )(ours, came)
+
+
+def gather_sum_kernel(came_ref, after_ref, *refs):
+    within_refs, out_refs = refs[:4], refs[4:]
+    for k, out_ref in enumerate(out_refs):
+        for parity in range(2):
+            keep_ref, twin_ref = within_refs[2 * parity : 2 * parity + 2]
+            total = keep_ref[k, 0].astype(jnp.float32) + twin_ref[k, 0].astype(jnp.float32)
+            total = total + came_ref[k, parity].astype(jnp.float32)
+            out_ref[0, parity] = total.astype(jnp.bfloat16)
+
+
+def gather_sum(came, kept, after):
+    vmem = pl.BlockSpec(memory_space=pltpu.VMEM)
+    zs = came.shape[0]
+    return pl.pallas_call(
+        gather_sum_kernel,
+        in_specs=[vmem, pl.BlockSpec(memory_space=pl.ANY)] + [vmem] * 4,
+        out_specs=[vmem] * zs,
+        out_shape=[jax.ShapeDtypeStruct((1,) + came.shape[1:], jnp.bfloat16)] * zs,
+        compiler_params=pltpu.CompilerParams(vmem_limit_bytes=8 * MIB),
+        cost_estimate=pl.CostEstimate(
+            flops=2 * came.size, bytes_accessed=8 * came.size, transcendentals=0
+        ),
+        name="gather_sum",
+    )(came, after, *kept)
 
 
 def on_device(devices, forces, mode_shapes, frf):
@@ -387,31 +449,29 @@
     inv = jnp.asarray(inverse_tables(steps, chips).astype(jnp.bfloat16))
 
     unit = frf.shape[0] // 8
-    keep, send, part0 = forward(
-        place, fwd, forces.reshape(2, half, dofs), shapes_t, frf, 2 * unit, chips
+    keep, send, folded, rest, shapes_v = across(
+        place, fwd, forces.reshape(2, half, dofs), shapes_t, zs
     )
-    part1 = load(frf, 2 * unit, unit, send)
-    slots = (2 * zs,) + keep.shape[2:]
-    here, there_near, there_far = add(
-        keep.reshape(slots), swap(send, 1).reshape(slots), 0, (zs, 1, zs - 1), part1
-    )
-    came_far, came_near = swap(there_far, 2), swap(there_near, 2)
-    part2 = load(frf, 3 * unit, 3 * unit, there_far)
-    pieces = add(here, came_far, 1, (1,) * (zs - 1), part2)
-    part3 = load(frf, 6 * unit, 2 * unit, pieces[0])
-    came = [swap(piece, 4 * k) for k, piece in enumerate(pieces, 1)]
-    response = respond([here[:1], came_near, *came], (part0, part1, part2, part3))
-
-    across = swap(response[None], 2)
+    given = (place, rest, folded, shapes_v, frf)
+    keep0, send0, part0 = within(0, *given, 0, unit, send, zs)
+    pair = add(keep, swap(send, 1))
+    came = swap(pair, 2)
+    keep1, send1, part1 = within(1, *given, unit, unit, pair, zs)
+    part2 = load(frf, 2 * unit, 3 * unit, send1)
+    pieces = gather_sum(came, (keep0, swap(send0, 1), keep1, swap(send1, 1)), part2)
+    part3 = load(frf, 5 * unit, 3 * unit, pieces[0])
+    pieces = [pieces[0]] + [swap(pieces[k], 4 * k) for k in range(1, zs)]
+    response = respond(pieces, (part0, part1, part2, part3))
+
+    over = swap(response[None], 2)
     shards = [swap(response, 4 * k) for k in range(1, zs)]
-    far, across = lax.optimization_barrier((jnp.stack(shards), across))
-    across_far = swap(far, 2)
+    far, over = lax.optimization_barrier((jnp.stack(shards), over))
+    over_far = swap(far, 2)
     own = jnp.concatenate([response[None], far])
-    twin, twin_across = swap(own, 1), swap(across, 1)
-    waves = inverse(place, inv, shapes_t, (own, twin))
-    across_far, waves = lax.optimization_barrier((across_far, waves))
-    groups = (across, twin_across, across_far, swap(across_far, 1))
-    out = inverse(place, inv, shapes_t, groups, waves)
+    twin, twin_over = swap(own, 1), swap(over, 1)
+    waves = inverse(place, inv, shapes_v, (own, twin))
+    over_far, waves = lax.optimization_barrier((over_far, waves))
+    out = inverse(place, inv, shapes_v, (over, twin_over, over_far, swap(over_far, 1)), waves)
     return out.reshape(1, steps, dofs)
 
 

time: 58.8 us -> 64.3 us (1.094)
  Pallas kernels: 33.2 us -> 37.7 us
  waiting for transfers between devices: 9.4 us -> 11.5 us
  starting transfers between devices: 15.8 us -> 14.7 us
    pallas_call x3 -> x5, Pallas kernels: 7.73 us -> 13.3 us  [the longest x2 7.53 us: within(): pl.pallas_call(functools.partial(within_kernel, parity, start), in_specs=...]
    ppermute x14 -> x15, waiting for transfers between devices: 9.4 us -> 11.5 us  [swap(): return lax.ppermute(values, 'dof', pairs)]
    ppermute x14 -> x15, starting transfers between devices: 15.8 us -> 14.7 us  [swap(): return lax.ppermute(values, 'dof', pairs)]
    pallas_call x3 -> x2, Pallas kernels: 9.47 us -> 8.49 us  [load(): pl.pallas_call(functools.partial(load_kernel, start), in_specs=[hbm, anyw...]
  transfers between devices with their start and end apart: 14 -> 15, of which waited for: 8 -> 9; matrix products, arithmetic and copies ran while one was open for 0% -> 0% of each run, Pallas kernels for 21% -> 29%
where the time goes in v5:
time: 64.3 us; the launch traced here: 64.2 us
  Pallas kernels  37.7 us (59%)
  starting transfers between devices  14.7 us (23%)
  waiting for transfers between devices  11.5 us (18%)
    ppermute x15, starting transfers between devices, swap(): return lax.ppermute(values, 'dof', pairs)  14.7 us
    ppermute x15, waiting for transfers between devices, swap(): return lax.ppermute(values, 'dof', pairs)  11.5 us
    pallas_call x1, Pallas kernels, respond(): pl.pallas_call(functools.partial(respond_kernel, len(pieces)), in_specs=[...  8.56 us
    pallas_call x2, Pallas kernels, load(): pl.pallas_call(functools.partial(load_kernel, start), in_specs=[hbm, anyw...  8.49 us
    pallas_call x2, Pallas kernels, within(): pl.pallas_call(functools.partial(within_kernel, parity, start), in_specs=...  7.53 us
    pallas_call x1, Pallas kernels, across(): pl.pallas_call(across_kernel, in_specs=[pl.BlockSpec(memory_space=pltpu.S...  5.64 us
    pallas_call x1, Pallas kernels, inverse(): pl.pallas_call(late_kernel, in_specs=in_specs + [vmem], out_specs=pl.Bloc...  4.51 us
    pallas_call x1, Pallas kernels, inverse(): pl.pallas_call(early_kernel, in_specs=in_specs, out_specs=vmem, out_shape...  2.8 us
  transfers between devices with their start and end apart: 15, of which 9 were waited for; matrix products, arithmetic and copies ran while one was open for 0% of the time, Pallas kernels for 29%

profile of v5, /device:TPU:0, one launch (start us, length us, event | category | flops | bytes accessed | tf_op | source)
XLA Modules:
  0.0 64.2 jit_solution(1411321738741568977)
XLA Ops:
  0.0 0.1 pad_add_fusion.place_ref
  0.1 5.6 %across.1 = (bf16[4,2,32,448]{3,2,1,0:T(8,128)(2,1)S(1)}, bf16[4,2,32,448]{3,2,1,0:T(8,128)(2,1)S(1)}, bf16[2,2048,768]{2,1,0:T(8,128)(2,1)S(1)}, bf16[2,256,2048]{2,1,0:T(8,128)(2,1)S(1)}, bf16[448,768]{1,0:T(8,128)(2,1)S(1)}) custom-call(s32[2]{0:T(128)S(1)} %pad_add_fusion.place_ref, bf16[2,2,256,2048]{3,2,1,0:T(8,128)(2,1)} %constant.32.clone.table_ref, ...), custom_call_target="tpu_custom_call" | custom-call | flops 1962934272 | bytes 12582912 | tf_op jit(solution)/shard_map/across/pallas_call | solution.py:123
  5.7 0.5 collective-permute-start
  6.2 1.2 %collective-permute-done.came_ref = bf16[4,2,32,448]{3,2,1,0:T(8,128)(2,1)S(1)} collective-permute-done((bf16[4,2,32,448]{3,2,1,0:T(8,128)(2,1)S(1)}, bf16[4,2,32,448]{3,2,1,0:T(8,128)(2,1)S(1)}, u32[]{:S(2)}, u32[]{:S(2)}) %collective-permute-start) | collective-permute-done | bytes 229408 | tf_op jit(solution)/shard_map/ppermute | solution.py:443
  7.4 0.1 add.9.after_ref
  7.5 3.0 %collective-permute-start.1 = (bf16[4,2,32,448]{3,2,1,0:T(8,128)(2,1)S(1)}, bf16[4,2,32,448]{3,2,1,0:T(8,128)(2,1)S(1)}, u32[]{:S(2)}, u32[]{:S(2)}) collective-permute-start(bf16[4,2,32,448]{3,2,1,0:T(8,128)(2,1)S(1)} %add.9.after_ref), channel_id=1, source_target_pairs={{0,2},{1,3},{2,0},{3,1},{4,6},{5,7},{6,4},{7,5},{8,10},{9,11},{10,... | collective-permute-start | bytes 688136 | tf_op jit(solution)/shard_map/ppermute | solution.py:443
  10.4 3.8 %within.3 = (bf16[4,1,32,448]{3,2,1,0:T(8,128)(2,1)S(1)}, bf16[4,1,32,448]{3,2,1,0:T(8,128)(2,1)S(1)}, bf16[4,2,448,448]{3,2,1,0:T(8,128)(2,1)S(1)}) custom-call(s32[2]{0:T(128)S(1)} %pad_add_fusion.place_ref, bf16[2,256,2048]{2,1,0:T(8,128)(2,1)S(1)} %get-tuple-element.27.table_ref, bf16[2,2048,768]{2,1,0:T(8,128)(2,1)S(1)} %get-tuple-element.28.folded_ref, ...), custom_call_target="tpu_custom_call" | custom-call | flops 981467136 | bytes 8388608 | tf_op jit(solution)/shard_map/within/pallas_call | solution.py:170
  14.2 0.1 collective-permute-start.2
  14.3 3.8 %within.2 = (bf16[4,1,32,448]{3,2,1,0:T(8,128)(2,1)S(1)}, bf16[4,1,32,448]{3,2,1,0:T(8,128)(2,1)S(1)}, bf16[4,2,448,448]{3,2,1,0:T(8,128)(2,1)S(1)}) custom-call(s32[2]{0:T(128)S(1)} %pad_add_fusion.place_ref, bf16[2,256,2048]{2,1,0:T(8,128)(2,1)S(1)} %get-tuple-element.27.table_ref, bf16[2,2048,768]{2,1,0:T(8,128)(2,1)S(1)} %get-tuple-element.28.folded_ref, ...), custom_call_target="tpu_custom_call" | custom-call | flops 981467136 | bytes 8388608 | tf_op jit(solution)/shard_map/within/pallas_call | solution.py:170
  18.1 0.6 collective-permute-start.3
  18.6 4.2 %load.2.after_ref.refs_6_ = bf16[12,2,448,448]{3,2,1,0:T(8,128)(2,1)S(1)} custom-call(bf16[32,2,448,448]{3,2,1,0:T(8,128)(2,1)} %frf_ref.7, bf16[4,1,32,448]{3,2,1,0:T(8,128)(2,1)S(1)} %get-tuple-element.29.after_ref), custom_call_target="tpu_custom_call" | custom-call | bytes 19267584 | tf_op jit(solution)/shard_map/load/pallas_call | solution.py:212
  22.9 0.0 collective-permute-done.2.refs_1_
  22.9 0.0 collective-permute-done.3.refs_3_
  22.9 0.0 collective-permute-done.1.came_ref
  22.9 0.1 gather_sum.1
  23.0 1.6 %collective-permute-start.4 = (bf16[1,2,32,448]{3,2,1,0:T(8,128)(2,1)S(1)}, bf16[1,2,32,448]{3,2,1,0:T(8,128)(2,1)S(1)}, u32[]{:S(2)}, u32[]{:S(2)}) collective-permute-start(bf16[1,2,32,448]{3,2,1,0:T(8,128)(2,1)S(1)} %get-tuple-element.34), channel_id=1, source_target_pairs={{0,4},{1,5},{2,6},{3,7},{4,0},{5,1},{6,2},{7,3},{8,12},{9,13},{10,... | collective-permute-start | bytes 172040 | tf_op jit(solution)/shard_map/ppermute | solution.py:443
  24.6 2.6 %collective-permute-start.5 = (bf16[1,2,32,448]{3,2,1,0:T(8,128)(2,1)S(1)}, bf16[1,2,32,448]{3,2,1,0:T(8,128)(2,1)S(1)}, u32[]{:S(2)}, u32[]{:S(2)}) collective-permute-start(bf16[1,2,32,448]{3,2,1,0:T(8,128)(2,1)S(1)} %get-tuple-element.35), channel_id=1, source_target_pairs={{0,8},{1,9},{2,10},{3,11},{4,12},{5,13},{6,14},{7,15},{8,0},{9,1},... | collective-permute-start | bytes 172040 | tf_op jit(solution)/shard_map/ppermute | solution.py:443
  27.2 0.2 collective-permute-start.6
  27.5 4.2 %load.3.refs_7_ = bf16[12,2,448,448]{3,2,1,0:T(8,128)(2,1)S(1)} custom-call(bf16[32,2,448,448]{3,2,1,0:T(8,128)(2,1)} %frf_ref.7, bf16[1,2,32,448]{3,2,1,0:T(8,128)(2,1)S(1)} %get-tuple-element.33.after_ref.refs_0_), custom_call_target="tpu_custom_call" | custom-call | bytes 19267584 | tf_op jit(solution)/shard_map/load/pallas_call | solution.py:212
  31.7 0.0 collective-permute-done.4.refs_1_
  31.7 0.4 collective-permute-done.5.refs_2_
  32.1 1.3 %collective-permute-done.6.refs_3_ = bf16[1,2,32,448]{3,2,1,0:T(8,128)(2,1)S(1)} collective-permute-done((bf16[1,2,32,448]{3,2,1,0:T(8,128)(2,1)S(1)}, bf16[1,2,32,448]{3,2,1,0:T(8,128)(2,1)S(1)}, u32[]{:S(2)}, u32[]{:S(2)}) %collective-permute-start.6) | collective-permute-done | bytes 57376 | tf_op jit(solution)/shard_map/ppermute | solution.py:443
  33.4 0.0 copy-start
  33.4 8.6 %respond.1 = bf16[2,32,448]{2,1,0:T(8,128)(2,1)S(1)} custom-call(bf16[1,2,32,448]{3,2,1,0:T(8,128)(2,1)S(1)} %get-tuple-element.33.after_ref.refs_0_, bf16[1,2,32,448]{3,2,1,0:T(8,128)(2,1)S(1)} %collective-permute-done.4.refs_1_, bf16[1,2,32,448]{3,2,1,0:T(8,128)(2,1)S(1)} %collective-permute-done.5.refs_2_, ...), custom_call_target="tpu_custom_call" | custom-call | flops 51380224 | bytes 25690112 | tf_op jit(solution)/shard_map/respond/pallas_call | solution.py:275
  42.0 2.0 %collective-permute-start.9 = (bf16[2,32,448]{2,1,0:T(8,128)(2,1)S(1)}, bf16[2,32,448]{2,1,0:T(8,128)(2,1)S(1)}, u32[]{:S(2)}, u32[]{:S(2)}) collective-permute-start(bf16[2,32,448]{2,1,0:T(8,128)(2,1)S(1)} %respond.1), channel_id=1, source_target_pairs={{0,12},{1,13},{2,14},{3,15},{4,8},{5,9},{6,10},{7,11},{8,4},{9,5},... | collective-permute-start | bytes 172040 | tf_op jit(solution)/shard_map/ppermute | solution.py:443
  44.0 0.2 collective-permute-start.8
  44.2 2.2 %collective-permute-start.7 = (bf16[2,32,448]{2,1,0:T(8,128)(2,1)S(1)}, bf16[2,32,448]{2,1,0:T(8,128)(2,1)S(1)}, u32[]{:S(2)}, u32[]{:S(2)}) collective-permute-start(bf16[2,32,448]{2,1,0:T(8,128)(2,1)S(1)} %respond.1), channel_id=1, source_target_pairs={{0,4},{1,5},{2,6},{3,7},{4,0},{5,1},{6,2},{7,3},{8,12},{9,13},{10,... | collective-permute-start | bytes 172040 | tf_op jit(solution)/shard_map/ppermute | solution.py:443
  46.4 0.5 collective-permute-start.10
  46.9 1.7 %collective-permute-done.9 = bf16[2,32,448]{2,1,0:T(8,128)(2,1)S(1)} collective-permute-done((bf16[2,32,448]{2,1,0:T(8,128)(2,1)S(1)}, bf16[2,32,448]{2,1,0:T(8,128)(2,1)S(1)}, u32[]{:S(2)}, u32[]{:S(2)}) %collective-permute-start.9) | collective-permute-done | bytes 57376 | tf_op jit(solution)/shard_map/ppermute | solution.py:443
  48.7 1.3 %collective-permute-done.8 = bf16[2,32,448]{2,1,0:T(8,128)(2,1)S(1)} collective-permute-done((bf16[2,32,448]{2,1,0:T(8,128)(2,1)S(1)}, bf16[2,32,448]{2,1,0:T(8,128)(2,1)S(1)}, u32[]{:S(2)}, u32[]{:S(2)}) %collective-permute-start.8) | collective-permute-done | bytes 57376 | tf_op jit(solution)/shard_map/ppermute | solution.py:443
  50.0 0.0 collective-permute-done.7
  50.0 0.7 %collective-permute-done.10.refs_0_ = bf16[1,2,32,448]{3,2,1,0:T(8,128)(2,1)S(1)} collective-permute-done((bf16[1,2,32,448]{3,2,1,0:T(8,128)(2,1)S(1)}, bf16[1,2,32,448]{3,2,1,0:T(8,128)(2,1)S(1)}, u32[]{:S(2)}, u32[]{:S(2)}) %collective-permute-start.10) | collective-permute-done | bytes 57376 | tf_op jit(solution)/shard_map/ppermute | solution.py:443
  50.7 0.1 collective-permute-start.13
  50.8 0.6 collective-permute-start.12
  51.4 0.9 %collective-permute-done.13.refs_1_ = bf16[4,2,32,448]{3,2,1,0:T(8,128)(2,1)S(1)} collective-permute-done((bf16[4,2,32,448]{3,2,1,0:T(8,128)(2,1)S(1)}, bf16[4,2,32,448]{3,2,1,0:T(8,128)(2,1)S(1)}, u32[]{:S(2)}, u32[]{:S(2)}) %collective-permute-start.13) | collective-permute-done | bytes 229408 | tf_op jit(solution)/shard_map/ppermute | solution.py:443
  52.3 0.0 copy-done
  52.3 2.8 %early.1.refs_4_ = f32[2,2048,768]{2,1,0:T(8,128)S(1)} custom-call(s32[2]{0:T(128)S(1)} %pad_add_fusion.place_ref, bf16[2,2,2048,256]{3,2,1,0:T(8,128)(2,1)S(1)} %copy-done, bf16[448,768]{1,0:T(8,128)(2,1)S(1)} %get-tuple-element.24.shapes_ref, bf16[4,2,32,448]{3,2,1,0:T(8,128)(2,1)S(1)} %pad_maximum_fusion.refs_0_, ...), custom_call_target="tpu_custom_call" | custom-call | flops 1000 | bytes 1000 | tf_op jit(solution)/shard_map/early/pallas_call | solution.py:366
  55.1 3.0 %collective-permute-done.12.refs_2_ = bf16[3,2,32,448]{3,2,1,0:T(8,128)(2,1)S(1)} collective-permute-done((bf16[3,2,32,448]{3,2,1,0:T(8,128)(2,1)S(1)}, bf16[3,2,32,448]{3,2,1,0:T(8,128)(2,1)S(1)}, u32[]{:S(2)}, u32[]{:S(2)}) %collective-permute-start.12) | collective-permute-done | bytes 172064 | tf_op jit(solution)/shard_map/ppermute | solution.py:443
  58.1 0.0 collective-permute-start.14
  58.1 0.5 collective-permute-start.11
  58.6 1.0 %collective-permute-done.11.refs_1_ = bf16[1,2,32,448]{3,2,1,0:T(8,128)(2,1)S(1)} collective-permute-done((bf16[1,2,32,448]{3,2,1,0:T(8,128)(2,1)S(1)}, bf16[1,2,32,448]{3,2,1,0:T(8,128)(2,1)S(1)}, u32[]{:S(2)}, u32[]{:S(2)}) %collective-permute-start.11) | collective-permute-done | bytes 57376 | tf_op jit(solution)/shard_map/ppermute | solution.py:443
  59.7 0.0 collective-permute-done.14.refs_3_
  59.7 4.5 %late.1 = bf16[2,2048,768]{2,1,0:T(8,128)(2,1)} custom-call(s32[2]{0:T(128)S(1)} %pad_add_fusion.place_ref, bf16[2,2,2048,256]{3,2,1,0:T(8,128)(2,1)S(1)} %copy-done, bf16[448,768]{1,0:T(8,128)(2,1)S(1)} %get-tuple-element.24.shapes_ref, bf16[1,2,32,448]{3,2,1,0:T(8,128)(2,1)S(1)} %collective-permute-done.10.refs_0_, ...), custom_call_target="tpu_custom_call" | custom-call | flops 1962934272 | bytes 8388608 | tf_op jit(solution)/shard_map/late/pallas_call | solution.py:376
  (2 shorter events, 0.1 us)
Async XLA Ops:
  5.7 1.7 %collective-permute-start = (bf16[4,2,32,448]{3,2,1,0:T(8,128)(2,1)S(1)}, bf16[4,2,32,448]{3,2,1,0:T(8,128)(2,1)S(1)}, u32[]{:S(2)}, u32[]{:S(2)}) collective-permute-start(bf16[4,2,32,448]{3,2,1,0:T(8,128)(2,1)S(1)} %get-tuple-element.26.after_ref), channel_id=1, source_target_pairs={{0,1},{1,0},{2,3},{3,2},{4,5},{5,4},{6,7},{7,6},{8,9},{9,8},{10,11... | collective-permute-start | bytes 688136 | tf_op jit(solution)/shard_map/ppermute | solution.py:443
  7.5 15.4 %collective-permute-start.1 = (bf16[4,2,32,448]{3,2,1,0:T(8,128)(2,1)S(1)}, bf16[4,2,32,448]{3,2,1,0:T(8,128)(2,1)S(1)}, u32[]{:S(2)}, u32[]{:S(2)}) collective-permute-start(bf16[4,2,32,448]{3,2,1,0:T(8,128)(2,1)S(1)} %add.9.after_ref), channel_id=1, source_target_pairs={{0,2},{1,3},{2,0},{3,1},{4,6},{5,7},{6,4},{7,5},{8,10},{9,11},{10,... | collective-permute-start | bytes 688136 | tf_op jit(solution)/shard_map/ppermute | solution.py:443
  14.2 8.7 %collective-permute-start.2 = (bf16[4,1,32,448]{3,2,1,0:T(8,128)(2,1)S(1)}, bf16[4,1,32,448]{3,2,1,0:T(8,128)(2,1)S(1)}, u32[]{:S(2)}, u32[]{:S(2)}) collective-permute-start(bf16[4,1,32,448]{3,2,1,0:T(8,128)(2,1)S(1)} %get-tuple-element.31), channel_id=1, source_target_pairs={{0,1},{1,0},{2,3},{3,2},{4,5},{5,4},{6,7},{7,6},{8,9},{9,8},{10,11... | collective-permute-start | bytes 344072 | tf_op jit(solution)/shard_map/ppermute | solution.py:443
  18.1 4.8 %collective-permute-start.3 = (bf16[4,1,32,448]{3,2,1,0:T(8,128)(2,1)S(1)}, bf16[4,1,32,448]{3,2,1,0:T(8,128)(2,1)S(1)}, u32[]{:S(2)}, u32[]{:S(2)}) collective-permute-start(bf16[4,1,32,448]{3,2,1,0:T(8,128)(2,1)S(1)} %get-tuple-element.29.after_ref), channel_id=1, source_target_pairs={{0,1},{1,0},{2,3},{3,2},{4,5},{5,4},{6,7},{7,6},{8,9},{9,8},{10,11... | collective-permute-start | bytes 344072 | tf_op jit(solution)/shard_map/ppermute | solution.py:443
  23.0 8.7 %collective-permute-start.4 = (bf16[1,2,32,448]{3,2,1,0:T(8,128)(2,1)S(1)}, bf16[1,2,32,448]{3,2,1,0:T(8,128)(2,1)S(1)}, u32[]{:S(2)}, u32[]{:S(2)}) collective-permute-start(bf16[1,2,32,448]{3,2,1,0:T(8,128)(2,1)S(1)} %get-tuple-element.34), channel_id=1, source_target_pairs={{0,4},{1,5},{2,6},{3,7},{4,0},{5,1},{6,2},{7,3},{8,12},{9,13},{10,... | collective-permute-start | bytes 172040 | tf_op jit(solution)/shard_map/ppermute | solution.py:443
  24.6 7.5 %collective-permute-start.5 = (bf16[1,2,32,448]{3,2,1,0:T(8,128)(2,1)S(1)}, bf16[1,2,32,448]{3,2,1,0:T(8,128)(2,1)S(1)}, u32[]{:S(2)}, u32[]{:S(2)}) collective-permute-start(bf16[1,2,32,448]{3,2,1,0:T(8,128)(2,1)S(1)} %get-tuple-element.35), channel_id=1, source_target_pairs={{0,8},{1,9},{2,10},{3,11},{4,12},{5,13},{6,14},{7,15},{8,0},{9,1},... | collective-permute-start | bytes 172040 | tf_op jit(solution)/shard_map/ppermute | solution.py:443
  27.2 6.2 %collective-permute-start.6 = (bf16[1,2,32,448]{3,2,1,0:T(8,128)(2,1)S(1)}, bf16[1,2,32,448]{3,2,1,0:T(8,128)(2,1)S(1)}, u32[]{:S(2)}, u32[]{:S(2)}) collective-permute-start(bf16[1,2,32,448]{3,2,1,0:T(8,128)(2,1)S(1)} %get-tuple-element.36), channel_id=1, source_target_pairs={{0,12},{1,13},{2,14},{3,15},{4,8},{5,9},{6,10},{7,11},{8,4},{9,5},... | collective-permute-start | bytes 172040 | tf_op jit(solution)/shard_map/ppermute | solution.py:443
  33.4 18.9 %copy-start = (bf16[2,2,2048,256]{3,2,1,0:T(8,128)(2,1)S(1)}, bf16[2,2,2048,256]{3,2,1,0:T(8,128)(2,1)}, u32[]{:S(2)}) copy-start(bf16[2,2,2048,256]{3,2,1,0:T(8,128)(2,1)} %constant.33.clone.table_ref) | copy-start | bytes 12582916
  42.0 6.7 %collective-permute-start.9 = (bf16[2,32,448]{2,1,0:T(8,128)(2,1)S(1)}, bf16[2,32,448]{2,1,0:T(8,128)(2,1)S(1)}, u32[]{:S(2)}, u32[]{:S(2)}) collective-permute-start(bf16[2,32,448]{2,1,0:T(8,128)(2,1)S(1)} %respond.1), channel_id=1, source_target_pairs={{0,12},{1,13},{2,14},{3,15},{4,8},{5,9},{6,10},{7,11},{8,4},{9,5},... | collective-permute-start | bytes 172040 | tf_op jit(solution)/shard_map/ppermute | solution.py:443
  44.0 6.0 %collective-permute-start.8 = (bf16[2,32,448]{2,1,0:T(8,128)(2,1)S(1)}, bf16[2,32,448]{2,1,0:T(8,128)(2,1)S(1)}, u32[]{:S(2)}, u32[]{:S(2)}) collective-permute-start(bf16[2,32,448]{2,1,0:T(8,128)(2,1)S(1)} %respond.1), channel_id=1, source_target_pairs={{0,8},{1,9},{2,10},{3,11},{4,12},{5,13},{6,14},{7,15},{8,0},{9,1},... | collective-permute-start | bytes 172040 | tf_op jit(solution)/shard_map/ppermute | solution.py:443
  44.2 5.7 %collective-permute-start.7 = (bf16[2,32,448]{2,1,0:T(8,128)(2,1)S(1)}, bf16[2,32,448]{2,1,0:T(8,128)(2,1)S(1)}, u32[]{:S(2)}, u32[]{:S(2)}) collective-permute-start(bf16[2,32,448]{2,1,0:T(8,128)(2,1)S(1)} %respond.1), channel_id=1, source_target_pairs={{0,4},{1,5},{2,6},{3,7},{4,0},{5,1},{6,2},{7,3},{8,12},{9,13},{10,... | collective-permute-start | bytes 172040 | tf_op jit(solution)/shard_map/ppermute | solution.py:443
  46.4 4.3 %collective-permute-start.10 = (bf16[1,2,32,448]{3,2,1,0:T(8,128)(2,1)S(1)}, bf16[1,2,32,448]{3,2,1,0:T(8,128)(2,1)S(1)}, u32[]{:S(2)}, u32[]{:S(2)}) collective-permute-start(bf16[1,2,32,448]{3,2,1,0:T(8,128)(2,1)S(1)} %bitcast.9), channel_id=1, source_target_pairs={{0,2},{1,3},{2,0},{3,1},{4,6},{5,7},{6,4},{7,5},{8,10},{9,11},{10,... | collective-permute-start | bytes 172040 | tf_op jit(solution)/shard_map/ppermute | solution.py:443
  50.7 1.6 %collective-permute-start.13 = (bf16[4,2,32,448]{3,2,1,0:T(8,128)(2,1)S(1)}, bf16[4,2,32,448]{3,2,1,0:T(8,128)(2,1)S(1)}, u32[]{:S(2)}, u32[]{:S(2)}) collective-permute-start(bf16[4,2,32,448]{3,2,1,0:T(8,128)(2,1)S(1)} %pad_maximum_fusion.refs_0_), channel_id=1, source_target_pairs={{0,1},{1,0},{2,3},{3,2},{4,5},{5,4},{6,7},{7,6},{8,9},{9,8},{10,11... | collective-permute-start | bytes 688136 | tf_op jit(solution)/shard_map/ppermute | solution.py:443
  50.8 7.3 %collective-permute-start.12 = (bf16[3,2,32,448]{3,2,1,0:T(8,128)(2,1)S(1)}, bf16[3,2,32,448]{3,2,1,0:T(8,128)(2,1)S(1)}, u32[]{:S(2)}, u32[]{:S(2)}) collective-permute-start(bf16[3,2,32,448]{3,2,1,0:T(8,128)(2,1)S(1)} %pad_maximum_fusion.1), channel_id=1, source_target_pairs={{0,2},{1,3},{2,0},{3,1},{4,6},{5,7},{6,4},{7,5},{8,10},{9,11},{10,... | collective-permute-start | bytes 516104 | tf_op jit(solution)/shard_map/ppermute | solution.py:443
  58.1 1.5 %collective-permute-start.14 = (bf16[3,2,32,448]{3,2,1,0:T(8,128)(2,1)S(1)}, bf16[3,2,32,448]{3,2,1,0:T(8,128)(2,1)S(1)}, u32[]{:S(2)}, u32[]{:S(2)}) collective-permute-start(bf16[3,2,32,448]{3,2,1,0:T(8,128)(2,1)S(1)} %collective-permute-done.12.refs_2_), channel_id=1, source_target_pairs={{0,1},{1,0},{2,3},{3,2},{4,5},{5,4},{6,7},{7,6},{8,9},{9,8},{10,11... | collective-permute-start | bytes 516104 | tf_op jit(solution)/shard_map/ppermute | solution.py:443
  58.1 1.5 %collective-permute-start.11 = (bf16[1,2,32,448]{3,2,1,0:T(8,128)(2,1)S(1)}, bf16[1,2,32,448]{3,2,1,0:T(8,128)(2,1)S(1)}, u32[]{:S(2)}, u32[]{:S(2)}) collective-permute-start(bf16[1,2,32,448]{3,2,1,0:T(8,128)(2,1)S(1)} %collective-permute-done.10.refs_0_), channel_id=1, source_target_pairs={{0,1},{1,0},{2,3},{3,2},{4,5},{5,4},{6,7},{7,6},{8,9},{9,8},{10,11... | collective-permute-start | bytes 172040 | tf_op jit(solution)/shard_map/ppermute | solution.py:443

commit v6 on v5

--- a/solution.py
+++ b/solution.py
@@ -11,6 +11,7 @@
 
 FREQS = 512
 CORES = 2
+CHUNK = 512
 MIB = 1 << 20
 
 
@@ -20,30 +21,28 @@
     return owned[..., parity].transpose(1, 2, 0, 3).reshape(-1)
 
 
-def forward_tables(steps, chips):
+def signed_tables(steps, chips):
     times = np.arange(steps // 2, dtype=np.int64)
     tables = []
     for parity in range(2):
         ids = frequency_order(chips, parity)
         angle = (ids[:, None] * times[None, :] % steps) * (2.0 * math.pi / steps)
         table = np.stack([np.cos(angle), -np.sin(angle)], axis=1) / math.sqrt(steps)
-        tables.append(table.reshape(FREQS, steps // 2))
-    return np.stack(tables).reshape(2, 2, FREQS // 2, steps // 2)
+        tables.append(table.reshape(2, FREQS // 2, steps // 2))
+    return np.stack(tables)
+
+
+def forward_tables(steps, chips):
+    tables = signed_tables(steps, chips).reshape(2, 2, FREQS // 2, -1, CHUNK)
+    return tables.transpose(1, 3, 0, 2, 4)
 
 
 def inverse_tables(steps, chips):
-    tables = forward_tables(steps, chips) * 2.0
+    tables = signed_tables(steps, chips) * 2.0
     for parity in range(2):
         weights = np.where(frequency_order(chips, parity) == 0, 0.5, 1.0)
         tables[parity] *= np.repeat(weights, 2).reshape(2, FREQS // 2, 1)
-    return tables.transpose(0, 1, 3, 2)
-
-
-def chunk_list(half):
-    unit = half // 8
-    sizes = (unit, unit, 2 * unit, 4 * unit)
-    starts = (0, unit, 2 * unit, 4 * unit)
-    return tuple(zip(starts, sizes))
+    return tables.transpose(1, 0, 3, 2)
 
 
 def split_cores(place_ref, spec, shapes_ref, parity, keep_ref, send_ref):
@@ -68,48 +67,44 @@
     table_buf, forces_buf, acc_ref, table_sem, forces_sem, rest_sem, shapes_sem,
 ):
     y = place_ref[1] % 2
-    chunks = chunk_list(forces_ref.shape[1])
-    copies = []
-    for n, (start, size) in enumerate(chunks):
-        part = pl.ds(start, size)
-        pair = (
+    count = folded_ref.shape[0]
+
+    def chunk_copies(n):
+        return (
             pltpu.make_async_copy(
-                forces_ref.at[:, part], forces_buf.at[:, part], forces_sem.at[n]
+                forces_ref.at[:, pl.ds(n * CHUNK, CHUNK)], forces_buf.at[n], forces_sem.at[n]
             ),
-            pltpu.make_async_copy(
-                table_ref.at[:, y ^ 1, :, part], table_buf.at[:, :, part], table_sem.at[n]
-            ),
+            pltpu.make_async_copy(table_ref.at[y ^ 1, n], table_buf.at[n], table_sem.at[n]),
         )
-        for copy in pair:
+
+    for n in range(count):
+        for copy in chunk_copies(n):
             copy.start()
-        copies.append(pair)
     later = (
         pltpu.make_async_copy(shapes_ref, shapes_buf, shapes_sem),
-        pltpu.make_async_copy(table_ref.at[:, y], rest_ref, rest_sem),
+        pltpu.make_async_copy(table_ref.at[y], rest_ref, rest_sem),
     )
     for copy in later:
         copy.start()
-
-    for n, (start, size) in enumerate(chunks):
-        for copy in copies[n]:
+    acc_ref[...] = jnp.zeros_like(acc_ref)
+
+    @pl.loop(0, count)
+    def _(n):
+        for copy in chunk_copies(n):
             copy.wait()
-        low = forces_buf[0, start : start + size]
-        high = forces_buf[1, start : start + size]
+        low, high = forces_buf[n, 0], forces_buf[n, 1]
         for parity, folded in enumerate((low + high, low - high)):
-            folded_ref[parity, start : start + size] = folded
-            part = jnp.dot(
-                table_buf[parity, :, start : start + size],
-                folded,
-                preferred_element_type=jnp.float32,
+            folded_ref[n, parity] = folded
+            acc_ref[parity] += jnp.dot(
+                table_buf[n, parity], folded, preferred_element_type=jnp.float32
             )
-            if n == 0:
-                acc_ref[parity] = part
-            else:
-                acc_ref[parity] += part
 
     later[0].wait()
-    for parity in range(2):
+
+    @pl.loop(0, 2)
+    def _(parity):
         split_cores(place_ref, acc_ref[parity], shapes_buf, parity, keep_ref, send_ref)
+
     later[1].wait()
 
 
@@ -119,7 +114,7 @@
     rows = FREQS // (2 * CORES * zs)
     out = jax.ShapeDtypeStruct((zs, 2, rows, modes), jnp.bfloat16)
     vmem, hbm = pl.BlockSpec(memory_space=pltpu.VMEM), pl.BlockSpec(memory_space=pltpu.HBM)
-    count = len(chunk_list(half))
+    count = half // CHUNK
     return pl.pallas_call(
         across_kernel,
         in_specs=[pl.BlockSpec(memory_space=pltpu.SMEM), hbm, hbm, hbm],
@@ -127,13 +122,13 @@
         out_shape=[
             out,
             out,
-            pltpu.VMEM(forces.shape, jnp.bfloat16),
-            pltpu.VMEM((2, FREQS // 2, half), jnp.bfloat16),
+            pltpu.VMEM((count, 2, CHUNK, dofs), jnp.bfloat16),
+            pltpu.VMEM(table.shape[1:], jnp.bfloat16),
             pltpu.VMEM(shapes_t.shape, jnp.bfloat16),
         ],
         scratch_shapes=[
-            pltpu.VMEM((2, FREQS // 2, half), jnp.bfloat16),
-            pltpu.VMEM(forces.shape, jnp.bfloat16),
+            pltpu.VMEM(table.shape[1:], jnp.bfloat16),
+            pltpu.VMEM((count, 2, CHUNK, dofs), jnp.bfloat16),
             pltpu.VMEM((2, FREQS // 2, dofs), jnp.float32),
             pltpu.SemaphoreType.DMA((count,)),
             pltpu.SemaphoreType.DMA((count,)),
@@ -150,19 +145,26 @@
 
 def within_kernel(
     parity, start, place_ref, table_ref, folded_ref, shapes_ref, frf_ref, after_ref,
-    keep_ref, send_ref, held_ref, sem,
+    keep_ref, send_ref, held_ref, acc_ref, sem,
 ):
     copies = load_copies(start, frf_ref, held_ref, sem)
     for copy in copies:
         copy.start()
-    spec = jnp.dot(table_ref[parity], folded_ref[parity], preferred_element_type=jnp.float32)
-    split_cores(place_ref, spec, shapes_ref, 0, keep_ref, send_ref)
+    acc_ref[...] = jnp.zeros_like(acc_ref)
+
+    @pl.loop(0, folded_ref.shape[0])
+    def _(n):
+        acc_ref[...] += jnp.dot(
+            table_ref[n, parity], folded_ref[n, parity], preferred_element_type=jnp.float32
+        )
+
+    split_cores(place_ref, acc_ref[...], shapes_ref, 0, keep_ref, send_ref)
     for copy in copies:
         copy.wait()
 
 
 def within(parity, place, table, folded, shapes_t, frf, start, held, after, zs):
-    _, half, dofs = folded.shape
+    count, _, chunk, dofs = folded.shape
     modes = shapes_t.shape[0]
     rows = FREQS // (2 * CORES * zs)
     out = jax.ShapeDtypeStruct((zs, 1, rows, modes), jnp.bfloat16)
@@ -173,10 +175,15 @@
         + [pl.BlockSpec(memory_space=pl.ANY)],
         out_specs=[vmem] * 3,
         out_shape=[out, out, pltpu.VMEM((held,) + frf.shape[1:], jnp.bfloat16)],
-        scratch_shapes=[pltpu.SemaphoreType.DMA((math.gcd(held, 4),))],
+        scratch_shapes=[
+            pltpu.VMEM((FREQS // 2, dofs), jnp.float32),
+            pltpu.SemaphoreType.DMA((math.gcd(held, 4),)),
+        ],
         compiler_params=pltpu.CompilerParams(vmem_limit_bytes=8 * MIB),
         cost_estimate=pl.CostEstimate(
-            flops=FREQS * dofs * (half + modes), bytes_accessed=8 * MIB, transcendentals=0
+            flops=FREQS * dofs * (count * chunk + modes),
+            bytes_accessed=8 * MIB,
+            transcendentals=0,
         ),
         name="within",
     )(place, table, folded, shapes_t, in_hbm(frf), after)
@@ -296,7 +303,9 @@
                         k, parity
                     ].astype(jnp.float32)
         start += own_ref.shape[0]
-    for parity in range(2):
+
+    @pl.loop(0, 2)
+    def _(parity):
         moved_ref[parity] = jnp.dot(
             order_ref[parity].reshape(FREQS // 2, modes).astype(jnp.bfloat16),
             shapes_ref[...],
@@ -308,12 +317,13 @@
     shards, (waves_ref, order_ref, moved_ref) = refs[:-3], refs[-3:]
     project(place_ref, shards, shapes_ref, order_ref, moved_ref)
     y = place_ref[1] % 2
-    block = waves_ref.shape[1] // 4
-    for step in range(4):
-        part = slice(step * block, (step + 1) * block)
+
+    @pl.loop(0, waves_ref.shape[1] // CHUNK)
+    def _(step):
+        part = pl.ds(step * CHUNK, CHUNK)
         for parity in range(2):
             waves_ref[parity, part] = jnp.dot(
-                table_ref[parity, y, part], moved_ref[parity], preferred_element_type=jnp.float32
+                table_ref[y, parity, part], moved_ref[parity], preferred_element_type=jnp.float32
             )
 
 
@@ -330,18 +340,20 @@
             out_buf.at[:, part], out_ref.at[:, part], out_sem.at[step]
         )
 
-    for step in range(count):
-        part = slice(step * block, (step + 1) * block)
+    @pl.loop(0, count)
+    def _(step):
+        part = pl.ds(step * block, block)
         even, odd = (
             waves_ref[parity, part]
             + jnp.dot(
-                table_ref[parity, y, part], moved_ref[parity], preferred_element_type=jnp.float32
+                table_ref[y, parity, part], moved_ref[parity], preferred_element_type=jnp.float32
             )
             for parity in range(2)
         )
         out_buf[0, part] = (even + odd).astype(jnp.bfloat16)
         out_buf[1, part] = (even - odd).astype(jnp.bfloat16)
         copy_out(step).start()
+
     for step in range(count):
         copy_out(step).wait()
 

time: 64.3 us -> 63.9 us (level)
  waiting for transfers between devices: 11.5 us -> 10.7 us
    pallas_call x2, Pallas kernels: 7.53 us -> 5.17 us  [within(): pl.pallas_call(functools.partial(within_kernel, parity, start), in_specs=...]
    pallas_call x1, Pallas kernels: 4.51 us -> 5.83 us  [inverse(): pl.pallas_call(late_kernel, in_specs=in_specs + [vmem], out_specs=pl.Bloc...]
    pallas_call x1, Pallas kernels: 2.8 us -> 3.69 us  [inverse(): pl.pallas_call(early_kernel, in_specs=in_specs, out_specs=vmem, out_shape...]
    ppermute x15, waiting for transfers between devices: 11.5 us -> 10.7 us  [swap(): return lax.ppermute(values, 'dof', pairs)]
  transfers between devices with their start and end apart: 15 -> 15, of which waited for: 9 -> 9; matrix products, arithmetic and copies ran while one was open for 0% -> 0% of each run, Pallas kernels for 29% -> 27%
where the time goes in v6:
time: 63.9 us; the launch traced here: 63.7 us
  Pallas kernels  38.2 us (60%)
  starting transfers between devices  14.7 us (23%)
  waiting for transfers between devices  10.7 us (17%)
    ppermute x15, starting transfers between devices, swap(): return lax.ppermute(values, 'dof', pairs)  14.7 us
    ppermute x15, waiting for transfers between devices, swap(): return lax.ppermute(values, 'dof', pairs)  10.7 us
    pallas_call x1, Pallas kernels, respond(): pl.pallas_call(functools.partial(respond_kernel, len(pieces)), in_specs=[...  8.56 us
    pallas_call x2, Pallas kernels, load(): pl.pallas_call(functools.partial(load_kernel, start), in_specs=[hbm, anyw...  8.49 us
    pallas_call x1, Pallas kernels, across(): pl.pallas_call(across_kernel, in_specs=[pl.BlockSpec(memory_space=pltpu.S...  6.27 us
    pallas_call x1, Pallas kernels, inverse(): pl.pallas_call(late_kernel, in_specs=in_specs + [vmem], out_specs=pl.Bloc...  5.83 us
    pallas_call x2, Pallas kernels, within(): pl.pallas_call(functools.partial(within_kernel, parity, start), in_specs=...  5.17 us
    pallas_call x1, Pallas kernels, inverse(): pl.pallas_call(early_kernel, in_specs=in_specs, out_specs=vmem, out_shape...  3.69 us
  transfers between devices with their start and end apart: 15, of which 9 were waited for; matrix products, arithmetic and copies ran while one was open for 0% of the time, Pallas kernels for 27%

profile of v6, /device:TPU:0, one launch (start us, length us, event | category | flops | bytes accessed | tf_op | source)
XLA Modules:
  0.0 63.7 jit_solution(2015518142459530616)
XLA Ops:
  0.0 0.1 pad_add_fusion.place_ref
  0.1 6.3 %across.1 = (bf16[4,2,32,448]{3,2,1,0:T(8,128)(2,1)S(1)}, bf16[4,2,32,448]{3,2,1,0:T(8,128)(2,1)S(1)}, bf16[4,2,512,768]{3,2,1,0:T(8,128)(2,1)S(1)}, bf16[4,2,25...) custom-call(s32[2]{0:T(128)S(1)} %pad_add_fusion.place_ref, bf16[2,4,2,256,512]{4,3,2,1,0:T(8,128)(2,1)} %constant.32.clone.table_ref, ...), custom_call_target="tpu_custom_call" | custom-call | flops 1962934272 | bytes 12582912 | tf_op jit(solution)/shard_map/across/pallas_call | solution.py:118
  6.4 0.5 collective-permute-start
  6.9 1.2 %collective-permute-done.came_ref = bf16[4,2,32,448]{3,2,1,0:T(8,128)(2,1)S(1)} collective-permute-done((bf16[4,2,32,448]{3,2,1,0:T(8,128)(2,1)S(1)}, bf16[4,2,32,448]{3,2,1,0:T(8,128)(2,1)S(1)}, u32[]{:S(2)}, u32[]{:S(2)}) %collective-permute-start) | collective-permute-done | bytes 229408 | tf_op jit(solution)/shard_map/ppermute | solution.py:455
  8.0 0.1 add.9.after_ref
  8.1 3.0 %collective-permute-start.1 = (bf16[4,2,32,448]{3,2,1,0:T(8,128)(2,1)S(1)}, bf16[4,2,32,448]{3,2,1,0:T(8,128)(2,1)S(1)}, u32[]{:S(2)}, u32[]{:S(2)}) collective-permute-start(bf16[4,2,32,448]{3,2,1,0:T(8,128)(2,1)S(1)} %add.9.after_ref), channel_id=1, source_target_pairs={{0,2},{1,3},{2,0},{3,1},{4,6},{5,7},{6,4},{7,5},{8,10},{9,11},{10,... | collective-permute-start | bytes 688136 | tf_op jit(solution)/shard_map/ppermute | solution.py:455
  11.1 2.6 %within.3 = (bf16[4,1,32,448]{3,2,1,0:T(8,128)(2,1)S(1)}, bf16[4,1,32,448]{3,2,1,0:T(8,128)(2,1)S(1)}, bf16[4,2,448,448]{3,2,1,0:T(8,128)(2,1)S(1)}) custom-call(s32[2]{0:T(128)S(1)} %pad_add_fusion.place_ref, bf16[4,2,256,512]{3,2,1,0:T(8,128)(2,1)S(1)} %get-tuple-element.27.table_ref, bf16[4,2,512,768]{3,2,1,0:T(8,128)(2,1)S(1)} %get-tuple-element.28.folded_ref, ...), custom_call_target="tpu_custom_call" | custom-call | flops 981467136 | bytes 8388608 | tf_op jit(solution)/shard_map/within/pallas_call | solution.py:172
  13.6 0.1 collective-permute-start.2
  13.7 2.6 %within.2 = (bf16[4,1,32,448]{3,2,1,0:T(8,128)(2,1)S(1)}, bf16[4,1,32,448]{3,2,1,0:T(8,128)(2,1)S(1)}, bf16[4,2,448,448]{3,2,1,0:T(8,128)(2,1)S(1)}) custom-call(s32[2]{0:T(128)S(1)} %pad_add_fusion.place_ref, bf16[4,2,256,512]{3,2,1,0:T(8,128)(2,1)S(1)} %get-tuple-element.27.table_ref, bf16[4,2,512,768]{3,2,1,0:T(8,128)(2,1)S(1)} %get-tuple-element.28.folded_ref, ...), custom_call_target="tpu_custom_call" | custom-call | flops 981467136 | bytes 8388608 | tf_op jit(solution)/shard_map/within/pallas_call | solution.py:172
  16.3 0.6 collective-permute-start.3
  16.9 4.2 %load.2.after_ref.refs_6_ = bf16[12,2,448,448]{3,2,1,0:T(8,128)(2,1)S(1)} custom-call(bf16[32,2,448,448]{3,2,1,0:T(8,128)(2,1)} %frf_ref.7, bf16[4,1,32,448]{3,2,1,0:T(8,128)(2,1)S(1)} %get-tuple-element.29.after_ref), custom_call_target="tpu_custom_call" | custom-call | bytes 19267584 | tf_op jit(solution)/shard_map/load/pallas_call | solution.py:219
  21.1 0.0 collective-permute-done.2.refs_1_
  21.1 0.0 collective-permute-done.3.refs_3_
  21.1 0.0 collective-permute-done.1.came_ref
  21.2 0.1 gather_sum.1
  21.3 1.6 %collective-permute-start.4 = (bf16[1,2,32,448]{3,2,1,0:T(8,128)(2,1)S(1)}, bf16[1,2,32,448]{3,2,1,0:T(8,128)(2,1)S(1)}, u32[]{:S(2)}, u32[]{:S(2)}) collective-permute-start(bf16[1,2,32,448]{3,2,1,0:T(8,128)(2,1)S(1)} %get-tuple-element.34), channel_id=1, source_target_pairs={{0,4},{1,5},{2,6},{3,7},{4,0},{5,1},{6,2},{7,3},{8,12},{9,13},{10,... | collective-permute-start | bytes 172040 | tf_op jit(solution)/shard_map/ppermute | solution.py:455
  22.9 2.6 %collective-permute-start.5 = (bf16[1,2,32,448]{3,2,1,0:T(8,128)(2,1)S(1)}, bf16[1,2,32,448]{3,2,1,0:T(8,128)(2,1)S(1)}, u32[]{:S(2)}, u32[]{:S(2)}) collective-permute-start(bf16[1,2,32,448]{3,2,1,0:T(8,128)(2,1)S(1)} %get-tuple-element.35), channel_id=1, source_target_pairs={{0,8},{1,9},{2,10},{3,11},{4,12},{5,13},{6,14},{7,15},{8,0},{9,1},... | collective-permute-start | bytes 172040 | tf_op jit(solution)/shard_map/ppermute | solution.py:455
  25.5 0.2 collective-permute-start.6
  25.7 4.2 %load.3.refs_7_ = bf16[12,2,448,448]{3,2,1,0:T(8,128)(2,1)S(1)} custom-call(bf16[32,2,448,448]{3,2,1,0:T(8,128)(2,1)} %frf_ref.7, bf16[1,2,32,448]{3,2,1,0:T(8,128)(2,1)S(1)} %get-tuple-element.33.after_ref.refs_0_), custom_call_target="tpu_custom_call" | custom-call | bytes 19267584 | tf_op jit(solution)/shard_map/load/pallas_call | solution.py:219
  30.0 0.0 collective-permute-done.4.refs_1_
  30.0 0.4 collective-permute-done.5.refs_2_
  30.4 1.3 %collective-permute-done.6.refs_3_ = bf16[1,2,32,448]{3,2,1,0:T(8,128)(2,1)S(1)} collective-permute-done((bf16[1,2,32,448]{3,2,1,0:T(8,128)(2,1)S(1)}, bf16[1,2,32,448]{3,2,1,0:T(8,128)(2,1)S(1)}, u32[]{:S(2)}, u32[]{:S(2)}) %collective-permute-start.6) | collective-permute-done | bytes 57376 | tf_op jit(solution)/shard_map/ppermute | solution.py:455
  31.7 0.0 copy-start
  31.7 8.6 %respond.1 = bf16[2,32,448]{2,1,0:T(8,128)(2,1)S(1)} custom-call(bf16[1,2,32,448]{3,2,1,0:T(8,128)(2,1)S(1)} %get-tuple-element.33.after_ref.refs_0_, bf16[1,2,32,448]{3,2,1,0:T(8,128)(2,1)S(1)} %collective-permute-done.4.refs_1_, bf16[1,2,32,448]{3,2,1,0:T(8,128)(2,1)S(1)} %collective-permute-done.5.refs_2_, ...), custom_call_target="tpu_custom_call" | custom-call | flops 51380224 | bytes 25690112 | tf_op jit(solution)/shard_map/respond/pallas_call | solution.py:282
  40.2 2.0 %collective-permute-start.9 = (bf16[2,32,448]{2,1,0:T(8,128)(2,1)S(1)}, bf16[2,32,448]{2,1,0:T(8,128)(2,1)S(1)}, u32[]{:S(2)}, u32[]{:S(2)}) collective-permute-start(bf16[2,32,448]{2,1,0:T(8,128)(2,1)S(1)} %respond.1), channel_id=1, source_target_pairs={{0,12},{1,13},{2,14},{3,15},{4,8},{5,9},{6,10},{7,11},{8,4},{9,5},... | collective-permute-start | bytes 172040 | tf_op jit(solution)/shard_map/ppermute | solution.py:455
  42.2 0.2 collective-permute-start.8
  42.5 2.2 %collective-permute-start.7 = (bf16[2,32,448]{2,1,0:T(8,128)(2,1)S(1)}, bf16[2,32,448]{2,1,0:T(8,128)(2,1)S(1)}, u32[]{:S(2)}, u32[]{:S(2)}) collective-permute-start(bf16[2,32,448]{2,1,0:T(8,128)(2,1)S(1)} %respond.1), channel_id=1, source_target_pairs={{0,4},{1,5},{2,6},{3,7},{4,0},{5,1},{6,2},{7,3},{8,12},{9,13},{10,... | collective-permute-start | bytes 172040 | tf_op jit(solution)/shard_map/ppermute | solution.py:455
  44.7 0.5 collective-permute-start.10
  45.2 1.7 %collective-permute-done.9 = bf16[2,32,448]{2,1,0:T(8,128)(2,1)S(1)} collective-permute-done((bf16[2,32,448]{2,1,0:T(8,128)(2,1)S(1)}, bf16[2,32,448]{2,1,0:T(8,128)(2,1)S(1)}, u32[]{:S(2)}, u32[]{:S(2)}) %collective-permute-start.9) | collective-permute-done | bytes 57376 | tf_op jit(solution)/shard_map/ppermute | solution.py:455
  46.9 1.3 %collective-permute-done.8 = bf16[2,32,448]{2,1,0:T(8,128)(2,1)S(1)} collective-permute-done((bf16[2,32,448]{2,1,0:T(8,128)(2,1)S(1)}, bf16[2,32,448]{2,1,0:T(8,128)(2,1)S(1)}, u32[]{:S(2)}, u32[]{:S(2)}) %collective-permute-start.8) | collective-permute-done | bytes 57376 | tf_op jit(solution)/shard_map/ppermute | solution.py:455
  48.2 0.0 collective-permute-done.7
  48.2 0.7 %collective-permute-done.10.refs_0_ = bf16[1,2,32,448]{3,2,1,0:T(8,128)(2,1)S(1)} collective-permute-done((bf16[1,2,32,448]{3,2,1,0:T(8,128)(2,1)S(1)}, bf16[1,2,32,448]{3,2,1,0:T(8,128)(2,1)S(1)}, u32[]{:S(2)}, u32[]{:S(2)}) %collective-permute-start.10) | collective-permute-done | bytes 57376 | tf_op jit(solution)/shard_map/ppermute | solution.py:455
  49.0 0.1 collective-permute-start.13
  49.1 0.6 collective-permute-start.12
  49.6 1.0 %collective-permute-done.13.refs_1_ = bf16[4,2,32,448]{3,2,1,0:T(8,128)(2,1)S(1)} collective-permute-done((bf16[4,2,32,448]{3,2,1,0:T(8,128)(2,1)S(1)}, bf16[4,2,32,448]{3,2,1,0:T(8,128)(2,1)S(1)}, u32[]{:S(2)}, u32[]{:S(2)}) %collective-permute-start.13) | collective-permute-done | bytes 229408 | tf_op jit(solution)/shard_map/ppermute | solution.py:455
  50.6 0.0 copy-done
  50.6 3.7 %early.1.refs_4_ = f32[2,2048,768]{2,1,0:T(8,128)S(1)} custom-call(s32[2]{0:T(128)S(1)} %pad_add_fusion.place_ref, bf16[2,2,2048,256]{3,2,1,0:T(8,128)(2,1)S(1)} %copy-done, bf16[448,768]{1,0:T(8,128)(2,1)S(1)} %get-tuple-element.24.shapes_ref, bf16[4,2,32,448]{3,2,1,0:T(8,128)(2,1)S(1)} %pad_maximum_fusion.refs_0_, ...), custom_call_target="tpu_custom_call" | custom-call | flops 1000 | bytes 1000 | tf_op jit(solution)/shard_map/early/pallas_call | solution.py:378
  54.3 2.1 %collective-permute-done.12.refs_2_ = bf16[3,2,32,448]{3,2,1,0:T(8,128)(2,1)S(1)} collective-permute-done((bf16[3,2,32,448]{3,2,1,0:T(8,128)(2,1)S(1)}, bf16[3,2,32,448]{3,2,1,0:T(8,128)(2,1)S(1)}, u32[]{:S(2)}, u32[]{:S(2)}) %collective-permute-start.12) | collective-permute-done | bytes 172064 | tf_op jit(solution)/shard_map/ppermute | solution.py:455
  56.4 0.0 collective-permute-start.14
  56.4 0.5 collective-permute-start.11
  56.9 1.0 %collective-permute-done.11.refs_1_ = bf16[1,2,32,448]{3,2,1,0:T(8,128)(2,1)S(1)} collective-permute-done((bf16[1,2,32,448]{3,2,1,0:T(8,128)(2,1)S(1)}, bf16[1,2,32,448]{3,2,1,0:T(8,128)(2,1)S(1)}, u32[]{:S(2)}, u32[]{:S(2)}) %collective-permute-start.11) | collective-permute-done | bytes 57376 | tf_op jit(solution)/shard_map/ppermute | solution.py:455
  57.9 0.0 collective-permute-done.14.refs_3_
  57.9 5.8 %late.1 = bf16[2,2048,768]{2,1,0:T(8,128)(2,1)} custom-call(s32[2]{0:T(128)S(1)} %pad_add_fusion.place_ref, bf16[2,2,2048,256]{3,2,1,0:T(8,128)(2,1)S(1)} %copy-done, bf16[448,768]{1,0:T(8,128)(2,1)S(1)} %get-tuple-element.24.shapes_ref, bf16[1,2,32,448]{3,2,1,0:T(8,128)(2,1)S(1)} %collective-permute-done.10.refs_0_, ...), custom_call_target="tpu_custom_call" | custom-call | flops 1962934272 | bytes 8388608 | tf_op jit(solution)/shard_map/late/pallas_call | solution.py:388
  (2 shorter events, 0.1 us)
Async XLA Ops:
  6.4 1.7 %collective-permute-start = (bf16[4,2,32,448]{3,2,1,0:T(8,128)(2,1)S(1)}, bf16[4,2,32,448]{3,2,1,0:T(8,128)(2,1)S(1)}, u32[]{:S(2)}, u32[]{:S(2)}) collective-permute-start(bf16[4,2,32,448]{3,2,1,0:T(8,128)(2,1)S(1)} %get-tuple-element.26.after_ref), channel_id=1, source_target_pairs={{0,1},{1,0},{2,3},{3,2},{4,5},{5,4},{6,7},{7,6},{8,9},{9,8},{10,11... | collective-permute-start | bytes 688136 | tf_op jit(solution)/shard_map/ppermute | solution.py:455
  8.1 13.0 %collective-permute-start.1 = (bf16[4,2,32,448]{3,2,1,0:T(8,128)(2,1)S(1)}, bf16[4,2,32,448]{3,2,1,0:T(8,128)(2,1)S(1)}, u32[]{:S(2)}, u32[]{:S(2)}) collective-permute-start(bf16[4,2,32,448]{3,2,1,0:T(8,128)(2,1)S(1)} %add.9.after_ref), channel_id=1, source_target_pairs={{0,2},{1,3},{2,0},{3,1},{4,6},{5,7},{6,4},{7,5},{8,10},{9,11},{10,... | collective-permute-start | bytes 688136 | tf_op jit(solution)/shard_map/ppermute | solution.py:455
  13.6 7.5 %collective-permute-start.2 = (bf16[4,1,32,448]{3,2,1,0:T(8,128)(2,1)S(1)}, bf16[4,1,32,448]{3,2,1,0:T(8,128)(2,1)S(1)}, u32[]{:S(2)}, u32[]{:S(2)}) collective-permute-start(bf16[4,1,32,448]{3,2,1,0:T(8,128)(2,1)S(1)} %get-tuple-element.31), channel_id=1, source_target_pairs={{0,1},{1,0},{2,3},{3,2},{4,5},{5,4},{6,7},{7,6},{8,9},{9,8},{10,11... | collective-permute-start | bytes 344072 | tf_op jit(solution)/shard_map/ppermute | solution.py:455
  16.3 4.8 %collective-permute-start.3 = (bf16[4,1,32,448]{3,2,1,0:T(8,128)(2,1)S(1)}, bf16[4,1,32,448]{3,2,1,0:T(8,128)(2,1)S(1)}, u32[]{:S(2)}, u32[]{:S(2)}) collective-permute-start(bf16[4,1,32,448]{3,2,1,0:T(8,128)(2,1)S(1)} %get-tuple-element.29.after_ref), channel_id=1, source_target_pairs={{0,1},{1,0},{2,3},{3,2},{4,5},{5,4},{6,7},{7,6},{8,9},{9,8},{10,11... | collective-permute-start | bytes 344072 | tf_op jit(solution)/shard_map/ppermute | solution.py:455
  21.3 8.7 %collective-permute-start.4 = (bf16[1,2,32,448]{3,2,1,0:T(8,128)(2,1)S(1)}, bf16[1,2,32,448]{3,2,1,0:T(8,128)(2,1)S(1)}, u32[]{:S(2)}, u32[]{:S(2)}) collective-permute-start(bf16[1,2,32,448]{3,2,1,0:T(8,128)(2,1)S(1)} %get-tuple-element.34), channel_id=1, source_target_pairs={{0,4},{1,5},{2,6},{3,7},{4,0},{5,1},{6,2},{7,3},{8,12},{9,13},{10,... | collective-permute-start | bytes 172040 | tf_op jit(solution)/shard_map/ppermute | solution.py:455
  22.9 7.5 %collective-permute-start.5 = (bf16[1,2,32,448]{3,2,1,0:T(8,128)(2,1)S(1)}, bf16[1,2,32,448]{3,2,1,0:T(8,128)(2,1)S(1)}, u32[]{:S(2)}, u32[]{:S(2)}) collective-permute-start(bf16[1,2,32,448]{3,2,1,0:T(8,128)(2,1)S(1)} %get-tuple-element.35), channel_id=1, source_target_pairs={{0,8},{1,9},{2,10},{3,11},{4,12},{5,13},{6,14},{7,15},{8,0},{9,1},... | collective-permute-start | bytes 172040 | tf_op jit(solution)/shard_map/ppermute | solution.py:455
  25.5 6.2 %collective-permute-start.6 = (bf16[1,2,32,448]{3,2,1,0:T(8,128)(2,1)S(1)}, bf16[1,2,32,448]{3,2,1,0:T(8,128)(2,1)S(1)}, u32[]{:S(2)}, u32[]{:S(2)}) collective-permute-start(bf16[1,2,32,448]{3,2,1,0:T(8,128)(2,1)S(1)} %get-tuple-element.36), channel_id=1, source_target_pairs={{0,12},{1,13},{2,14},{3,15},{4,8},{5,9},{6,10},{7,11},{8,4},{9,5},... | collective-permute-start | bytes 172040 | tf_op jit(solution)/shard_map/ppermute | solution.py:455
  31.7 18.9 %copy-start = (bf16[2,2,2048,256]{3,2,1,0:T(8,128)(2,1)S(1)}, bf16[2,2,2048,256]{3,2,1,0:T(8,128)(2,1)}, u32[]{:S(2)}) copy-start(bf16[2,2,2048,256]{3,2,1,0:T(8,128)(2,1)} %constant.33.clone.table_ref) | copy-start | bytes 12582916
  40.2 6.7 %collective-permute-start.9 = (bf16[2,32,448]{2,1,0:T(8,128)(2,1)S(1)}, bf16[2,32,448]{2,1,0:T(8,128)(2,1)S(1)}, u32[]{:S(2)}, u32[]{:S(2)}) collective-permute-start(bf16[2,32,448]{2,1,0:T(8,128)(2,1)S(1)} %respond.1), channel_id=1, source_target_pairs={{0,12},{1,13},{2,14},{3,15},{4,8},{5,9},{6,10},{7,11},{8,4},{9,5},... | collective-permute-start | bytes 172040 | tf_op jit(solution)/shard_map/ppermute | solution.py:455
  42.2 6.0 %collective-permute-start.8 = (bf16[2,32,448]{2,1,0:T(8,128)(2,1)S(1)}, bf16[2,32,448]{2,1,0:T(8,128)(2,1)S(1)}, u32[]{:S(2)}, u32[]{:S(2)}) collective-permute-start(bf16[2,32,448]{2,1,0:T(8,128)(2,1)S(1)} %respond.1), channel_id=1, source_target_pairs={{0,8},{1,9},{2,10},{3,11},{4,12},{5,13},{6,14},{7,15},{8,0},{9,1},... | collective-permute-start | bytes 172040 | tf_op jit(solution)/shard_map/ppermute | solution.py:455
  42.5 5.7 %collective-permute-start.7 = (bf16[2,32,448]{2,1,0:T(8,128)(2,1)S(1)}, bf16[2,32,448]{2,1,0:T(8,128)(2,1)S(1)}, u32[]{:S(2)}, u32[]{:S(2)}) collective-permute-start(bf16[2,32,448]{2,1,0:T(8,128)(2,1)S(1)} %respond.1), channel_id=1, source_target_pairs={{0,4},{1,5},{2,6},{3,7},{4,0},{5,1},{6,2},{7,3},{8,12},{9,13},{10,... | collective-permute-start | bytes 172040 | tf_op jit(solution)/shard_map/ppermute | solution.py:455
  44.7 4.3 %collective-permute-start.10 = (bf16[1,2,32,448]{3,2,1,0:T(8,128)(2,1)S(1)}, bf16[1,2,32,448]{3,2,1,0:T(8,128)(2,1)S(1)}, u32[]{:S(2)}, u32[]{:S(2)}) collective-permute-start(bf16[1,2,32,448]{3,2,1,0:T(8,128)(2,1)S(1)} %bitcast.9), channel_id=1, source_target_pairs={{0,2},{1,3},{2,0},{3,1},{4,6},{5,7},{6,4},{7,5},{8,10},{9,11},{10,... | collective-permute-start | bytes 172040 | tf_op jit(solution)/shard_map/ppermute | solution.py:455
  49.0 1.6 %collective-permute-start.13 = (bf16[4,2,32,448]{3,2,1,0:T(8,128)(2,1)S(1)}, bf16[4,2,32,448]{3,2,1,0:T(8,128)(2,1)S(1)}, u32[]{:S(2)}, u32[]{:S(2)}) collective-permute-start(bf16[4,2,32,448]{3,2,1,0:T(8,128)(2,1)S(1)} %pad_maximum_fusion.refs_0_), channel_id=1, source_target_pairs={{0,1},{1,0},{2,3},{3,2},{4,5},{5,4},{6,7},{7,6},{8,9},{9,8},{10,11... | collective-permute-start | bytes 688136 | tf_op jit(solution)/shard_map/ppermute | solution.py:455
  49.1 7.3 %collective-permute-start.12 = (bf16[3,2,32,448]{3,2,1,0:T(8,128)(2,1)S(1)}, bf16[3,2,32,448]{3,2,1,0:T(8,128)(2,1)S(1)}, u32[]{:S(2)}, u32[]{:S(2)}) collective-permute-start(bf16[3,2,32,448]{3,2,1,0:T(8,128)(2,1)S(1)} %pad_maximum_fusion.1), channel_id=1, source_target_pairs={{0,2},{1,3},{2,0},{3,1},{4,6},{5,7},{6,4},{7,5},{8,10},{9,11},{10,... | collective-permute-start | bytes 516104 | tf_op jit(solution)/shard_map/ppermute | solution.py:455
  56.4 1.5 %collective-permute-start.14 = (bf16[3,2,32,448]{3,2,1,0:T(8,128)(2,1)S(1)}, bf16[3,2,32,448]{3,2,1,0:T(8,128)(2,1)S(1)}, u32[]{:S(2)}, u32[]{:S(2)}) collective-permute-start(bf16[3,2,32,448]{3,2,1,0:T(8,128)(2,1)S(1)} %collective-permute-done.12.refs_2_), channel_id=1, source_target_pairs={{0,1},{1,0},{2,3},{3,2},{4,5},{5,4},{6,7},{7,6},{8,9},{9,8},{10,11... | collective-permute-start | bytes 516104 | tf_op jit(solution)/shard_map/ppermute | solution.py:455
  56.4 1.5 %collective-permute-start.11 = (bf16[1,2,32,448]{3,2,1,0:T(8,128)(2,1)S(1)}, bf16[1,2,32,448]{3,2,1,0:T(8,128)(2,1)S(1)}, u32[]{:S(2)}, u32[]{:S(2)}) collective-permute-start(bf16[1,2,32,448]{3,2,1,0:T(8,128)(2,1)S(1)} %collective-permute-done.10.refs_0_), channel_id=1, source_target_pairs={{0,1},{1,0},{2,3},{3,2},{4,5},{5,4},{6,7},{7,6},{8,9},{9,8},{10,11... | collective-permute-start | bytes 172040 | tf_op jit(solution)/shard_map/ppermute | solution.py:455

commit v7 on v5

--- a/solution.py
+++ b/solution.py
@@ -11,6 +11,7 @@
 
 FREQS = 512
 CORES = 2
+CHUNK = 512
 MIB = 1 << 20
 
 
@@ -20,54 +21,65 @@
     return owned[..., parity].transpose(1, 2, 0, 3).reshape(-1)
 
 
-def forward_tables(steps, chips):
+def signed_tables(steps, chips):
     times = np.arange(steps // 2, dtype=np.int64)
     tables = []
     for parity in range(2):
         ids = frequency_order(chips, parity)
         angle = (ids[:, None] * times[None, :] % steps) * (2.0 * math.pi / steps)
         table = np.stack([np.cos(angle), -np.sin(angle)], axis=1) / math.sqrt(steps)
-        tables.append(table.reshape(FREQS, steps // 2))
-    return np.stack(tables).reshape(2, 2, FREQS // 2, steps // 2)
+        tables.append(table.reshape(2, FREQS // 2, steps // 2))
+    return np.stack(tables)
+
+
+def forward_tables(steps, chips):
+    return signed_tables(steps, chips).reshape(2, FREQS, steps // 2)
 
 
 def inverse_tables(steps, chips):
-    tables = forward_tables(steps, chips) * 2.0
+    tables = signed_tables(steps, chips) * 2.0
     for parity in range(2):
         weights = np.where(frequency_order(chips, parity) == 0, 0.5, 1.0)
         tables[parity] *= np.repeat(weights, 2).reshape(2, FREQS // 2, 1)
-    return tables.transpose(0, 1, 3, 2)
+    return tables.transpose(1, 0, 3, 2)
 
 
 def chunk_list(half):
     unit = half // 8
-    sizes = (unit, unit, 2 * unit, 4 * unit)
-    starts = (0, unit, 2 * unit, 4 * unit)
-    return tuple(zip(starts, sizes))
-
-
-def split_cores(place_ref, spec, shapes_ref, parity, keep_ref, send_ref):
-    zs, _, rows, modes = keep_ref.shape
-    first, z = place_ref[0] == 0, place_ref[1] // 2
+    sizes = (unit, unit, 2 * unit, 2 * unit, 2 * unit)
+    return tuple((sum(sizes[:n]), size) for n, size in enumerate(sizes))
+
+
+def split_cores(place_ref, spec_ref, shapes_ref, keep_ref, send_ref):
+    _, zs, rows, modes = keep_ref.shape
+    first, y, z = place_ref[0] == 0, place_ref[1] % 2, place_ref[1] // 2
     spec = lax.dot_general(
-        spec.astype(jnp.bfloat16),
+        spec_ref[...].astype(jnp.bfloat16),
         shapes_ref[...],
         (((1,), (1,)), ((), ())),
         preferred_element_type=jnp.float32,
-    ).reshape(CORES, zs, rows, modes)
-    keep = jnp.where(first, spec[0], spec[1]).astype(jnp.bfloat16)
-    send = jnp.where(first, spec[1], spec[0]).astype(jnp.bfloat16)
-    for k in range(zs):
-        keep_ref[z ^ k, parity] = keep[k]
-        send_ref[z ^ k, parity] = send[k]
-
-
-def across_kernel(
+    ).reshape(2, CORES, zs, rows, modes)
+    for j in range(2):
+        keep = jnp.where(first, spec[j, 0], spec[j, 1]).astype(jnp.bfloat16)
+        send = jnp.where(first, spec[j, 1], spec[j, 0]).astype(jnp.bfloat16)
+        for k in range(zs):
+            keep_ref[y ^ j, z ^ k] = keep[k]
+            send_ref[y ^ j, z ^ k] = send[k]
+
+
+def add_product(acc_ref, first, table, steps):
+    part = jnp.dot(table, steps, preferred_element_type=jnp.float32)
+    if first:
+        acc_ref[...] = part
+    else:
+        acc_ref[...] += part
+
+
+def even_kernel(
     place_ref, table_ref, forces_ref, shapes_ref,
-    keep_ref, send_ref, folded_ref, rest_ref, shapes_buf,
+    keep_ref, send_ref, odd_ref, rest_ref, shapes_buf,
     table_buf, forces_buf, acc_ref, table_sem, forces_sem, rest_sem, shapes_sem,
 ):
-    y = place_ref[1] % 2
     chunks = chunk_list(forces_ref.shape[1])
     copies = []
     for n, (start, size) in enumerate(chunks):
@@ -77,7 +89,7 @@
                 forces_ref.at[:, part], forces_buf.at[:, part], forces_sem.at[n]
             ),
             pltpu.make_async_copy(
-                table_ref.at[:, y ^ 1, :, part], table_buf.at[:, :, part], table_sem.at[n]
+                table_ref.at[0, :, part], table_buf.at[:, part], table_sem.at[n]
             ),
         )
         for copy in pair:
@@ -85,56 +97,46 @@
         copies.append(pair)
     later = (
         pltpu.make_async_copy(shapes_ref, shapes_buf, shapes_sem),
-        pltpu.make_async_copy(table_ref.at[:, y], rest_ref, rest_sem),
+        pltpu.make_async_copy(table_ref.at[1], rest_ref, rest_sem),
     )
     for copy in later:
         copy.start()
 
     for n, (start, size) in enumerate(chunks):
+        part = slice(start, start + size)
         for copy in copies[n]:
             copy.wait()
-        low = forces_buf[0, start : start + size]
-        high = forces_buf[1, start : start + size]
-        for parity, folded in enumerate((low + high, low - high)):
-            folded_ref[parity, start : start + size] = folded
-            part = jnp.dot(
-                table_buf[parity, :, start : start + size],
-                folded,
-                preferred_element_type=jnp.float32,
-            )
-            if n == 0:
-                acc_ref[parity] = part
-            else:
-                acc_ref[parity] += part
+        low, high = forces_buf[0, part], forces_buf[1, part]
+        odd_ref[part] = low - high
+        add_product(acc_ref, n == 0, table_buf[:, part], low + high)
 
     later[0].wait()
-    for parity in range(2):
-        split_cores(place_ref, acc_ref[parity], shapes_buf, parity, keep_ref, send_ref)
+    split_cores(place_ref, acc_ref, shapes_buf, keep_ref, send_ref)
     later[1].wait()
 
 
-def across(place, table, forces, shapes_t, zs):
+def even_spectra(place, table, forces, shapes_t, zs):
     _, half, dofs = forces.shape
     modes = shapes_t.shape[0]
     rows = FREQS // (2 * CORES * zs)
-    out = jax.ShapeDtypeStruct((zs, 2, rows, modes), jnp.bfloat16)
+    out = jax.ShapeDtypeStruct((2, zs, rows, modes), jnp.bfloat16)
     vmem, hbm = pl.BlockSpec(memory_space=pltpu.VMEM), pl.BlockSpec(memory_space=pltpu.HBM)
     count = len(chunk_list(half))
     return pl.pallas_call(
-        across_kernel,
+        even_kernel,
         in_specs=[pl.BlockSpec(memory_space=pltpu.SMEM), hbm, hbm, hbm],
         out_specs=[vmem] * 5,
         out_shape=[
             out,
             out,
-            pltpu.VMEM(forces.shape, jnp.bfloat16),
-            pltpu.VMEM((2, FREQS // 2, half), jnp.bfloat16),
+            pltpu.VMEM((half, dofs), jnp.bfloat16),
+            pltpu.VMEM((FREQS, half), jnp.bfloat16),
             pltpu.VMEM(shapes_t.shape, jnp.bfloat16),
         ],
         scratch_shapes=[
-            pltpu.VMEM((2, FREQS // 2, half), jnp.bfloat16),
+            pltpu.VMEM((FREQS, half), jnp.bfloat16),
             pltpu.VMEM(forces.shape, jnp.bfloat16),
-            pltpu.VMEM((2, FREQS // 2, dofs), jnp.float32),
+            pltpu.VMEM((FREQS, dofs), jnp.float32),
             pltpu.SemaphoreType.DMA((count,)),
             pltpu.SemaphoreType.DMA((count,)),
             pltpu.SemaphoreType.DMA,
@@ -144,42 +146,66 @@
         cost_estimate=pl.CostEstimate(
             flops=2 * FREQS * dofs * (half + modes), bytes_accessed=12 * MIB, transcendentals=0
         ),
-        name="across",
+        name="even_spectra",
     )(place, in_hbm(table), in_hbm(forces), in_hbm(shapes_t))
 
 
-def within_kernel(
-    parity, start, place_ref, table_ref, folded_ref, shapes_ref, frf_ref, after_ref,
-    keep_ref, send_ref, held_ref, sem,
-):
+def odd_sum_kernel(begin, end, start, table_ref, odd_ref, frf_ref, before_ref, after_ref,
+                   acc_ref, held_ref, sem):
     copies = load_copies(start, frf_ref, held_ref, sem)
     for copy in copies:
         copy.start()
-    spec = jnp.dot(table_ref[parity], folded_ref[parity], preferred_element_type=jnp.float32)
-    split_cores(place_ref, spec, shapes_ref, 0, keep_ref, send_ref)
+    for first in range(begin, end, CHUNK):
+        part = slice(first, first + CHUNK)
+        add_product(acc_ref, first == begin, table_ref[:, part], odd_ref[part])
+    if begin > 0:
+        acc_ref[...] += before_ref[...]
     for copy in copies:
         copy.wait()
 
 
-def within(parity, place, table, folded, shapes_t, frf, start, held, after, zs):
-    _, half, dofs = folded.shape
-    modes = shapes_t.shape[0]
-    rows = FREQS // (2 * CORES * zs)
-    out = jax.ShapeDtypeStruct((zs, 1, rows, modes), jnp.bfloat16)
+def odd_sum(table, odd, frf, begin, end, start, held, before, after):
+    dofs = odd.shape[1]
     vmem, hbm = pl.BlockSpec(memory_space=pltpu.VMEM), pl.BlockSpec(memory_space=pltpu.HBM)
-    return pl.pallas_call(
-        functools.partial(within_kernel, parity, start),
-        in_specs=[pl.BlockSpec(memory_space=pltpu.SMEM), vmem, vmem, vmem, hbm]
-        + [pl.BlockSpec(memory_space=pl.ANY)],
-        out_specs=[vmem] * 3,
-        out_shape=[out, out, pltpu.VMEM((held,) + frf.shape[1:], jnp.bfloat16)],
+    anywhere = pl.BlockSpec(memory_space=pl.ANY)
+    return pl.pallas_call(
+        functools.partial(odd_sum_kernel, begin, end, start),
+        in_specs=[vmem, vmem, hbm, vmem if begin > 0 else anywhere, anywhere],
+        out_specs=[vmem] * 2,
+        out_shape=[
+            pltpu.VMEM((FREQS, dofs), jnp.float32),
+            pltpu.VMEM((held,) + frf.shape[1:], jnp.bfloat16),
+        ],
         scratch_shapes=[pltpu.SemaphoreType.DMA((math.gcd(held, 4),))],
         compiler_params=pltpu.CompilerParams(vmem_limit_bytes=8 * MIB),
         cost_estimate=pl.CostEstimate(
-            flops=FREQS * dofs * (half + modes), bytes_accessed=8 * MIB, transcendentals=0
+            flops=2 * FREQS * dofs * (end - begin), bytes_accessed=8 * MIB, transcendentals=0
         ),
-        name="within",
-    )(place, table, folded, shapes_t, in_hbm(frf), after)
+        name="odd_sum",
+    )(table, odd, in_hbm(frf), before, after)
+
+
+def odd_modes_kernel(place_ref, acc_ref, shapes_ref, after_ref, keep_ref, send_ref):
+    split_cores(place_ref, acc_ref, shapes_ref, keep_ref, send_ref)
+
+
+def odd_modes(place, sums, shapes_t, zs, after):
+    modes, dofs = shapes_t.shape
+    rows = FREQS // (2 * CORES * zs)
+    vmem = pl.BlockSpec(memory_space=pltpu.VMEM)
+    out = jax.ShapeDtypeStruct((2, zs, rows, modes), jnp.bfloat16)
+    return pl.pallas_call(
+        odd_modes_kernel,
+        in_specs=[pl.BlockSpec(memory_space=pltpu.SMEM), vmem, vmem]
+        + [pl.BlockSpec(memory_space=pl.ANY)],
+        out_specs=[vmem] * 2,
+        out_shape=[out, out],
+        compiler_params=pltpu.CompilerParams(vmem_limit_bytes=8 * MIB),
+        cost_estimate=pl.CostEstimate(
+            flops=2 * FREQS * dofs * modes, bytes_accessed=3 * MIB, transcendentals=0
+        ),
+        name="odd_modes",
+    )(place, sums, shapes_t, after)
 
 
 def in_hbm(array):
@@ -207,7 +233,7 @@
         copy.wait()
 
 
-def load(frf, start, size, after):
+def load(frf, start, size, after, weight=4):
     hbm, anywhere = pl.BlockSpec(memory_space=pltpu.HBM), pl.BlockSpec(memory_space=pl.ANY)
     return pl.pallas_call(
         functools.partial(load_kernel, start),
@@ -217,7 +243,7 @@
         scratch_shapes=[pltpu.SemaphoreType.DMA((math.gcd(size, 4),))],
         compiler_params=pltpu.CompilerParams(vmem_limit_bytes=2 * MIB),
         cost_estimate=pl.CostEstimate(
-            flops=0, bytes_accessed=4 * size * math.prod(frf.shape[1:]), transcendentals=0
+            flops=0, bytes_accessed=weight * size * math.prod(frf.shape[1:]), transcendentals=0
         ),
         name="load",
     )(in_hbm(frf), after)
@@ -227,7 +253,7 @@
     pieces, parts = refs[:count], refs[count:-4]
     out_ref, direct_ref, turned_ref, result_ref = refs[-4:]
     _, rows, modes = out_ref.shape
-    total = sum(piece[0].astype(jnp.float32) for piece in pieces).reshape(2 * rows, modes)
+    total = sum(piece[...].astype(jnp.float32) for piece in pieces).reshape(2 * rows, modes)
     total = total.astype(jnp.bfloat16).astype(jnp.float32)
     row = lax.broadcasted_iota(jnp.int32, total.shape, 0)
     turned = jnp.where(row % 2 == 0, -jnp.roll(total, -1, axis=0), jnp.roll(total, 1, axis=0))
@@ -269,7 +295,7 @@
 
 
 def respond(pieces, parts):
-    rows, modes = pieces[0].shape[2:]
+    rows, modes = pieces[0].shape[1:]
     vmem = pl.BlockSpec(memory_space=pltpu.VMEM)
     size = sum(part.size for part in parts)
     return pl.pallas_call(
@@ -308,12 +334,12 @@
     shards, (waves_ref, order_ref, moved_ref) = refs[:-3], refs[-3:]
     project(place_ref, shards, shapes_ref, order_ref, moved_ref)
     y = place_ref[1] % 2
-    block = waves_ref.shape[1] // 4
-    for step in range(4):
-        part = slice(step * block, (step + 1) * block)
+    block = 2 * CHUNK
+    for start in range(0, waves_ref.shape[1], block):
+        part = slice(start, start + block)
         for parity in range(2):
             waves_ref[parity, part] = jnp.dot(
-                table_ref[parity, y, part], moved_ref[parity], preferred_element_type=jnp.float32
+                table_ref[y, parity, part], moved_ref[parity], preferred_element_type=jnp.float32
             )
 
 
@@ -335,13 +361,14 @@
         even, odd = (
             waves_ref[parity, part]
             + jnp.dot(
-                table_ref[parity, y, part], moved_ref[parity], preferred_element_type=jnp.float32
+                table_ref[y, parity, part], moved_ref[parity], preferred_element_type=jnp.float32
             )
             for parity in range(2)
         )
         out_buf[0, part] = (even + odd).astype(jnp.bfloat16)
         out_buf[1, part] = (even - odd).astype(jnp.bfloat16)
         copy_out(step).start()
+
     for step in range(count):
         copy_out(step).wait()
 
@@ -379,57 +406,58 @@
         out_specs=pl.BlockSpec(memory_space=pltpu.HBM),
         out_shape=jax.ShapeDtypeStruct((2, half, dofs), jnp.bfloat16),
         scratch_shapes=scratch
-        + [pltpu.VMEM((2, half, dofs), jnp.bfloat16), pltpu.SemaphoreType.DMA((8,))],
+        + [pltpu.VMEM((2, half, dofs), jnp.bfloat16), pltpu.SemaphoreType.DMA((half // CHUNK,))],
         compiler_params=params,
         cost_estimate=cost,
         name="late",
     )(*given, waves)
 
 
-def add_kernel(ours_ref, came_ref, out_ref):
-    total = ours_ref[...].astype(jnp.float32) + came_ref[...].astype(jnp.float32)
-    out_ref[...] = total.astype(jnp.bfloat16)
-
-
-def add(ours, came):
+def add_kernel(count, ours_ref, came_ref, *refs):
+    out_refs = refs[count:]
+    for n, out_ref in enumerate(out_refs):
+        total = ours_ref[n].astype(jnp.float32) + came_ref[n].astype(jnp.float32)
+        out_ref[...] = total.astype(jnp.bfloat16)
+
+
+def add(ours, came, *after):
     vmem = pl.BlockSpec(memory_space=pltpu.VMEM)
     return pl.pallas_call(
-        add_kernel,
-        in_specs=[vmem] * 2,
-        out_specs=vmem,
-        out_shape=jax.ShapeDtypeStruct(ours.shape, jnp.bfloat16),
+        functools.partial(add_kernel, len(after)),
+        in_specs=[vmem] * 2 + [pl.BlockSpec(memory_space=pl.ANY)] * len(after),
+        out_specs=[vmem] * ours.shape[0],
+        out_shape=[jax.ShapeDtypeStruct(ours.shape[1:], jnp.bfloat16)] * ours.shape[0],
         compiler_params=pltpu.CompilerParams(vmem_limit_bytes=8 * MIB),
         cost_estimate=pl.CostEstimate(
             flops=came.size, bytes_accessed=6 * came.size, transcendentals=0
         ),
         name="add",
-    )(ours, came)
-
-
-def gather_sum_kernel(came_ref, after_ref, *refs):
-    within_refs, out_refs = refs[:4], refs[4:]
+    )(ours, came, *after)
+
+
+def gather_sum_kernel(after_ref, *refs):
+    pairs, out_refs = refs[:4], refs[4:]
     for k, out_ref in enumerate(out_refs):
         for parity in range(2):
-            keep_ref, twin_ref = within_refs[2 * parity : 2 * parity + 2]
-            total = keep_ref[k, 0].astype(jnp.float32) + twin_ref[k, 0].astype(jnp.float32)
-            total = total + came_ref[k, parity].astype(jnp.float32)
-            out_ref[0, parity] = total.astype(jnp.bfloat16)
-
-
-def gather_sum(came, kept, after):
+            ours_ref, came_ref = pairs[2 * parity : 2 * parity + 2]
+            total = ours_ref[k].astype(jnp.float32) + came_ref[k].astype(jnp.float32)
+            out_ref[parity] = total.astype(jnp.bfloat16)
+
+
+def gather_sum(pairs, after):
     vmem = pl.BlockSpec(memory_space=pltpu.VMEM)
-    zs = came.shape[0]
+    zs, rows, modes = pairs[0].shape
     return pl.pallas_call(
         gather_sum_kernel,
-        in_specs=[vmem, pl.BlockSpec(memory_space=pl.ANY)] + [vmem] * 4,
+        in_specs=[pl.BlockSpec(memory_space=pl.ANY)] + [vmem] * 4,
         out_specs=[vmem] * zs,
-        out_shape=[jax.ShapeDtypeStruct((1,) + came.shape[1:], jnp.bfloat16)] * zs,
+        out_shape=[jax.ShapeDtypeStruct((2, rows, modes), jnp.bfloat16)] * zs,
         compiler_params=pltpu.CompilerParams(vmem_limit_bytes=8 * MIB),
         cost_estimate=pl.CostEstimate(
-            flops=2 * came.size, bytes_accessed=8 * came.size, transcendentals=0
+            flops=pairs[0].size, bytes_accessed=12 * pairs[0].size, transcendentals=0
         ),
         name="gather_sum",
-    )(came, after, *kept)
+    )(after, *pairs)
 
 
 def on_device(devices, forces, mode_shapes, frf):
@@ -449,19 +477,21 @@
     inv = jnp.asarray(inverse_tables(steps, chips).astype(jnp.bfloat16))
 
     unit = frf.shape[0] // 8
-    keep, send, folded, rest, shapes_v = across(
+    keep, send, odd, rest, shapes_v = even_spectra(
         place, fwd, forces.reshape(2, half, dofs), shapes_t, zs
     )
-    given = (place, rest, folded, shapes_v, frf)
-    keep0, send0, part0 = within(0, *given, 0, unit, send, zs)
-    pair = add(keep, swap(send, 1))
-    came = swap(pair, 2)
-    keep1, send1, part1 = within(1, *given, unit, unit, pair, zs)
-    part2 = load(frf, 2 * unit, 3 * unit, send1)
-    pieces = gather_sum(came, (keep0, swap(send0, 1), keep1, swap(send1, 1)), part2)
-    part3 = load(frf, 5 * unit, 3 * unit, pieces[0])
+    sums, part0 = odd_sum(rest, odd, frf, 0, CHUNK, 0, unit, shapes_v, keep)
+    here, there = add(keep, swap(send, 1), part0)
+    came = swap(there, 2)
+    sums, part1 = odd_sum(rest, odd, frf, CHUNK, half, unit, unit, sums, there)
+    odd_keep, odd_send = odd_modes(place, sums, shapes_v, zs, came)
+    part2 = load(frf, 2 * unit, unit, odd_send)
+    odd_here, odd_there = add(odd_keep, swap(odd_send, 1), part2)
+    part3 = load(frf, 3 * unit, 2 * unit, odd_there)
+    pieces = gather_sum((here, came, odd_here, swap(odd_there, 2)), part3)
+    part4 = load(frf, 5 * unit, 3 * unit, pieces[0])
     pieces = [pieces[0]] + [swap(pieces[k], 4 * k) for k in range(1, zs)]
-    response = respond(pieces, (part0, part1, part2, part3))
+    response = respond(pieces, (part0, part1, part2, part3, part4))
 
     over = swap(response[None], 2)
     shards = [swap(response, 4 * k) for k in range(1, zs)]

time: 64.3 us -> 66.5 us (1.034)
  starting transfers between devices: 14.7 us -> 17.6 us
  Pallas kernels: 37.7 us -> 36.8 us
    ppermute x15, starting transfers between devices: 14.7 us -> 17.6 us  [swap(): return lax.ppermute(values, 'dof', pairs)]
    pallas_call x5 -> x7, Pallas kernels: 13.3 us -> 11.4 us  [the longest x1 5.72 us: even_spectra(): pl.pallas_call(even_kernel, in_specs=[pl.BlockSpec(memory_space=pltpu.SME...]
    pallas_call x2 -> x3, Pallas kernels: 8.49 us -> 9.48 us  [load(): pl.pallas_call(functools.partial(load_kernel, start), in_specs=[hbm, anyw...]
  transfers between devices with their start and end apart: 15 -> 15, of which waited for: 9 -> 9; matrix products, arithmetic and copies ran while one was open for 0% -> 0% of each run, Pallas kernels for 29% -> 25%
where the time goes in v7:
time: 66.5 us; the launch traced here: 66.4 us
  Pallas kernels  36.8 us (55%)
  starting transfers between devices  17.6 us (26%)
  waiting for transfers between devices  11.5 us (17%)
    ppermute x15, starting transfers between devices, swap(): return lax.ppermute(values, 'dof', pairs)  17.6 us
    ppermute x15, waiting for transfers between devices, swap(): return lax.ppermute(values, 'dof', pairs)  11.5 us
    pallas_call x3, Pallas kernels, load(): pl.pallas_call(functools.partial(load_kernel, start), in_specs=[hbm, anyw...  9.48 us
    pallas_call x1, Pallas kernels, respond(): pl.pallas_call(functools.partial(respond_kernel, len(pieces)), in_specs=[...  8.45 us
    pallas_call x1, Pallas kernels, even_spectra(): pl.pallas_call(even_kernel, in_specs=[pl.BlockSpec(memory_space=pltpu.SME...  5.72 us
    pallas_call x1, Pallas kernels, inverse(): pl.pallas_call(late_kernel, in_specs=in_specs + [vmem], out_specs=pl.Bloc...  4.72 us
    pallas_call x2, Pallas kernels, odd_sum(): pl.pallas_call(functools.partial(odd_sum_kernel, begin, end, start), in_s...  4.35 us
    pallas_call x1, Pallas kernels, inverse(): pl.pallas_call(early_kernel, in_specs=in_specs, out_specs=vmem, out_shape...  2.81 us
  transfers between devices with their start and end apart: 15, of which 9 were waited for; matrix products, arithmetic and copies ran while one was open for 0% of the time, Pallas kernels for 25%

profile of v7, /device:TPU:0, one launch (start us, length us, event | category | flops | bytes accessed | tf_op | source)
XLA Modules:
  0.0 66.4 jit_solution(18235273959426595882)
XLA Ops:
  0.0 0.1 pad_add_fusion.place_ref
  0.1 5.7 %even_spectra.1 = (bf16[2,4,32,448]{3,2,1,0:T(8,128)(2,1)S(1)}, bf16[2,4,32,448]{3,2,1,0:T(8,128)(2,1)S(1)}, bf16[2048,768]{1,0:T(8,128)(2,1)S(1)}, bf16[512,2048]{1,0:T(8,128)(2,1)S(1)}, bf16[448,768]{1,0:T(8,128)(2,1)S(1)}) custom-call(s32[2]{0:T(128)S(1)} %pad_add_fusion.place_ref, bf16[2,512,2048]{2,1,0:T(8,128)(2,1)} %constant.32.clone.table_ref, ...), custom_call_target="tpu_custom_call" | custom-call | flops 1962934272 | bytes 12582912 | tf_op jit(solution)/shard_map/even_spectra/pallas_call | solution.py:125
  5.8 0.5 collective-permute-start
  6.3 2.3 %odd_sum.2 = (f32[512,768]{1,0:T(8,128)S(1)}, bf16[4,2,448,448]{3,2,1,0:T(8,128)(2,1)S(1)}) custom-call(bf16[512,2048]{1,0:T(8,128)(2,1)S(1)} %get-tuple-element.29.table_ref, bf16[2048,768]{1,0:T(8,128)(2,1)S(1)} %get-tuple-element.30.odd_ref, bf16[32,2,448,448]{3,2,1,0:T(8,128)(2,1)} %frf_ref.9, ...), custom_call_target="tpu_custom_call" | custom-call | flops 402653184 | bytes 8388608 | tf_op jit(solution)/shard_map/odd_sum/pallas_call | solution.py:171
  8.6 0.0 collective-permute-done.came_ref
  8.6 0.1 add.10
  8.7 2.6 %collective-permute-start.1 = (bf16[4,32,448]{2,1,0:T(8,128)(2,1)S(1)}, bf16[4,32,448]{2,1,0:T(8,128)(2,1)S(1)}, u32[]{:S(2)}, u32[]{:S(2)}) collective-permute-start(bf16[4,32,448]{2,1,0:T(8,128)(2,1)S(1)} %get-tuple-element.35.after_ref), channel_id=1, source_target_pairs={{0,2},{1,3},{2,0},{3,1},{4,6},{5,7},{6,4},{7,5},{8,10},{9,11},{10,... | collective-permute-start | bytes 344072 | tf_op jit(solution)/shard_map/ppermute | solution.py:471
  11.3 2.1 %odd_sum.3 = (f32[512,768]{1,0:T(8,128)S(1)}, bf16[4,2,448,448]{3,2,1,0:T(8,128)(2,1)S(1)}) custom-call(bf16[512,2048]{1,0:T(8,128)(2,1)S(1)} %get-tuple-element.29.table_ref, bf16[2048,768]{1,0:T(8,128)(2,1)S(1)} %get-tuple-element.30.odd_ref, bf16[32,2,448,448]{3,2,1,0:T(8,128)(2,1)} %frf_ref.9, f32[512,768]{1,0:T(8,128)S(1)} %get-tuple-element.32.before_ref, ...), custom_call_target="tpu_custom_call" | custom-call | flops 1207959552 | bytes 8388608 | tf_op jit(solution)/shard_map/odd_sum/pallas_call | solution.py:171
  13.4 2.1 %collective-permute-done.1.after_ref.refs_1_ = bf16[4,32,448]{2,1,0:T(8,128)(2,1)S(1)} collective-permute-done((bf16[4,32,448]{2,1,0:T(8,128)(2,1)S(1)}, bf16[4,32,448]{2,1,0:T(8,128)(2,1)S(1)}, u32[]{:S(2)}, u32[]{:S(2)}) %collective-permute-start.1) | collective-permute-done | bytes 114720 | tf_op jit(solution)/shard_map/ppermute | solution.py:471
  15.5 1.1 %odd_modes.1 = (bf16[2,4,32,448]{3,2,1,0:T(8,128)(2,1)S(1)}, bf16[2,4,32,448]{3,2,1,0:T(8,128)(2,1)S(1)}) custom-call(s32[2]{0:T(128)S(1)} %pad_add_fusion.place_ref, f32[512,768]{1,0:T(8,128)S(1)} %get-tuple-element.36.acc_ref, bf16[448,768]{1,0:T(8,128)(2,1)S(1)} %get-tuple-element.28.before_ref.shapes_ref, ...), custom_call_target="tpu_custom_call" | custom-call | flops 352321536 | bytes 3145728 | tf_op jit(solution)/shard_map/odd_modes/pallas_call | solution.py:197
  16.6 0.1 collective-permute-start.2
  16.7 2.0 %load.3.refs_0_.refs_6_ = bf16[4,2,448,448]{3,2,1,0:T(8,128)(2,1)S(1)} custom-call(bf16[32,2,448,448]{3,2,1,0:T(8,128)(2,1)} %frf_ref.9, bf16[2,4,32,448]{3,2,1,0:T(8,128)(2,1)S(1)} %get-tuple-element.38.after_ref), custom_call_target="tpu_custom_call" | custom-call | bytes 6422528 | tf_op jit(solution)/shard_map/load/pallas_call | solution.py:238
  18.7 0.0 collective-permute-done.2.came_ref
  18.7 0.1 add.11
  18.8 1.8 %collective-permute-start.3 = (bf16[4,32,448]{2,1,0:T(8,128)(2,1)S(1)}, bf16[4,32,448]{2,1,0:T(8,128)(2,1)S(1)}, u32[]{:S(2)}, u32[]{:S(2)}) collective-permute-start(bf16[4,32,448]{2,1,0:T(8,128)(2,1)S(1)} %get-tuple-element.39.after_ref), channel_id=1, source_target_pairs={{0,2},{1,3},{2,0},{3,1},{4,6},{5,7},{6,4},{7,5},{8,10},{9,11},{10,... | collective-permute-start | bytes 344072 | tf_op jit(solution)/shard_map/ppermute | solution.py:471
  20.6 3.2 %load.4.after_ref.refs_7_ = bf16[8,2,448,448]{3,2,1,0:T(8,128)(2,1)S(1)} custom-call(bf16[32,2,448,448]{3,2,1,0:T(8,128)(2,1)} %frf_ref.9, bf16[4,32,448]{2,1,0:T(8,128)(2,1)S(1)} %get-tuple-element.39.after_ref), custom_call_target="tpu_custom_call" | custom-call | bytes 12845056 | tf_op jit(solution)/shard_map/load/pallas_call | solution.py:238
  23.8 1.0 %collective-permute-done.3.refs_3_ = bf16[4,32,448]{2,1,0:T(8,128)(2,1)S(1)} collective-permute-done((bf16[4,32,448]{2,1,0:T(8,128)(2,1)S(1)}, bf16[4,32,448]{2,1,0:T(8,128)(2,1)S(1)}, u32[]{:S(2)}, u32[]{:S(2)}) %collective-permute-start.3) | collective-permute-done | bytes 114720 | tf_op jit(solution)/shard_map/ppermute | solution.py:471
  24.8 0.1 gather_sum.1
  24.8 1.9 %collective-permute-start.4 = (bf16[2,32,448]{2,1,0:T(8,128)(2,1)S(1)}, bf16[2,32,448]{2,1,0:T(8,128)(2,1)S(1)}, u32[]{:S(2)}, u32[]{:S(2)}) collective-permute-start(bf16[2,32,448]{2,1,0:T(8,128)(2,1)S(1)} %get-tuple-element.43), channel_id=1, source_target_pairs={{0,4},{1,5},{2,6},{3,7},{4,0},{5,1},{6,2},{7,3},{8,12},{9,13},{10,... | collective-permute-start | bytes 172040 | tf_op jit(solution)/shard_map/ppermute | solution.py:471
  26.7 2.6 %collective-permute-start.5 = (bf16[2,32,448]{2,1,0:T(8,128)(2,1)S(1)}, bf16[2,32,448]{2,1,0:T(8,128)(2,1)S(1)}, u32[]{:S(2)}, u32[]{:S(2)}) collective-permute-start(bf16[2,32,448]{2,1,0:T(8,128)(2,1)S(1)} %get-tuple-element.44), channel_id=1, source_target_pairs={{0,8},{1,9},{2,10},{3,11},{4,12},{5,13},{6,14},{7,15},{8,0},{9,1},... | collective-permute-start | bytes 172040 | tf_op jit(solution)/shard_map/ppermute | solution.py:471
  29.3 0.0 collective-permute-start.6
  29.3 4.2 %load.5.refs_8_ = bf16[12,2,448,448]{3,2,1,0:T(8,128)(2,1)S(1)} custom-call(bf16[32,2,448,448]{3,2,1,0:T(8,128)(2,1)} %frf_ref.9, bf16[2,32,448]{2,1,0:T(8,128)(2,1)S(1)} %get-tuple-element.42.after_ref.refs_0_), custom_call_target="tpu_custom_call" | custom-call | bytes 19267584 | tf_op jit(solution)/shard_map/load/pallas_call | solution.py:238
  33.5 0.0 collective-permute-done.4.refs_1_
  33.6 0.3 collective-permute-done.5.refs_2_
  33.8 1.5 %collective-permute-done.6.refs_3_ = bf16[2,32,448]{2,1,0:T(8,128)(2,1)S(1)} collective-permute-done((bf16[2,32,448]{2,1,0:T(8,128)(2,1)S(1)}, bf16[2,32,448]{2,1,0:T(8,128)(2,1)S(1)}, u32[]{:S(2)}, u32[]{:S(2)}) %collective-permute-start.6) | collective-permute-done | bytes 57376 | tf_op jit(solution)/shard_map/ppermute | solution.py:471
  35.4 0.0 copy-start
  35.4 8.4 %respond.1 = bf16[2,32,448]{2,1,0:T(8,128)(2,1)S(1)} custom-call(bf16[2,32,448]{2,1,0:T(8,128)(2,1)S(1)} %get-tuple-element.42.after_ref.refs_0_, bf16[2,32,448]{2,1,0:T(8,128)(2,1)S(1)} %collective-permute-done.4.refs_1_, bf16[2,32,448]{2,1,0:T(8,128)(2,1)S(1)} %collective-permute-done.5.refs_2_, bf16[2,32,448]{2,1,0:T(8,128)(2,1)S(1)} %collective-permute-done.6.refs_3_, ...), custom_call_target="tpu_custom_call" | custom-call | flops 51380224 | bytes 25690112 | tf_op jit(solution)/shard_map/respond/pallas_call | solution.py:301
  43.8 2.1 %collective-permute-start.9 = (bf16[2,32,448]{2,1,0:T(8,128)(2,1)S(1)}, bf16[2,32,448]{2,1,0:T(8,128)(2,1)S(1)}, u32[]{:S(2)}, u32[]{:S(2)}) collective-permute-start(bf16[2,32,448]{2,1,0:T(8,128)(2,1)S(1)} %respond.1), channel_id=1, source_target_pairs={{0,12},{1,13},{2,14},{3,15},{4,8},{5,9},{6,10},{7,11},{8,4},{9,5},... | collective-permute-start | bytes 172040 | tf_op jit(solution)/shard_map/ppermute | solution.py:471
  45.9 0.0 collective-permute-start.8
  45.9 2.3 %collective-permute-start.7 = (bf16[2,32,448]{2,1,0:T(8,128)(2,1)S(1)}, bf16[2,32,448]{2,1,0:T(8,128)(2,1)S(1)}, u32[]{:S(2)}, u32[]{:S(2)}) collective-permute-start(bf16[2,32,448]{2,1,0:T(8,128)(2,1)S(1)} %respond.1), channel_id=1, source_target_pairs={{0,4},{1,5},{2,6},{3,7},{4,0},{5,1},{6,2},{7,3},{8,12},{9,13},{10,... | collective-permute-start | bytes 172040 | tf_op jit(solution)/shard_map/ppermute | solution.py:471
  48.3 1.5 %collective-permute-start.10 = (bf16[1,2,32,448]{3,2,1,0:T(8,128)(2,1)S(1)}, bf16[1,2,32,448]{3,2,1,0:T(8,128)(2,1)S(1)}, u32[]{:S(2)}, u32[]{:S(2)}) collective-permute-start(bf16[1,2,32,448]{3,2,1,0:T(8,128)(2,1)S(1)} %bitcast.9), channel_id=1, source_target_pairs={{0,2},{1,3},{2,0},{3,1},{4,6},{5,7},{6,4},{7,5},{8,10},{9,11},{10,... | collective-permute-start | bytes 172040 | tf_op jit(solution)/shard_map/ppermute | solution.py:471
  49.8 1.0 %collective-permute-done.9 = bf16[2,32,448]{2,1,0:T(8,128)(2,1)S(1)} collective-permute-done((bf16[2,32,448]{2,1,0:T(8,128)(2,1)S(1)}, bf16[2,32,448]{2,1,0:T(8,128)(2,1)S(1)}, u32[]{:S(2)}, u32[]{:S(2)}) %collective-permute-start.9) | collective-permute-done | bytes 57376 | tf_op jit(solution)/shard_map/ppermute | solution.py:471
  50.8 1.1 %collective-permute-done.8 = bf16[2,32,448]{2,1,0:T(8,128)(2,1)S(1)} collective-permute-done((bf16[2,32,448]{2,1,0:T(8,128)(2,1)S(1)}, bf16[2,32,448]{2,1,0:T(8,128)(2,1)S(1)}, u32[]{:S(2)}, u32[]{:S(2)}) %collective-permute-start.8) | collective-permute-done | bytes 57376 | tf_op jit(solution)/shard_map/ppermute | solution.py:471
  51.9 0.0 collective-permute-done.7
  52.0 0.6 collective-permute-done.10.refs_0_
  52.6 0.1 collective-permute-start.13
  52.6 1.6 %collective-permute-start.12 = (bf16[3,2,32,448]{3,2,1,0:T(8,128)(2,1)S(1)}, bf16[3,2,32,448]{3,2,1,0:T(8,128)(2,1)S(1)}, u32[]{:S(2)}, u32[]{:S(2)}) collective-permute-start(bf16[3,2,32,448]{3,2,1,0:T(8,128)(2,1)S(1)} %pad_maximum_fusion.1), channel_id=1, source_target_pairs={{0,2},{1,3},{2,0},{3,1},{4,6},{5,7},{6,4},{7,5},{8,10},{9,11},{10,... | collective-permute-start | bytes 516104 | tf_op jit(solution)/shard_map/ppermute | solution.py:471
  54.2 0.0 collective-permute-done.13.refs_1_
  54.2 0.0 copy-done
  54.2 2.8 %early.1.refs_4_ = f32[2,2048,768]{2,1,0:T(8,128)S(1)} custom-call(s32[2]{0:T(128)S(1)} %pad_add_fusion.place_ref, bf16[2,2,2048,256]{3,2,1,0:T(8,128)(2,1)S(1)} %copy-done, bf16[448,768]{1,0:T(8,128)(2,1)S(1)} %get-tuple-element.28.before_ref.shapes_ref, bf16[4,2,32,448]{3,2,1,0:T(8,128)(2,1)S(1)} %pad_maximum_fusion.refs_0_, ...), custom_call_target="tpu_custom_call" | custom-call | flops 1000 | bytes 1000 | tf_op jit(solution)/shard_map/early/pallas_call | solution.py:393
  57.0 2.9 %collective-permute-done.12.refs_2_ = bf16[3,2,32,448]{3,2,1,0:T(8,128)(2,1)S(1)} collective-permute-done((bf16[3,2,32,448]{3,2,1,0:T(8,128)(2,1)S(1)}, bf16[3,2,32,448]{3,2,1,0:T(8,128)(2,1)S(1)}, u32[]{:S(2)}, u32[]{:S(2)}) %collective-permute-start.12) | collective-permute-done | bytes 172064 | tf_op jit(solution)/shard_map/ppermute | solution.py:471
  60.0 0.0 collective-permute-start.14
  60.0 0.5 collective-permute-start.11
  60.5 1.0 %collective-permute-done.11.refs_1_ = bf16[1,2,32,448]{3,2,1,0:T(8,128)(2,1)S(1)} collective-permute-done((bf16[1,2,32,448]{3,2,1,0:T(8,128)(2,1)S(1)}, bf16[1,2,32,448]{3,2,1,0:T(8,128)(2,1)S(1)}, u32[]{:S(2)}, u32[]{:S(2)}) %collective-permute-start.11) | collective-permute-done | bytes 57376 | tf_op jit(solution)/shard_map/ppermute | solution.py:471
  61.5 0.0 collective-permute-done.14.refs_3_
  61.5 4.7 %late.1 = bf16[2,2048,768]{2,1,0:T(8,128)(2,1)} custom-call(s32[2]{0:T(128)S(1)} %pad_add_fusion.place_ref, bf16[2,2,2048,256]{3,2,1,0:T(8,128)(2,1)S(1)} %copy-done, bf16[448,768]{1,0:T(8,128)(2,1)S(1)} %get-tuple-element.28.before_ref.shapes_ref, bf16[1,2,32,448]{3,2,1,0:T(8,128)(2,1)S(1)} %collective-permute-done.10.refs_0_, ...), custom_call_target="tpu_custom_call" | custom-call | flops 1962934272 | bytes 8388608 | tf_op jit(solution)/shard_map/late/pallas_call | solution.py:403
  (2 shorter events, 0.1 us)
Async XLA Ops:
  5.8 2.8 %collective-permute-start = (bf16[2,4,32,448]{3,2,1,0:T(8,128)(2,1)S(1)}, bf16[2,4,32,448]{3,2,1,0:T(8,128)(2,1)S(1)}, u32[]{:S(2)}, u32[]{:S(2)}) collective-permute-start(bf16[2,4,32,448]{3,2,1,0:T(8,128)(2,1)S(1)} %get-tuple-element.33), channel_id=1, source_target_pairs={{0,1},{1,0},{2,3},{3,2},{4,5},{5,4},{6,7},{7,6},{8,9},{9,8},{10,11... | collective-permute-start | bytes 688136 | tf_op jit(solution)/shard_map/ppermute | solution.py:471
  8.7 6.7 %collective-permute-start.1 = (bf16[4,32,448]{2,1,0:T(8,128)(2,1)S(1)}, bf16[4,32,448]{2,1,0:T(8,128)(2,1)S(1)}, u32[]{:S(2)}, u32[]{:S(2)}) collective-permute-start(bf16[4,32,448]{2,1,0:T(8,128)(2,1)S(1)} %get-tuple-element.35.after_ref), channel_id=1, source_target_pairs={{0,2},{1,3},{2,0},{3,1},{4,6},{5,7},{6,4},{7,5},{8,10},{9,11},{10,... | collective-permute-start | bytes 344072 | tf_op jit(solution)/shard_map/ppermute | solution.py:471
  16.6 2.1 %collective-permute-start.2 = (bf16[2,4,32,448]{3,2,1,0:T(8,128)(2,1)S(1)}, bf16[2,4,32,448]{3,2,1,0:T(8,128)(2,1)S(1)}, u32[]{:S(2)}, u32[]{:S(2)}) collective-permute-start(bf16[2,4,32,448]{3,2,1,0:T(8,128)(2,1)S(1)} %get-tuple-element.38.after_ref), channel_id=1, source_target_pairs={{0,1},{1,0},{2,3},{3,2},{4,5},{5,4},{6,7},{7,6},{8,9},{9,8},{10,11... | collective-permute-start | bytes 688136 | tf_op jit(solution)/shard_map/ppermute | solution.py:471
  18.8 6.0 %collective-permute-start.3 = (bf16[4,32,448]{2,1,0:T(8,128)(2,1)S(1)}, bf16[4,32,448]{2,1,0:T(8,128)(2,1)S(1)}, u32[]{:S(2)}, u32[]{:S(2)}) collective-permute-start(bf16[4,32,448]{2,1,0:T(8,128)(2,1)S(1)} %get-tuple-element.39.after_ref), channel_id=1, source_target_pairs={{0,2},{1,3},{2,0},{3,1},{4,6},{5,7},{6,4},{7,5},{8,10},{9,11},{10,... | collective-permute-start | bytes 344072 | tf_op jit(solution)/shard_map/ppermute | solution.py:471
  24.8 8.7 %collective-permute-start.4 = (bf16[2,32,448]{2,1,0:T(8,128)(2,1)S(1)}, bf16[2,32,448]{2,1,0:T(8,128)(2,1)S(1)}, u32[]{:S(2)}, u32[]{:S(2)}) collective-permute-start(bf16[2,32,448]{2,1,0:T(8,128)(2,1)S(1)} %get-tuple-element.43), channel_id=1, source_target_pairs={{0,4},{1,5},{2,6},{3,7},{4,0},{5,1},{6,2},{7,3},{8,12},{9,13},{10,... | collective-permute-start | bytes 172040 | tf_op jit(solution)/shard_map/ppermute | solution.py:471
  26.7 7.1 %collective-permute-start.5 = (bf16[2,32,448]{2,1,0:T(8,128)(2,1)S(1)}, bf16[2,32,448]{2,1,0:T(8,128)(2,1)S(1)}, u32[]{:S(2)}, u32[]{:S(2)}) collective-permute-start(bf16[2,32,448]{2,1,0:T(8,128)(2,1)S(1)} %get-tuple-element.44), channel_id=1, source_target_pairs={{0,8},{1,9},{2,10},{3,11},{4,12},{5,13},{6,14},{7,15},{8,0},{9,1},... | collective-permute-start | bytes 172040 | tf_op jit(solution)/shard_map/ppermute | solution.py:471
  29.3 6.1 %collective-permute-start.6 = (bf16[2,32,448]{2,1,0:T(8,128)(2,1)S(1)}, bf16[2,32,448]{2,1,0:T(8,128)(2,1)S(1)}, u32[]{:S(2)}, u32[]{:S(2)}) collective-permute-start(bf16[2,32,448]{2,1,0:T(8,128)(2,1)S(1)} %get-tuple-element.45), channel_id=1, source_target_pairs={{0,12},{1,13},{2,14},{3,15},{4,8},{5,9},{6,10},{7,11},{8,4},{9,5},... | collective-permute-start | bytes 172040 | tf_op jit(solution)/shard_map/ppermute | solution.py:471
  35.4 18.9 %copy-start = (bf16[2,2,2048,256]{3,2,1,0:T(8,128)(2,1)S(1)}, bf16[2,2,2048,256]{3,2,1,0:T(8,128)(2,1)}, u32[]{:S(2)}) copy-start(bf16[2,2,2048,256]{3,2,1,0:T(8,128)(2,1)} %constant.33.clone.table_ref) | copy-start | bytes 12582916
  43.8 7.0 %collective-permute-start.9 = (bf16[2,32,448]{2,1,0:T(8,128)(2,1)S(1)}, bf16[2,32,448]{2,1,0:T(8,128)(2,1)S(1)}, u32[]{:S(2)}, u32[]{:S(2)}) collective-permute-start(bf16[2,32,448]{2,1,0:T(8,128)(2,1)S(1)} %respond.1), channel_id=1, source_target_pairs={{0,12},{1,13},{2,14},{3,15},{4,8},{5,9},{6,10},{7,11},{8,4},{9,5},... | collective-permute-start | bytes 172040 | tf_op jit(solution)/shard_map/ppermute | solution.py:471
  45.9 6.0 %collective-permute-start.8 = (bf16[2,32,448]{2,1,0:T(8,128)(2,1)S(1)}, bf16[2,32,448]{2,1,0:T(8,128)(2,1)S(1)}, u32[]{:S(2)}, u32[]{:S(2)}) collective-permute-start(bf16[2,32,448]{2,1,0:T(8,128)(2,1)S(1)} %respond.1), channel_id=1, source_target_pairs={{0,8},{1,9},{2,10},{3,11},{4,12},{5,13},{6,14},{7,15},{8,0},{9,1},... | collective-permute-start | bytes 172040 | tf_op jit(solution)/shard_map/ppermute | solution.py:471
  45.9 6.0 %collective-permute-start.7 = (bf16[2,32,448]{2,1,0:T(8,128)(2,1)S(1)}, bf16[2,32,448]{2,1,0:T(8,128)(2,1)S(1)}, u32[]{:S(2)}, u32[]{:S(2)}) collective-permute-start(bf16[2,32,448]{2,1,0:T(8,128)(2,1)S(1)} %respond.1), channel_id=1, source_target_pairs={{0,4},{1,5},{2,6},{3,7},{4,0},{5,1},{6,2},{7,3},{8,12},{9,13},{10,... | collective-permute-start | bytes 172040 | tf_op jit(solution)/shard_map/ppermute | solution.py:471
  48.3 4.3 %collective-permute-start.10 = (bf16[1,2,32,448]{3,2,1,0:T(8,128)(2,1)S(1)}, bf16[1,2,32,448]{3,2,1,0:T(8,128)(2,1)S(1)}, u32[]{:S(2)}, u32[]{:S(2)}) collective-permute-start(bf16[1,2,32,448]{3,2,1,0:T(8,128)(2,1)S(1)} %bitcast.9), channel_id=1, source_target_pairs={{0,2},{1,3},{2,0},{3,1},{4,6},{5,7},{6,4},{7,5},{8,10},{9,11},{10,... | collective-permute-start | bytes 172040 | tf_op jit(solution)/shard_map/ppermute | solution.py:471
  52.6 1.7 %collective-permute-start.13 = (bf16[4,2,32,448]{3,2,1,0:T(8,128)(2,1)S(1)}, bf16[4,2,32,448]{3,2,1,0:T(8,128)(2,1)S(1)}, u32[]{:S(2)}, u32[]{:S(2)}) collective-permute-start(bf16[4,2,32,448]{3,2,1,0:T(8,128)(2,1)S(1)} %pad_maximum_fusion.refs_0_), channel_id=1, source_target_pairs={{0,1},{1,0},{2,3},{3,2},{4,5},{5,4},{6,7},{7,6},{8,9},{9,8},{10,11... | collective-permute-start | bytes 688136 | tf_op jit(solution)/shard_map/ppermute | solution.py:471
  52.6 7.3 %collective-permute-start.12 = (bf16[3,2,32,448]{3,2,1,0:T(8,128)(2,1)S(1)}, bf16[3,2,32,448]{3,2,1,0:T(8,128)(2,1)S(1)}, u32[]{:S(2)}, u32[]{:S(2)}) collective-permute-start(bf16[3,2,32,448]{3,2,1,0:T(8,128)(2,1)S(1)} %pad_maximum_fusion.1), channel_id=1, source_target_pairs={{0,2},{1,3},{2,0},{3,1},{4,6},{5,7},{6,4},{7,5},{8,10},{9,11},{10,... | collective-permute-start | bytes 516104 | tf_op jit(solution)/shard_map/ppermute | solution.py:471
  60.0 1.5 %collective-permute-start.14 = (bf16[3,2,32,448]{3,2,1,0:T(8,128)(2,1)S(1)}, bf16[3,2,32,448]{3,2,1,0:T(8,128)(2,1)S(1)}, u32[]{:S(2)}, u32[]{:S(2)}) collective-permute-start(bf16[3,2,32,448]{3,2,1,0:T(8,128)(2,1)S(1)} %collective-permute-done.12.refs_2_), channel_id=1, source_target_pairs={{0,1},{1,0},{2,3},{3,2},{4,5},{5,4},{6,7},{7,6},{8,9},{9,8},{10,11... | collective-permute-start | bytes 516104 | tf_op jit(solution)/shard_map/ppermute | solution.py:471
  60.0 1.5 %collective-permute-start.11 = (bf16[1,2,32,448]{3,2,1,0:T(8,128)(2,1)S(1)}, bf16[1,2,32,448]{3,2,1,0:T(8,128)(2,1)S(1)}, u32[]{:S(2)}, u32[]{:S(2)}) collective-permute-start(bf16[1,2,32,448]{3,2,1,0:T(8,128)(2,1)S(1)} %collective-permute-done.10.refs_0_), channel_id=1, source_target_pairs={{0,1},{1,0},{2,3},{3,2},{4,5},{5,4},{6,7},{7,6},{8,9},{9,8},{10,11... | collective-permute-start | bytes 172040 | tf_op jit(solution)/shard_map/ppermute | solution.py:471

commit v8 on v5

--- a/solution.py
+++ b/solution.py
@@ -11,6 +11,7 @@
 
 FREQS = 512
 CORES = 2
+CHUNK = 512
 MIB = 1 << 20
 
 
@@ -41,9 +42,8 @@
 
 def chunk_list(half):
     unit = half // 8
-    sizes = (unit, unit, 2 * unit, 4 * unit)
-    starts = (0, unit, 2 * unit, 4 * unit)
-    return tuple(zip(starts, sizes))
+    sizes = (unit, unit, 2 * unit, 2 * unit, 2 * unit)
+    return tuple((sum(sizes[:n]), size) for n, size in enumerate(sizes))
 
 
 def split_cores(place_ref, spec, shapes_ref, parity, keep_ref, send_ref):
@@ -59,7 +59,10 @@
     send = jnp.where(first, spec[1], spec[0]).astype(jnp.bfloat16)
     for k in range(zs):
         keep_ref[z ^ k, parity] = keep[k]
-        send_ref[z ^ k, parity] = send[k]
+        if len(send_ref.shape) == 3:
+            send_ref[z ^ k] = send[k]
+        else:
+            send_ref[z ^ k, parity] = send[k]
 
 
 def across_kernel(
@@ -149,34 +152,50 @@
 
 
 def within_kernel(
-    parity, start, place_ref, table_ref, folded_ref, shapes_ref, frf_ref, after_ref,
-    keep_ref, send_ref, held_ref, sem,
+    place_ref, table_ref, folded_ref, shapes_ref, frf_ref, after_ref,
+    keep_ref, send0_ref, send1_ref, held_ref, acc_ref, sem,
 ):
-    copies = load_copies(start, frf_ref, held_ref, sem)
+    copies = load_copies(0, frf_ref, held_ref, sem)
     for copy in copies:
         copy.start()
-    spec = jnp.dot(table_ref[parity], folded_ref[parity], preferred_element_type=jnp.float32)
-    split_cores(place_ref, spec, shapes_ref, 0, keep_ref, send_ref)
+    for parity in range(2):
+        for first in range(0, folded_ref.shape[1], CHUNK):
+            part = slice(first, first + CHUNK)
+            product = jnp.dot(
+                table_ref[parity, :, part],
+                folded_ref[parity, part],
+                preferred_element_type=jnp.float32,
+            )
+            if first == 0:
+                acc_ref[parity] = product
+            else:
+                acc_ref[parity] += product
+    for parity, send_ref in enumerate((send0_ref, send1_ref)):
+        split_cores(place_ref, acc_ref[parity], shapes_ref, parity, keep_ref, send_ref)
     for copy in copies:
         copy.wait()
 
 
-def within(parity, place, table, folded, shapes_t, frf, start, held, after, zs):
+def within(place, table, folded, shapes_t, frf, held, after, zs):
     _, half, dofs = folded.shape
     modes = shapes_t.shape[0]
     rows = FREQS // (2 * CORES * zs)
-    out = jax.ShapeDtypeStruct((zs, 1, rows, modes), jnp.bfloat16)
+    out = jax.ShapeDtypeStruct((zs, 2, rows, modes), jnp.bfloat16)
+    send = jax.ShapeDtypeStruct((zs, rows, modes), jnp.bfloat16)
     vmem, hbm = pl.BlockSpec(memory_space=pltpu.VMEM), pl.BlockSpec(memory_space=pltpu.HBM)
     return pl.pallas_call(
-        functools.partial(within_kernel, parity, start),
+        within_kernel,
         in_specs=[pl.BlockSpec(memory_space=pltpu.SMEM), vmem, vmem, vmem, hbm]
         + [pl.BlockSpec(memory_space=pl.ANY)],
-        out_specs=[vmem] * 3,
-        out_shape=[out, out, pltpu.VMEM((held,) + frf.shape[1:], jnp.bfloat16)],
-        scratch_shapes=[pltpu.SemaphoreType.DMA((math.gcd(held, 4),))],
-        compiler_params=pltpu.CompilerParams(vmem_limit_bytes=8 * MIB),
+        out_specs=[vmem] * 4,
+        out_shape=[out, send, send, pltpu.VMEM((held,) + frf.shape[1:], jnp.bfloat16)],
+        scratch_shapes=[
+            pltpu.VMEM((2, FREQS // 2, dofs), jnp.float32),
+            pltpu.SemaphoreType.DMA((math.gcd(held, 4),)),
+        ],
+        compiler_params=pltpu.CompilerParams(vmem_limit_bytes=10 * MIB),
         cost_estimate=pl.CostEstimate(
-            flops=FREQS * dofs * (half + modes), bytes_accessed=8 * MIB, transcendentals=0
+            flops=2 * FREQS * dofs * (half + modes), bytes_accessed=12 * MIB, transcendentals=0
         ),
         name="within",
     )(place, table, folded, shapes_t, in_hbm(frf), after)
@@ -207,7 +226,7 @@
         copy.wait()
 
 
-def load(frf, start, size, after):
+def load(frf, start, size, after, weight=4):
     hbm, anywhere = pl.BlockSpec(memory_space=pltpu.HBM), pl.BlockSpec(memory_space=pl.ANY)
     return pl.pallas_call(
         functools.partial(load_kernel, start),
@@ -217,17 +236,21 @@
         scratch_shapes=[pltpu.SemaphoreType.DMA((math.gcd(size, 4),))],
         compiler_params=pltpu.CompilerParams(vmem_limit_bytes=2 * MIB),
         cost_estimate=pl.CostEstimate(
-            flops=0, bytes_accessed=4 * size * math.prod(frf.shape[1:]), transcendentals=0
+            flops=0, bytes_accessed=weight * size * math.prod(frf.shape[1:]), transcendentals=0
         ),
         name="load",
     )(in_hbm(frf), after)
 
 
 def respond_kernel(count, *refs):
-    pieces, parts = refs[:count], refs[count:-4]
-    out_ref, direct_ref, turned_ref, result_ref = refs[-4:]
+    pieces, parts = refs[:count], refs[count:-7]
+    frf_ref, out_ref, direct_ref, turned_ref, result_ref, rest_ref, sem = refs[-7:]
+    held = sum(part.shape[0] for part in parts)
+    copies = load_copies(held, frf_ref, rest_ref, sem)
+    for copy in copies:
+        copy.start()
     _, rows, modes = out_ref.shape
-    total = sum(piece[0].astype(jnp.float32) for piece in pieces).reshape(2 * rows, modes)
+    total = sum(piece[...].astype(jnp.float32) for piece in pieces).reshape(2 * rows, modes)
     total = total.astype(jnp.bfloat16).astype(jnp.float32)
     row = lax.broadcasted_iota(jnp.int32, total.shape, 0)
     turned = jnp.where(row % 2 == 0, -jnp.roll(total, -1, axis=0), jnp.roll(total, 1, axis=0))
@@ -241,24 +264,35 @@
         at = place(f)
         direct_ref[f, 0:2] = total[at : at + 2]
         turned_ref[f, 0:2] = turned[at : at + 2]
+
+    def multiply(matrix_ref, step, f):
+        products = [
+            lax.dot_general(
+                ref[f].astype(jnp.bfloat16),
+                matrix_ref[step, which],
+                (((1,), (1,)), ((), ())),
+                preferred_element_type=jnp.float32,
+            )
+            for which, ref in enumerate((direct_ref, turned_ref))
+        ]
+        result_ref[f] = products[0] + products[1]
+
     base = 0
     for part in parts:
 
         @pl.loop(0, part.shape[0], unroll=math.gcd(4, part.shape[0]))
         def _(step, part=part, base=base):
-            f = base + step
-            products = [
-                lax.dot_general(
-                    ref[f].astype(jnp.bfloat16),
-                    part[step, which],
-                    (((1,), (1,)), ((), ())),
-                    preferred_element_type=jnp.float32,
-                )
-                for which, ref in enumerate((direct_ref, turned_ref))
-            ]
-            result_ref[f] = products[0] + products[1]
+            multiply(part, step, base + step)
 
         base += part.shape[0]
+
+    each = rest_ref.shape[0] // len(copies)
+    for n, copy in enumerate(copies):
+        copy.wait()
+
+        @pl.loop(n * each, (n + 1) * each, unroll=each)
+        def _(step):
+            multiply(rest_ref, step, held + step)
 
     for f in range(rows):
         at = place(f)
@@ -268,20 +302,26 @@
     )
 
 
-def respond(pieces, parts):
-    rows, modes = pieces[0].shape[2:]
-    vmem = pl.BlockSpec(memory_space=pltpu.VMEM)
-    size = sum(part.size for part in parts)
+def respond(pieces, parts, frf):
+    rows, modes = pieces[0].shape[1:]
+    vmem, hbm = pl.BlockSpec(memory_space=pltpu.VMEM), pl.BlockSpec(memory_space=pltpu.HBM)
+    rest = frf.shape[0] - sum(part.shape[0] for part in parts)
     return pl.pallas_call(
         functools.partial(respond_kernel, len(pieces)),
-        in_specs=[vmem] * (len(pieces) + len(parts)),
+        in_specs=[vmem] * (len(pieces) + len(parts)) + [hbm],
         out_specs=vmem,
         out_shape=jax.ShapeDtypeStruct((2, rows, modes), jnp.bfloat16),
-        scratch_shapes=[pltpu.VMEM((rows, 8, modes), jnp.float32)] * 3,
-        compiler_params=pltpu.CompilerParams(vmem_limit_bytes=12 * MIB),
-        cost_estimate=pl.CostEstimate(flops=4 * size, bytes_accessed=2 * size, transcendentals=0),
+        scratch_shapes=[pltpu.VMEM((rows, 8, modes), jnp.float32)] * 3
+        + [
+            pltpu.VMEM((rest,) + frf.shape[1:], jnp.bfloat16),
+            pltpu.SemaphoreType.DMA((rest // math.gcd(rest, 4),)),
+        ],
+        compiler_params=pltpu.CompilerParams(vmem_limit_bytes=36 * MIB),
+        cost_estimate=pl.CostEstimate(
+            flops=4 * frf.size, bytes_accessed=2 * frf.size, transcendentals=0
+        ),
         name="respond",
-    )(*pieces, *parts)
+    )(*pieces, *parts, in_hbm(frf))
 
 
 def project(place_ref, shards, shapes_ref, order_ref, moved_ref):
@@ -406,30 +446,28 @@
     )(ours, came)
 
 
-def gather_sum_kernel(came_ref, after_ref, *refs):
-    within_refs, out_refs = refs[:4], refs[4:]
+def gather_sum_kernel(came_ref, keep_ref, twin0_ref, twin1_ref, after_ref, *out_refs):
     for k, out_ref in enumerate(out_refs):
-        for parity in range(2):
-            keep_ref, twin_ref = within_refs[2 * parity : 2 * parity + 2]
-            total = keep_ref[k, 0].astype(jnp.float32) + twin_ref[k, 0].astype(jnp.float32)
+        for parity, twin_ref in enumerate((twin0_ref, twin1_ref)):
+            total = keep_ref[k, parity].astype(jnp.float32) + twin_ref[k].astype(jnp.float32)
             total = total + came_ref[k, parity].astype(jnp.float32)
-            out_ref[0, parity] = total.astype(jnp.bfloat16)
-
-
-def gather_sum(came, kept, after):
+            out_ref[parity] = total.astype(jnp.bfloat16)
+
+
+def gather_sum(came, keep, twin0, twin1, after):
     vmem = pl.BlockSpec(memory_space=pltpu.VMEM)
     zs = came.shape[0]
     return pl.pallas_call(
         gather_sum_kernel,
-        in_specs=[vmem, pl.BlockSpec(memory_space=pl.ANY)] + [vmem] * 4,
+        in_specs=[vmem] * 4 + [pl.BlockSpec(memory_space=pl.ANY)],
         out_specs=[vmem] * zs,
-        out_shape=[jax.ShapeDtypeStruct((1,) + came.shape[1:], jnp.bfloat16)] * zs,
+        out_shape=[jax.ShapeDtypeStruct(came.shape[1:], jnp.bfloat16)] * zs,
         compiler_params=pltpu.CompilerParams(vmem_limit_bytes=8 * MIB),
         cost_estimate=pl.CostEstimate(
             flops=2 * came.size, bytes_accessed=8 * came.size, transcendentals=0
         ),
         name="gather_sum",
-    )(came, after, *kept)
+    )(came, keep, twin0, twin1, after)
 
 
 def on_device(devices, forces, mode_shapes, frf):
@@ -448,20 +486,17 @@
     fwd = jnp.asarray(forward_tables(steps, chips).astype(jnp.bfloat16))
     inv = jnp.asarray(inverse_tables(steps, chips).astype(jnp.bfloat16))
 
-    unit = frf.shape[0] // 8
     keep, send, folded, rest, shapes_v = across(
         place, fwd, forces.reshape(2, half, dofs), shapes_t, zs
     )
-    given = (place, rest, folded, shapes_v, frf)
-    keep0, send0, part0 = within(0, *given, 0, unit, send, zs)
     pair = add(keep, swap(send, 1))
     came = swap(pair, 2)
-    keep1, send1, part1 = within(1, *given, unit, unit, pair, zs)
-    part2 = load(frf, 2 * unit, 3 * unit, send1)
-    pieces = gather_sum(came, (keep0, swap(send0, 1), keep1, swap(send1, 1)), part2)
-    part3 = load(frf, 5 * unit, 3 * unit, pieces[0])
+    unit = frf.shape[0] // 8
+    keep, send0, send1, part0 = within(place, rest, folded, shapes_v, frf, 2 * unit, pair, zs)
+    part1 = load(frf, 2 * unit, unit, send1)
+    pieces = gather_sum(came, keep, swap(send0, 1), swap(send1, 1), part1)
     pieces = [pieces[0]] + [swap(pieces[k], 4 * k) for k in range(1, zs)]
-    response = respond(pieces, (part0, part1, part2, part3))
+    response = respond(pieces, (part0, part1), frf)
 
     over = swap(response[None], 2)
     shards = [swap(response, 4 * k) for k in range(1, zs)]

time: 64.3 us -> 60.3 us (0.938)
  Pallas kernels: 37.7 us -> 29.3 us
  waiting for transfers between devices: 11.5 us -> 15.8 us
    pallas_call x2 -> x1, Pallas kernels: 8.49 us -> 2.04 us  [load(): pl.pallas_call(functools.partial(load_kernel, start), in_specs=[hbm, anyw...]
    ppermute x15, waiting for transfers between devices: 11.5 us -> 15.8 us  [swap(): return lax.ppermute(values, 'dof', pairs)]
    pallas_call x3 -> x2, Pallas kernels: 7.63 us -> 5.78 us  [the longest x1 5.67 us: within(): pl.pallas_call(within_kernel, in_specs=[pl.BlockSpec(memory_space=pltpu.S...]
  transfers between devices with their start and end apart: 15 -> 15, of which waited for: 9 -> 9; matrix products, arithmetic and copies ran while one was open for 0% -> 0% of each run, Pallas kernels for 29% -> 17%
where the time goes in v8:
time: 60.3 us; the launch traced here: 60.2 us
  Pallas kernels  29.3 us (49%)
  waiting for transfers between devices  15.8 us (26%)
  starting transfers between devices  14.6 us (24%)
    ppermute x15, waiting for transfers between devices, swap(): return lax.ppermute(values, 'dof', pairs)  15.8 us
    ppermute x15, starting transfers between devices, swap(): return lax.ppermute(values, 'dof', pairs)  14.6 us
    pallas_call x1, Pallas kernels, respond(): pl.pallas_call(functools.partial(respond_kernel, len(pieces)), in_specs=[...  8.92 us
    pallas_call x1, Pallas kernels, within(): pl.pallas_call(within_kernel, in_specs=[pl.BlockSpec(memory_space=pltpu.S...  5.67 us
    pallas_call x1, Pallas kernels, across(): pl.pallas_call(across_kernel, in_specs=[pl.BlockSpec(memory_space=pltpu.S...  5.24 us
    pallas_call x1, Pallas kernels, inverse(): pl.pallas_call(late_kernel, in_specs=in_specs + [vmem], out_specs=pl.Bloc...  4.51 us
    pallas_call x1, Pallas kernels, inverse(): pl.pallas_call(early_kernel, in_specs=in_specs, out_specs=vmem, out_shape...  2.8 us
    pallas_call x1, Pallas kernels, load(): pl.pallas_call(functools.partial(load_kernel, start), in_specs=[hbm, anyw...  2.04 us
  transfers between devices with their start and end apart: 15, of which 9 were waited for; matrix products, arithmetic and copies ran while one was open for 0% of the time, Pallas kernels for 17%

profile of v8, /device:TPU:0, one launch (start us, length us, event | category | flops | bytes accessed | tf_op | source)
XLA Modules:
  0.0 60.2 jit_solution(15349244631912166044)
XLA Ops:
  0.0 0.1 pad_add_fusion.place_ref
  0.1 5.2 %across.1 = (bf16[4,2,32,448]{3,2,1,0:T(8,128)(2,1)S(1)}, bf16[4,2,32,448]{3,2,1,0:T(8,128)(2,1)S(1)}, bf16[2,2048,768]{2,1,0:T(8,128)(2,1)S(1)}, bf16[2,256,2048]{2,1,0:T(8,128)(2,1)S(1)}, bf16[448,768]{1,0:T(8,128)(2,1)S(1)}) custom-call(s32[2]{0:T(128)S(1)} %pad_add_fusion.place_ref, bf16[2,2,256,2048]{3,2,1,0:T(8,128)(2,1)} %constant.32.clone.table_ref, ...), custom_call_target="tpu_custom_call" | custom-call | flops 1962934272 | bytes 12582912 | tf_op jit(solution)/shard_map/across/pallas_call | solution.py:126
  5.3 0.5 collective-permute-start
  5.8 1.2 %collective-permute-done.came_ref = bf16[4,2,32,448]{3,2,1,0:T(8,128)(2,1)S(1)} collective-permute-done((bf16[4,2,32,448]{3,2,1,0:T(8,128)(2,1)S(1)}, bf16[4,2,32,448]{3,2,1,0:T(8,128)(2,1)S(1)}, u32[]{:S(2)}, u32[]{:S(2)}) %collective-permute-start) | collective-permute-done | bytes 229408 | tf_op jit(solution)/shard_map/ppermute | solution.py:481
  7.0 0.1 add.9.after_ref
  7.1 3.0 %collective-permute-start.1 = (bf16[4,2,32,448]{3,2,1,0:T(8,128)(2,1)S(1)}, bf16[4,2,32,448]{3,2,1,0:T(8,128)(2,1)S(1)}, u32[]{:S(2)}, u32[]{:S(2)}) collective-permute-start(bf16[4,2,32,448]{3,2,1,0:T(8,128)(2,1)S(1)} %add.9.after_ref), channel_id=1, source_target_pairs={{0,2},{1,3},{2,0},{3,1},{4,6},{5,7},{6,4},{7,5},{8,10},{9,11},{10,... | collective-permute-start | bytes 688136 | tf_op jit(solution)/shard_map/ppermute | solution.py:481
  10.0 5.7 %within.1 = (bf16[4,2,32,448]{3,2,1,0:T(8,128)(2,1)S(1)}, bf16[4,32,448]{2,1,0:T(8,128)(2,1)S(1)}, bf16[4,32,448]{2,1,0:T(8,128)(2,1)S(1)}, bf16[8,2,448,448]{3,2,1,0:T(8,128)(2,1)S(1)}) custom-call(s32[2]{0:T(128)S(1)} %pad_add_fusion.place_ref, bf16[2,256,2048]{2,1,0:T(8,128)(2,1)S(1)} %get-tuple-element.25.table_ref, ...), custom_call_target="tpu_custom_call" | custom-call | flops 1962934272 | bytes 12582912 | tf_op jit(solution)/shard_map/within/pallas_call | solution.py:186
  15.7 0.1 collective-permute-start.2
  15.8 0.5 collective-permute-start.3
  16.3 2.0 %load.1.after_ref.refs_5_ = bf16[4,2,448,448]{3,2,1,0:T(8,128)(2,1)S(1)} custom-call(bf16[32,2,448,448]{3,2,1,0:T(8,128)(2,1)} %refs_6_.1, bf16[4,32,448]{2,1,0:T(8,128)(2,1)S(1)} %get-tuple-element.29.after_ref), custom_call_target="tpu_custom_call" | custom-call | bytes 6422528 | tf_op jit(solution)/shard_map/load/pallas_call | solution.py:231
  18.3 0.0 collective-permute-done.2.twin0_ref
  18.3 0.0 collective-permute-done.3.twin1_ref
  18.3 0.0 collective-permute-done.1.came_ref
  18.4 0.1 gather_sum.1
  18.5 1.6 %collective-permute-start.4 = (bf16[2,32,448]{2,1,0:T(8,128)(2,1)S(1)}, bf16[2,32,448]{2,1,0:T(8,128)(2,1)S(1)}, u32[]{:S(2)}, u32[]{:S(2)}) collective-permute-start(bf16[2,32,448]{2,1,0:T(8,128)(2,1)S(1)} %get-tuple-element.31), channel_id=1, source_target_pairs={{0,4},{1,5},{2,6},{3,7},{4,0},{5,1},{6,2},{7,3},{8,12},{9,13},{10,... | collective-permute-start | bytes 172040 | tf_op jit(solution)/shard_map/ppermute | solution.py:481
  20.1 2.6 %collective-permute-start.5 = (bf16[2,32,448]{2,1,0:T(8,128)(2,1)S(1)}, bf16[2,32,448]{2,1,0:T(8,128)(2,1)S(1)}, u32[]{:S(2)}, u32[]{:S(2)}) collective-permute-start(bf16[2,32,448]{2,1,0:T(8,128)(2,1)S(1)} %get-tuple-element.32), channel_id=1, source_target_pairs={{0,8},{1,9},{2,10},{3,11},{4,12},{5,13},{6,14},{7,15},{8,0},{9,1},... | collective-permute-start | bytes 172040 | tf_op jit(solution)/shard_map/ppermute | solution.py:481
  22.7 0.2 collective-permute-start.6
  22.9 0.0 collective-permute-done.4.refs_1_
  22.9 4.7 %collective-permute-done.5.refs_2_ = bf16[2,32,448]{2,1,0:T(8,128)(2,1)S(1)} collective-permute-done((bf16[2,32,448]{2,1,0:T(8,128)(2,1)S(1)}, bf16[2,32,448]{2,1,0:T(8,128)(2,1)S(1)}, u32[]{:S(2)}, u32[]{:S(2)}) %collective-permute-start.5) | collective-permute-done | bytes 57376 | tf_op jit(solution)/shard_map/ppermute | solution.py:481
  27.6 1.3 %collective-permute-done.6.refs_3_ = bf16[2,32,448]{2,1,0:T(8,128)(2,1)S(1)} collective-permute-done((bf16[2,32,448]{2,1,0:T(8,128)(2,1)S(1)}, bf16[2,32,448]{2,1,0:T(8,128)(2,1)S(1)}, u32[]{:S(2)}, u32[]{:S(2)}) %collective-permute-start.6) | collective-permute-done | bytes 57376 | tf_op jit(solution)/shard_map/ppermute | solution.py:481
  28.9 0.0 copy-start
  28.9 8.9 %respond.1 = bf16[2,32,448]{2,1,0:T(8,128)(2,1)S(1)} custom-call(bf16[2,32,448]{2,1,0:T(8,128)(2,1)S(1)} %get-tuple-element.30.refs_0_, bf16[2,32,448]{2,1,0:T(8,128)(2,1)S(1)} %collective-permute-done.4.refs_1_, bf16[2,32,448]{2,1,0:T(8,128)(2,1)S(1)} %collective-permute-done.5.refs_2_, bf16[2,32,448]{2,1,0:T(8,128)(2,1)S(1)} %collective-permute-done.6.refs_3_, ...), custom_call_target="tpu_custom_call" | custom-call | flops 51380224 | bytes 25690112 | tf_op jit(solution)/shard_map/respond/pallas_call | solution.py:309
  37.8 2.0 %collective-permute-start.9 = (bf16[2,32,448]{2,1,0:T(8,128)(2,1)S(1)}, bf16[2,32,448]{2,1,0:T(8,128)(2,1)S(1)}, u32[]{:S(2)}, u32[]{:S(2)}) collective-permute-start(bf16[2,32,448]{2,1,0:T(8,128)(2,1)S(1)} %respond.1), channel_id=1, source_target_pairs={{0,12},{1,13},{2,14},{3,15},{4,8},{5,9},{6,10},{7,11},{8,4},{9,5},... | collective-permute-start | bytes 172040 | tf_op jit(solution)/shard_map/ppermute | solution.py:481
  39.8 0.3 collective-permute-start.8
  40.1 2.2 %collective-permute-start.7 = (bf16[2,32,448]{2,1,0:T(8,128)(2,1)S(1)}, bf16[2,32,448]{2,1,0:T(8,128)(2,1)S(1)}, u32[]{:S(2)}, u32[]{:S(2)}) collective-permute-start(bf16[2,32,448]{2,1,0:T(8,128)(2,1)S(1)} %respond.1), channel_id=1, source_target_pairs={{0,4},{1,5},{2,6},{3,7},{4,0},{5,1},{6,2},{7,3},{8,12},{9,13},{10,... | collective-permute-start | bytes 172040 | tf_op jit(solution)/shard_map/ppermute | solution.py:481
  42.3 0.5 collective-permute-start.10
  42.8 1.3 %collective-permute-done.9 = bf16[2,32,448]{2,1,0:T(8,128)(2,1)S(1)} collective-permute-done((bf16[2,32,448]{2,1,0:T(8,128)(2,1)S(1)}, bf16[2,32,448]{2,1,0:T(8,128)(2,1)S(1)}, u32[]{:S(2)}, u32[]{:S(2)}) %collective-permute-start.9) | collective-permute-done | bytes 57376 | tf_op jit(solution)/shard_map/ppermute | solution.py:481
  44.1 1.5 %collective-permute-done.8 = bf16[2,32,448]{2,1,0:T(8,128)(2,1)S(1)} collective-permute-done((bf16[2,32,448]{2,1,0:T(8,128)(2,1)S(1)}, bf16[2,32,448]{2,1,0:T(8,128)(2,1)S(1)}, u32[]{:S(2)}, u32[]{:S(2)}) %collective-permute-start.8) | collective-permute-done | bytes 57376 | tf_op jit(solution)/shard_map/ppermute | solution.py:481
  45.5 0.0 collective-permute-done.7
  45.6 0.9 %collective-permute-done.10.refs_0_ = bf16[1,2,32,448]{3,2,1,0:T(8,128)(2,1)S(1)} collective-permute-done((bf16[1,2,32,448]{3,2,1,0:T(8,128)(2,1)S(1)}, bf16[1,2,32,448]{3,2,1,0:T(8,128)(2,1)S(1)}, u32[]{:S(2)}, u32[]{:S(2)}) %collective-permute-start.10) | collective-permute-done | bytes 57376 | tf_op jit(solution)/shard_map/ppermute | solution.py:481
  46.6 0.1 collective-permute-start.13
  46.6 0.6 collective-permute-start.12
  47.2 1.0 %collective-permute-done.13.refs_1_ = bf16[4,2,32,448]{3,2,1,0:T(8,128)(2,1)S(1)} collective-permute-done((bf16[4,2,32,448]{3,2,1,0:T(8,128)(2,1)S(1)}, bf16[4,2,32,448]{3,2,1,0:T(8,128)(2,1)S(1)}, u32[]{:S(2)}, u32[]{:S(2)}) %collective-permute-start.13) | collective-permute-done | bytes 229408 | tf_op jit(solution)/shard_map/ppermute | solution.py:481
  48.2 0.0 copy-done
  48.2 2.8 %early.1.refs_4_ = f32[2,2048,768]{2,1,0:T(8,128)S(1)} custom-call(s32[2]{0:T(128)S(1)} %pad_add_fusion.place_ref, bf16[2,2,2048,256]{3,2,1,0:T(8,128)(2,1)S(1)} %copy-done, bf16[448,768]{1,0:T(8,128)(2,1)S(1)} %get-tuple-element.22.shapes_ref, bf16[4,2,32,448]{3,2,1,0:T(8,128)(2,1)S(1)} %pad_maximum_fusion.refs_0_, ...), custom_call_target="tpu_custom_call" | custom-call | flops 1000 | bytes 1000 | tf_op jit(solution)/shard_map/early/pallas_call | solution.py:406
  51.0 3.0 %collective-permute-done.12.refs_2_ = bf16[3,2,32,448]{3,2,1,0:T(8,128)(2,1)S(1)} collective-permute-done((bf16[3,2,32,448]{3,2,1,0:T(8,128)(2,1)S(1)}, bf16[3,2,32,448]{3,2,1,0:T(8,128)(2,1)S(1)}, u32[]{:S(2)}, u32[]{:S(2)}) %collective-permute-start.12) | collective-permute-done | bytes 172064 | tf_op jit(solution)/shard_map/ppermute | solution.py:481
  54.0 0.0 collective-permute-start.14
  54.0 0.5 collective-permute-start.11
  54.5 1.0 %collective-permute-done.11.refs_1_ = bf16[1,2,32,448]{3,2,1,0:T(8,128)(2,1)S(1)} collective-permute-done((bf16[1,2,32,448]{3,2,1,0:T(8,128)(2,1)S(1)}, bf16[1,2,32,448]{3,2,1,0:T(8,128)(2,1)S(1)}, u32[]{:S(2)}, u32[]{:S(2)}) %collective-permute-start.11) | collective-permute-done | bytes 57376 | tf_op jit(solution)/shard_map/ppermute | solution.py:481
  55.5 0.0 collective-permute-done.14.refs_3_
  55.5 4.5 %late.1 = bf16[2,2048,768]{2,1,0:T(8,128)(2,1)} custom-call(s32[2]{0:T(128)S(1)} %pad_add_fusion.place_ref, bf16[2,2,2048,256]{3,2,1,0:T(8,128)(2,1)S(1)} %copy-done, bf16[448,768]{1,0:T(8,128)(2,1)S(1)} %get-tuple-element.22.shapes_ref, bf16[1,2,32,448]{3,2,1,0:T(8,128)(2,1)S(1)} %collective-permute-done.10.refs_0_, ...), custom_call_target="tpu_custom_call" | custom-call | flops 1962934272 | bytes 8388608 | tf_op jit(solution)/shard_map/late/pallas_call | solution.py:416
  (2 shorter events, 0.1 us)
Async XLA Ops:
  5.3 1.7 %collective-permute-start = (bf16[4,2,32,448]{3,2,1,0:T(8,128)(2,1)S(1)}, bf16[4,2,32,448]{3,2,1,0:T(8,128)(2,1)S(1)}, u32[]{:S(2)}, u32[]{:S(2)}) collective-permute-start(bf16[4,2,32,448]{3,2,1,0:T(8,128)(2,1)S(1)} %get-tuple-element.24), channel_id=1, source_target_pairs={{0,1},{1,0},{2,3},{3,2},{4,5},{5,4},{6,7},{7,6},{8,9},{9,8},{10,11... | collective-permute-start | bytes 688136 | tf_op jit(solution)/shard_map/ppermute | solution.py:481
  7.1 11.3 %collective-permute-start.1 = (bf16[4,2,32,448]{3,2,1,0:T(8,128)(2,1)S(1)}, bf16[4,2,32,448]{3,2,1,0:T(8,128)(2,1)S(1)}, u32[]{:S(2)}, u32[]{:S(2)}) collective-permute-start(bf16[4,2,32,448]{3,2,1,0:T(8,128)(2,1)S(1)} %add.9.after_ref), channel_id=1, source_target_pairs={{0,2},{1,3},{2,0},{3,1},{4,6},{5,7},{6,4},{7,5},{8,10},{9,11},{10,... | collective-permute-start | bytes 688136 | tf_op jit(solution)/shard_map/ppermute | solution.py:481
  15.7 2.6 %collective-permute-start.2 = (bf16[4,32,448]{2,1,0:T(8,128)(2,1)S(1)}, bf16[4,32,448]{2,1,0:T(8,128)(2,1)S(1)}, u32[]{:S(2)}, u32[]{:S(2)}) collective-permute-start(bf16[4,32,448]{2,1,0:T(8,128)(2,1)S(1)} %get-tuple-element.28), channel_id=1, source_target_pairs={{0,1},{1,0},{2,3},{3,2},{4,5},{5,4},{6,7},{7,6},{8,9},{9,8},{10,11... | collective-permute-start | bytes 344072 | tf_op jit(solution)/shard_map/ppermute | solution.py:481
  15.8 2.6 %collective-permute-start.3 = (bf16[4,32,448]{2,1,0:T(8,128)(2,1)S(1)}, bf16[4,32,448]{2,1,0:T(8,128)(2,1)S(1)}, u32[]{:S(2)}, u32[]{:S(2)}) collective-permute-start(bf16[4,32,448]{2,1,0:T(8,128)(2,1)S(1)} %get-tuple-element.29.after_ref), channel_id=1, source_target_pairs={{0,1},{1,0},{2,3},{3,2},{4,5},{5,4},{6,7},{7,6},{8,9},{9,8},{10,11... | collective-permute-start | bytes 344072 | tf_op jit(solution)/shard_map/ppermute | solution.py:481
  18.5 4.5 %collective-permute-start.4 = (bf16[2,32,448]{2,1,0:T(8,128)(2,1)S(1)}, bf16[2,32,448]{2,1,0:T(8,128)(2,1)S(1)}, u32[]{:S(2)}, u32[]{:S(2)}) collective-permute-start(bf16[2,32,448]{2,1,0:T(8,128)(2,1)S(1)} %get-tuple-element.31), channel_id=1, source_target_pairs={{0,4},{1,5},{2,6},{3,7},{4,0},{5,1},{6,2},{7,3},{8,12},{9,13},{10,... | collective-permute-start | bytes 172040 | tf_op jit(solution)/shard_map/ppermute | solution.py:481
  20.1 7.5 %collective-permute-start.5 = (bf16[2,32,448]{2,1,0:T(8,128)(2,1)S(1)}, bf16[2,32,448]{2,1,0:T(8,128)(2,1)S(1)}, u32[]{:S(2)}, u32[]{:S(2)}) collective-permute-start(bf16[2,32,448]{2,1,0:T(8,128)(2,1)S(1)} %get-tuple-element.32), channel_id=1, source_target_pairs={{0,8},{1,9},{2,10},{3,11},{4,12},{5,13},{6,14},{7,15},{8,0},{9,1},... | collective-permute-start | bytes 172040 | tf_op jit(solution)/shard_map/ppermute | solution.py:481
  22.7 6.2 %collective-permute-start.6 = (bf16[2,32,448]{2,1,0:T(8,128)(2,1)S(1)}, bf16[2,32,448]{2,1,0:T(8,128)(2,1)S(1)}, u32[]{:S(2)}, u32[]{:S(2)}) collective-permute-start(bf16[2,32,448]{2,1,0:T(8,128)(2,1)S(1)} %get-tuple-element.33), channel_id=1, source_target_pairs={{0,12},{1,13},{2,14},{3,15},{4,8},{5,9},{6,10},{7,11},{8,4},{9,5},... | collective-permute-start | bytes 172040 | tf_op jit(solution)/shard_map/ppermute | solution.py:481
  28.9 19.3 %copy-start = (bf16[2,2,2048,256]{3,2,1,0:T(8,128)(2,1)S(1)}, bf16[2,2,2048,256]{3,2,1,0:T(8,128)(2,1)}, u32[]{:S(2)}) copy-start(bf16[2,2,2048,256]{3,2,1,0:T(8,128)(2,1)} %constant.33.clone.table_ref) | copy-start | bytes 12582916
  37.8 6.3 %collective-permute-start.9 = (bf16[2,32,448]{2,1,0:T(8,128)(2,1)S(1)}, bf16[2,32,448]{2,1,0:T(8,128)(2,1)S(1)}, u32[]{:S(2)}, u32[]{:S(2)}) collective-permute-start(bf16[2,32,448]{2,1,0:T(8,128)(2,1)S(1)} %respond.1), channel_id=1, source_target_pairs={{0,12},{1,13},{2,14},{3,15},{4,8},{5,9},{6,10},{7,11},{8,4},{9,5},... | collective-permute-start | bytes 172040 | tf_op jit(solution)/shard_map/ppermute | solution.py:481
  39.8 5.7 %collective-permute-start.8 = (bf16[2,32,448]{2,1,0:T(8,128)(2,1)S(1)}, bf16[2,32,448]{2,1,0:T(8,128)(2,1)S(1)}, u32[]{:S(2)}, u32[]{:S(2)}) collective-permute-start(bf16[2,32,448]{2,1,0:T(8,128)(2,1)S(1)} %respond.1), channel_id=1, source_target_pairs={{0,8},{1,9},{2,10},{3,11},{4,12},{5,13},{6,14},{7,15},{8,0},{9,1},... | collective-permute-start | bytes 172040 | tf_op jit(solution)/shard_map/ppermute | solution.py:481
  40.1 5.4 %collective-permute-start.7 = (bf16[2,32,448]{2,1,0:T(8,128)(2,1)S(1)}, bf16[2,32,448]{2,1,0:T(8,128)(2,1)S(1)}, u32[]{:S(2)}, u32[]{:S(2)}) collective-permute-start(bf16[2,32,448]{2,1,0:T(8,128)(2,1)S(1)} %respond.1), channel_id=1, source_target_pairs={{0,4},{1,5},{2,6},{3,7},{4,0},{5,1},{6,2},{7,3},{8,12},{9,13},{10,... | collective-permute-start | bytes 172040 | tf_op jit(solution)/shard_map/ppermute | solution.py:481
  42.3 4.3 %collective-permute-start.10 = (bf16[1,2,32,448]{3,2,1,0:T(8,128)(2,1)S(1)}, bf16[1,2,32,448]{3,2,1,0:T(8,128)(2,1)S(1)}, u32[]{:S(2)}, u32[]{:S(2)}) collective-permute-start(bf16[1,2,32,448]{3,2,1,0:T(8,128)(2,1)S(1)} %bitcast.9), channel_id=1, source_target_pairs={{0,2},{1,3},{2,0},{3,1},{4,6},{5,7},{6,4},{7,5},{8,10},{9,11},{10,... | collective-permute-start | bytes 172040 | tf_op jit(solution)/shard_map/ppermute | solution.py:481
  46.6 1.6 %collective-permute-start.13 = (bf16[4,2,32,448]{3,2,1,0:T(8,128)(2,1)S(1)}, bf16[4,2,32,448]{3,2,1,0:T(8,128)(2,1)S(1)}, u32[]{:S(2)}, u32[]{:S(2)}) collective-permute-start(bf16[4,2,32,448]{3,2,1,0:T(8,128)(2,1)S(1)} %pad_maximum_fusion.refs_0_), channel_id=1, source_target_pairs={{0,1},{1,0},{2,3},{3,2},{4,5},{5,4},{6,7},{7,6},{8,9},{9,8},{10,11... | collective-permute-start | bytes 688136 | tf_op jit(solution)/shard_map/ppermute | solution.py:481
  46.6 7.3 %collective-permute-start.12 = (bf16[3,2,32,448]{3,2,1,0:T(8,128)(2,1)S(1)}, bf16[3,2,32,448]{3,2,1,0:T(8,128)(2,1)S(1)}, u32[]{:S(2)}, u32[]{:S(2)}) collective-permute-start(bf16[3,2,32,448]{3,2,1,0:T(8,128)(2,1)S(1)} %pad_maximum_fusion.1), channel_id=1, source_target_pairs={{0,2},{1,3},{2,0},{3,1},{4,6},{5,7},{6,4},{7,5},{8,10},{9,11},{10,... | collective-permute-start | bytes 516104 | tf_op jit(solution)/shard_map/ppermute | solution.py:481
  54.0 1.5 %collective-permute-start.14 = (bf16[3,2,32,448]{3,2,1,0:T(8,128)(2,1)S(1)}, bf16[3,2,32,448]{3,2,1,0:T(8,128)(2,1)S(1)}, u32[]{:S(2)}, u32[]{:S(2)}) collective-permute-start(bf16[3,2,32,448]{3,2,1,0:T(8,128)(2,1)S(1)} %collective-permute-done.12.refs_2_), channel_id=1, source_target_pairs={{0,1},{1,0},{2,3},{3,2},{4,5},{5,4},{6,7},{7,6},{8,9},{9,8},{10,11... | collective-permute-start | bytes 516104 | tf_op jit(solution)/shard_map/ppermute | solution.py:481
  54.0 1.5 %collective-permute-start.11 = (bf16[1,2,32,448]{3,2,1,0:T(8,128)(2,1)S(1)}, bf16[1,2,32,448]{3,2,1,0:T(8,128)(2,1)S(1)}, u32[]{:S(2)}, u32[]{:S(2)}) collective-permute-start(bf16[1,2,32,448]{3,2,1,0:T(8,128)(2,1)S(1)} %collective-permute-done.10.refs_0_), channel_id=1, source_target_pairs={{0,1},{1,0},{2,3},{3,2},{4,5},{5,4},{6,7},{7,6},{8,9},{9,8},{10,11... | collective-permute-start | bytes 172040 | tf_op jit(solution)/shard_map/ppermute | solution.py:481

commit v9 on v4

--- a/solution.py
+++ b/solution.py
@@ -41,14 +41,13 @@
 
 def chunk_list(half):
     unit = half // 8
-    sizes = (unit, unit, 2 * unit, 4 * unit)
-    starts = (0, unit, 2 * unit, 4 * unit)
-    return tuple(zip(starts, sizes))
+    sizes = (unit, unit, 2 * unit, 2 * unit, 2 * unit)
+    return tuple((sum(sizes[:n]), size) for n, size in enumerate(sizes))
 
 
 def forward_kernel(
-    place_ref, table_ref, forces_ref, shapes_ref, frf_ref, keep_ref, send_ref, held_ref,
-    table_buf, forces_buf, shapes_buf, acc_ref, table_sem, forces_sem, shapes_sem, held_sem,
+    place_ref, table_ref, forces_ref, shapes_ref, keep_ref, send_ref,
+    table_buf, forces_buf, shapes_buf, acc_ref, table_sem, forces_sem, shapes_sem,
 ):
     _, zs, _, rows, modes = keep_ref.shape
     chunks = chunk_list(forces_ref.shape[1])
@@ -68,10 +67,6 @@
         copies.append(pair)
     shapes_copy = pltpu.make_async_copy(shapes_ref, shapes_buf, shapes_sem)
     shapes_copy.start()
-    held_copy = pltpu.make_async_copy(
-        frf_ref.at[pl.ds(0, held_ref.shape[0])], held_ref, held_sem
-    )
-    held_copy.start()
 
     for n, (start, size) in enumerate(chunks):
         for copy in copies[n]:
@@ -105,14 +100,13 @@
                 slot = chip ^ (2 * z + y)
                 keep_ref[slot % 2, slot // 2, parity] = keep[z]
                 send_ref[slot % 2, slot // 2, parity] = send[z]
-    held_copy.wait()
 
 
 def in_hbm(array):
     return pltpu.with_memory_space_constraint(array, pltpu.HBM)
 
 
-def forward(place, table, forces, shapes_t, frf, held, chips):
+def forward(place, table, forces, shapes_t, chips):
     _, half, dofs = forces.shape
     modes = shapes_t.shape[0]
     rows = FREQS // (chips * CORES)
@@ -121,9 +115,9 @@
     count = len(chunk_list(half))
     return pl.pallas_call(
         forward_kernel,
-        in_specs=[pl.BlockSpec(memory_space=pltpu.SMEM), hbm, hbm, hbm, hbm],
-        out_specs=[vmem, vmem, vmem],
-        out_shape=[out, out, pltpu.VMEM((held,) + frf.shape[1:], jnp.bfloat16)],
+        in_specs=[pl.BlockSpec(memory_space=pltpu.SMEM), hbm, hbm, hbm],
+        out_specs=[vmem, vmem],
+        out_shape=[out, out],
         scratch_shapes=[
             pltpu.VMEM(table.shape, jnp.bfloat16),
             pltpu.VMEM(forces.shape, jnp.bfloat16),
@@ -132,14 +126,13 @@
             pltpu.SemaphoreType.DMA((count,)),
             pltpu.SemaphoreType.DMA((count,)),
             pltpu.SemaphoreType.DMA,
-            pltpu.SemaphoreType.DMA,
         ],
         compiler_params=pltpu.CompilerParams(vmem_limit_bytes=24 * MIB),
         cost_estimate=pl.CostEstimate(
-            flops=4 * FREQS * dofs * (half + modes), bytes_accessed=20 * MIB, transcendentals=0
+            flops=4 * FREQS * dofs * (half + modes), bytes_accessed=12 * MIB, transcendentals=0
         ),
         name="forward",
-    )(place, in_hbm(table), in_hbm(forces), in_hbm(shapes_t), in_hbm(frf))
+    )(place, in_hbm(table), in_hbm(forces), in_hbm(shapes_t))
 
 
 def load_copies(start, frf_ref, held_ref, sem):
@@ -180,8 +173,12 @@
 
 
 def respond_kernel(count, *refs):
-    pieces, parts = refs[:count], refs[count:-4]
-    out_ref, direct_ref, turned_ref, result_ref = refs[-4:]
+    pieces, parts = refs[:count], refs[count:-7]
+    frf_ref, out_ref, direct_ref, turned_ref, result_ref, rest_ref, sem = refs[-7:]
+    held = sum(part.shape[0] for part in parts)
+    copies = load_copies(held, frf_ref, rest_ref, sem)
+    for copy in copies:
+        copy.start()
     _, rows, modes = out_ref.shape
     total = sum(piece[0].astype(jnp.float32) for piece in pieces).reshape(2 * rows, modes)
     total = total.astype(jnp.bfloat16).astype(jnp.float32)
@@ -197,24 +194,35 @@
         at = place(f)
         direct_ref[f, 0:2] = total[at : at + 2]
         turned_ref[f, 0:2] = turned[at : at + 2]
+
+    def multiply(matrix_ref, step, f):
+        products = [
+            lax.dot_general(
+                ref[f].astype(jnp.bfloat16),
+                matrix_ref[step, which],
+                (((1,), (1,)), ((), ())),
+                preferred_element_type=jnp.float32,
+            )
+            for which, ref in enumerate((direct_ref, turned_ref))
+        ]
+        result_ref[f] = products[0] + products[1]
+
     base = 0
     for part in parts:
 
         @pl.loop(0, part.shape[0], unroll=math.gcd(4, part.shape[0]))
         def _(step, part=part, base=base):
-            f = base + step
-            products = [
-                lax.dot_general(
-                    ref[f].astype(jnp.bfloat16),
-                    part[step, which],
-                    (((1,), (1,)), ((), ())),
-                    preferred_element_type=jnp.float32,
-                )
-                for which, ref in enumerate((direct_ref, turned_ref))
-            ]
-            result_ref[f] = products[0] + products[1]
+            multiply(part, step, base + step)
 
         base += part.shape[0]
+
+    each = rest_ref.shape[0] // len(copies)
+    for n, copy in enumerate(copies):
+        copy.wait()
+
+        @pl.loop(n * each, (n + 1) * each, unroll=each)
+        def _(step):
+            multiply(rest_ref, step, held + step)
 
     for f in range(rows):
         at = place(f)
@@ -224,34 +232,34 @@
     )
 
 
-def respond(pieces, parts):
+def respond(pieces, parts, frf):
     rows, modes = pieces[0].shape[2:]
-    vmem = pl.BlockSpec(memory_space=pltpu.VMEM)
-    size = sum(part.size for part in parts)
+    vmem, hbm = pl.BlockSpec(memory_space=pltpu.VMEM), pl.BlockSpec(memory_space=pltpu.HBM)
+    rest = frf.shape[0] - sum(part.shape[0] for part in parts)
     return pl.pallas_call(
         functools.partial(respond_kernel, len(pieces)),
-        in_specs=[vmem] * (len(pieces) + len(parts)),
+        in_specs=[vmem] * (len(pieces) + len(parts)) + [hbm],
         out_specs=vmem,
         out_shape=jax.ShapeDtypeStruct((2, rows, modes), jnp.bfloat16),
-        scratch_shapes=[pltpu.VMEM((rows, 8, modes), jnp.float32)] * 3,
-        compiler_params=pltpu.CompilerParams(vmem_limit_bytes=12 * MIB),
-        cost_estimate=pl.CostEstimate(flops=4 * size, bytes_accessed=2 * size, transcendentals=0),
+        scratch_shapes=[pltpu.VMEM((rows, 8, modes), jnp.float32)] * 3
+        + [
+            pltpu.VMEM((rest,) + frf.shape[1:], jnp.bfloat16),
+            pltpu.SemaphoreType.DMA((rest // math.gcd(rest, 4),)),
+        ],
+        compiler_params=pltpu.CompilerParams(vmem_limit_bytes=36 * MIB),
+        cost_estimate=pl.CostEstimate(
+            flops=4 * frf.size, bytes_accessed=2 * frf.size, transcendentals=0
+        ),
         name="respond",
-    )(*pieces, *parts)
-
-
-def project(place_ref, shards, shapes_ref, order_ref, moved_ref):
+    )(*pieces, *parts, in_hbm(frf))
+
+
+def project(place_ref, slots, shapes_ref, order_ref, moved_ref):
     _, _, zs, rows, modes = order_ref.shape
     core, z = place_ref[0], place_ref[1] // 2
-    start = 0
-    for own_ref, twin_ref in zip(shards[::2], shards[1::2]):
-        for far, shard_ref in enumerate((own_ref, twin_ref)):
-            for k in range(shard_ref.shape[0]):
-                for parity in range(2):
-                    order_ref[parity, core ^ far, z ^ (start + k)] = shard_ref[
-                        k, parity
-                    ].astype(jnp.float32)
-        start += own_ref.shape[0]
+    for shard_ref, n, far, k in slots:
+        for parity in range(2):
+            order_ref[parity, core ^ far, z ^ k] = shard_ref[n, parity].astype(jnp.float32)
     for parity in range(2):
         moved_ref[parity] = jnp.dot(
             order_ref[parity].reshape(FREQS // 2, modes).astype(jnp.bfloat16),
@@ -260,9 +268,13 @@
         ).astype(jnp.bfloat16)
 
 
-def early_kernel(place_ref, table_ref, shapes_ref, *refs):
+def named_slots(plan, shards):
+    return [(shards[which], n, far, k) for which, n, far, k in plan]
+
+
+def early_kernel(plan, place_ref, table_ref, shapes_ref, *refs):
     shards, (waves_ref, order_ref, moved_ref) = refs[:-3], refs[-3:]
-    project(place_ref, shards, shapes_ref, order_ref, moved_ref)
+    project(place_ref, named_slots(plan, shards), shapes_ref, order_ref, moved_ref)
     y = place_ref[1] % 2
     block = waves_ref.shape[1] // 4
     for step in range(4):
@@ -273,9 +285,9 @@
             )
 
 
-def late_kernel(place_ref, table_ref, shapes_ref, *refs):
+def late_kernel(plan, place_ref, table_ref, shapes_ref, *refs):
     shards, (waves_ref, out_ref, order_ref, moved_ref, out_buf, out_sem) = refs[:-6], refs[-6:]
-    project(place_ref, shards, shapes_ref, order_ref, moved_ref)
+    project(place_ref, named_slots(plan, shards), shapes_ref, order_ref, moved_ref)
     y = (place_ref[1] % 2) ^ 1
     count = out_sem.shape[0]
     block = out_ref.shape[1] // count
@@ -302,11 +314,11 @@
         copy_out(step).wait()
 
 
-def inverse(place, table, shapes_t, shards, waves=None):
+def inverse(place, table, shapes_t, shards, plan, waves=None):
     half = table.shape[2]
     modes, dofs = shapes_t.shape
     rows = shards[0].shape[2]
-    zs = sum(shard.shape[0] for shard in shards) // 2
+    zs = len(plan) // 2
     vmem = pl.BlockSpec(memory_space=pltpu.VMEM)
     scratch = [
         pltpu.VMEM((2, CORES, zs, rows, modes), jnp.float32),
@@ -320,17 +332,17 @@
     )
     if waves is None:
         return pl.pallas_call(
-            early_kernel,
+            functools.partial(early_kernel, plan),
             in_specs=in_specs,
             out_specs=vmem,
             out_shape=pltpu.VMEM((2, half, dofs), jnp.float32),
             scratch_shapes=scratch,
             compiler_params=params,
-            cost_estimate=cost,
+            cost_estimate=pl.CostEstimate(flops=1000, bytes_accessed=1000, transcendentals=0),
             name="early",
         )(*given)
     return pl.pallas_call(
-        late_kernel,
+        functools.partial(late_kernel, plan),
         in_specs=in_specs + [vmem],
         out_specs=pl.BlockSpec(memory_space=pltpu.HBM),
         out_shape=jax.ShapeDtypeStruct((2, half, dofs), jnp.bfloat16),
@@ -387,31 +399,37 @@
     inv = jnp.asarray(inverse_tables(steps, chips).astype(jnp.bfloat16))
 
     unit = frf.shape[0] // 8
-    keep, send, part0 = forward(
-        place, fwd, forces.reshape(2, half, dofs), shapes_t, frf, 2 * unit, chips
-    )
-    part1 = load(frf, 2 * unit, unit, send)
+    keep, send = forward(place, fwd, forces.reshape(2, half, dofs), shapes_t, chips)
     slots = (2 * zs,) + keep.shape[2:]
     here, there_near, there_far = add(
-        keep.reshape(slots), swap(send, 1).reshape(slots), 0, (zs, 1, zs - 1), part1
+        keep.reshape(slots), swap(send, 1).reshape(slots), 0, (zs, 1, zs - 1), send
     )
     came_far, came_near = swap(there_far, 2), swap(there_near, 2)
-    part2 = load(frf, 3 * unit, 3 * unit, there_far)
-    pieces = add(here, came_far, 1, (1,) * (zs - 1), part2)
-    part3 = load(frf, 6 * unit, 2 * unit, pieces[0])
+    part0 = load(frf, 0, 3 * unit, there_far)
+    pieces = add(here, came_far, 1, (1,) * (zs - 1), part0)
+    part1 = load(frf, 3 * unit, 3 * unit, pieces[0])
     came = [swap(piece, 4 * k) for k, piece in enumerate(pieces, 1)]
-    response = respond([here[:1], came_near, *came], (part0, part1, part2, part3))
-
-    across = swap(response[None], 2)
+    response = respond([here[:1], came_near, *came], (part0, part1), frf)
+
+    own = response[None]
+    over = swap(own, 2)
     shards = [swap(response, 4 * k) for k in range(1, zs)]
-    far, across = lax.optimization_barrier((jnp.stack(shards), across))
-    across_far = swap(far, 2)
-    own = jnp.concatenate([response[None], far])
-    twin, twin_across = swap(own, 1), swap(across, 1)
-    waves = inverse(place, inv, shapes_t, (own, twin))
-    across_far, waves = lax.optimization_barrier((across_far, waves))
-    groups = (across, twin_across, across_far, swap(across_far, 1))
-    out = inverse(place, inv, shapes_t, groups, waves)
+    far, over = lax.optimization_barrier((jnp.stack(shards), over))
+    over_far = swap(far, 2)
+    cut = (zs - 1) // 2
+    twin = swap(jnp.concatenate([own, over]), 1)
+    twin_far = [swap(jnp.stack(shards[:-cut]), 1), swap(jnp.stack(shards[-cut:]), 1)]
+    plan = [(0, 0, 0, 0), (2, 0, 1, 0)]
+    for k in range(1, zs):
+        at = k - 1
+        plan += [(1, at, 0, k)]
+        plan += [(3, at, 1, k) if at < zs - 1 - cut else (4, at - (zs - 1 - cut), 1, k)]
+    waves = inverse(place, inv, shapes_t, (own, far, twin, *twin_far), plan)
+    over_far, waves = lax.optimization_barrier((over_far, waves))
+    plan = [(0, 0, 0, 0), (2, 1, 1, 0)]
+    for k in range(1, zs):
+        plan += [(1, k - 1, 0, k), (3, k - 1, 1, k)]
+    out = inverse(place, inv, shapes_t, (over, over_far, twin, swap(over_far, 1)), plan, waves)
     return out.reshape(1, steps, dofs)
 
 

time: 58.8 us -> 65.5 us (1.11)
  local copies, waits for them, and re-layouts: 0.01 us -> 4.18 us
  Pallas kernels: 33.2 us -> 36.1 us
  waiting for transfers between devices: 9.4 us -> 8.11 us
  starting transfers between devices: 15.8 us -> 16.7 us
    pallas_call x1, Pallas kernels: 8.71 us -> 13.1 us  [respond(): pl.pallas_call(functools.partial(respond_kernel, len(pieces)), in_specs=[...]
    unnamed x4 -> x6, local copies, waits for them, and re-layouts: 0.01 us -> 4.18 us
    ppermute x14 -> x15, waiting for transfers between devices: 9.4 us -> 8.11 us  [swap(): return lax.ppermute(values, 'dof', pairs)]
    pallas_call x3 -> x2, Pallas kernels: 9.47 us -> 8.49 us  [load(): pl.pallas_call(functools.partial(load_kernel, start), in_specs=[hbm, anyw...]
    ppermute x14 -> x15, starting transfers between devices: 15.8 us -> 16.7 us  [swap(): return lax.ppermute(values, 'dof', pairs)]
  transfers between devices with their start and end apart: 14 -> 15, of which waited for: 8 -> 6; matrix products, arithmetic and copies ran while one was open for 0% -> 0% of each run, Pallas kernels for 21% -> 17%
where the time goes in v9:
time: 65.5 us; the launch traced here: 65.4 us
  Pallas kernels  36.1 us (55%)
  starting transfers between devices  16.7 us (25%)
  waiting for transfers between devices  8.11 us (12%)
  local copies, waits for them, and re-layouts  4.18 us (6%)
    ppermute x15, starting transfers between devices, swap(): return lax.ppermute(values, 'dof', pairs)  16.7 us
    pallas_call x1, Pallas kernels, respond(): pl.pallas_call(functools.partial(respond_kernel, len(pieces)), in_specs=[...  13.1 us
    pallas_call x2, Pallas kernels, load(): pl.pallas_call(functools.partial(load_kernel, start), in_specs=[hbm, anyw...  8.49 us
    ppermute x15, waiting for transfers between devices, swap(): return lax.ppermute(values, 'dof', pairs)  8.11 us
    pallas_call x1, Pallas kernels, forward(): pl.pallas_call(forward_kernel, in_specs=[pl.BlockSpec(memory_space=pltpu....  7.09 us
    pallas_call x1, Pallas kernels, inverse(): pl.pallas_call(functools.partial(late_kernel, plan), in_specs=in_specs +...  4.5 us
    unnamed x6, local copies, waits for them, and re-layouts  4.18 us
    pallas_call x1, Pallas kernels, inverse(): pl.pallas_call(functools.partial(early_kernel, plan), in_specs=in_specs,...  2.8 us
  transfers between devices with their start and end apart: 15, of which 6 were waited for; matrix products, arithmetic and copies ran while one was open for 0% of the time, Pallas kernels for 17%

profile of v9, /device:TPU:0, one launch (start us, length us, event | category | flops | bytes accessed | tf_op | source)
XLA Modules:
  0.0 65.4 jit_solution(15415620838126876854)
XLA Ops:
  0.0 0.1 pad_add_fusion.place_ref
  0.1 7.1 %forward.1 = (bf16[2,4,2,32,448]{4,3,2,1,0:T(8,128)(2,1)S(1)}, bf16[2,4,2,32,448]{4,3,2,1,0:T(8,128)(2,1)S(1)}) custom-call(s32[2]{0:T(128)S(1)} %pad_add_fusion.place_ref, bf16[2,512,2048]{2,1,0:T(8,128)(2,1)} %constant.32.clone.table_ref, bf16[2,2048,768]{2,1,0:T(8,128)(2,1)} %bitcast.25, bf16[448,768]{1,0:T(8,128)(2,1)} %bitcast.11), custom_call_target="tpu_custom_call" | custom-call | flops 3925868544 | bytes 12582912 | tf_op jit(solution)/shard_map/forward/pallas_call | solution.py:116
  7.2 0.5 collective-permute-start
  7.7 1.5 %collective-permute-done = bf16[2,4,2,32,448]{4,3,2,1,0:T(8,128)(2,1)S(1)} collective-permute-done((bf16[2,4,2,32,448]{4,3,2,1,0:T(8,128)(2,1)S(1)}, bf16[2,4,2,32,448]{4,3,2,1,0:T(8,128)(2,1)S(1)}, u32[]{:S(2)}, u32[]{:S(2)}) %collective-permute-start) | collective-permute-done | bytes 458784 | tf_op jit(solution)/shard_map/ppermute | solution.py:393
  9.2 0.1 add.10
  9.4 2.9 %collective-permute-start.2 = (bf16[3,2,32,448]{3,2,1,0:T(8,128)(2,1)S(1)}, bf16[3,2,32,448]{3,2,1,0:T(8,128)(2,1)S(1)}, u32[]{:S(2)}, u32[]{:S(2)}) collective-permute-start(bf16[3,2,32,448]{3,2,1,0:T(8,128)(2,1)S(1)} %get-tuple-element.21.after_ref), channel_id=1, source_target_pairs={{0,2},{1,3},{2,0},{3,1},{4,6},{5,7},{6,4},{7,5},{8,10},{9,11},{10,... | collective-permute-start | bytes 516104 | tf_op jit(solution)/shard_map/ppermute | solution.py:393
  12.3 0.1 collective-permute-start.1
  12.4 4.2 %load.2.after_ref.refs_5_ = bf16[12,2,448,448]{3,2,1,0:T(8,128)(2,1)S(1)} custom-call(bf16[32,2,448,448]{3,2,1,0:T(8,128)(2,1)} %refs_7_.1, bf16[3,2,32,448]{3,2,1,0:T(8,128)(2,1)S(1)} %get-tuple-element.21.after_ref), custom_call_target="tpu_custom_call" | custom-call | bytes 19267584 | tf_op jit(solution)/shard_map/load/pallas_call | solution.py:161
  16.6 1.4 %collective-permute-done.2.came_ref = bf16[3,2,32,448]{3,2,1,0:T(8,128)(2,1)S(1)} collective-permute-done((bf16[3,2,32,448]{3,2,1,0:T(8,128)(2,1)S(1)}, bf16[3,2,32,448]{3,2,1,0:T(8,128)(2,1)S(1)}, u32[]{:S(2)}, u32[]{:S(2)}) %collective-permute-start.2) | collective-permute-done | bytes 172064 | tf_op jit(solution)/shard_map/ppermute | solution.py:393
  18.0 3.1 %collective-permute-start.4 = (bf16[1,2,32,448]{3,2,1,0:T(8,128)(2,1)S(1)}, bf16[1,2,32,448]{3,2,1,0:T(8,128)(2,1)S(1)}, u32[]{:S(2)}, u32[]{:S(2)}) collective-permute-start(bf16[1,2,32,448]{3,2,1,0:T(8,128)(2,1)S(1)} %get-tuple-element.23), channel_id=1, source_target_pairs={{0,8},{1,9},{2,10},{3,11},{4,12},{5,13},{6,14},{7,15},{8,0},{9,1},... | collective-permute-start | bytes 172040 | tf_op jit(solution)/shard_map/ppermute | solution.py:393
  21.1 1.3 %collective-permute-start.5 = (bf16[1,2,32,448]{3,2,1,0:T(8,128)(2,1)S(1)}, bf16[1,2,32,448]{3,2,1,0:T(8,128)(2,1)S(1)}, u32[]{:S(2)}, u32[]{:S(2)}) collective-permute-start(bf16[1,2,32,448]{3,2,1,0:T(8,128)(2,1)S(1)} %get-tuple-element.24), channel_id=1, source_target_pairs={{0,12},{1,13},{2,14},{3,15},{4,8},{5,9},{6,10},{7,11},{8,4},{9,5},... | collective-permute-start | bytes 172040 | tf_op jit(solution)/shard_map/ppermute | solution.py:393
  22.5 0.2 collective-permute-start.3
  22.7 4.2 %load.3.refs_6_ = bf16[12,2,448,448]{3,2,1,0:T(8,128)(2,1)S(1)} custom-call(bf16[32,2,448,448]{3,2,1,0:T(8,128)(2,1)} %refs_7_.1, bf16[1,2,32,448]{3,2,1,0:T(8,128)(2,1)S(1)} %get-tuple-element.22.after_ref), custom_call_target="tpu_custom_call" | custom-call | bytes 19267584 | tf_op jit(solution)/shard_map/load/pallas_call | solution.py:161
  27.0 0.0 copy-start
  27.0 4.2 %copy-done = bf16[12,2,448,448]{3,2,1,0:T(8,128)(2,1)} copy-done((bf16[12,2,448,448]{3,2,1,0:T(8,128)(2,1)}, bf16[12,2,448,448]{3,2,1,0:T(8,128)(2,1)S(1)}, u32[]{:S(2)}) %copy-start) | copy-done | bytes 9633816
  31.2 0.0 copy-start.1
  31.2 0.0 copy-start.2
  31.2 0.0 collective-permute-done.1.refs_1_
  31.2 0.0 collective-permute-done.4.refs_3_
  31.2 0.0 collective-permute-done.5.refs_4_
  31.2 0.0 collective-permute-done.3.refs_2_
  31.2 13.1 %respond.1 = bf16[2,32,448]{2,1,0:T(8,128)(2,1)S(1)} custom-call(bf16[1,2,32,448]{3,2,1,0:T(8,128)(2,1)S(1)} %slice.3.refs_0_, bf16[1,2,32,448]{3,2,1,0:T(8,128)(2,1)S(1)} %collective-permute-done.1.refs_1_, bf16[1,2,32,448]{3,2,1,0:T(8,128)(2,1)S(1)} %collective-permute-done.3.refs_2_, bf16[1,2,32,448]{3,2,1,0:T(8,128)(2,1)S(1)} %collective-permute-done.4.refs_3_, ...), custom_call_target="tpu_custom_call" | custom-call | flops 51380224 | bytes 25690112 | tf_op jit(solution)/shard_map/respond/pallas_call | solution.py:239
  44.3 3.0 %collective-permute-start.8 = (bf16[2,32,448]{2,1,0:T(8,128)(2,1)S(1)}, bf16[2,32,448]{2,1,0:T(8,128)(2,1)S(1)}, u32[]{:S(2)}, u32[]{:S(2)}) collective-permute-start(bf16[2,32,448]{2,1,0:T(8,128)(2,1)S(1)} %respond.1), channel_id=1, source_target_pairs={{0,12},{1,13},{2,14},{3,15},{4,8},{5,9},{6,10},{7,11},{8,4},{9,5},... | collective-permute-start | bytes 172040 | tf_op jit(solution)/shard_map/ppermute | solution.py:393
  47.2 0.3 collective-permute-start.7
  47.6 1.1 %collective-permute-start.6 = (bf16[2,32,448]{2,1,0:T(8,128)(2,1)S(1)}, bf16[2,32,448]{2,1,0:T(8,128)(2,1)S(1)}, u32[]{:S(2)}, u32[]{:S(2)}) collective-permute-start(bf16[2,32,448]{2,1,0:T(8,128)(2,1)S(1)} %respond.1), channel_id=1, source_target_pairs={{0,4},{1,5},{2,6},{3,7},{4,0},{5,1},{6,2},{7,3},{8,12},{9,13},{10,... | collective-permute-start | bytes 172040 | tf_op jit(solution)/shard_map/ppermute | solution.py:393
  48.7 1.5 %collective-permute-start.9 = (bf16[1,2,32,448]{3,2,1,0:T(8,128)(2,1)S(1)}, bf16[1,2,32,448]{3,2,1,0:T(8,128)(2,1)S(1)}, u32[]{:S(2)}, u32[]{:S(2)}) collective-permute-start(bf16[1,2,32,448]{3,2,1,0:T(8,128)(2,1)S(1)} %bitcast.14), channel_id=1, source_target_pairs={{0,2},{1,3},{2,0},{3,1},{4,6},{5,7},{6,4},{7,5},{8,10},{9,11},{10,... | collective-permute-start | bytes 172040 | tf_op jit(solution)/shard_map/ppermute | solution.py:393
  50.2 0.7 %collective-permute-done.8 = bf16[2,32,448]{2,1,0:T(8,128)(2,1)S(1)} collective-permute-done((bf16[2,32,448]{2,1,0:T(8,128)(2,1)S(1)}, bf16[2,32,448]{2,1,0:T(8,128)(2,1)S(1)}, u32[]{:S(2)}, u32[]{:S(2)}) %collective-permute-start.8) | collective-permute-done | bytes 57376 | tf_op jit(solution)/shard_map/ppermute | solution.py:393
  50.9 2.1 %collective-permute-done.7 = bf16[2,32,448]{2,1,0:T(8,128)(2,1)S(1)} collective-permute-done((bf16[2,32,448]{2,1,0:T(8,128)(2,1)S(1)}, bf16[2,32,448]{2,1,0:T(8,128)(2,1)S(1)}, u32[]{:S(2)}, u32[]{:S(2)}) %collective-permute-start.7) | collective-permute-done | bytes 57376 | tf_op jit(solution)/shard_map/ppermute | solution.py:393
  53.0 0.0 collective-permute-done.6
  53.1 0.0 collective-permute-done.9.refs_0_
  53.1 1.6 %collective-permute-start.10 = (bf16[3,2,32,448]{3,2,1,0:T(8,128)(2,1)S(1)}, bf16[3,2,32,448]{3,2,1,0:T(8,128)(2,1)S(1)}, u32[]{:S(2)}, u32[]{:S(2)}) collective-permute-start(bf16[3,2,32,448]{3,2,1,0:T(8,128)(2,1)S(1)} %pad_maximum_fusion.refs_1_), channel_id=1, source_target_pairs={{0,2},{1,3},{2,0},{3,1},{4,6},{5,7},{6,4},{7,5},{8,10},{9,11},{10,... | collective-permute-start | bytes 516104 | tf_op jit(solution)/shard_map/ppermute | solution.py:393
  54.7 0.1 collective-permute-start.11
  54.8 0.5 collective-permute-start.12
  55.2 0.1 collective-permute-start.13
  55.3 1.2 %collective-permute-done.13.refs_4_ = bf16[1,2,32,448]{3,2,1,0:T(8,128)(2,1)S(1)} collective-permute-done((bf16[1,2,32,448]{3,2,1,0:T(8,128)(2,1)S(1)}, bf16[1,2,32,448]{3,2,1,0:T(8,128)(2,1)S(1)}, u32[]{:S(2)}, u32[]{:S(2)}) %collective-permute-start.13) | collective-permute-done | bytes 57376 | tf_op jit(solution)/shard_map/ppermute | solution.py:393
  56.5 0.0 collective-permute-done.11.refs_2_
  56.5 0.0 collective-permute-done.12.refs_3_
  56.5 0.0 copy-done.1
  56.5 0.0 copy-done.2
  56.5 2.8 %early.1.refs_4_ = f32[2,2048,768]{2,1,0:T(8,128)S(1)} custom-call(s32[2]{0:T(128)S(1)} %pad_add_fusion.place_ref, bf16[2,2,2048,256]{3,2,1,0:T(8,128)(2,1)S(1)} %copy-done.1, bf16[448,768]{1,0:T(8,128)(2,1)S(1)} %bitcast.12, bf16[1,2,32,448]{3,2,1,0:T(8,128)(2,1)S(1)} %bitcast.16, bf16[3,2,32,448]{3,2,1,0:T(8,128)(2,1)S(1)} %pad_maximum_fusion.refs_1_, ...), custom_call_target="tpu_custom_call" | custom-call | flops 1000 | bytes 1000 | tf_op jit(solution)/shard_map/early/pallas_call | solution.py:334
  59.3 0.0 collective-permute-done.10.refs_1_
  59.3 0.3 collective-permute-start.14
  59.6 1.3 %collective-permute-done.14.refs_3_ = bf16[3,2,32,448]{3,2,1,0:T(8,128)(2,1)S(1)} collective-permute-done((bf16[3,2,32,448]{3,2,1,0:T(8,128)(2,1)S(1)}, bf16[3,2,32,448]{3,2,1,0:T(8,128)(2,1)S(1)}, u32[]{:S(2)}, u32[]{:S(2)}) %collective-permute-start.14) | collective-permute-done | bytes 172064 | tf_op jit(solution)/shard_map/ppermute | solution.py:393
  60.8 4.5 %late.1 = bf16[2,2048,768]{2,1,0:T(8,128)(2,1)} custom-call(s32[2]{0:T(128)S(1)} %pad_add_fusion.place_ref, bf16[2,2,2048,256]{3,2,1,0:T(8,128)(2,1)S(1)} %copy-done.1, bf16[448,768]{1,0:T(8,128)(2,1)S(1)} %bitcast.13, bf16[1,2,32,448]{3,2,1,0:T(8,128)(2,1)S(1)} %collective-permute-done.9.refs_0_, ...), custom_call_target="tpu_custom_call" | custom-call | flops 1962934272 | bytes 8388608 | tf_op jit(solution)/shard_map/late/pallas_call | solution.py:344
  (5 shorter events, 0.1 us)
Async XLA Ops:
  7.2 2.1 %collective-permute-start = (bf16[2,4,2,32,448]{4,3,2,1,0:T(8,128)(2,1)S(1)}, bf16[2,4,2,32,448]{4,3,2,1,0:T(8,128)(2,1)S(1)}, u32[]{:S(2)}, u32[]{:S(2)}) collective-permute-start(bf16[2,4,2,32,448]{4,3,2,1,0:T(8,128)(2,1)S(1)} %get-tuple-element.18.after_ref), channel_id=1, source_target_pairs={{0,1},{1,0},{2,3},{3,2},{4,5},{5,4},{6,7},{7,6},{8,9},{9,8},{10,11... | collective-permute-start | bytes 1376264 | tf_op jit(solution)/shard_map/ppermute | solution.py:393
  9.4 8.6 %collective-permute-start.2 = (bf16[3,2,32,448]{3,2,1,0:T(8,128)(2,1)S(1)}, bf16[3,2,32,448]{3,2,1,0:T(8,128)(2,1)S(1)}, u32[]{:S(2)}, u32[]{:S(2)}) collective-permute-start(bf16[3,2,32,448]{3,2,1,0:T(8,128)(2,1)S(1)} %get-tuple-element.21.after_ref), channel_id=1, source_target_pairs={{0,2},{1,3},{2,0},{3,1},{4,6},{5,7},{6,4},{7,5},{8,10},{9,11},{10,... | collective-permute-start | bytes 516104 | tf_op jit(solution)/shard_map/ppermute | solution.py:393
  12.3 18.9 %collective-permute-start.1 = (bf16[1,2,32,448]{3,2,1,0:T(8,128)(2,1)S(1)}, bf16[1,2,32,448]{3,2,1,0:T(8,128)(2,1)S(1)}, u32[]{:S(2)}, u32[]{:S(2)}) collective-permute-start(bf16[1,2,32,448]{3,2,1,0:T(8,128)(2,1)S(1)} %get-tuple-element.20), channel_id=1, source_target_pairs={{0,2},{1,3},{2,0},{3,1},{4,6},{5,7},{6,4},{7,5},{8,10},{9,11},{10,... | collective-permute-start | bytes 172040 | tf_op jit(solution)/shard_map/ppermute | solution.py:393
  18.0 13.1 %collective-permute-start.4 = (bf16[1,2,32,448]{3,2,1,0:T(8,128)(2,1)S(1)}, bf16[1,2,32,448]{3,2,1,0:T(8,128)(2,1)S(1)}, u32[]{:S(2)}, u32[]{:S(2)}) collective-permute-start(bf16[1,2,32,448]{3,2,1,0:T(8,128)(2,1)S(1)} %get-tuple-element.23), channel_id=1, source_target_pairs={{0,8},{1,9},{2,10},{3,11},{4,12},{5,13},{6,14},{7,15},{8,0},{9,1},... | collective-permute-start | bytes 172040 | tf_op jit(solution)/shard_map/ppermute | solution.py:393
  21.1 10.0 %collective-permute-start.5 = (bf16[1,2,32,448]{3,2,1,0:T(8,128)(2,1)S(1)}, bf16[1,2,32,448]{3,2,1,0:T(8,128)(2,1)S(1)}, u32[]{:S(2)}, u32[]{:S(2)}) collective-permute-start(bf16[1,2,32,448]{3,2,1,0:T(8,128)(2,1)S(1)} %get-tuple-element.24), channel_id=1, source_target_pairs={{0,12},{1,13},{2,14},{3,15},{4,8},{5,9},{6,10},{7,11},{8,4},{9,5},... | collective-permute-start | bytes 172040 | tf_op jit(solution)/shard_map/ppermute | solution.py:393
  22.5 8.7 %collective-permute-start.3 = (bf16[1,2,32,448]{3,2,1,0:T(8,128)(2,1)S(1)}, bf16[1,2,32,448]{3,2,1,0:T(8,128)(2,1)S(1)}, u32[]{:S(2)}, u32[]{:S(2)}) collective-permute-start(bf16[1,2,32,448]{3,2,1,0:T(8,128)(2,1)S(1)} %get-tuple-element.22.after_ref), channel_id=1, source_target_pairs={{0,4},{1,5},{2,6},{3,7},{4,0},{5,1},{6,2},{7,3},{8,12},{9,13},{10,... | collective-permute-start | bytes 172040 | tf_op jit(solution)/shard_map/ppermute | solution.py:393
  27.0 4.2 %copy-start = (bf16[12,2,448,448]{3,2,1,0:T(8,128)(2,1)}, bf16[12,2,448,448]{3,2,1,0:T(8,128)(2,1)S(1)}, u32[]{:S(2)}) copy-start(bf16[12,2,448,448]{3,2,1,0:T(8,128)(2,1)S(1)} %load.3.refs_6_) | copy-start | bytes 28901380
  31.2 25.4 %copy-start.1 = (bf16[2,2,2048,256]{3,2,1,0:T(8,128)(2,1)S(1)}, bf16[2,2,2048,256]{3,2,1,0:T(8,128)(2,1)}, u32[]{:S(2)}) copy-start(bf16[2,2,2048,256]{3,2,1,0:T(8,128)(2,1)} %constant.33.clone.table_ref) | copy-start | bytes 12582916
  31.2 25.4 %copy-start.2 = (bf16[768,448]{0,1:T(8,128)(2,1)S(1)}, bf16[768,448]{0,1:T(8,128)(2,1)}, u32[]{:S(2)}) copy-start(bf16[768,448]{0,1:T(8,128)(2,1)} %param.6) | copy-start | bytes 2064388
  44.3 6.7 %collective-permute-start.8 = (bf16[2,32,448]{2,1,0:T(8,128)(2,1)S(1)}, bf16[2,32,448]{2,1,0:T(8,128)(2,1)S(1)}, u32[]{:S(2)}, u32[]{:S(2)}) collective-permute-start(bf16[2,32,448]{2,1,0:T(8,128)(2,1)S(1)} %respond.1), channel_id=1, source_target_pairs={{0,12},{1,13},{2,14},{3,15},{4,8},{5,9},{6,10},{7,11},{8,4},{9,5},... | collective-permute-start | bytes 172040 | tf_op jit(solution)/shard_map/ppermute | solution.py:393
  47.2 5.7 %collective-permute-start.7 = (bf16[2,32,448]{2,1,0:T(8,128)(2,1)S(1)}, bf16[2,32,448]{2,1,0:T(8,128)(2,1)S(1)}, u32[]{:S(2)}, u32[]{:S(2)}) collective-permute-start(bf16[2,32,448]{2,1,0:T(8,128)(2,1)S(1)} %respond.1), channel_id=1, source_target_pairs={{0,8},{1,9},{2,10},{3,11},{4,12},{5,13},{6,14},{7,15},{8,0},{9,1},... | collective-permute-start | bytes 172040 | tf_op jit(solution)/shard_map/ppermute | solution.py:393
  47.6 5.4 %collective-permute-start.6 = (bf16[2,32,448]{2,1,0:T(8,128)(2,1)S(1)}, bf16[2,32,448]{2,1,0:T(8,128)(2,1)S(1)}, u32[]{:S(2)}, u32[]{:S(2)}) collective-permute-start(bf16[2,32,448]{2,1,0:T(8,128)(2,1)S(1)} %respond.1), channel_id=1, source_target_pairs={{0,4},{1,5},{2,6},{3,7},{4,0},{5,1},{6,2},{7,3},{8,12},{9,13},{10,... | collective-permute-start | bytes 172040 | tf_op jit(solution)/shard_map/ppermute | solution.py:393
  48.7 4.3 %collective-permute-start.9 = (bf16[1,2,32,448]{3,2,1,0:T(8,128)(2,1)S(1)}, bf16[1,2,32,448]{3,2,1,0:T(8,128)(2,1)S(1)}, u32[]{:S(2)}, u32[]{:S(2)}) collective-permute-start(bf16[1,2,32,448]{3,2,1,0:T(8,128)(2,1)S(1)} %bitcast.14), channel_id=1, source_target_pairs={{0,2},{1,3},{2,0},{3,1},{4,6},{5,7},{6,4},{7,5},{8,10},{9,11},{10,... | collective-permute-start | bytes 172040 | tf_op jit(solution)/shard_map/ppermute | solution.py:393
  53.1 6.3 %collective-permute-start.10 = (bf16[3,2,32,448]{3,2,1,0:T(8,128)(2,1)S(1)}, bf16[3,2,32,448]{3,2,1,0:T(8,128)(2,1)S(1)}, u32[]{:S(2)}, u32[]{:S(2)}) collective-permute-start(bf16[3,2,32,448]{3,2,1,0:T(8,128)(2,1)S(1)} %pad_maximum_fusion.refs_1_), channel_id=1, source_target_pairs={{0,2},{1,3},{2,0},{3,1},{4,6},{5,7},{6,4},{7,5},{8,10},{9,11},{10,... | collective-permute-start | bytes 516104 | tf_op jit(solution)/shard_map/ppermute | solution.py:393
  54.7 1.8 %collective-permute-start.11 = (bf16[2,2,32,448]{3,2,1,0:T(8,128)(2,1)S(1)}, bf16[2,2,32,448]{3,2,1,0:T(8,128)(2,1)S(1)}, u32[]{:S(2)}, u32[]{:S(2)}) collective-permute-start(bf16[2,2,32,448]{3,2,1,0:T(8,128)(2,1)S(1)} %pad_maximum_fusion.1), channel_id=1, source_target_pairs={{0,1},{1,0},{2,3},{3,2},{4,5},{5,4},{6,7},{7,6},{8,9},{9,8},{10,11... | collective-permute-start | bytes 344072 | tf_op jit(solution)/shard_map/ppermute | solution.py:393
  54.8 1.8 %collective-permute-start.12 = (bf16[2,2,32,448]{3,2,1,0:T(8,128)(2,1)S(1)}, bf16[2,2,32,448]{3,2,1,0:T(8,128)(2,1)S(1)}, u32[]{:S(2)}, u32[]{:S(2)}) collective-permute-start(bf16[2,2,32,448]{3,2,1,0:T(8,128)(2,1)S(1)} %pad_maximum_fusion.2), channel_id=1, source_target_pairs={{0,1},{1,0},{2,3},{3,2},{4,5},{5,4},{6,7},{7,6},{8,9},{9,8},{10,11... | collective-permute-start | bytes 344072 | tf_op jit(solution)/shard_map/ppermute | solution.py:393
  55.2 1.3 %collective-permute-start.13 = (bf16[1,2,32,448]{3,2,1,0:T(8,128)(2,1)S(1)}, bf16[1,2,32,448]{3,2,1,0:T(8,128)(2,1)S(1)}, u32[]{:S(2)}, u32[]{:S(2)}) collective-permute-start(bf16[1,2,32,448]{3,2,1,0:T(8,128)(2,1)S(1)} %bitcast.24), channel_id=1, source_target_pairs={{0,1},{1,0},{2,3},{3,2},{4,5},{5,4},{6,7},{7,6},{8,9},{9,8},{10,11... | collective-permute-start | bytes 172040 | tf_op jit(solution)/shard_map/ppermute | solution.py:393
  59.3 1.5 %collective-permute-start.14 = (bf16[3,2,32,448]{3,2,1,0:T(8,128)(2,1)S(1)}, bf16[3,2,32,448]{3,2,1,0:T(8,128)(2,1)S(1)}, u32[]{:S(2)}, u32[]{:S(2)}) collective-permute-start(bf16[3,2,32,448]{3,2,1,0:T(8,128)(2,1)S(1)} %collective-permute-done.10.refs_1_), channel_id=1, source_target_pairs={{0,1},{1,0},{2,3},{3,2},{4,5},{5,4},{6,7},{7,6},{8,9},{9,8},{10,11... | collective-permute-start | bytes 516104 | tf_op jit(solution)/shard_map/ppermute | solution.py:393

commit v10 on v9

--- a/solution.py
+++ b/solution.py
@@ -246,7 +246,7 @@
             pltpu.VMEM((rest,) + frf.shape[1:], jnp.bfloat16),
             pltpu.SemaphoreType.DMA((rest // math.gcd(rest, 4),)),
         ],
-        compiler_params=pltpu.CompilerParams(vmem_limit_bytes=36 * MIB),
+        compiler_params=pltpu.CompilerParams(vmem_limit_bytes=16 * MIB),
         cost_estimate=pl.CostEstimate(
             flops=4 * frf.size, bytes_accessed=2 * frf.size, transcendentals=0
         ),

time: 65.5 us -> 58 us (0.89)
  Pallas kernels: 36.1 us -> 31.8 us
  local copies, waits for them, and re-layouts: 4.18 us -> 0.02 us
  waiting for transfers between devices: 8.11 us -> 9.15 us
    pallas_call x1, Pallas kernels: 13.1 us -> 8.77 us  [respond(): pl.pallas_call(functools.partial(respond_kernel, len(pieces)), in_specs=[...]
    unnamed x6 -> x4, local copies, waits for them, and re-layouts: 4.18 us -> 0.01 us
    ppermute x15, waiting for transfers between devices: 8.11 us -> 9.15 us  [swap(): return lax.ppermute(values, 'dof', pairs)]
  transfers between devices with their start and end apart: 15 -> 15, of which waited for: 6 -> 9; matrix products, arithmetic and copies ran while one was open for 0% -> 0% of each run, Pallas kernels for 17% -> 20%
where the time goes in v10:
time: 58 us; the launch traced here: 57.9 us
  Pallas kernels  31.8 us (55%)
  starting transfers between devices  16.6 us (29%)
  waiting for transfers between devices  9.15 us (16%)
    ppermute x15, starting transfers between devices, swap(): return lax.ppermute(values, 'dof', pairs)  16.6 us
    ppermute x15, waiting for transfers between devices, swap(): return lax.ppermute(values, 'dof', pairs)  9.15 us
    pallas_call x1, Pallas kernels, respond(): pl.pallas_call(functools.partial(respond_kernel, len(pieces)), in_specs=[...  8.77 us
    pallas_call x2, Pallas kernels, load(): pl.pallas_call(functools.partial(load_kernel, start), in_specs=[hbm, anyw...  8.49 us
    pallas_call x1, Pallas kernels, forward(): pl.pallas_call(forward_kernel, in_specs=[pl.BlockSpec(memory_space=pltpu....  7.09 us
    pallas_call x1, Pallas kernels, inverse(): pl.pallas_call(functools.partial(late_kernel, plan), in_specs=in_specs +...  4.51 us
    pallas_call x1, Pallas kernels, inverse(): pl.pallas_call(functools.partial(early_kernel, plan), in_specs=in_specs,...  2.8 us
  transfers between devices with their start and end apart: 15, of which 9 were waited for; matrix products, arithmetic and copies ran while one was open for 0% of the time, Pallas kernels for 20%

profile of v10, /device:TPU:0, one launch (start us, length us, event | category | flops | bytes accessed | tf_op | source)
XLA Modules:
  0.0 57.9 jit_solution(15111536548699316667)
XLA Ops:
  0.0 0.1 pad_add_fusion.place_ref
  0.1 7.1 %forward.1 = (bf16[2,4,2,32,448]{4,3,2,1,0:T(8,128)(2,1)S(1)}, bf16[2,4,2,32,448]{4,3,2,1,0:T(8,128)(2,1)S(1)}) custom-call(s32[2]{0:T(128)S(1)} %pad_add_fusion.place_ref, bf16[2,512,2048]{2,1,0:T(8,128)(2,1)} %constant.32.clone.table_ref, bf16[2,2048,768]{2,1,0:T(8,128)(2,1)} %bitcast.25, bf16[448,768]{1,0:T(8,128)(2,1)} %bitcast.11), custom_call_target="tpu_custom_call" | custom-call | flops 3925868544 | bytes 12582912 | tf_op jit(solution)/shard_map/forward/pallas_call | solution.py:116
  7.2 0.5 collective-permute-start
  7.7 1.5 %collective-permute-done = bf16[2,4,2,32,448]{4,3,2,1,0:T(8,128)(2,1)S(1)} collective-permute-done((bf16[2,4,2,32,448]{4,3,2,1,0:T(8,128)(2,1)S(1)}, bf16[2,4,2,32,448]{4,3,2,1,0:T(8,128)(2,1)S(1)}, u32[]{:S(2)}, u32[]{:S(2)}) %collective-permute-start) | collective-permute-done | bytes 458784 | tf_op jit(solution)/shard_map/ppermute | solution.py:393
  9.2 0.1 add.10
  9.4 2.9 %collective-permute-start.2 = (bf16[3,2,32,448]{3,2,1,0:T(8,128)(2,1)S(1)}, bf16[3,2,32,448]{3,2,1,0:T(8,128)(2,1)S(1)}, u32[]{:S(2)}, u32[]{:S(2)}) collective-permute-start(bf16[3,2,32,448]{3,2,1,0:T(8,128)(2,1)S(1)} %get-tuple-element.21.after_ref), channel_id=1, source_target_pairs={{0,2},{1,3},{2,0},{3,1},{4,6},{5,7},{6,4},{7,5},{8,10},{9,11},{10,... | collective-permute-start | bytes 516104 | tf_op jit(solution)/shard_map/ppermute | solution.py:393
  12.3 0.1 collective-permute-start.1
  12.4 4.2 %load.2.after_ref.refs_5_ = bf16[12,2,448,448]{3,2,1,0:T(8,128)(2,1)S(1)} custom-call(bf16[32,2,448,448]{3,2,1,0:T(8,128)(2,1)} %refs_7_.1, bf16[3,2,32,448]{3,2,1,0:T(8,128)(2,1)S(1)} %get-tuple-element.21.after_ref), custom_call_target="tpu_custom_call" | custom-call | bytes 19267584 | tf_op jit(solution)/shard_map/load/pallas_call | solution.py:161
  16.6 1.4 %collective-permute-done.2.came_ref = bf16[3,2,32,448]{3,2,1,0:T(8,128)(2,1)S(1)} collective-permute-done((bf16[3,2,32,448]{3,2,1,0:T(8,128)(2,1)S(1)}, bf16[3,2,32,448]{3,2,1,0:T(8,128)(2,1)S(1)}, u32[]{:S(2)}, u32[]{:S(2)}) %collective-permute-start.2) | collective-permute-done | bytes 172064 | tf_op jit(solution)/shard_map/ppermute | solution.py:393
  18.0 3.1 %collective-permute-start.4 = (bf16[1,2,32,448]{3,2,1,0:T(8,128)(2,1)S(1)}, bf16[1,2,32,448]{3,2,1,0:T(8,128)(2,1)S(1)}, u32[]{:S(2)}, u32[]{:S(2)}) collective-permute-start(bf16[1,2,32,448]{3,2,1,0:T(8,128)(2,1)S(1)} %get-tuple-element.23), channel_id=1, source_target_pairs={{0,8},{1,9},{2,10},{3,11},{4,12},{5,13},{6,14},{7,15},{8,0},{9,1},... | collective-permute-start | bytes 172040 | tf_op jit(solution)/shard_map/ppermute | solution.py:393
  21.1 1.3 %collective-permute-start.5 = (bf16[1,2,32,448]{3,2,1,0:T(8,128)(2,1)S(1)}, bf16[1,2,32,448]{3,2,1,0:T(8,128)(2,1)S(1)}, u32[]{:S(2)}, u32[]{:S(2)}) collective-permute-start(bf16[1,2,32,448]{3,2,1,0:T(8,128)(2,1)S(1)} %get-tuple-element.24), channel_id=1, source_target_pairs={{0,12},{1,13},{2,14},{3,15},{4,8},{5,9},{6,10},{7,11},{8,4},{9,5},... | collective-permute-start | bytes 172040 | tf_op jit(solution)/shard_map/ppermute | solution.py:393
  22.5 0.2 collective-permute-start.3
  22.7 4.2 %load.3.refs_6_ = bf16[12,2,448,448]{3,2,1,0:T(8,128)(2,1)S(1)} custom-call(bf16[32,2,448,448]{3,2,1,0:T(8,128)(2,1)} %refs_7_.1, bf16[1,2,32,448]{3,2,1,0:T(8,128)(2,1)S(1)} %get-tuple-element.22.after_ref), custom_call_target="tpu_custom_call" | custom-call | bytes 19267584 | tf_op jit(solution)/shard_map/load/pallas_call | solution.py:161
  27.0 0.0 copy-start
  27.0 0.0 copy-start.1
  27.0 0.0 collective-permute-done.1.refs_1_
  27.0 0.0 collective-permute-done.4.refs_3_
  27.0 0.3 collective-permute-done.5.refs_4_
  27.3 0.1 collective-permute-done.3.refs_2_
  27.5 8.8 %respond.1 = bf16[2,32,448]{2,1,0:T(8,128)(2,1)S(1)} custom-call(bf16[1,2,32,448]{3,2,1,0:T(8,128)(2,1)S(1)} %slice.3.refs_0_, bf16[1,2,32,448]{3,2,1,0:T(8,128)(2,1)S(1)} %collective-permute-done.1.refs_1_, bf16[1,2,32,448]{3,2,1,0:T(8,128)(2,1)S(1)} %collective-permute-done.3.refs_2_, bf16[1,2,32,448]{3,2,1,0:T(8,128)(2,1)S(1)} %collective-permute-done.4.refs_3_, ...), custom_call_target="tpu_custom_call" | custom-call | flops 51380224 | bytes 25690112 | tf_op jit(solution)/shard_map/respond/pallas_call | solution.py:239
  36.2 2.6 %collective-permute-start.8 = (bf16[2,32,448]{2,1,0:T(8,128)(2,1)S(1)}, bf16[2,32,448]{2,1,0:T(8,128)(2,1)S(1)}, u32[]{:S(2)}, u32[]{:S(2)}) collective-permute-start(bf16[2,32,448]{2,1,0:T(8,128)(2,1)S(1)} %respond.1), channel_id=1, source_target_pairs={{0,12},{1,13},{2,14},{3,15},{4,8},{5,9},{6,10},{7,11},{8,4},{9,5},... | collective-permute-start | bytes 172040 | tf_op jit(solution)/shard_map/ppermute | solution.py:393
  38.8 0.3 collective-permute-start.7
  39.2 1.5 %collective-permute-start.6 = (bf16[2,32,448]{2,1,0:T(8,128)(2,1)S(1)}, bf16[2,32,448]{2,1,0:T(8,128)(2,1)S(1)}, u32[]{:S(2)}, u32[]{:S(2)}) collective-permute-start(bf16[2,32,448]{2,1,0:T(8,128)(2,1)S(1)} %respond.1), channel_id=1, source_target_pairs={{0,4},{1,5},{2,6},{3,7},{4,0},{5,1},{6,2},{7,3},{8,12},{9,13},{10,... | collective-permute-start | bytes 172040 | tf_op jit(solution)/shard_map/ppermute | solution.py:393
  40.7 1.5 %collective-permute-start.9 = (bf16[1,2,32,448]{3,2,1,0:T(8,128)(2,1)S(1)}, bf16[1,2,32,448]{3,2,1,0:T(8,128)(2,1)S(1)}, u32[]{:S(2)}, u32[]{:S(2)}) collective-permute-start(bf16[1,2,32,448]{3,2,1,0:T(8,128)(2,1)S(1)} %bitcast.14), channel_id=1, source_target_pairs={{0,2},{1,3},{2,0},{3,1},{4,6},{5,7},{6,4},{7,5},{8,10},{9,11},{10,... | collective-permute-start | bytes 172040 | tf_op jit(solution)/shard_map/ppermute | solution.py:393
  42.2 0.3 collective-permute-done.8
  42.5 2.1 %collective-permute-done.7 = bf16[2,32,448]{2,1,0:T(8,128)(2,1)S(1)} collective-permute-done((bf16[2,32,448]{2,1,0:T(8,128)(2,1)S(1)}, bf16[2,32,448]{2,1,0:T(8,128)(2,1)S(1)}, u32[]{:S(2)}, u32[]{:S(2)}) %collective-permute-start.7) | collective-permute-done | bytes 57376 | tf_op jit(solution)/shard_map/ppermute | solution.py:393
  44.6 0.0 collective-permute-done.6
  44.6 1.0 %collective-permute-done.9.refs_0_ = bf16[1,2,32,448]{3,2,1,0:T(8,128)(2,1)S(1)} collective-permute-done((bf16[1,2,32,448]{3,2,1,0:T(8,128)(2,1)S(1)}, bf16[1,2,32,448]{3,2,1,0:T(8,128)(2,1)S(1)}, u32[]{:S(2)}, u32[]{:S(2)}) %collective-permute-start.9) | collective-permute-done | bytes 57376 | tf_op jit(solution)/shard_map/ppermute | solution.py:393
  45.7 1.5 %collective-permute-start.10 = (bf16[3,2,32,448]{3,2,1,0:T(8,128)(2,1)S(1)}, bf16[3,2,32,448]{3,2,1,0:T(8,128)(2,1)S(1)}, u32[]{:S(2)}, u32[]{:S(2)}) collective-permute-start(bf16[3,2,32,448]{3,2,1,0:T(8,128)(2,1)S(1)} %pad_maximum_fusion.refs_1_), channel_id=1, source_target_pairs={{0,2},{1,3},{2,0},{3,1},{4,6},{5,7},{6,4},{7,5},{8,10},{9,11},{10,... | collective-permute-start | bytes 516104 | tf_op jit(solution)/shard_map/ppermute | solution.py:393
  47.2 0.1 collective-permute-start.11
  47.3 0.5 collective-permute-start.12
  47.8 0.1 collective-permute-start.13
  47.9 1.2 %collective-permute-done.13.refs_4_ = bf16[1,2,32,448]{3,2,1,0:T(8,128)(2,1)S(1)} collective-permute-done((bf16[1,2,32,448]{3,2,1,0:T(8,128)(2,1)S(1)}, bf16[1,2,32,448]{3,2,1,0:T(8,128)(2,1)S(1)}, u32[]{:S(2)}, u32[]{:S(2)}) %collective-permute-start.13) | collective-permute-done | bytes 57376 | tf_op jit(solution)/shard_map/ppermute | solution.py:393
  49.0 0.0 collective-permute-done.11.refs_2_
  49.0 0.0 collective-permute-done.12.refs_3_
  49.0 0.0 copy-done
  49.0 0.0 copy-done.1
  49.1 2.8 %early.1.refs_4_ = f32[2,2048,768]{2,1,0:T(8,128)S(1)} custom-call(s32[2]{0:T(128)S(1)} %pad_add_fusion.place_ref, bf16[2,2,2048,256]{3,2,1,0:T(8,128)(2,1)S(1)} %copy-done, bf16[448,768]{1,0:T(8,128)(2,1)S(1)} %bitcast.12, bf16[1,2,32,448]{3,2,1,0:T(8,128)(2,1)S(1)} %bitcast.16, bf16[3,2,32,448]{3,2,1,0:T(8,128)(2,1)S(1)} %pad_maximum_fusion.refs_1_, ...), custom_call_target="tpu_custom_call" | custom-call | flops 1000 | bytes 1000 | tf_op jit(solution)/shard_map/early/pallas_call | solution.py:334
  51.9 0.0 collective-permute-done.10.refs_1_
  51.9 0.3 collective-permute-start.14
  52.1 1.3 %collective-permute-done.14.refs_3_ = bf16[3,2,32,448]{3,2,1,0:T(8,128)(2,1)S(1)} collective-permute-done((bf16[3,2,32,448]{3,2,1,0:T(8,128)(2,1)S(1)}, bf16[3,2,32,448]{3,2,1,0:T(8,128)(2,1)S(1)}, u32[]{:S(2)}, u32[]{:S(2)}) %collective-permute-start.14) | collective-permute-done | bytes 172064 | tf_op jit(solution)/shard_map/ppermute | solution.py:393
  53.4 4.5 %late.1 = bf16[2,2048,768]{2,1,0:T(8,128)(2,1)} custom-call(s32[2]{0:T(128)S(1)} %pad_add_fusion.place_ref, bf16[2,2,2048,256]{3,2,1,0:T(8,128)(2,1)S(1)} %copy-done, bf16[448,768]{1,0:T(8,128)(2,1)S(1)} %bitcast.13, bf16[1,2,32,448]{3,2,1,0:T(8,128)(2,1)S(1)} %collective-permute-done.9.refs_0_, bf16[3,2,32,448]{3,2,1,0:T(8,128)(2,1)S(1)} %collective-permute-done.10.refs_1_, ...), custom_call_target="tpu_custom_call" | custom-call | flops 1962934272 | bytes 8388608 | tf_op jit(solution)/shard_map/late/pallas_call | solution.py:344
  (5 shorter events, 0.1 us)
Async XLA Ops:
  7.2 2.1 %collective-permute-start = (bf16[2,4,2,32,448]{4,3,2,1,0:T(8,128)(2,1)S(1)}, bf16[2,4,2,32,448]{4,3,2,1,0:T(8,128)(2,1)S(1)}, u32[]{:S(2)}, u32[]{:S(2)}) collective-permute-start(bf16[2,4,2,32,448]{4,3,2,1,0:T(8,128)(2,1)S(1)} %get-tuple-element.18.after_ref), channel_id=1, source_target_pairs={{0,1},{1,0},{2,3},{3,2},{4,5},{5,4},{6,7},{7,6},{8,9},{9,8},{10,11... | collective-permute-start | bytes 1376264 | tf_op jit(solution)/shard_map/ppermute | solution.py:393
  9.4 8.6 %collective-permute-start.2 = (bf16[3,2,32,448]{3,2,1,0:T(8,128)(2,1)S(1)}, bf16[3,2,32,448]{3,2,1,0:T(8,128)(2,1)S(1)}, u32[]{:S(2)}, u32[]{:S(2)}) collective-permute-start(bf16[3,2,32,448]{3,2,1,0:T(8,128)(2,1)S(1)} %get-tuple-element.21.after_ref), channel_id=1, source_target_pairs={{0,2},{1,3},{2,0},{3,1},{4,6},{5,7},{6,4},{7,5},{8,10},{9,11},{10,... | collective-permute-start | bytes 516104 | tf_op jit(solution)/shard_map/ppermute | solution.py:393
  12.3 14.7 %collective-permute-start.1 = (bf16[1,2,32,448]{3,2,1,0:T(8,128)(2,1)S(1)}, bf16[1,2,32,448]{3,2,1,0:T(8,128)(2,1)S(1)}, u32[]{:S(2)}, u32[]{:S(2)}) collective-permute-start(bf16[1,2,32,448]{3,2,1,0:T(8,128)(2,1)S(1)} %get-tuple-element.20), channel_id=1, source_target_pairs={{0,2},{1,3},{2,0},{3,1},{4,6},{5,7},{6,4},{7,5},{8,10},{9,11},{10,... | collective-permute-start | bytes 172040 | tf_op jit(solution)/shard_map/ppermute | solution.py:393
  18.0 9.0 %collective-permute-start.4 = (bf16[1,2,32,448]{3,2,1,0:T(8,128)(2,1)S(1)}, bf16[1,2,32,448]{3,2,1,0:T(8,128)(2,1)S(1)}, u32[]{:S(2)}, u32[]{:S(2)}) collective-permute-start(bf16[1,2,32,448]{3,2,1,0:T(8,128)(2,1)S(1)} %get-tuple-element.23), channel_id=1, source_target_pairs={{0,8},{1,9},{2,10},{3,11},{4,12},{5,13},{6,14},{7,15},{8,0},{9,1},... | collective-permute-start | bytes 172040 | tf_op jit(solution)/shard_map/ppermute | solution.py:393
  21.1 6.2 %collective-permute-start.5 = (bf16[1,2,32,448]{3,2,1,0:T(8,128)(2,1)S(1)}, bf16[1,2,32,448]{3,2,1,0:T(8,128)(2,1)S(1)}, u32[]{:S(2)}, u32[]{:S(2)}) collective-permute-start(bf16[1,2,32,448]{3,2,1,0:T(8,128)(2,1)S(1)} %get-tuple-element.24), channel_id=1, source_target_pairs={{0,12},{1,13},{2,14},{3,15},{4,8},{5,9},{6,10},{7,11},{8,4},{9,5},... | collective-permute-start | bytes 172040 | tf_op jit(solution)/shard_map/ppermute | solution.py:393
  22.5 5.0 %collective-permute-start.3 = (bf16[1,2,32,448]{3,2,1,0:T(8,128)(2,1)S(1)}, bf16[1,2,32,448]{3,2,1,0:T(8,128)(2,1)S(1)}, u32[]{:S(2)}, u32[]{:S(2)}) collective-permute-start(bf16[1,2,32,448]{3,2,1,0:T(8,128)(2,1)S(1)} %get-tuple-element.22.after_ref), channel_id=1, source_target_pairs={{0,4},{1,5},{2,6},{3,7},{4,0},{5,1},{6,2},{7,3},{8,12},{9,13},{10,... | collective-permute-start | bytes 172040 | tf_op jit(solution)/shard_map/ppermute | solution.py:393
  27.0 22.1 %copy-start = (bf16[2,2,2048,256]{3,2,1,0:T(8,128)(2,1)S(1)}, bf16[2,2,2048,256]{3,2,1,0:T(8,128)(2,1)}, u32[]{:S(2)}) copy-start(bf16[2,2,2048,256]{3,2,1,0:T(8,128)(2,1)} %constant.33.clone.table_ref) | copy-start | bytes 12582916
  27.0 22.1 %copy-start.1 = (bf16[768,448]{0,1:T(8,128)(2,1)S(1)}, bf16[768,448]{0,1:T(8,128)(2,1)}, u32[]{:S(2)}) copy-start(bf16[768,448]{0,1:T(8,128)(2,1)} %param.6) | copy-start | bytes 2064388
  36.2 6.2 %collective-permute-start.8 = (bf16[2,32,448]{2,1,0:T(8,128)(2,1)S(1)}, bf16[2,32,448]{2,1,0:T(8,128)(2,1)S(1)}, u32[]{:S(2)}, u32[]{:S(2)}) collective-permute-start(bf16[2,32,448]{2,1,0:T(8,128)(2,1)S(1)} %respond.1), channel_id=1, source_target_pairs={{0,12},{1,13},{2,14},{3,15},{4,8},{5,9},{6,10},{7,11},{8,4},{9,5},... | collective-permute-start | bytes 172040 | tf_op jit(solution)/shard_map/ppermute | solution.py:393
  38.8 5.7 %collective-permute-start.7 = (bf16[2,32,448]{2,1,0:T(8,128)(2,1)S(1)}, bf16[2,32,448]{2,1,0:T(8,128)(2,1)S(1)}, u32[]{:S(2)}, u32[]{:S(2)}) collective-permute-start(bf16[2,32,448]{2,1,0:T(8,128)(2,1)S(1)} %respond.1), channel_id=1, source_target_pairs={{0,8},{1,9},{2,10},{3,11},{4,12},{5,13},{6,14},{7,15},{8,0},{9,1},... | collective-permute-start | bytes 172040 | tf_op jit(solution)/shard_map/ppermute | solution.py:393
  39.2 5.4 %collective-permute-start.6 = (bf16[2,32,448]{2,1,0:T(8,128)(2,1)S(1)}, bf16[2,32,448]{2,1,0:T(8,128)(2,1)S(1)}, u32[]{:S(2)}, u32[]{:S(2)}) collective-permute-start(bf16[2,32,448]{2,1,0:T(8,128)(2,1)S(1)} %respond.1), channel_id=1, source_target_pairs={{0,4},{1,5},{2,6},{3,7},{4,0},{5,1},{6,2},{7,3},{8,12},{9,13},{10,... | collective-permute-start | bytes 172040 | tf_op jit(solution)/shard_map/ppermute | solution.py:393
  40.7 5.0 %collective-permute-start.9 = (bf16[1,2,32,448]{3,2,1,0:T(8,128)(2,1)S(1)}, bf16[1,2,32,448]{3,2,1,0:T(8,128)(2,1)S(1)}, u32[]{:S(2)}, u32[]{:S(2)}) collective-permute-start(bf16[1,2,32,448]{3,2,1,0:T(8,128)(2,1)S(1)} %bitcast.14), channel_id=1, source_target_pairs={{0,2},{1,3},{2,0},{3,1},{4,6},{5,7},{6,4},{7,5},{8,10},{9,11},{10,... | collective-permute-start | bytes 172040 | tf_op jit(solution)/shard_map/ppermute | solution.py:393
  45.7 6.2 %collective-permute-start.10 = (bf16[3,2,32,448]{3,2,1,0:T(8,128)(2,1)S(1)}, bf16[3,2,32,448]{3,2,1,0:T(8,128)(2,1)S(1)}, u32[]{:S(2)}, u32[]{:S(2)}) collective-permute-start(bf16[3,2,32,448]{3,2,1,0:T(8,128)(2,1)S(1)} %pad_maximum_fusion.refs_1_), channel_id=1, source_target_pairs={{0,2},{1,3},{2,0},{3,1},{4,6},{5,7},{6,4},{7,5},{8,10},{9,11},{10,... | collective-permute-start | bytes 516104 | tf_op jit(solution)/shard_map/ppermute | solution.py:393
  47.2 1.8 %collective-permute-start.11 = (bf16[2,2,32,448]{3,2,1,0:T(8,128)(2,1)S(1)}, bf16[2,2,32,448]{3,2,1,0:T(8,128)(2,1)S(1)}, u32[]{:S(2)}, u32[]{:S(2)}) collective-permute-start(bf16[2,2,32,448]{3,2,1,0:T(8,128)(2,1)S(1)} %pad_maximum_fusion.1), channel_id=1, source_target_pairs={{0,1},{1,0},{2,3},{3,2},{4,5},{5,4},{6,7},{7,6},{8,9},{9,8},{10,11... | collective-permute-start | bytes 344072 | tf_op jit(solution)/shard_map/ppermute | solution.py:393
  47.3 1.8 %collective-permute-start.12 = (bf16[2,2,32,448]{3,2,1,0:T(8,128)(2,1)S(1)}, bf16[2,2,32,448]{3,2,1,0:T(8,128)(2,1)S(1)}, u32[]{:S(2)}, u32[]{:S(2)}) collective-permute-start(bf16[2,2,32,448]{3,2,1,0:T(8,128)(2,1)S(1)} %pad_maximum_fusion.2), channel_id=1, source_target_pairs={{0,1},{1,0},{2,3},{3,2},{4,5},{5,4},{6,7},{7,6},{8,9},{9,8},{10,11... | collective-permute-start | bytes 344072 | tf_op jit(solution)/shard_map/ppermute | solution.py:393
  47.8 1.3 %collective-permute-start.13 = (bf16[1,2,32,448]{3,2,1,0:T(8,128)(2,1)S(1)}, bf16[1,2,32,448]{3,2,1,0:T(8,128)(2,1)S(1)}, u32[]{:S(2)}, u32[]{:S(2)}) collective-permute-start(bf16[1,2,32,448]{3,2,1,0:T(8,128)(2,1)S(1)} %bitcast.24), channel_id=1, source_target_pairs={{0,1},{1,0},{2,3},{3,2},{4,5},{5,4},{6,7},{7,6},{8,9},{9,8},{10,11... | collective-permute-start | bytes 172040 | tf_op jit(solution)/shard_map/ppermute | solution.py:393
  51.9 1.5 %collective-permute-start.14 = (bf16[3,2,32,448]{3,2,1,0:T(8,128)(2,1)S(1)}, bf16[3,2,32,448]{3,2,1,0:T(8,128)(2,1)S(1)}, u32[]{:S(2)}, u32[]{:S(2)}) collective-permute-start(bf16[3,2,32,448]{3,2,1,0:T(8,128)(2,1)S(1)} %collective-permute-done.10.refs_1_), channel_id=1, source_target_pairs={{0,1},{1,0},{2,3},{3,2},{4,5},{5,4},{6,7},{7,6},{8,9},{9,8},{10,11... | collective-permute-start | bytes 516104 | tf_op jit(solution)/shard_map/ppermute | solution.py:393

commit v11 on v10

--- a/solution.py
+++ b/solution.py
@@ -407,29 +407,21 @@
     came_far, came_near = swap(there_far, 2), swap(there_near, 2)
     part0 = load(frf, 0, 3 * unit, there_far)
     pieces = add(here, came_far, 1, (1,) * (zs - 1), part0)
-    part1 = load(frf, 3 * unit, 3 * unit, pieces[0])
+    part1 = load(frf, 3 * unit, 2 * unit, pieces[0])
     came = [swap(piece, 4 * k) for k, piece in enumerate(pieces, 1)]
     response = respond([here[:1], came_near, *came], (part0, part1), frf)
 
-    own = response[None]
+    shards = [response] + [swap(response, 4 * k) for k in range(1, zs)]
+    own = jnp.stack(shards)
     over = swap(own, 2)
-    shards = [swap(response, 4 * k) for k in range(1, zs)]
-    far, over = lax.optimization_barrier((jnp.stack(shards), over))
-    over_far = swap(far, 2)
-    cut = (zs - 1) // 2
-    twin = swap(jnp.concatenate([own, over]), 1)
-    twin_far = [swap(jnp.stack(shards[:-cut]), 1), swap(jnp.stack(shards[-cut:]), 1)]
-    plan = [(0, 0, 0, 0), (2, 0, 1, 0)]
-    for k in range(1, zs):
-        at = k - 1
-        plan += [(1, at, 0, k)]
-        plan += [(3, at, 1, k) if at < zs - 1 - cut else (4, at - (zs - 1 - cut), 1, k)]
-    waves = inverse(place, inv, shapes_t, (own, far, twin, *twin_far), plan)
-    over_far, waves = lax.optimization_barrier((over_far, waves))
-    plan = [(0, 0, 0, 0), (2, 1, 1, 0)]
-    for k in range(1, zs):
-        plan += [(1, k - 1, 0, k), (3, k - 1, 1, k)]
-    out = inverse(place, inv, shapes_t, (over, over_far, twin, swap(over_far, 1)), plan, waves)
+    cut = zs // 2
+    twin = [swap(jnp.stack(half_shards), 1) for half_shards in (shards[:cut], shards[cut:])]
+    plan = [(0, k, 0, k) for k in range(zs)]
+    plan += [(1 + k // cut, k % cut, 1, k) for k in range(zs)]
+    waves = inverse(place, inv, shapes_t, (own, *twin), plan)
+    over, waves = lax.optimization_barrier((over, waves))
+    plan = [(far, k, far, k) for far in range(CORES) for k in range(zs)]
+    out = inverse(place, inv, shapes_t, (over, swap(over, 1)), plan, waves)
     return out.reshape(1, steps, dofs)
 
 

time: 58 us -> 58 us (level)
  waiting for transfers between devices: 9.15 us -> 12.5 us
  starting transfers between devices: 16.6 us -> 13.9 us
  Pallas kernels: 31.8 us -> 31 us
    ppermute x15 -> x13, waiting for transfers between devices: 9.15 us -> 12.5 us  [swap(): return lax.ppermute(values, 'dof', pairs)]
    ppermute x15 -> x13, starting transfers between devices: 16.6 us -> 13.9 us  [swap(): return lax.ppermute(values, 'dof', pairs)]
    pallas_call x2, Pallas kernels: 8.49 us -> 7.43 us  [load(): pl.pallas_call(functools.partial(load_kernel, start), in_specs=[hbm, anyw...]
  transfers between devices with their start and end apart: 15 -> 13, of which waited for: 9 -> 11; matrix products, arithmetic and copies ran while one was open for 0% -> 0% of each run, Pallas kernels for 20% -> 18%
where the time goes in v11:
time: 58 us; the launch traced here: 57.9 us
  Pallas kernels  31 us (53%)
  starting transfers between devices  13.9 us (24%)
  waiting for transfers between devices  12.5 us (22%)
    ppermute x13, starting transfers between devices, swap(): return lax.ppermute(values, 'dof', pairs)  13.9 us
    ppermute x13, waiting for transfers between devices, swap(): return lax.ppermute(values, 'dof', pairs)  12.5 us
    pallas_call x1, Pallas kernels, respond(): pl.pallas_call(functools.partial(respond_kernel, len(pieces)), in_specs=[...  8.96 us
    pallas_call x2, Pallas kernels, load(): pl.pallas_call(functools.partial(load_kernel, start), in_specs=[hbm, anyw...  7.43 us
    pallas_call x1, Pallas kernels, forward(): pl.pallas_call(forward_kernel, in_specs=[pl.BlockSpec(memory_space=pltpu....  7.09 us
    pallas_call x1, Pallas kernels, inverse(): pl.pallas_call(functools.partial(late_kernel, plan), in_specs=in_specs +...  4.53 us
    pallas_call x1, Pallas kernels, inverse(): pl.pallas_call(functools.partial(early_kernel, plan), in_specs=in_specs,...  2.82 us
  transfers between devices with their start and end apart: 13, of which 11 were waited for; matrix products, arithmetic and copies ran while one was open for 0% of the time, Pallas kernels for 18%

profile of v11, /device:TPU:0, one launch (start us, length us, event | category | flops | bytes accessed | tf_op | source)
XLA Modules:
  0.0 57.9 jit_solution(17851694886761602703)
XLA Ops:
  0.0 0.1 pad_add_fusion.place_ref
  0.1 7.1 %forward.1 = (bf16[2,4,2,32,448]{4,3,2,1,0:T(8,128)(2,1)S(1)}, bf16[2,4,2,32,448]{4,3,2,1,0:T(8,128)(2,1)S(1)}) custom-call(s32[2]{0:T(128)S(1)} %pad_add_fusion.place_ref, bf16[2,512,2048]{2,1,0:T(8,128)(2,1)} %constant.32.clone.table_ref, bf16[2,2048,768]{2,1,0:T(8,128)(2,1)} %bitcast.24, bf16[448,768]{1,0:T(8,128)(2,1)} %bitcast.11), custom_call_target="tpu_custom_call" | custom-call | flops 3925868544 | bytes 12582912 | tf_op jit(solution)/shard_map/forward/pallas_call | solution.py:116
  7.2 0.5 collective-permute-start
  7.7 1.5 %collective-permute-done = bf16[2,4,2,32,448]{4,3,2,1,0:T(8,128)(2,1)S(1)} collective-permute-done((bf16[2,4,2,32,448]{4,3,2,1,0:T(8,128)(2,1)S(1)}, bf16[2,4,2,32,448]{4,3,2,1,0:T(8,128)(2,1)S(1)}, u32[]{:S(2)}, u32[]{:S(2)}) %collective-permute-start) | collective-permute-done | bytes 458784 | tf_op jit(solution)/shard_map/ppermute | solution.py:393
  9.2 0.1 add.10
  9.4 2.9 %collective-permute-start.2 = (bf16[3,2,32,448]{3,2,1,0:T(8,128)(2,1)S(1)}, bf16[3,2,32,448]{3,2,1,0:T(8,128)(2,1)S(1)}, u32[]{:S(2)}, u32[]{:S(2)}) collective-permute-start(bf16[3,2,32,448]{3,2,1,0:T(8,128)(2,1)S(1)} %get-tuple-element.19.after_ref), channel_id=1, source_target_pairs={{0,2},{1,3},{2,0},{3,1},{4,6},{5,7},{6,4},{7,5},{8,10},{9,11},{10,... | collective-permute-start | bytes 516104 | tf_op jit(solution)/shard_map/ppermute | solution.py:393
  12.3 0.1 collective-permute-start.1
  12.4 4.2 %load.2.after_ref.refs_5_ = bf16[12,2,448,448]{3,2,1,0:T(8,128)(2,1)S(1)} custom-call(bf16[32,2,448,448]{3,2,1,0:T(8,128)(2,1)} %refs_7_.1, bf16[3,2,32,448]{3,2,1,0:T(8,128)(2,1)S(1)} %get-tuple-element.19.after_ref), custom_call_target="tpu_custom_call" | custom-call | bytes 19267584 | tf_op jit(solution)/shard_map/load/pallas_call | solution.py:161
  16.6 1.4 %collective-permute-done.2.came_ref = bf16[3,2,32,448]{3,2,1,0:T(8,128)(2,1)S(1)} collective-permute-done((bf16[3,2,32,448]{3,2,1,0:T(8,128)(2,1)S(1)}, bf16[3,2,32,448]{3,2,1,0:T(8,128)(2,1)S(1)}, u32[]{:S(2)}, u32[]{:S(2)}) %collective-permute-start.2) | collective-permute-done | bytes 172064 | tf_op jit(solution)/shard_map/ppermute | solution.py:393
  18.0 3.1 %collective-permute-start.4 = (bf16[1,2,32,448]{3,2,1,0:T(8,128)(2,1)S(1)}, bf16[1,2,32,448]{3,2,1,0:T(8,128)(2,1)S(1)}, u32[]{:S(2)}, u32[]{:S(2)}) collective-permute-start(bf16[1,2,32,448]{3,2,1,0:T(8,128)(2,1)S(1)} %get-tuple-element.21), channel_id=1, source_target_pairs={{0,8},{1,9},{2,10},{3,11},{4,12},{5,13},{6,14},{7,15},{8,0},{9,1},... | collective-permute-start | bytes 172040 | tf_op jit(solution)/shard_map/ppermute | solution.py:393
  21.1 1.4 %collective-permute-start.5 = (bf16[1,2,32,448]{3,2,1,0:T(8,128)(2,1)S(1)}, bf16[1,2,32,448]{3,2,1,0:T(8,128)(2,1)S(1)}, u32[]{:S(2)}, u32[]{:S(2)}) collective-permute-start(bf16[1,2,32,448]{3,2,1,0:T(8,128)(2,1)S(1)} %get-tuple-element.22), channel_id=1, source_target_pairs={{0,12},{1,13},{2,14},{3,15},{4,8},{5,9},{6,10},{7,11},{8,4},{9,5},... | collective-permute-start | bytes 172040 | tf_op jit(solution)/shard_map/ppermute | solution.py:393
  22.5 0.2 collective-permute-start.3
  22.7 3.2 %load.3.refs_6_ = bf16[8,2,448,448]{3,2,1,0:T(8,128)(2,1)S(1)} custom-call(bf16[32,2,448,448]{3,2,1,0:T(8,128)(2,1)} %refs_7_.1, bf16[1,2,32,448]{3,2,1,0:T(8,128)(2,1)S(1)} %get-tuple-element.20.after_ref), custom_call_target="tpu_custom_call" | custom-call | bytes 12845056 | tf_op jit(solution)/shard_map/load/pallas_call | solution.py:161
  25.9 0.0 copy-start
  25.9 0.0 copy-start.1
  25.9 0.0 collective-permute-done.1.refs_1_
  26.0 0.0 collective-permute-done.4.refs_3_
  26.0 1.3 %collective-permute-done.5.refs_4_ = bf16[1,2,32,448]{3,2,1,0:T(8,128)(2,1)S(1)} collective-permute-done((bf16[1,2,32,448]{3,2,1,0:T(8,128)(2,1)S(1)}, bf16[1,2,32,448]{3,2,1,0:T(8,128)(2,1)S(1)}, u32[]{:S(2)}, u32[]{:S(2)}) %collective-permute-start.5) | collective-permute-done | bytes 57376 | tf_op jit(solution)/shard_map/ppermute | solution.py:393
  27.3 0.1 collective-permute-done.3.refs_2_
  27.5 9.0 %respond.1 = bf16[2,32,448]{2,1,0:T(8,128)(2,1)S(1)} custom-call(bf16[1,2,32,448]{3,2,1,0:T(8,128)(2,1)S(1)} %slice.3.refs_0_, bf16[1,2,32,448]{3,2,1,0:T(8,128)(2,1)S(1)} %collective-permute-done.1.refs_1_, bf16[1,2,32,448]{3,2,1,0:T(8,128)(2,1)S(1)} %collective-permute-done.3.refs_2_, bf16[1,2,32,448]{3,2,1,0:T(8,128)(2,1)S(1)} %collective-permute-done.4.refs_3_, ...), custom_call_target="tpu_custom_call" | custom-call | flops 51380224 | bytes 25690112 | tf_op jit(solution)/shard_map/respond/pallas_call | solution.py:239
  36.4 0.4 collective-permute-start.6
  36.8 2.5 %collective-permute-start.8 = (bf16[2,32,448]{2,1,0:T(8,128)(2,1)S(1)}, bf16[2,32,448]{2,1,0:T(8,128)(2,1)S(1)}, u32[]{:S(2)}, u32[]{:S(2)}) collective-permute-start(bf16[2,32,448]{2,1,0:T(8,128)(2,1)S(1)} %respond.1), channel_id=1, source_target_pairs={{0,12},{1,13},{2,14},{3,15},{4,8},{5,9},{6,10},{7,11},{8,4},{9,5},... | collective-permute-start | bytes 172040 | tf_op jit(solution)/shard_map/ppermute | solution.py:393
  39.4 0.6 %collective-permute-start.7 = (bf16[2,32,448]{2,1,0:T(8,128)(2,1)S(1)}, bf16[2,32,448]{2,1,0:T(8,128)(2,1)S(1)}, u32[]{:S(2)}, u32[]{:S(2)}) collective-permute-start(bf16[2,32,448]{2,1,0:T(8,128)(2,1)S(1)} %respond.1), channel_id=1, source_target_pairs={{0,8},{1,9},{2,10},{3,11},{4,12},{5,13},{6,14},{7,15},{8,0},{9,1},... | collective-permute-start | bytes 172040 | tf_op jit(solution)/shard_map/ppermute | solution.py:393
  40.0 0.8 %collective-permute-done.6 = bf16[2,32,448]{2,1,0:T(8,128)(2,1)S(1)} collective-permute-done((bf16[2,32,448]{2,1,0:T(8,128)(2,1)S(1)}, bf16[2,32,448]{2,1,0:T(8,128)(2,1)S(1)}, u32[]{:S(2)}, u32[]{:S(2)}) %collective-permute-start.6) | collective-permute-done | bytes 57376 | tf_op jit(solution)/shard_map/ppermute | solution.py:393
  40.8 2.2 %collective-permute-done.8 = bf16[2,32,448]{2,1,0:T(8,128)(2,1)S(1)} collective-permute-done((bf16[2,32,448]{2,1,0:T(8,128)(2,1)S(1)}, bf16[2,32,448]{2,1,0:T(8,128)(2,1)S(1)}, u32[]{:S(2)}, u32[]{:S(2)}) %collective-permute-start.8) | collective-permute-done | bytes 57376 | tf_op jit(solution)/shard_map/ppermute | solution.py:393
  43.0 2.2 %collective-permute-done.7 = bf16[2,32,448]{2,1,0:T(8,128)(2,1)S(1)} collective-permute-done((bf16[2,32,448]{2,1,0:T(8,128)(2,1)S(1)}, bf16[2,32,448]{2,1,0:T(8,128)(2,1)S(1)}, u32[]{:S(2)}, u32[]{:S(2)}) %collective-permute-start.7) | collective-permute-done | bytes 57376 | tf_op jit(solution)/shard_map/ppermute | solution.py:393
  45.2 1.6 %collective-permute-start.9 = (bf16[4,2,32,448]{3,2,1,0:T(8,128)(2,1)S(1)}, bf16[4,2,32,448]{3,2,1,0:T(8,128)(2,1)S(1)}, u32[]{:S(2)}, u32[]{:S(2)}) collective-permute-start(bf16[4,2,32,448]{3,2,1,0:T(8,128)(2,1)S(1)} %pad_maximum_fusion.refs_0_), channel_id=1, source_target_pairs={{0,2},{1,3},{2,0},{3,1},{4,6},{5,7},{6,4},{7,5},{8,10},{9,11},{10,... | collective-permute-start | bytes 688136 | tf_op jit(solution)/shard_map/ppermute | solution.py:393
  46.8 0.1 collective-permute-start.11
  46.9 0.5 collective-permute-start.10
  47.4 0.8 %collective-permute-done.11.refs_2_ = bf16[2,2,32,448]{3,2,1,0:T(8,128)(2,1)S(1)} collective-permute-done((bf16[2,2,32,448]{3,2,1,0:T(8,128)(2,1)S(1)}, bf16[2,2,32,448]{3,2,1,0:T(8,128)(2,1)S(1)}, u32[]{:S(2)}, u32[]{:S(2)}) %collective-permute-start.11) | collective-permute-done | bytes 114720 | tf_op jit(solution)/shard_map/ppermute | solution.py:393
  48.2 0.2 collective-permute-done.10.refs_1_
  48.4 0.0 copy-done
  48.4 0.0 copy-done.1
  48.4 2.8 %early.1.refs_2_ = f32[2,2048,768]{2,1,0:T(8,128)S(1)} custom-call(s32[2]{0:T(128)S(1)} %pad_add_fusion.place_ref, bf16[2,2,2048,256]{3,2,1,0:T(8,128)(2,1)S(1)} %copy-done, bf16[448,768]{1,0:T(8,128)(2,1)S(1)} %bitcast.12, bf16[4,2,32,448]{3,2,1,0:T(8,128)(2,1)S(1)} %pad_maximum_fusion.refs_0_, bf16[2,2,32,448]{3,2,1,0:T(8,128)(2,1)S(1)} %collective-permute-done.10.refs_1_, ...), custom_call_target="tpu_custom_call" | custom-call | flops 1000 | bytes 1000 | tf_op jit(solution)/shard_map/early/pallas_call | solution.py:334
  51.3 0.4 collective-permute-done.9.refs_0_
  51.7 0.0 collective-permute-start.12
  51.7 1.5 %collective-permute-done.12.refs_1_ = bf16[4,2,32,448]{3,2,1,0:T(8,128)(2,1)S(1)} collective-permute-done((bf16[4,2,32,448]{3,2,1,0:T(8,128)(2,1)S(1)}, bf16[4,2,32,448]{3,2,1,0:T(8,128)(2,1)S(1)}, u32[]{:S(2)}, u32[]{:S(2)}) %collective-permute-start.12) | collective-permute-done | bytes 229408 | tf_op jit(solution)/shard_map/ppermute | solution.py:393
  53.2 4.5 %late.1 = bf16[2,2048,768]{2,1,0:T(8,128)(2,1)} custom-call(s32[2]{0:T(128)S(1)} %pad_add_fusion.place_ref, bf16[2,2,2048,256]{3,2,1,0:T(8,128)(2,1)S(1)} %copy-done, bf16[448,768]{1,0:T(8,128)(2,1)S(1)} %bitcast.13, bf16[4,2,32,448]{3,2,1,0:T(8,128)(2,1)S(1)} %collective-permute-done.9.refs_0_, bf16[4,2,32,448]{3,2,1,0:T(8,128)(2,1)S(1)} %collective-permute-done.12.refs_1_, ...), custom_call_target="tpu_custom_call" | custom-call | flops 1962934272 | bytes 8388608 | tf_op jit(solution)/shard_map/late/pallas_call | solution.py:344
  (5 shorter events, 0.1 us)
Async XLA Ops:
  7.2 2.1 %collective-permute-start = (bf16[2,4,2,32,448]{4,3,2,1,0:T(8,128)(2,1)S(1)}, bf16[2,4,2,32,448]{4,3,2,1,0:T(8,128)(2,1)S(1)}, u32[]{:S(2)}, u32[]{:S(2)}) collective-permute-start(bf16[2,4,2,32,448]{4,3,2,1,0:T(8,128)(2,1)S(1)} %get-tuple-element.16.after_ref), channel_id=1, source_target_pairs={{0,1},{1,0},{2,3},{3,2},{4,5},{5,4},{6,7},{7,6},{8,9},{9,8},{10,11... | collective-permute-start | bytes 1376264 | tf_op jit(solution)/shard_map/ppermute | solution.py:393
  9.4 8.6 %collective-permute-start.2 = (bf16[3,2,32,448]{3,2,1,0:T(8,128)(2,1)S(1)}, bf16[3,2,32,448]{3,2,1,0:T(8,128)(2,1)S(1)}, u32[]{:S(2)}, u32[]{:S(2)}) collective-permute-start(bf16[3,2,32,448]{3,2,1,0:T(8,128)(2,1)S(1)} %get-tuple-element.19.after_ref), channel_id=1, source_target_pairs={{0,2},{1,3},{2,0},{3,1},{4,6},{5,7},{6,4},{7,5},{8,10},{9,11},{10,... | collective-permute-start | bytes 516104 | tf_op jit(solution)/shard_map/ppermute | solution.py:393
  12.3 13.6 %collective-permute-start.1 = (bf16[1,2,32,448]{3,2,1,0:T(8,128)(2,1)S(1)}, bf16[1,2,32,448]{3,2,1,0:T(8,128)(2,1)S(1)}, u32[]{:S(2)}, u32[]{:S(2)}) collective-permute-start(bf16[1,2,32,448]{3,2,1,0:T(8,128)(2,1)S(1)} %get-tuple-element.18), channel_id=1, source_target_pairs={{0,2},{1,3},{2,0},{3,1},{4,6},{5,7},{6,4},{7,5},{8,10},{9,11},{10,... | collective-permute-start | bytes 172040 | tf_op jit(solution)/shard_map/ppermute | solution.py:393
  18.0 7.9 %collective-permute-start.4 = (bf16[1,2,32,448]{3,2,1,0:T(8,128)(2,1)S(1)}, bf16[1,2,32,448]{3,2,1,0:T(8,128)(2,1)S(1)}, u32[]{:S(2)}, u32[]{:S(2)}) collective-permute-start(bf16[1,2,32,448]{3,2,1,0:T(8,128)(2,1)S(1)} %get-tuple-element.21), channel_id=1, source_target_pairs={{0,8},{1,9},{2,10},{3,11},{4,12},{5,13},{6,14},{7,15},{8,0},{9,1},... | collective-permute-start | bytes 172040 | tf_op jit(solution)/shard_map/ppermute | solution.py:393
  21.1 6.2 %collective-permute-start.5 = (bf16[1,2,32,448]{3,2,1,0:T(8,128)(2,1)S(1)}, bf16[1,2,32,448]{3,2,1,0:T(8,128)(2,1)S(1)}, u32[]{:S(2)}, u32[]{:S(2)}) collective-permute-start(bf16[1,2,32,448]{3,2,1,0:T(8,128)(2,1)S(1)} %get-tuple-element.22), channel_id=1, source_target_pairs={{0,12},{1,13},{2,14},{3,15},{4,8},{5,9},{6,10},{7,11},{8,4},{9,5},... | collective-permute-start | bytes 172040 | tf_op jit(solution)/shard_map/ppermute | solution.py:393
  22.5 5.0 %collective-permute-start.3 = (bf16[1,2,32,448]{3,2,1,0:T(8,128)(2,1)S(1)}, bf16[1,2,32,448]{3,2,1,0:T(8,128)(2,1)S(1)}, u32[]{:S(2)}, u32[]{:S(2)}) collective-permute-start(bf16[1,2,32,448]{3,2,1,0:T(8,128)(2,1)S(1)} %get-tuple-element.20.after_ref), channel_id=1, source_target_pairs={{0,4},{1,5},{2,6},{3,7},{4,0},{5,1},{6,2},{7,3},{8,12},{9,13},{10,... | collective-permute-start | bytes 172040 | tf_op jit(solution)/shard_map/ppermute | solution.py:393
  25.9 22.5 %copy-start = (bf16[2,2,2048,256]{3,2,1,0:T(8,128)(2,1)S(1)}, bf16[2,2,2048,256]{3,2,1,0:T(8,128)(2,1)}, u32[]{:S(2)}) copy-start(bf16[2,2,2048,256]{3,2,1,0:T(8,128)(2,1)} %constant.33.clone.table_ref) | copy-start | bytes 12582916
  25.9 22.5 %copy-start.1 = (bf16[768,448]{0,1:T(8,128)(2,1)S(1)}, bf16[768,448]{0,1:T(8,128)(2,1)}, u32[]{:S(2)}) copy-start(bf16[768,448]{0,1:T(8,128)(2,1)} %param.6) | copy-start | bytes 2064388
  36.4 4.3 %collective-permute-start.6 = (bf16[2,32,448]{2,1,0:T(8,128)(2,1)S(1)}, bf16[2,32,448]{2,1,0:T(8,128)(2,1)S(1)}, u32[]{:S(2)}, u32[]{:S(2)}) collective-permute-start(bf16[2,32,448]{2,1,0:T(8,128)(2,1)S(1)} %respond.1), channel_id=1, source_target_pairs={{0,4},{1,5},{2,6},{3,7},{4,0},{5,1},{6,2},{7,3},{8,12},{9,13},{10,... | collective-permute-start | bytes 172040 | tf_op jit(solution)/shard_map/ppermute | solution.py:393
  36.8 6.2 %collective-permute-start.8 = (bf16[2,32,448]{2,1,0:T(8,128)(2,1)S(1)}, bf16[2,32,448]{2,1,0:T(8,128)(2,1)S(1)}, u32[]{:S(2)}, u32[]{:S(2)}) collective-permute-start(bf16[2,32,448]{2,1,0:T(8,128)(2,1)S(1)} %respond.1), channel_id=1, source_target_pairs={{0,12},{1,13},{2,14},{3,15},{4,8},{5,9},{6,10},{7,11},{8,4},{9,5},... | collective-permute-start | bytes 172040 | tf_op jit(solution)/shard_map/ppermute | solution.py:393
  39.4 5.8 %collective-permute-start.7 = (bf16[2,32,448]{2,1,0:T(8,128)(2,1)S(1)}, bf16[2,32,448]{2,1,0:T(8,128)(2,1)S(1)}, u32[]{:S(2)}, u32[]{:S(2)}) collective-permute-start(bf16[2,32,448]{2,1,0:T(8,128)(2,1)S(1)} %respond.1), channel_id=1, source_target_pairs={{0,8},{1,9},{2,10},{3,11},{4,12},{5,13},{6,14},{7,15},{8,0},{9,1},... | collective-permute-start | bytes 172040 | tf_op jit(solution)/shard_map/ppermute | solution.py:393
  45.2 6.4 %collective-permute-start.9 = (bf16[4,2,32,448]{3,2,1,0:T(8,128)(2,1)S(1)}, bf16[4,2,32,448]{3,2,1,0:T(8,128)(2,1)S(1)}, u32[]{:S(2)}, u32[]{:S(2)}) collective-permute-start(bf16[4,2,32,448]{3,2,1,0:T(8,128)(2,1)S(1)} %pad_maximum_fusion.refs_0_), channel_id=1, source_target_pairs={{0,2},{1,3},{2,0},{3,1},{4,6},{5,7},{6,4},{7,5},{8,10},{9,11},{10,... | collective-permute-start | bytes 688136 | tf_op jit(solution)/shard_map/ppermute | solution.py:393
  46.8 1.4 %collective-permute-start.11 = (bf16[2,2,32,448]{3,2,1,0:T(8,128)(2,1)S(1)}, bf16[2,2,32,448]{3,2,1,0:T(8,128)(2,1)S(1)}, u32[]{:S(2)}, u32[]{:S(2)}) collective-permute-start(bf16[2,2,32,448]{3,2,1,0:T(8,128)(2,1)S(1)} %pad_maximum_fusion.2), channel_id=1, source_target_pairs={{0,1},{1,0},{2,3},{3,2},{4,5},{5,4},{6,7},{7,6},{8,9},{9,8},{10,11... | collective-permute-start | bytes 344072 | tf_op jit(solution)/shard_map/ppermute | solution.py:393
  46.9 1.5 %collective-permute-start.10 = (bf16[2,2,32,448]{3,2,1,0:T(8,128)(2,1)S(1)}, bf16[2,2,32,448]{3,2,1,0:T(8,128)(2,1)S(1)}, u32[]{:S(2)}, u32[]{:S(2)}) collective-permute-start(bf16[2,2,32,448]{3,2,1,0:T(8,128)(2,1)S(1)} %pad_maximum_fusion.1), channel_id=1, source_target_pairs={{0,1},{1,0},{2,3},{3,2},{4,5},{5,4},{6,7},{7,6},{8,9},{9,8},{10,11... | collective-permute-start | bytes 344072 | tf_op jit(solution)/shard_map/ppermute | solution.py:393
  51.7 1.5 %collective-permute-start.12 = (bf16[4,2,32,448]{3,2,1,0:T(8,128)(2,1)S(1)}, bf16[4,2,32,448]{3,2,1,0:T(8,128)(2,1)S(1)}, u32[]{:S(2)}, u32[]{:S(2)}) collective-permute-start(bf16[4,2,32,448]{3,2,1,0:T(8,128)(2,1)S(1)} %collective-permute-done.9.refs_0_), channel_id=1, source_target_pairs={{0,1},{1,0},{2,3},{3,2},{4,5},{5,4},{6,7},{7,6},{8,9},{9,8},{10,11... | collective-permute-start | bytes 688136 | tf_op jit(solution)/shard_map/ppermute | solution.py:393

commit v12 on v11

--- a/solution.py
+++ b/solution.py
@@ -210,19 +210,18 @@
     base = 0
     for part in parts:
 
-        @pl.loop(0, part.shape[0], unroll=math.gcd(4, part.shape[0]))
+        @pl.loop(0, part.shape[0], unroll=part.shape[0])
         def _(step, part=part, base=base):
             multiply(part, step, base + step)
 
         base += part.shape[0]
 
-    each = rest_ref.shape[0] // len(copies)
-    for n, copy in enumerate(copies):
+    for copy in copies:
         copy.wait()
 
-        @pl.loop(n * each, (n + 1) * each, unroll=each)
-        def _(step):
-            multiply(rest_ref, step, held + step)
+    @pl.loop(0, rest_ref.shape[0], unroll=rest_ref.shape[0])
+    def _(step):
+        multiply(rest_ref, step, held + step)
 
     for f in range(rows):
         at = place(f)

time: 58 us -> 59.9 us (1.033)
  Pallas kernels: 31 us -> 33 us
    pallas_call x1, Pallas kernels: 8.96 us -> 11 us  [respond(): pl.pallas_call(functools.partial(respond_kernel, len(pieces)), in_specs=[...]
  transfers between devices with their start and end apart: 13 -> 13, of which waited for: 11 -> 11; matrix products, arithmetic and copies ran while one was open for 0% -> 0% of each run, Pallas kernels for 18% -> 17%
where the time goes in v12:
time: 59.9 us; the launch traced here: 59.7 us
  Pallas kernels  33 us (55%)
  starting transfers between devices  13.9 us (23%)
  waiting for transfers between devices  12.5 us (21%)
    ppermute x13, starting transfers between devices, swap(): return lax.ppermute(values, 'dof', pairs)  13.9 us
    ppermute x13, waiting for transfers between devices, swap(): return lax.ppermute(values, 'dof', pairs)  12.5 us
    pallas_call x1, Pallas kernels, respond(): pl.pallas_call(functools.partial(respond_kernel, len(pieces)), in_specs=[...  11 us
    pallas_call x2, Pallas kernels, load(): pl.pallas_call(functools.partial(load_kernel, start), in_specs=[hbm, anyw...  7.43 us
    pallas_call x1, Pallas kernels, forward(): pl.pallas_call(forward_kernel, in_specs=[pl.BlockSpec(memory_space=pltpu....  7.09 us
    pallas_call x1, Pallas kernels, inverse(): pl.pallas_call(functools.partial(late_kernel, plan), in_specs=in_specs +...  4.53 us
    pallas_call x1, Pallas kernels, inverse(): pl.pallas_call(functools.partial(early_kernel, plan), in_specs=in_specs,...  2.81 us
  transfers between devices with their start and end apart: 13, of which 11 were waited for; matrix products, arithmetic and copies ran while one was open for 0% of the time, Pallas kernels for 17%

profile of v12, /device:TPU:0, one launch (start us, length us, event | category | flops | bytes accessed | tf_op | source)
XLA Modules:
  0.0 59.7 jit_solution(13066637591793430032)
XLA Ops:
  0.0 0.1 pad_add_fusion.place_ref
  0.1 7.1 %forward.1 = (bf16[2,4,2,32,448]{4,3,2,1,0:T(8,128)(2,1)S(1)}, bf16[2,4,2,32,448]{4,3,2,1,0:T(8,128)(2,1)S(1)}) custom-call(s32[2]{0:T(128)S(1)} %pad_add_fusion.place_ref, bf16[2,512,2048]{2,1,0:T(8,128)(2,1)} %constant.32.clone.table_ref, bf16[2,2048,768]{2,1,0:T(8,128)(2,1)} %bitcast.24, bf16[448,768]{1,0:T(8,128)(2,1)} %bitcast.11), custom_call_target="tpu_custom_call" | custom-call | flops 3925868544 | bytes 12582912 | tf_op jit(solution)/shard_map/forward/pallas_call | solution.py:116
  7.2 0.5 collective-permute-start
  7.7 1.5 %collective-permute-done = bf16[2,4,2,32,448]{4,3,2,1,0:T(8,128)(2,1)S(1)} collective-permute-done((bf16[2,4,2,32,448]{4,3,2,1,0:T(8,128)(2,1)S(1)}, bf16[2,4,2,32,448]{4,3,2,1,0:T(8,128)(2,1)S(1)}, u32[]{:S(2)}, u32[]{:S(2)}) %collective-permute-start) | collective-permute-done | bytes 458784 | tf_op jit(solution)/shard_map/ppermute | solution.py:392
  9.2 0.1 add.10
  9.4 2.9 %collective-permute-start.2 = (bf16[3,2,32,448]{3,2,1,0:T(8,128)(2,1)S(1)}, bf16[3,2,32,448]{3,2,1,0:T(8,128)(2,1)S(1)}, u32[]{:S(2)}, u32[]{:S(2)}) collective-permute-start(bf16[3,2,32,448]{3,2,1,0:T(8,128)(2,1)S(1)} %get-tuple-element.19.after_ref), channel_id=1, source_target_pairs={{0,2},{1,3},{2,0},{3,1},{4,6},{5,7},{6,4},{7,5},{8,10},{9,11},{10,... | collective-permute-start | bytes 516104 | tf_op jit(solution)/shard_map/ppermute | solution.py:392
  12.3 0.1 collective-permute-start.1
  12.4 4.2 %load.2.after_ref.refs_5_ = bf16[12,2,448,448]{3,2,1,0:T(8,128)(2,1)S(1)} custom-call(bf16[32,2,448,448]{3,2,1,0:T(8,128)(2,1)} %refs_7_.1, bf16[3,2,32,448]{3,2,1,0:T(8,128)(2,1)S(1)} %get-tuple-element.19.after_ref), custom_call_target="tpu_custom_call" | custom-call | bytes 19267584 | tf_op jit(solution)/shard_map/load/pallas_call | solution.py:161
  16.6 1.4 %collective-permute-done.2.came_ref = bf16[3,2,32,448]{3,2,1,0:T(8,128)(2,1)S(1)} collective-permute-done((bf16[3,2,32,448]{3,2,1,0:T(8,128)(2,1)S(1)}, bf16[3,2,32,448]{3,2,1,0:T(8,128)(2,1)S(1)}, u32[]{:S(2)}, u32[]{:S(2)}) %collective-permute-start.2) | collective-permute-done | bytes 172064 | tf_op jit(solution)/shard_map/ppermute | solution.py:392
  18.0 3.1 %collective-permute-start.4 = (bf16[1,2,32,448]{3,2,1,0:T(8,128)(2,1)S(1)}, bf16[1,2,32,448]{3,2,1,0:T(8,128)(2,1)S(1)}, u32[]{:S(2)}, u32[]{:S(2)}) collective-permute-start(bf16[1,2,32,448]{3,2,1,0:T(8,128)(2,1)S(1)} %get-tuple-element.21), channel_id=1, source_target_pairs={{0,8},{1,9},{2,10},{3,11},{4,12},{5,13},{6,14},{7,15},{8,0},{9,1},... | collective-permute-start | bytes 172040 | tf_op jit(solution)/shard_map/ppermute | solution.py:392
  21.1 1.3 %collective-permute-start.5 = (bf16[1,2,32,448]{3,2,1,0:T(8,128)(2,1)S(1)}, bf16[1,2,32,448]{3,2,1,0:T(8,128)(2,1)S(1)}, u32[]{:S(2)}, u32[]{:S(2)}) collective-permute-start(bf16[1,2,32,448]{3,2,1,0:T(8,128)(2,1)S(1)} %get-tuple-element.22), channel_id=1, source_target_pairs={{0,12},{1,13},{2,14},{3,15},{4,8},{5,9},{6,10},{7,11},{8,4},{9,5},... | collective-permute-start | bytes 172040 | tf_op jit(solution)/shard_map/ppermute | solution.py:392
  22.5 0.2 collective-permute-start.3
  22.7 3.2 %load.3.refs_6_ = bf16[8,2,448,448]{3,2,1,0:T(8,128)(2,1)S(1)} custom-call(bf16[32,2,448,448]{3,2,1,0:T(8,128)(2,1)} %refs_7_.1, bf16[1,2,32,448]{3,2,1,0:T(8,128)(2,1)S(1)} %get-tuple-element.20.after_ref), custom_call_target="tpu_custom_call" | custom-call | bytes 12845056 | tf_op jit(solution)/shard_map/load/pallas_call | solution.py:161
  25.9 0.0 copy-start
  25.9 0.0 copy-start.1
  25.9 0.0 collective-permute-done.1.refs_1_
  26.0 0.0 collective-permute-done.4.refs_3_
  26.0 1.3 %collective-permute-done.5.refs_4_ = bf16[1,2,32,448]{3,2,1,0:T(8,128)(2,1)S(1)} collective-permute-done((bf16[1,2,32,448]{3,2,1,0:T(8,128)(2,1)S(1)}, bf16[1,2,32,448]{3,2,1,0:T(8,128)(2,1)S(1)}, u32[]{:S(2)}, u32[]{:S(2)}) %collective-permute-start.5) | collective-permute-done | bytes 57376 | tf_op jit(solution)/shard_map/ppermute | solution.py:392
  27.3 0.1 collective-permute-done.3.refs_2_
  27.5 11.0 %respond.1 = bf16[2,32,448]{2,1,0:T(8,128)(2,1)S(1)} custom-call(bf16[1,2,32,448]{3,2,1,0:T(8,128)(2,1)S(1)} %slice.3.refs_0_, bf16[1,2,32,448]{3,2,1,0:T(8,128)(2,1)S(1)} %collective-permute-done.1.refs_1_, bf16[1,2,32,448]{3,2,1,0:T(8,128)(2,1)S(1)} %collective-permute-done.3.refs_2_, bf16[1,2,32,448]{3,2,1,0:T(8,128)(2,1)S(1)} %collective-permute-done.4.refs_3_, ...), custom_call_target="tpu_custom_call" | custom-call | flops 51380224 | bytes 25690112 | tf_op jit(solution)/shard_map/respond/pallas_call | solution.py:238
  38.4 0.4 collective-permute-start.6
  38.8 2.5 %collective-permute-start.8 = (bf16[2,32,448]{2,1,0:T(8,128)(2,1)S(1)}, bf16[2,32,448]{2,1,0:T(8,128)(2,1)S(1)}, u32[]{:S(2)}, u32[]{:S(2)}) collective-permute-start(bf16[2,32,448]{2,1,0:T(8,128)(2,1)S(1)} %respond.1), channel_id=1, source_target_pairs={{0,12},{1,13},{2,14},{3,15},{4,8},{5,9},{6,10},{7,11},{8,4},{9,5},... | collective-permute-start | bytes 172040 | tf_op jit(solution)/shard_map/ppermute | solution.py:392
  41.4 0.6 %collective-permute-start.7 = (bf16[2,32,448]{2,1,0:T(8,128)(2,1)S(1)}, bf16[2,32,448]{2,1,0:T(8,128)(2,1)S(1)}, u32[]{:S(2)}, u32[]{:S(2)}) collective-permute-start(bf16[2,32,448]{2,1,0:T(8,128)(2,1)S(1)} %respond.1), channel_id=1, source_target_pairs={{0,8},{1,9},{2,10},{3,11},{4,12},{5,13},{6,14},{7,15},{8,0},{9,1},... | collective-permute-start | bytes 172040 | tf_op jit(solution)/shard_map/ppermute | solution.py:392
  42.0 0.8 %collective-permute-done.6 = bf16[2,32,448]{2,1,0:T(8,128)(2,1)S(1)} collective-permute-done((bf16[2,32,448]{2,1,0:T(8,128)(2,1)S(1)}, bf16[2,32,448]{2,1,0:T(8,128)(2,1)S(1)}, u32[]{:S(2)}, u32[]{:S(2)}) %collective-permute-start.6) | collective-permute-done | bytes 57376 | tf_op jit(solution)/shard_map/ppermute | solution.py:392
  42.8 2.2 %collective-permute-done.8 = bf16[2,32,448]{2,1,0:T(8,128)(2,1)S(1)} collective-permute-done((bf16[2,32,448]{2,1,0:T(8,128)(2,1)S(1)}, bf16[2,32,448]{2,1,0:T(8,128)(2,1)S(1)}, u32[]{:S(2)}, u32[]{:S(2)}) %collective-permute-start.8) | collective-permute-done | bytes 57376 | tf_op jit(solution)/shard_map/ppermute | solution.py:392
  45.0 2.2 %collective-permute-done.7 = bf16[2,32,448]{2,1,0:T(8,128)(2,1)S(1)} collective-permute-done((bf16[2,32,448]{2,1,0:T(8,128)(2,1)S(1)}, bf16[2,32,448]{2,1,0:T(8,128)(2,1)S(1)}, u32[]{:S(2)}, u32[]{:S(2)}) %collective-permute-start.7) | collective-permute-done | bytes 57376 | tf_op jit(solution)/shard_map/ppermute | solution.py:392
  47.2 1.6 %collective-permute-start.9 = (bf16[4,2,32,448]{3,2,1,0:T(8,128)(2,1)S(1)}, bf16[4,2,32,448]{3,2,1,0:T(8,128)(2,1)S(1)}, u32[]{:S(2)}, u32[]{:S(2)}) collective-permute-start(bf16[4,2,32,448]{3,2,1,0:T(8,128)(2,1)S(1)} %pad_maximum_fusion.refs_0_), channel_id=1, source_target_pairs={{0,2},{1,3},{2,0},{3,1},{4,6},{5,7},{6,4},{7,5},{8,10},{9,11},{10,... | collective-permute-start | bytes 688136 | tf_op jit(solution)/shard_map/ppermute | solution.py:392
  48.8 0.1 collective-permute-start.11
  48.9 0.5 collective-permute-start.10
  49.4 0.8 %collective-permute-done.11.refs_2_ = bf16[2,2,32,448]{3,2,1,0:T(8,128)(2,1)S(1)} collective-permute-done((bf16[2,2,32,448]{3,2,1,0:T(8,128)(2,1)S(1)}, bf16[2,2,32,448]{3,2,1,0:T(8,128)(2,1)S(1)}, u32[]{:S(2)}, u32[]{:S(2)}) %collective-permute-start.11) | collective-permute-done | bytes 114720 | tf_op jit(solution)/shard_map/ppermute | solution.py:392
  50.2 0.2 collective-permute-done.10.refs_1_
  50.4 0.0 copy-done
  50.4 0.0 copy-done.1
  50.4 2.8 %early.1.refs_2_ = f32[2,2048,768]{2,1,0:T(8,128)S(1)} custom-call(s32[2]{0:T(128)S(1)} %pad_add_fusion.place_ref, bf16[2,2,2048,256]{3,2,1,0:T(8,128)(2,1)S(1)} %copy-done, bf16[448,768]{1,0:T(8,128)(2,1)S(1)} %bitcast.12, bf16[4,2,32,448]{3,2,1,0:T(8,128)(2,1)S(1)} %pad_maximum_fusion.refs_0_, bf16[2,2,32,448]{3,2,1,0:T(8,128)(2,1)S(1)} %collective-permute-done.10.refs_1_, ...), custom_call_target="tpu_custom_call" | custom-call | flops 1000 | bytes 1000 | tf_op jit(solution)/shard_map/early/pallas_call | solution.py:333
  53.3 0.4 collective-permute-done.9.refs_0_
  53.7 0.0 collective-permute-start.12
  53.7 1.5 %collective-permute-done.12.refs_1_ = bf16[4,2,32,448]{3,2,1,0:T(8,128)(2,1)S(1)} collective-permute-done((bf16[4,2,32,448]{3,2,1,0:T(8,128)(2,1)S(1)}, bf16[4,2,32,448]{3,2,1,0:T(8,128)(2,1)S(1)}, u32[]{:S(2)}, u32[]{:S(2)}) %collective-permute-start.12) | collective-permute-done | bytes 229408 | tf_op jit(solution)/shard_map/ppermute | solution.py:392
  55.2 4.5 %late.1 = bf16[2,2048,768]{2,1,0:T(8,128)(2,1)} custom-call(s32[2]{0:T(128)S(1)} %pad_add_fusion.place_ref, bf16[2,2,2048,256]{3,2,1,0:T(8,128)(2,1)S(1)} %copy-done, bf16[448,768]{1,0:T(8,128)(2,1)S(1)} %bitcast.13, bf16[4,2,32,448]{3,2,1,0:T(8,128)(2,1)S(1)} %collective-permute-done.9.refs_0_, bf16[4,2,32,448]{3,2,1,0:T(8,128)(2,1)S(1)} %collective-permute-done.12.refs_1_, ...), custom_call_target="tpu_custom_call" | custom-call | flops 1962934272 | bytes 8388608 | tf_op jit(solution)/shard_map/late/pallas_call | solution.py:343
  (5 shorter events, 0.1 us)
Async XLA Ops:
  7.2 2.1 %collective-permute-start = (bf16[2,4,2,32,448]{4,3,2,1,0:T(8,128)(2,1)S(1)}, bf16[2,4,2,32,448]{4,3,2,1,0:T(8,128)(2,1)S(1)}, u32[]{:S(2)}, u32[]{:S(2)}) collective-permute-start(bf16[2,4,2,32,448]{4,3,2,1,0:T(8,128)(2,1)S(1)} %get-tuple-element.16.after_ref), channel_id=1, source_target_pairs={{0,1},{1,0},{2,3},{3,2},{4,5},{5,4},{6,7},{7,6},{8,9},{9,8},{10,11... | collective-permute-start | bytes 1376264 | tf_op jit(solution)/shard_map/ppermute | solution.py:392
  9.4 8.6 %collective-permute-start.2 = (bf16[3,2,32,448]{3,2,1,0:T(8,128)(2,1)S(1)}, bf16[3,2,32,448]{3,2,1,0:T(8,128)(2,1)S(1)}, u32[]{:S(2)}, u32[]{:S(2)}) collective-permute-start(bf16[3,2,32,448]{3,2,1,0:T(8,128)(2,1)S(1)} %get-tuple-element.19.after_ref), channel_id=1, source_target_pairs={{0,2},{1,3},{2,0},{3,1},{4,6},{5,7},{6,4},{7,5},{8,10},{9,11},{10,... | collective-permute-start | bytes 516104 | tf_op jit(solution)/shard_map/ppermute | solution.py:392
  12.3 13.6 %collective-permute-start.1 = (bf16[1,2,32,448]{3,2,1,0:T(8,128)(2,1)S(1)}, bf16[1,2,32,448]{3,2,1,0:T(8,128)(2,1)S(1)}, u32[]{:S(2)}, u32[]{:S(2)}) collective-permute-start(bf16[1,2,32,448]{3,2,1,0:T(8,128)(2,1)S(1)} %get-tuple-element.18), channel_id=1, source_target_pairs={{0,2},{1,3},{2,0},{3,1},{4,6},{5,7},{6,4},{7,5},{8,10},{9,11},{10,... | collective-permute-start | bytes 172040 | tf_op jit(solution)/shard_map/ppermute | solution.py:392
  18.0 7.9 %collective-permute-start.4 = (bf16[1,2,32,448]{3,2,1,0:T(8,128)(2,1)S(1)}, bf16[1,2,32,448]{3,2,1,0:T(8,128)(2,1)S(1)}, u32[]{:S(2)}, u32[]{:S(2)}) collective-permute-start(bf16[1,2,32,448]{3,2,1,0:T(8,128)(2,1)S(1)} %get-tuple-element.21), channel_id=1, source_target_pairs={{0,8},{1,9},{2,10},{3,11},{4,12},{5,13},{6,14},{7,15},{8,0},{9,1},... | collective-permute-start | bytes 172040 | tf_op jit(solution)/shard_map/ppermute | solution.py:392
  21.1 6.2 %collective-permute-start.5 = (bf16[1,2,32,448]{3,2,1,0:T(8,128)(2,1)S(1)}, bf16[1,2,32,448]{3,2,1,0:T(8,128)(2,1)S(1)}, u32[]{:S(2)}, u32[]{:S(2)}) collective-permute-start(bf16[1,2,32,448]{3,2,1,0:T(8,128)(2,1)S(1)} %get-tuple-element.22), channel_id=1, source_target_pairs={{0,12},{1,13},{2,14},{3,15},{4,8},{5,9},{6,10},{7,11},{8,4},{9,5},... | collective-permute-start | bytes 172040 | tf_op jit(solution)/shard_map/ppermute | solution.py:392
  22.5 5.0 %collective-permute-start.3 = (bf16[1,2,32,448]{3,2,1,0:T(8,128)(2,1)S(1)}, bf16[1,2,32,448]{3,2,1,0:T(8,128)(2,1)S(1)}, u32[]{:S(2)}, u32[]{:S(2)}) collective-permute-start(bf16[1,2,32,448]{3,2,1,0:T(8,128)(2,1)S(1)} %get-tuple-element.20.after_ref), channel_id=1, source_target_pairs={{0,4},{1,5},{2,6},{3,7},{4,0},{5,1},{6,2},{7,3},{8,12},{9,13},{10,... | collective-permute-start | bytes 172040 | tf_op jit(solution)/shard_map/ppermute | solution.py:392
  25.9 24.5 %copy-start = (bf16[2,2,2048,256]{3,2,1,0:T(8,128)(2,1)S(1)}, bf16[2,2,2048,256]{3,2,1,0:T(8,128)(2,1)}, u32[]{:S(2)}) copy-start(bf16[2,2,2048,256]{3,2,1,0:T(8,128)(2,1)} %constant.33.clone.table_ref) | copy-start | bytes 12582916
  25.9 24.5 %copy-start.1 = (bf16[768,448]{0,1:T(8,128)(2,1)S(1)}, bf16[768,448]{0,1:T(8,128)(2,1)}, u32[]{:S(2)}) copy-start(bf16[768,448]{0,1:T(8,128)(2,1)} %param.6) | copy-start | bytes 2064388
  38.4 4.3 %collective-permute-start.6 = (bf16[2,32,448]{2,1,0:T(8,128)(2,1)S(1)}, bf16[2,32,448]{2,1,0:T(8,128)(2,1)S(1)}, u32[]{:S(2)}, u32[]{:S(2)}) collective-permute-start(bf16[2,32,448]{2,1,0:T(8,128)(2,1)S(1)} %respond.1), channel_id=1, source_target_pairs={{0,4},{1,5},{2,6},{3,7},{4,0},{5,1},{6,2},{7,3},{8,12},{9,13},{10,... | collective-permute-start | bytes 172040 | tf_op jit(solution)/shard_map/ppermute | solution.py:392
  38.8 6.2 %collective-permute-start.8 = (bf16[2,32,448]{2,1,0:T(8,128)(2,1)S(1)}, bf16[2,32,448]{2,1,0:T(8,128)(2,1)S(1)}, u32[]{:S(2)}, u32[]{:S(2)}) collective-permute-start(bf16[2,32,448]{2,1,0:T(8,128)(2,1)S(1)} %respond.1), channel_id=1, source_target_pairs={{0,12},{1,13},{2,14},{3,15},{4,8},{5,9},{6,10},{7,11},{8,4},{9,5},... | collective-permute-start | bytes 172040 | tf_op jit(solution)/shard_map/ppermute | solution.py:392
  41.4 5.8 %collective-permute-start.7 = (bf16[2,32,448]{2,1,0:T(8,128)(2,1)S(1)}, bf16[2,32,448]{2,1,0:T(8,128)(2,1)S(1)}, u32[]{:S(2)}, u32[]{:S(2)}) collective-permute-start(bf16[2,32,448]{2,1,0:T(8,128)(2,1)S(1)} %respond.1), channel_id=1, source_target_pairs={{0,8},{1,9},{2,10},{3,11},{4,12},{5,13},{6,14},{7,15},{8,0},{9,1},... | collective-permute-start | bytes 172040 | tf_op jit(solution)/shard_map/ppermute | solution.py:392
  47.2 6.4 %collective-permute-start.9 = (bf16[4,2,32,448]{3,2,1,0:T(8,128)(2,1)S(1)}, bf16[4,2,32,448]{3,2,1,0:T(8,128)(2,1)S(1)}, u32[]{:S(2)}, u32[]{:S(2)}) collective-permute-start(bf16[4,2,32,448]{3,2,1,0:T(8,128)(2,1)S(1)} %pad_maximum_fusion.refs_0_), channel_id=1, source_target_pairs={{0,2},{1,3},{2,0},{3,1},{4,6},{5,7},{6,4},{7,5},{8,10},{9,11},{10,... | collective-permute-start | bytes 688136 | tf_op jit(solution)/shard_map/ppermute | solution.py:392
  48.8 1.4 %collective-permute-start.11 = (bf16[2,2,32,448]{3,2,1,0:T(8,128)(2,1)S(1)}, bf16[2,2,32,448]{3,2,1,0:T(8,128)(2,1)S(1)}, u32[]{:S(2)}, u32[]{:S(2)}) collective-permute-start(bf16[2,2,32,448]{3,2,1,0:T(8,128)(2,1)S(1)} %pad_maximum_fusion.2), channel_id=1, source_target_pairs={{0,1},{1,0},{2,3},{3,2},{4,5},{5,4},{6,7},{7,6},{8,9},{9,8},{10,11... | collective-permute-start | bytes 344072 | tf_op jit(solution)/shard_map/ppermute | solution.py:392
  48.9 1.5 %collective-permute-start.10 = (bf16[2,2,32,448]{3,2,1,0:T(8,128)(2,1)S(1)}, bf16[2,2,32,448]{3,2,1,0:T(8,128)(2,1)S(1)}, u32[]{:S(2)}, u32[]{:S(2)}) collective-permute-start(bf16[2,2,32,448]{3,2,1,0:T(8,128)(2,1)S(1)} %pad_maximum_fusion.1), channel_id=1, source_target_pairs={{0,1},{1,0},{2,3},{3,2},{4,5},{5,4},{6,7},{7,6},{8,9},{9,8},{10,11... | collective-permute-start | bytes 344072 | tf_op jit(solution)/shard_map/ppermute | solution.py:392
  53.7 1.5 %collective-permute-start.12 = (bf16[4,2,32,448]{3,2,1,0:T(8,128)(2,1)S(1)}, bf16[4,2,32,448]{3,2,1,0:T(8,128)(2,1)S(1)}, u32[]{:S(2)}, u32[]{:S(2)}) collective-permute-start(bf16[4,2,32,448]{3,2,1,0:T(8,128)(2,1)S(1)} %collective-permute-done.9.refs_0_), channel_id=1, source_target_pairs={{0,1},{1,0},{2,3},{3,2},{4,5},{5,4},{6,7},{7,6},{8,9},{9,8},{10,11... | collective-permute-start | bytes 688136 | tf_op jit(solution)/shard_map/ppermute | solution.py:392

commit v13 on v12

--- a/solution.py
+++ b/solution.py
@@ -210,7 +210,7 @@
     base = 0
     for part in parts:
 
-        @pl.loop(0, part.shape[0], unroll=part.shape[0])
+        @pl.loop(0, part.shape[0], unroll=math.gcd(4, part.shape[0]))
         def _(step, part=part, base=base):
             multiply(part, step, base + step)
 
@@ -219,7 +219,7 @@
     for copy in copies:
         copy.wait()
 
-    @pl.loop(0, rest_ref.shape[0], unroll=rest_ref.shape[0])
+    @pl.loop(0, rest_ref.shape[0], unroll=math.gcd(4, rest_ref.shape[0]))
     def _(step):
         multiply(rest_ref, step, held + step)
 

time: 59.9 us -> 57.7 us (0.963)
  Pallas kernels: 33 us -> 30.8 us
    pallas_call x1, Pallas kernels: 11 us -> 8.8 us  [respond(): pl.pallas_call(functools.partial(respond_kernel, len(pieces)), in_specs=[...]
  transfers between devices with their start and end apart: 13 -> 13, of which waited for: 11 -> 11; matrix products, arithmetic and copies ran while one was open for 0% -> 0% of each run, Pallas kernels for 17% -> 18%
where the time goes in v13:
time: 57.7 us; the launch traced here: 57.6 us
  Pallas kernels  30.8 us (53%)
  starting transfers between devices  13.9 us (24%)
  waiting for transfers between devices  12.5 us (22%)
    ppermute x13, starting transfers between devices, swap(): return lax.ppermute(values, 'dof', pairs)  13.9 us
    ppermute x13, waiting for transfers between devices, swap(): return lax.ppermute(values, 'dof', pairs)  12.5 us
    pallas_call x1, Pallas kernels, respond(): pl.pallas_call(functools.partial(respond_kernel, len(pieces)), in_specs=[...  8.8 us
    pallas_call x2, Pallas kernels, load(): pl.pallas_call(functools.partial(load_kernel, start), in_specs=[hbm, anyw...  7.43 us
    pallas_call x1, Pallas kernels, forward(): pl.pallas_call(forward_kernel, in_specs=[pl.BlockSpec(memory_space=pltpu....  7.09 us
    pallas_call x1, Pallas kernels, inverse(): pl.pallas_call(functools.partial(late_kernel, plan), in_specs=in_specs +...  4.53 us
    pallas_call x1, Pallas kernels, inverse(): pl.pallas_call(functools.partial(early_kernel, plan), in_specs=in_specs,...  2.82 us
  transfers between devices with their start and end apart: 13, of which 11 were waited for; matrix products, arithmetic and copies ran while one was open for 0% of the time, Pallas kernels for 18%

profile of v13, /device:TPU:0, one launch (start us, length us, event | category | flops | bytes accessed | tf_op | source)
XLA Modules:
  0.0 57.6 jit_solution(12756464015045501816)
XLA Ops:
  0.0 0.1 pad_add_fusion.place_ref
  0.1 7.1 %forward.1 = (bf16[2,4,2,32,448]{4,3,2,1,0:T(8,128)(2,1)S(1)}, bf16[2,4,2,32,448]{4,3,2,1,0:T(8,128)(2,1)S(1)}) custom-call(s32[2]{0:T(128)S(1)} %pad_add_fusion.place_ref, bf16[2,512,2048]{2,1,0:T(8,128)(2,1)} %constant.32.clone.table_ref, bf16[2,2048,768]{2,1,0:T(8,128)(2,1)} %bitcast.24, bf16[448,768]{1,0:T(8,128)(2,1)} %bitcast.11), custom_call_target="tpu_custom_call" | custom-call | flops 3925868544 | bytes 12582912 | tf_op jit(solution)/shard_map/forward/pallas_call | solution.py:116
  7.2 0.5 collective-permute-start
  7.7 1.5 %collective-permute-done = bf16[2,4,2,32,448]{4,3,2,1,0:T(8,128)(2,1)S(1)} collective-permute-done((bf16[2,4,2,32,448]{4,3,2,1,0:T(8,128)(2,1)S(1)}, bf16[2,4,2,32,448]{4,3,2,1,0:T(8,128)(2,1)S(1)}, u32[]{:S(2)}, u32[]{:S(2)}) %collective-permute-start) | collective-permute-done | bytes 458784 | tf_op jit(solution)/shard_map/ppermute | solution.py:392
  9.2 0.1 add.10
  9.4 2.9 %collective-permute-start.2 = (bf16[3,2,32,448]{3,2,1,0:T(8,128)(2,1)S(1)}, bf16[3,2,32,448]{3,2,1,0:T(8,128)(2,1)S(1)}, u32[]{:S(2)}, u32[]{:S(2)}) collective-permute-start(bf16[3,2,32,448]{3,2,1,0:T(8,128)(2,1)S(1)} %get-tuple-element.19.after_ref), channel_id=1, source_target_pairs={{0,2},{1,3},{2,0},{3,1},{4,6},{5,7},{6,4},{7,5},{8,10},{9,11},{10,... | collective-permute-start | bytes 516104 | tf_op jit(solution)/shard_map/ppermute | solution.py:392
  12.3 0.1 collective-permute-start.1
  12.4 4.2 %load.2.after_ref.refs_5_ = bf16[12,2,448,448]{3,2,1,0:T(8,128)(2,1)S(1)} custom-call(bf16[32,2,448,448]{3,2,1,0:T(8,128)(2,1)} %refs_7_.1, bf16[3,2,32,448]{3,2,1,0:T(8,128)(2,1)S(1)} %get-tuple-element.19.after_ref), custom_call_target="tpu_custom_call" | custom-call | bytes 19267584 | tf_op jit(solution)/shard_map/load/pallas_call | solution.py:161
  16.6 1.4 %collective-permute-done.2.came_ref = bf16[3,2,32,448]{3,2,1,0:T(8,128)(2,1)S(1)} collective-permute-done((bf16[3,2,32,448]{3,2,1,0:T(8,128)(2,1)S(1)}, bf16[3,2,32,448]{3,2,1,0:T(8,128)(2,1)S(1)}, u32[]{:S(2)}, u32[]{:S(2)}) %collective-permute-start.2) | collective-permute-done | bytes 172064 | tf_op jit(solution)/shard_map/ppermute | solution.py:392
  18.0 3.1 %collective-permute-start.4 = (bf16[1,2,32,448]{3,2,1,0:T(8,128)(2,1)S(1)}, bf16[1,2,32,448]{3,2,1,0:T(8,128)(2,1)S(1)}, u32[]{:S(2)}, u32[]{:S(2)}) collective-permute-start(bf16[1,2,32,448]{3,2,1,0:T(8,128)(2,1)S(1)} %get-tuple-element.21), channel_id=1, source_target_pairs={{0,8},{1,9},{2,10},{3,11},{4,12},{5,13},{6,14},{7,15},{8,0},{9,1},... | collective-permute-start | bytes 172040 | tf_op jit(solution)/shard_map/ppermute | solution.py:392
  21.1 1.3 %collective-permute-start.5 = (bf16[1,2,32,448]{3,2,1,0:T(8,128)(2,1)S(1)}, bf16[1,2,32,448]{3,2,1,0:T(8,128)(2,1)S(1)}, u32[]{:S(2)}, u32[]{:S(2)}) collective-permute-start(bf16[1,2,32,448]{3,2,1,0:T(8,128)(2,1)S(1)} %get-tuple-element.22), channel_id=1, source_target_pairs={{0,12},{1,13},{2,14},{3,15},{4,8},{5,9},{6,10},{7,11},{8,4},{9,5},... | collective-permute-start | bytes 172040 | tf_op jit(solution)/shard_map/ppermute | solution.py:392
  22.5 0.2 collective-permute-start.3
  22.7 3.2 %load.3.refs_6_ = bf16[8,2,448,448]{3,2,1,0:T(8,128)(2,1)S(1)} custom-call(bf16[32,2,448,448]{3,2,1,0:T(8,128)(2,1)} %refs_7_.1, bf16[1,2,32,448]{3,2,1,0:T(8,128)(2,1)S(1)} %get-tuple-element.20.after_ref), custom_call_target="tpu_custom_call" | custom-call | bytes 12845056 | tf_op jit(solution)/shard_map/load/pallas_call | solution.py:161
  25.9 0.0 copy-start
  25.9 0.0 copy-start.1
  25.9 0.0 collective-permute-done.1.refs_1_
  26.0 0.0 collective-permute-done.4.refs_3_
  26.0 1.3 %collective-permute-done.5.refs_4_ = bf16[1,2,32,448]{3,2,1,0:T(8,128)(2,1)S(1)} collective-permute-done((bf16[1,2,32,448]{3,2,1,0:T(8,128)(2,1)S(1)}, bf16[1,2,32,448]{3,2,1,0:T(8,128)(2,1)S(1)}, u32[]{:S(2)}, u32[]{:S(2)}) %collective-permute-start.5) | collective-permute-done | bytes 57376 | tf_op jit(solution)/shard_map/ppermute | solution.py:392
  27.3 0.1 collective-permute-done.3.refs_2_
  27.5 8.8 %respond.1 = bf16[2,32,448]{2,1,0:T(8,128)(2,1)S(1)} custom-call(bf16[1,2,32,448]{3,2,1,0:T(8,128)(2,1)S(1)} %slice.3.refs_0_, bf16[1,2,32,448]{3,2,1,0:T(8,128)(2,1)S(1)} %collective-permute-done.1.refs_1_, bf16[1,2,32,448]{3,2,1,0:T(8,128)(2,1)S(1)} %collective-permute-done.3.refs_2_, bf16[1,2,32,448]{3,2,1,0:T(8,128)(2,1)S(1)} %collective-permute-done.4.refs_3_, ...), custom_call_target="tpu_custom_call" | custom-call | flops 51380224 | bytes 25690112 | tf_op jit(solution)/shard_map/respond/pallas_call | solution.py:238
  36.3 0.4 collective-permute-start.6
  36.7 2.5 %collective-permute-start.8 = (bf16[2,32,448]{2,1,0:T(8,128)(2,1)S(1)}, bf16[2,32,448]{2,1,0:T(8,128)(2,1)S(1)}, u32[]{:S(2)}, u32[]{:S(2)}) collective-permute-start(bf16[2,32,448]{2,1,0:T(8,128)(2,1)S(1)} %respond.1), channel_id=1, source_target_pairs={{0,12},{1,13},{2,14},{3,15},{4,8},{5,9},{6,10},{7,11},{8,4},{9,5},... | collective-permute-start | bytes 172040 | tf_op jit(solution)/shard_map/ppermute | solution.py:392
  39.2 0.6 %collective-permute-start.7 = (bf16[2,32,448]{2,1,0:T(8,128)(2,1)S(1)}, bf16[2,32,448]{2,1,0:T(8,128)(2,1)S(1)}, u32[]{:S(2)}, u32[]{:S(2)}) collective-permute-start(bf16[2,32,448]{2,1,0:T(8,128)(2,1)S(1)} %respond.1), channel_id=1, source_target_pairs={{0,8},{1,9},{2,10},{3,11},{4,12},{5,13},{6,14},{7,15},{8,0},{9,1},... | collective-permute-start | bytes 172040 | tf_op jit(solution)/shard_map/ppermute | solution.py:392
  39.8 0.8 %collective-permute-done.6 = bf16[2,32,448]{2,1,0:T(8,128)(2,1)S(1)} collective-permute-done((bf16[2,32,448]{2,1,0:T(8,128)(2,1)S(1)}, bf16[2,32,448]{2,1,0:T(8,128)(2,1)S(1)}, u32[]{:S(2)}, u32[]{:S(2)}) %collective-permute-start.6) | collective-permute-done | bytes 57376 | tf_op jit(solution)/shard_map/ppermute | solution.py:392
  40.6 2.2 %collective-permute-done.8 = bf16[2,32,448]{2,1,0:T(8,128)(2,1)S(1)} collective-permute-done((bf16[2,32,448]{2,1,0:T(8,128)(2,1)S(1)}, bf16[2,32,448]{2,1,0:T(8,128)(2,1)S(1)}, u32[]{:S(2)}, u32[]{:S(2)}) %collective-permute-start.8) | collective-permute-done | bytes 57376 | tf_op jit(solution)/shard_map/ppermute | solution.py:392
  42.8 2.2 %collective-permute-done.7 = bf16[2,32,448]{2,1,0:T(8,128)(2,1)S(1)} collective-permute-done((bf16[2,32,448]{2,1,0:T(8,128)(2,1)S(1)}, bf16[2,32,448]{2,1,0:T(8,128)(2,1)S(1)}, u32[]{:S(2)}, u32[]{:S(2)}) %collective-permute-start.7) | collective-permute-done | bytes 57376 | tf_op jit(solution)/shard_map/ppermute | solution.py:392
  45.1 1.6 %collective-permute-start.9 = (bf16[4,2,32,448]{3,2,1,0:T(8,128)(2,1)S(1)}, bf16[4,2,32,448]{3,2,1,0:T(8,128)(2,1)S(1)}, u32[]{:S(2)}, u32[]{:S(2)}) collective-permute-start(bf16[4,2,32,448]{3,2,1,0:T(8,128)(2,1)S(1)} %pad_maximum_fusion.refs_0_), channel_id=1, source_target_pairs={{0,2},{1,3},{2,0},{3,1},{4,6},{5,7},{6,4},{7,5},{8,10},{9,11},{10,... | collective-permute-start | bytes 688136 | tf_op jit(solution)/shard_map/ppermute | solution.py:392
  46.7 0.1 collective-permute-start.11
  46.7 0.5 collective-permute-start.10
  47.2 0.8 %collective-permute-done.11.refs_2_ = bf16[2,2,32,448]{3,2,1,0:T(8,128)(2,1)S(1)} collective-permute-done((bf16[2,2,32,448]{3,2,1,0:T(8,128)(2,1)S(1)}, bf16[2,2,32,448]{3,2,1,0:T(8,128)(2,1)S(1)}, u32[]{:S(2)}, u32[]{:S(2)}) %collective-permute-start.11) | collective-permute-done | bytes 114720 | tf_op jit(solution)/shard_map/ppermute | solution.py:392
  48.1 0.2 collective-permute-done.10.refs_1_
  48.3 0.0 copy-done
  48.3 0.0 copy-done.1
  48.3 2.8 %early.1.refs_2_ = f32[2,2048,768]{2,1,0:T(8,128)S(1)} custom-call(s32[2]{0:T(128)S(1)} %pad_add_fusion.place_ref, bf16[2,2,2048,256]{3,2,1,0:T(8,128)(2,1)S(1)} %copy-done, bf16[448,768]{1,0:T(8,128)(2,1)S(1)} %bitcast.12, bf16[4,2,32,448]{3,2,1,0:T(8,128)(2,1)S(1)} %pad_maximum_fusion.refs_0_, bf16[2,2,32,448]{3,2,1,0:T(8,128)(2,1)S(1)} %collective-permute-done.10.refs_1_, ...), custom_call_target="tpu_custom_call" | custom-call | flops 1000 | bytes 1000 | tf_op jit(solution)/shard_map/early/pallas_call | solution.py:333
  51.1 0.4 collective-permute-done.9.refs_0_
  51.5 0.0 collective-permute-start.12
  51.5 1.5 %collective-permute-done.12.refs_1_ = bf16[4,2,32,448]{3,2,1,0:T(8,128)(2,1)S(1)} collective-permute-done((bf16[4,2,32,448]{3,2,1,0:T(8,128)(2,1)S(1)}, bf16[4,2,32,448]{3,2,1,0:T(8,128)(2,1)S(1)}, u32[]{:S(2)}, u32[]{:S(2)}) %collective-permute-start.12) | collective-permute-done | bytes 229408 | tf_op jit(solution)/shard_map/ppermute | solution.py:392
  53.0 4.5 %late.1 = bf16[2,2048,768]{2,1,0:T(8,128)(2,1)} custom-call(s32[2]{0:T(128)S(1)} %pad_add_fusion.place_ref, bf16[2,2,2048,256]{3,2,1,0:T(8,128)(2,1)S(1)} %copy-done, bf16[448,768]{1,0:T(8,128)(2,1)S(1)} %bitcast.13, bf16[4,2,32,448]{3,2,1,0:T(8,128)(2,1)S(1)} %collective-permute-done.9.refs_0_, bf16[4,2,32,448]{3,2,1,0:T(8,128)(2,1)S(1)} %collective-permute-done.12.refs_1_, ...), custom_call_target="tpu_custom_call" | custom-call | flops 1962934272 | bytes 8388608 | tf_op jit(solution)/shard_map/late/pallas_call | solution.py:343
  (5 shorter events, 0.1 us)
Async XLA Ops:
  7.2 2.1 %collective-permute-start = (bf16[2,4,2,32,448]{4,3,2,1,0:T(8,128)(2,1)S(1)}, bf16[2,4,2,32,448]{4,3,2,1,0:T(8,128)(2,1)S(1)}, u32[]{:S(2)}, u32[]{:S(2)}) collective-permute-start(bf16[2,4,2,32,448]{4,3,2,1,0:T(8,128)(2,1)S(1)} %get-tuple-element.16.after_ref), channel_id=1, source_target_pairs={{0,1},{1,0},{2,3},{3,2},{4,5},{5,4},{6,7},{7,6},{8,9},{9,8},{10,11... | collective-permute-start | bytes 1376264 | tf_op jit(solution)/shard_map/ppermute | solution.py:392
  9.4 8.6 %collective-permute-start.2 = (bf16[3,2,32,448]{3,2,1,0:T(8,128)(2,1)S(1)}, bf16[3,2,32,448]{3,2,1,0:T(8,128)(2,1)S(1)}, u32[]{:S(2)}, u32[]{:S(2)}) collective-permute-start(bf16[3,2,32,448]{3,2,1,0:T(8,128)(2,1)S(1)} %get-tuple-element.19.after_ref), channel_id=1, source_target_pairs={{0,2},{1,3},{2,0},{3,1},{4,6},{5,7},{6,4},{7,5},{8,10},{9,11},{10,... | collective-permute-start | bytes 516104 | tf_op jit(solution)/shard_map/ppermute | solution.py:392
  12.3 13.6 %collective-permute-start.1 = (bf16[1,2,32,448]{3,2,1,0:T(8,128)(2,1)S(1)}, bf16[1,2,32,448]{3,2,1,0:T(8,128)(2,1)S(1)}, u32[]{:S(2)}, u32[]{:S(2)}) collective-permute-start(bf16[1,2,32,448]{3,2,1,0:T(8,128)(2,1)S(1)} %get-tuple-element.18), channel_id=1, source_target_pairs={{0,2},{1,3},{2,0},{3,1},{4,6},{5,7},{6,4},{7,5},{8,10},{9,11},{10,... | collective-permute-start | bytes 172040 | tf_op jit(solution)/shard_map/ppermute | solution.py:392
  18.0 7.9 %collective-permute-start.4 = (bf16[1,2,32,448]{3,2,1,0:T(8,128)(2,1)S(1)}, bf16[1,2,32,448]{3,2,1,0:T(8,128)(2,1)S(1)}, u32[]{:S(2)}, u32[]{:S(2)}) collective-permute-start(bf16[1,2,32,448]{3,2,1,0:T(8,128)(2,1)S(1)} %get-tuple-element.21), channel_id=1, source_target_pairs={{0,8},{1,9},{2,10},{3,11},{4,12},{5,13},{6,14},{7,15},{8,0},{9,1},... | collective-permute-start | bytes 172040 | tf_op jit(solution)/shard_map/ppermute | solution.py:392
  21.1 6.2 %collective-permute-start.5 = (bf16[1,2,32,448]{3,2,1,0:T(8,128)(2,1)S(1)}, bf16[1,2,32,448]{3,2,1,0:T(8,128)(2,1)S(1)}, u32[]{:S(2)}, u32[]{:S(2)}) collective-permute-start(bf16[1,2,32,448]{3,2,1,0:T(8,128)(2,1)S(1)} %get-tuple-element.22), channel_id=1, source_target_pairs={{0,12},{1,13},{2,14},{3,15},{4,8},{5,9},{6,10},{7,11},{8,4},{9,5},... | collective-permute-start | bytes 172040 | tf_op jit(solution)/shard_map/ppermute | solution.py:392
  22.5 5.0 %collective-permute-start.3 = (bf16[1,2,32,448]{3,2,1,0:T(8,128)(2,1)S(1)}, bf16[1,2,32,448]{3,2,1,0:T(8,128)(2,1)S(1)}, u32[]{:S(2)}, u32[]{:S(2)}) collective-permute-start(bf16[1,2,32,448]{3,2,1,0:T(8,128)(2,1)S(1)} %get-tuple-element.20.after_ref), channel_id=1, source_target_pairs={{0,4},{1,5},{2,6},{3,7},{4,0},{5,1},{6,2},{7,3},{8,12},{9,13},{10,... | collective-permute-start | bytes 172040 | tf_op jit(solution)/shard_map/ppermute | solution.py:392
  25.9 22.3 %copy-start = (bf16[2,2,2048,256]{3,2,1,0:T(8,128)(2,1)S(1)}, bf16[2,2,2048,256]{3,2,1,0:T(8,128)(2,1)}, u32[]{:S(2)}) copy-start(bf16[2,2,2048,256]{3,2,1,0:T(8,128)(2,1)} %constant.33.clone.table_ref) | copy-start | bytes 12582916
  25.9 22.3 %copy-start.1 = (bf16[768,448]{0,1:T(8,128)(2,1)S(1)}, bf16[768,448]{0,1:T(8,128)(2,1)}, u32[]{:S(2)}) copy-start(bf16[768,448]{0,1:T(8,128)(2,1)} %param.6) | copy-start | bytes 2064388
  36.3 4.3 %collective-permute-start.6 = (bf16[2,32,448]{2,1,0:T(8,128)(2,1)S(1)}, bf16[2,32,448]{2,1,0:T(8,128)(2,1)S(1)}, u32[]{:S(2)}, u32[]{:S(2)}) collective-permute-start(bf16[2,32,448]{2,1,0:T(8,128)(2,1)S(1)} %respond.1), channel_id=1, source_target_pairs={{0,4},{1,5},{2,6},{3,7},{4,0},{5,1},{6,2},{7,3},{8,12},{9,13},{10,... | collective-permute-start | bytes 172040 | tf_op jit(solution)/shard_map/ppermute | solution.py:392
  36.7 6.2 %collective-permute-start.8 = (bf16[2,32,448]{2,1,0:T(8,128)(2,1)S(1)}, bf16[2,32,448]{2,1,0:T(8,128)(2,1)S(1)}, u32[]{:S(2)}, u32[]{:S(2)}) collective-permute-start(bf16[2,32,448]{2,1,0:T(8,128)(2,1)S(1)} %respond.1), channel_id=1, source_target_pairs={{0,12},{1,13},{2,14},{3,15},{4,8},{5,9},{6,10},{7,11},{8,4},{9,5},... | collective-permute-start | bytes 172040 | tf_op jit(solution)/shard_map/ppermute | solution.py:392
  39.2 5.8 %collective-permute-start.7 = (bf16[2,32,448]{2,1,0:T(8,128)(2,1)S(1)}, bf16[2,32,448]{2,1,0:T(8,128)(2,1)S(1)}, u32[]{:S(2)}, u32[]{:S(2)}) collective-permute-start(bf16[2,32,448]{2,1,0:T(8,128)(2,1)S(1)} %respond.1), channel_id=1, source_target_pairs={{0,8},{1,9},{2,10},{3,11},{4,12},{5,13},{6,14},{7,15},{8,0},{9,1},... | collective-permute-start | bytes 172040 | tf_op jit(solution)/shard_map/ppermute | solution.py:392
  45.1 6.4 %collective-permute-start.9 = (bf16[4,2,32,448]{3,2,1,0:T(8,128)(2,1)S(1)}, bf16[4,2,32,448]{3,2,1,0:T(8,128)(2,1)S(1)}, u32[]{:S(2)}, u32[]{:S(2)}) collective-permute-start(bf16[4,2,32,448]{3,2,1,0:T(8,128)(2,1)S(1)} %pad_maximum_fusion.refs_0_), channel_id=1, source_target_pairs={{0,2},{1,3},{2,0},{3,1},{4,6},{5,7},{6,4},{7,5},{8,10},{9,11},{10,... | collective-permute-start | bytes 688136 | tf_op jit(solution)/shard_map/ppermute | solution.py:392
  46.7 1.4 %collective-permute-start.11 = (bf16[2,2,32,448]{3,2,1,0:T(8,128)(2,1)S(1)}, bf16[2,2,32,448]{3,2,1,0:T(8,128)(2,1)S(1)}, u32[]{:S(2)}, u32[]{:S(2)}) collective-permute-start(bf16[2,2,32,448]{3,2,1,0:T(8,128)(2,1)S(1)} %pad_maximum_fusion.2), channel_id=1, source_target_pairs={{0,1},{1,0},{2,3},{3,2},{4,5},{5,4},{6,7},{7,6},{8,9},{9,8},{10,11... | collective-permute-start | bytes 344072 | tf_op jit(solution)/shard_map/ppermute | solution.py:392
  46.7 1.5 %collective-permute-start.10 = (bf16[2,2,32,448]{3,2,1,0:T(8,128)(2,1)S(1)}, bf16[2,2,32,448]{3,2,1,0:T(8,128)(2,1)S(1)}, u32[]{:S(2)}, u32[]{:S(2)}) collective-permute-start(bf16[2,2,32,448]{3,2,1,0:T(8,128)(2,1)S(1)} %pad_maximum_fusion.1), channel_id=1, source_target_pairs={{0,1},{1,0},{2,3},{3,2},{4,5},{5,4},{6,7},{7,6},{8,9},{9,8},{10,11... | collective-permute-start | bytes 344072 | tf_op jit(solution)/shard_map/ppermute | solution.py:392
  51.5 1.5 %collective-permute-start.12 = (bf16[4,2,32,448]{3,2,1,0:T(8,128)(2,1)S(1)}, bf16[4,2,32,448]{3,2,1,0:T(8,128)(2,1)S(1)}, u32[]{:S(2)}, u32[]{:S(2)}) collective-permute-start(bf16[4,2,32,448]{3,2,1,0:T(8,128)(2,1)S(1)} %collective-permute-done.9.refs_0_), channel_id=1, source_target_pairs={{0,1},{1,0},{2,3},{3,2},{4,5},{5,4},{6,7},{7,6},{8,9},{9,8},{10,11... | collective-permute-start | bytes 688136 | tf_op jit(solution)/shard_map/ppermute | solution.py:392

commit v14 on v13

--- a/solution.py
+++ b/solution.py
@@ -210,7 +210,7 @@
     base = 0
     for part in parts:
 
-        @pl.loop(0, part.shape[0], unroll=math.gcd(4, part.shape[0]))
+        @pl.loop(0, part.shape[0], unroll=math.gcd(2, part.shape[0]))
         def _(step, part=part, base=base):
             multiply(part, step, base + step)
 
@@ -219,7 +219,7 @@
     for copy in copies:
         copy.wait()
 
-    @pl.loop(0, rest_ref.shape[0], unroll=math.gcd(4, rest_ref.shape[0]))
+    @pl.loop(0, rest_ref.shape[0], unroll=math.gcd(2, rest_ref.shape[0]))
     def _(step):
         multiply(rest_ref, step, held + step)
 

time: 57.7 us -> 58.6 us (1.016)
  Pallas kernels: 30.8 us -> 31.7 us
    pallas_call x1, Pallas kernels: 8.8 us -> 9.71 us  [respond(): pl.pallas_call(functools.partial(respond_kernel, len(pieces)), in_specs=[...]
where the time goes in v14:
time: 58.6 us; the launch traced here: 58.5 us
  Pallas kernels  31.7 us (54%)
  starting transfers between devices  13.9 us (24%)
  waiting for transfers between devices  12.5 us (21%)
    ppermute x13, starting transfers between devices, swap(): return lax.ppermute(values, 'dof', pairs)  13.9 us
    ppermute x13, waiting for transfers between devices, swap(): return lax.ppermute(values, 'dof', pairs)  12.5 us
    pallas_call x1, Pallas kernels, respond(): pl.pallas_call(functools.partial(respond_kernel, len(pieces)), in_specs=[...  9.71 us
    pallas_call x2, Pallas kernels, load(): pl.pallas_call(functools.partial(load_kernel, start), in_specs=[hbm, anyw...  7.43 us
    pallas_call x1, Pallas kernels, forward(): pl.pallas_call(forward_kernel, in_specs=[pl.BlockSpec(memory_space=pltpu....  7.09 us
    pallas_call x1, Pallas kernels, inverse(): pl.pallas_call(functools.partial(late_kernel, plan), in_specs=in_specs +...  4.53 us
    pallas_call x1, Pallas kernels, inverse(): pl.pallas_call(functools.partial(early_kernel, plan), in_specs=in_specs,...  2.81 us
  transfers between devices with their start and end apart: 13, of which 11 were waited for; matrix products, arithmetic and copies ran while one was open for 0% of the time, Pallas kernels for 18%

profile of v14, /device:TPU:0, one launch (start us, length us, event | category | flops | bytes accessed | tf_op | source)
XLA Modules:
  0.0 58.5 jit_solution(16123478182087740191)
XLA Ops:
  0.0 0.1 pad_add_fusion.place_ref
  0.1 7.1 %forward.1 = (bf16[2,4,2,32,448]{4,3,2,1,0:T(8,128)(2,1)S(1)}, bf16[2,4,2,32,448]{4,3,2,1,0:T(8,128)(2,1)S(1)}) custom-call(s32[2]{0:T(128)S(1)} %pad_add_fusion.place_ref, bf16[2,512,2048]{2,1,0:T(8,128)(2,1)} %constant.32.clone.table_ref, bf16[2,2048,768]{2,1,0:T(8,128)(2,1)} %bitcast.24, bf16[448,768]{1,0:T(8,128)(2,1)} %bitcast.11), custom_call_target="tpu_custom_call" | custom-call | flops 3925868544 | bytes 12582912 | tf_op jit(solution)/shard_map/forward/pallas_call | solution.py:116
  7.2 0.5 collective-permute-start
  7.7 1.5 %collective-permute-done = bf16[2,4,2,32,448]{4,3,2,1,0:T(8,128)(2,1)S(1)} collective-permute-done((bf16[2,4,2,32,448]{4,3,2,1,0:T(8,128)(2,1)S(1)}, bf16[2,4,2,32,448]{4,3,2,1,0:T(8,128)(2,1)S(1)}, u32[]{:S(2)}, u32[]{:S(2)}) %collective-permute-start) | collective-permute-done | bytes 458784 | tf_op jit(solution)/shard_map/ppermute | solution.py:392
  9.2 0.1 add.10
  9.4 2.9 %collective-permute-start.2 = (bf16[3,2,32,448]{3,2,1,0:T(8,128)(2,1)S(1)}, bf16[3,2,32,448]{3,2,1,0:T(8,128)(2,1)S(1)}, u32[]{:S(2)}, u32[]{:S(2)}) collective-permute-start(bf16[3,2,32,448]{3,2,1,0:T(8,128)(2,1)S(1)} %get-tuple-element.19.after_ref), channel_id=1, source_target_pairs={{0,2},{1,3},{2,0},{3,1},{4,6},{5,7},{6,4},{7,5},{8,10},{9,11},{10,... | collective-permute-start | bytes 516104 | tf_op jit(solution)/shard_map/ppermute | solution.py:392
  12.3 0.1 collective-permute-start.1
  12.4 4.2 %load.2.after_ref.refs_5_ = bf16[12,2,448,448]{3,2,1,0:T(8,128)(2,1)S(1)} custom-call(bf16[32,2,448,448]{3,2,1,0:T(8,128)(2,1)} %refs_7_.1, bf16[3,2,32,448]{3,2,1,0:T(8,128)(2,1)S(1)} %get-tuple-element.19.after_ref), custom_call_target="tpu_custom_call" | custom-call | bytes 19267584 | tf_op jit(solution)/shard_map/load/pallas_call | solution.py:161
  16.6 1.4 %collective-permute-done.2.came_ref = bf16[3,2,32,448]{3,2,1,0:T(8,128)(2,1)S(1)} collective-permute-done((bf16[3,2,32,448]{3,2,1,0:T(8,128)(2,1)S(1)}, bf16[3,2,32,448]{3,2,1,0:T(8,128)(2,1)S(1)}, u32[]{:S(2)}, u32[]{:S(2)}) %collective-permute-start.2) | collective-permute-done | bytes 172064 | tf_op jit(solution)/shard_map/ppermute | solution.py:392
  18.0 3.1 %collective-permute-start.4 = (bf16[1,2,32,448]{3,2,1,0:T(8,128)(2,1)S(1)}, bf16[1,2,32,448]{3,2,1,0:T(8,128)(2,1)S(1)}, u32[]{:S(2)}, u32[]{:S(2)}) collective-permute-start(bf16[1,2,32,448]{3,2,1,0:T(8,128)(2,1)S(1)} %get-tuple-element.21), channel_id=1, source_target_pairs={{0,8},{1,9},{2,10},{3,11},{4,12},{5,13},{6,14},{7,15},{8,0},{9,1},... | collective-permute-start | bytes 172040 | tf_op jit(solution)/shard_map/ppermute | solution.py:392
  21.1 1.3 %collective-permute-start.5 = (bf16[1,2,32,448]{3,2,1,0:T(8,128)(2,1)S(1)}, bf16[1,2,32,448]{3,2,1,0:T(8,128)(2,1)S(1)}, u32[]{:S(2)}, u32[]{:S(2)}) collective-permute-start(bf16[1,2,32,448]{3,2,1,0:T(8,128)(2,1)S(1)} %get-tuple-element.22), channel_id=1, source_target_pairs={{0,12},{1,13},{2,14},{3,15},{4,8},{5,9},{6,10},{7,11},{8,4},{9,5},... | collective-permute-start | bytes 172040 | tf_op jit(solution)/shard_map/ppermute | solution.py:392
  22.5 0.2 collective-permute-start.3
  22.7 3.2 %load.3.refs_6_ = bf16[8,2,448,448]{3,2,1,0:T(8,128)(2,1)S(1)} custom-call(bf16[32,2,448,448]{3,2,1,0:T(8,128)(2,1)} %refs_7_.1, bf16[1,2,32,448]{3,2,1,0:T(8,128)(2,1)S(1)} %get-tuple-element.20.after_ref), custom_call_target="tpu_custom_call" | custom-call | bytes 12845056 | tf_op jit(solution)/shard_map/load/pallas_call | solution.py:161
  25.9 0.0 copy-start
  25.9 0.0 copy-start.1
  25.9 0.0 collective-permute-done.1.refs_1_
  26.0 0.0 collective-permute-done.4.refs_3_
  26.0 1.3 %collective-permute-done.5.refs_4_ = bf16[1,2,32,448]{3,2,1,0:T(8,128)(2,1)S(1)} collective-permute-done((bf16[1,2,32,448]{3,2,1,0:T(8,128)(2,1)S(1)}, bf16[1,2,32,448]{3,2,1,0:T(8,128)(2,1)S(1)}, u32[]{:S(2)}, u32[]{:S(2)}) %collective-permute-start.5) | collective-permute-done | bytes 57376 | tf_op jit(solution)/shard_map/ppermute | solution.py:392
  27.3 0.1 collective-permute-done.3.refs_2_
  27.5 9.7 %respond.1 = bf16[2,32,448]{2,1,0:T(8,128)(2,1)S(1)} custom-call(bf16[1,2,32,448]{3,2,1,0:T(8,128)(2,1)S(1)} %slice.3.refs_0_, bf16[1,2,32,448]{3,2,1,0:T(8,128)(2,1)S(1)} %collective-permute-done.1.refs_1_, bf16[1,2,32,448]{3,2,1,0:T(8,128)(2,1)S(1)} %collective-permute-done.3.refs_2_, bf16[1,2,32,448]{3,2,1,0:T(8,128)(2,1)S(1)} %collective-permute-done.4.refs_3_, ...), custom_call_target="tpu_custom_call" | custom-call | flops 51380224 | bytes 25690112 | tf_op jit(solution)/shard_map/respond/pallas_call | solution.py:238
  37.2 0.4 collective-permute-start.6
  37.6 2.5 %collective-permute-start.8 = (bf16[2,32,448]{2,1,0:T(8,128)(2,1)S(1)}, bf16[2,32,448]{2,1,0:T(8,128)(2,1)S(1)}, u32[]{:S(2)}, u32[]{:S(2)}) collective-permute-start(bf16[2,32,448]{2,1,0:T(8,128)(2,1)S(1)} %respond.1), channel_id=1, source_target_pairs={{0,12},{1,13},{2,14},{3,15},{4,8},{5,9},{6,10},{7,11},{8,4},{9,5},... | collective-permute-start | bytes 172040 | tf_op jit(solution)/shard_map/ppermute | solution.py:392
  40.1 0.6 %collective-permute-start.7 = (bf16[2,32,448]{2,1,0:T(8,128)(2,1)S(1)}, bf16[2,32,448]{2,1,0:T(8,128)(2,1)S(1)}, u32[]{:S(2)}, u32[]{:S(2)}) collective-permute-start(bf16[2,32,448]{2,1,0:T(8,128)(2,1)S(1)} %respond.1), channel_id=1, source_target_pairs={{0,8},{1,9},{2,10},{3,11},{4,12},{5,13},{6,14},{7,15},{8,0},{9,1},... | collective-permute-start | bytes 172040 | tf_op jit(solution)/shard_map/ppermute | solution.py:392
  40.7 0.8 %collective-permute-done.6 = bf16[2,32,448]{2,1,0:T(8,128)(2,1)S(1)} collective-permute-done((bf16[2,32,448]{2,1,0:T(8,128)(2,1)S(1)}, bf16[2,32,448]{2,1,0:T(8,128)(2,1)S(1)}, u32[]{:S(2)}, u32[]{:S(2)}) %collective-permute-start.6) | collective-permute-done | bytes 57376 | tf_op jit(solution)/shard_map/ppermute | solution.py:392
  41.5 2.2 %collective-permute-done.8 = bf16[2,32,448]{2,1,0:T(8,128)(2,1)S(1)} collective-permute-done((bf16[2,32,448]{2,1,0:T(8,128)(2,1)S(1)}, bf16[2,32,448]{2,1,0:T(8,128)(2,1)S(1)}, u32[]{:S(2)}, u32[]{:S(2)}) %collective-permute-start.8) | collective-permute-done | bytes 57376 | tf_op jit(solution)/shard_map/ppermute | solution.py:392
  43.7 2.2 %collective-permute-done.7 = bf16[2,32,448]{2,1,0:T(8,128)(2,1)S(1)} collective-permute-done((bf16[2,32,448]{2,1,0:T(8,128)(2,1)S(1)}, bf16[2,32,448]{2,1,0:T(8,128)(2,1)S(1)}, u32[]{:S(2)}, u32[]{:S(2)}) %collective-permute-start.7) | collective-permute-done | bytes 57376 | tf_op jit(solution)/shard_map/ppermute | solution.py:392
  46.0 1.6 %collective-permute-start.9 = (bf16[4,2,32,448]{3,2,1,0:T(8,128)(2,1)S(1)}, bf16[4,2,32,448]{3,2,1,0:T(8,128)(2,1)S(1)}, u32[]{:S(2)}, u32[]{:S(2)}) collective-permute-start(bf16[4,2,32,448]{3,2,1,0:T(8,128)(2,1)S(1)} %pad_maximum_fusion.refs_0_), channel_id=1, source_target_pairs={{0,2},{1,3},{2,0},{3,1},{4,6},{5,7},{6,4},{7,5},{8,10},{9,11},{10,... | collective-permute-start | bytes 688136 | tf_op jit(solution)/shard_map/ppermute | solution.py:392
  47.6 0.1 collective-permute-start.11
  47.7 0.5 collective-permute-start.10
  48.2 0.8 %collective-permute-done.11.refs_2_ = bf16[2,2,32,448]{3,2,1,0:T(8,128)(2,1)S(1)} collective-permute-done((bf16[2,2,32,448]{3,2,1,0:T(8,128)(2,1)S(1)}, bf16[2,2,32,448]{3,2,1,0:T(8,128)(2,1)S(1)}, u32[]{:S(2)}, u32[]{:S(2)}) %collective-permute-start.11) | collective-permute-done | bytes 114720 | tf_op jit(solution)/shard_map/ppermute | solution.py:392
  49.0 0.2 collective-permute-done.10.refs_1_
  49.2 0.0 copy-done
  49.2 0.0 copy-done.1
  49.2 2.8 %early.1.refs_2_ = f32[2,2048,768]{2,1,0:T(8,128)S(1)} custom-call(s32[2]{0:T(128)S(1)} %pad_add_fusion.place_ref, bf16[2,2,2048,256]{3,2,1,0:T(8,128)(2,1)S(1)} %copy-done, bf16[448,768]{1,0:T(8,128)(2,1)S(1)} %bitcast.12, bf16[4,2,32,448]{3,2,1,0:T(8,128)(2,1)S(1)} %pad_maximum_fusion.refs_0_, bf16[2,2,32,448]{3,2,1,0:T(8,128)(2,1)S(1)} %collective-permute-done.10.refs_1_, ...), custom_call_target="tpu_custom_call" | custom-call | flops 1000 | bytes 1000 | tf_op jit(solution)/shard_map/early/pallas_call | solution.py:333
  52.0 0.4 collective-permute-done.9.refs_0_
  52.4 0.0 collective-permute-start.12
  52.4 1.5 %collective-permute-done.12.refs_1_ = bf16[4,2,32,448]{3,2,1,0:T(8,128)(2,1)S(1)} collective-permute-done((bf16[4,2,32,448]{3,2,1,0:T(8,128)(2,1)S(1)}, bf16[4,2,32,448]{3,2,1,0:T(8,128)(2,1)S(1)}, u32[]{:S(2)}, u32[]{:S(2)}) %collective-permute-start.12) | collective-permute-done | bytes 229408 | tf_op jit(solution)/shard_map/ppermute | solution.py:392
  53.9 4.5 %late.1 = bf16[2,2048,768]{2,1,0:T(8,128)(2,1)} custom-call(s32[2]{0:T(128)S(1)} %pad_add_fusion.place_ref, bf16[2,2,2048,256]{3,2,1,0:T(8,128)(2,1)S(1)} %copy-done, bf16[448,768]{1,0:T(8,128)(2,1)S(1)} %bitcast.13, bf16[4,2,32,448]{3,2,1,0:T(8,128)(2,1)S(1)} %collective-permute-done.9.refs_0_, bf16[4,2,32,448]{3,2,1,0:T(8,128)(2,1)S(1)} %collective-permute-done.12.refs_1_, ...), custom_call_target="tpu_custom_call" | custom-call | flops 1962934272 | bytes 8388608 | tf_op jit(solution)/shard_map/late/pallas_call | solution.py:343
  (5 shorter events, 0.1 us)
Async XLA Ops:
  7.2 2.1 %collective-permute-start = (bf16[2,4,2,32,448]{4,3,2,1,0:T(8,128)(2,1)S(1)}, bf16[2,4,2,32,448]{4,3,2,1,0:T(8,128)(2,1)S(1)}, u32[]{:S(2)}, u32[]{:S(2)}) collective-permute-start(bf16[2,4,2,32,448]{4,3,2,1,0:T(8,128)(2,1)S(1)} %get-tuple-element.16.after_ref), channel_id=1, source_target_pairs={{0,1},{1,0},{2,3},{3,2},{4,5},{5,4},{6,7},{7,6},{8,9},{9,8},{10,11... | collective-permute-start | bytes 1376264 | tf_op jit(solution)/shard_map/ppermute | solution.py:392
  9.4 8.6 %collective-permute-start.2 = (bf16[3,2,32,448]{3,2,1,0:T(8,128)(2,1)S(1)}, bf16[3,2,32,448]{3,2,1,0:T(8,128)(2,1)S(1)}, u32[]{:S(2)}, u32[]{:S(2)}) collective-permute-start(bf16[3,2,32,448]{3,2,1,0:T(8,128)(2,1)S(1)} %get-tuple-element.19.after_ref), channel_id=1, source_target_pairs={{0,2},{1,3},{2,0},{3,1},{4,6},{5,7},{6,4},{7,5},{8,10},{9,11},{10,... | collective-permute-start | bytes 516104 | tf_op jit(solution)/shard_map/ppermute | solution.py:392
  12.3 13.6 %collective-permute-start.1 = (bf16[1,2,32,448]{3,2,1,0:T(8,128)(2,1)S(1)}, bf16[1,2,32,448]{3,2,1,0:T(8,128)(2,1)S(1)}, u32[]{:S(2)}, u32[]{:S(2)}) collective-permute-start(bf16[1,2,32,448]{3,2,1,0:T(8,128)(2,1)S(1)} %get-tuple-element.18), channel_id=1, source_target_pairs={{0,2},{1,3},{2,0},{3,1},{4,6},{5,7},{6,4},{7,5},{8,10},{9,11},{10,... | collective-permute-start | bytes 172040 | tf_op jit(solution)/shard_map/ppermute | solution.py:392
  18.0 7.9 %collective-permute-start.4 = (bf16[1,2,32,448]{3,2,1,0:T(8,128)(2,1)S(1)}, bf16[1,2,32,448]{3,2,1,0:T(8,128)(2,1)S(1)}, u32[]{:S(2)}, u32[]{:S(2)}) collective-permute-start(bf16[1,2,32,448]{3,2,1,0:T(8,128)(2,1)S(1)} %get-tuple-element.21), channel_id=1, source_target_pairs={{0,8},{1,9},{2,10},{3,11},{4,12},{5,13},{6,14},{7,15},{8,0},{9,1},... | collective-permute-start | bytes 172040 | tf_op jit(solution)/shard_map/ppermute | solution.py:392
  21.1 6.2 %collective-permute-start.5 = (bf16[1,2,32,448]{3,2,1,0:T(8,128)(2,1)S(1)}, bf16[1,2,32,448]{3,2,1,0:T(8,128)(2,1)S(1)}, u32[]{:S(2)}, u32[]{:S(2)}) collective-permute-start(bf16[1,2,32,448]{3,2,1,0:T(8,128)(2,1)S(1)} %get-tuple-element.22), channel_id=1, source_target_pairs={{0,12},{1,13},{2,14},{3,15},{4,8},{5,9},{6,10},{7,11},{8,4},{9,5},... | collective-permute-start | bytes 172040 | tf_op jit(solution)/shard_map/ppermute | solution.py:392
  22.5 5.0 %collective-permute-start.3 = (bf16[1,2,32,448]{3,2,1,0:T(8,128)(2,1)S(1)}, bf16[1,2,32,448]{3,2,1,0:T(8,128)(2,1)S(1)}, u32[]{:S(2)}, u32[]{:S(2)}) collective-permute-start(bf16[1,2,32,448]{3,2,1,0:T(8,128)(2,1)S(1)} %get-tuple-element.20.after_ref), channel_id=1, source_target_pairs={{0,4},{1,5},{2,6},{3,7},{4,0},{5,1},{6,2},{7,3},{8,12},{9,13},{10,... | collective-permute-start | bytes 172040 | tf_op jit(solution)/shard_map/ppermute | solution.py:392
  25.9 23.3 %copy-start = (bf16[2,2,2048,256]{3,2,1,0:T(8,128)(2,1)S(1)}, bf16[2,2,2048,256]{3,2,1,0:T(8,128)(2,1)}, u32[]{:S(2)}) copy-start(bf16[2,2,2048,256]{3,2,1,0:T(8,128)(2,1)} %constant.33.clone.table_ref) | copy-start | bytes 12582916
  25.9 23.3 %copy-start.1 = (bf16[768,448]{0,1:T(8,128)(2,1)S(1)}, bf16[768,448]{0,1:T(8,128)(2,1)}, u32[]{:S(2)}) copy-start(bf16[768,448]{0,1:T(8,128)(2,1)} %param.6) | copy-start | bytes 2064388
  37.2 4.3 %collective-permute-start.6 = (bf16[2,32,448]{2,1,0:T(8,128)(2,1)S(1)}, bf16[2,32,448]{2,1,0:T(8,128)(2,1)S(1)}, u32[]{:S(2)}, u32[]{:S(2)}) collective-permute-start(bf16[2,32,448]{2,1,0:T(8,128)(2,1)S(1)} %respond.1), channel_id=1, source_target_pairs={{0,4},{1,5},{2,6},{3,7},{4,0},{5,1},{6,2},{7,3},{8,12},{9,13},{10,... | collective-permute-start | bytes 172040 | tf_op jit(solution)/shard_map/ppermute | solution.py:392
  37.6 6.2 %collective-permute-start.8 = (bf16[2,32,448]{2,1,0:T(8,128)(2,1)S(1)}, bf16[2,32,448]{2,1,0:T(8,128)(2,1)S(1)}, u32[]{:S(2)}, u32[]{:S(2)}) collective-permute-start(bf16[2,32,448]{2,1,0:T(8,128)(2,1)S(1)} %respond.1), channel_id=1, source_target_pairs={{0,12},{1,13},{2,14},{3,15},{4,8},{5,9},{6,10},{7,11},{8,4},{9,5},... | collective-permute-start | bytes 172040 | tf_op jit(solution)/shard_map/ppermute | solution.py:392
  40.1 5.8 %collective-permute-start.7 = (bf16[2,32,448]{2,1,0:T(8,128)(2,1)S(1)}, bf16[2,32,448]{2,1,0:T(8,128)(2,1)S(1)}, u32[]{:S(2)}, u32[]{:S(2)}) collective-permute-start(bf16[2,32,448]{2,1,0:T(8,128)(2,1)S(1)} %respond.1), channel_id=1, source_target_pairs={{0,8},{1,9},{2,10},{3,11},{4,12},{5,13},{6,14},{7,15},{8,0},{9,1},... | collective-permute-start | bytes 172040 | tf_op jit(solution)/shard_map/ppermute | solution.py:392
  46.0 6.4 %collective-permute-start.9 = (bf16[4,2,32,448]{3,2,1,0:T(8,128)(2,1)S(1)}, bf16[4,2,32,448]{3,2,1,0:T(8,128)(2,1)S(1)}, u32[]{:S(2)}, u32[]{:S(2)}) collective-permute-start(bf16[4,2,32,448]{3,2,1,0:T(8,128)(2,1)S(1)} %pad_maximum_fusion.refs_0_), channel_id=1, source_target_pairs={{0,2},{1,3},{2,0},{3,1},{4,6},{5,7},{6,4},{7,5},{8,10},{9,11},{10,... | collective-permute-start | bytes 688136 | tf_op jit(solution)/shard_map/ppermute | solution.py:392
  47.6 1.4 %collective-permute-start.11 = (bf16[2,2,32,448]{3,2,1,0:T(8,128)(2,1)S(1)}, bf16[2,2,32,448]{3,2,1,0:T(8,128)(2,1)S(1)}, u32[]{:S(2)}, u32[]{:S(2)}) collective-permute-start(bf16[2,2,32,448]{3,2,1,0:T(8,128)(2,1)S(1)} %pad_maximum_fusion.2), channel_id=1, source_target_pairs={{0,1},{1,0},{2,3},{3,2},{4,5},{5,4},{6,7},{7,6},{8,9},{9,8},{10,11... | collective-permute-start | bytes 344072 | tf_op jit(solution)/shard_map/ppermute | solution.py:392
  47.7 1.5 %collective-permute-start.10 = (bf16[2,2,32,448]{3,2,1,0:T(8,128)(2,1)S(1)}, bf16[2,2,32,448]{3,2,1,0:T(8,128)(2,1)S(1)}, u32[]{:S(2)}, u32[]{:S(2)}) collective-permute-start(bf16[2,2,32,448]{3,2,1,0:T(8,128)(2,1)S(1)} %pad_maximum_fusion.1), channel_id=1, source_target_pairs={{0,1},{1,0},{2,3},{3,2},{4,5},{5,4},{6,7},{7,6},{8,9},{9,8},{10,11... | collective-permute-start | bytes 344072 | tf_op jit(solution)/shard_map/ppermute | solution.py:392
  52.4 1.5 %collective-permute-start.12 = (bf16[4,2,32,448]{3,2,1,0:T(8,128)(2,1)S(1)}, bf16[4,2,32,448]{3,2,1,0:T(8,128)(2,1)S(1)}, u32[]{:S(2)}, u32[]{:S(2)}) collective-permute-start(bf16[4,2,32,448]{3,2,1,0:T(8,128)(2,1)S(1)} %collective-permute-done.9.refs_0_), channel_id=1, source_target_pairs={{0,1},{1,0},{2,3},{3,2},{4,5},{5,4},{6,7},{7,6},{8,9},{9,8},{10,11... | collective-permute-start | bytes 688136 | tf_op jit(solution)/shard_map/ppermute | solution.py:392
